TPU v7x, 32 devices: a whole 2x2x4 slice. The times are simulated.
32 devices in a mesh: ens: 2 (over x), tile: 16 (over z, y, core).
Axes of the slice: x: 2, y: 2, z: 4, core: 2. Of those that a mesh axis runs over, the one named last changes fastest.
Arguments:
- rain: bfloat16 [8192, 256], P(('ens', 'tile')), parts along dimension 0, may hold values from 0.049804688 to 8
- soil: float32 [8192], P(('ens', 'tile')), parts along dimension 0, may hold values from 0.5 to 4
- tile_area: float32 [8192], P(('ens', 'tile')), parts along dimension 0, may hold values from 0.25 to 2
- tile_dest: int32 [8192, 1], P(('ens', 'tile')), parts along dimension 0, may hold values from 0 to 15; in each aligned block of 256 rows (0 to 255, 256 to 511, ...) at most 32 rows name the same one
- tile_reach: int32 [8192], P(('ens', 'tile')), parts along dimension 0, may hold values from 0 to 255
- reach_basin: int32 [8192], P(('ens', 'tile')), parts along dimension 0, may hold values from 0 to 31
- reach_kind: int32 [8192], P(('ens', 'tile')), parts along dimension 0, may hold values from 0 to 7
- reach_lag: int32 [8192], P(('ens', 'tile')), parts along dimension 0, may hold values from 0 to 72
- irf: float32 [8, 48], replicated, may hold values from 0.004166667 to 0.041666668
- outlet_level: int32 [1024], P(('ens', 'tile')), parts along dimension 0, may hold values from 0 to 2, as said below
- outlet_parent: int32 [1024], P(('ens', 'tile')), parts along dimension 0, may hold values from -1 to 511, as said below
Outputs:
- section: float32 [1024, 256], P(('ens', 'tile')), parts along dimension 0
There are 2 independent parts, one for each index of `ens`. A program takes and returns all parts, laid end to end along the dimension named above; an argument that names none is the same for every part. Nothing has to cross between parts.
Inputs may be any that keep to these rules, and one draw needn't show every extreme that they name: `tile_dest`: among the rows of one device, at most 32 name the same owner. `outlet_level`: on every device, half of the 32 outlets have level 0, a quarter level 1 and a quarter level 2. `outlet_parent`: an outlet of level 0 drains to an outlet of level 1, one of level 1 to one of level 2, and one of level 2 has -1. Of the outlets of one level on one device, at most 2 drain to outlets of one device; for each of the levels 0 and 1 some device receives exactly 2 from every device.
All inputs are finite; a program needn't handle non-finite values.
Results may differ from a plain program's by a relative error of at most 0.0003.
Values may be sent and summed in bfloat16 or wider, within the bound.
No kernel may reach another device: no remote copies, remote signals or barrier semaphores. Data moves between devices by JAX's collectives and lax.ppermute only.
A program may use at most 64 MiB of HBM per device.

v0:
```python
import jax
import jax.numpy as jnp
from jax import lax
from jax.sharding import PartitionSpec as P

LINK = 6


PRECISE = lax.Precision.HIGHEST


def delayed(values, delay):
    padding = jnp.zeros(values.shape[:-1] + (delay,), values.dtype)
    return jnp.concatenate([padding, values[..., : values.shape[-1] - delay]], axis=-1)


def slot_ranks(target, valid, owners):
    hits = jnp.logical_and(
        target[:, None] == jnp.arange(owners, dtype=jnp.int32)[None, :], valid[:, None]
    ).astype(jnp.int32)
    before = jnp.cumsum(hits, axis=0) - hits
    return jnp.sum(before * hits, axis=1)


def lag_rows(inflow, reach_lag):
    reach_rows, hour_count = inflow.shape
    block_hours = 128
    blocks = hour_count // block_hours
    group_rows = 64
    groups = reach_rows // group_rows
    spans = jnp.concatenate([jnp.zeros((reach_rows, block_hours), jnp.float32), inflow], axis=1)
    windows = jnp.stack(
        [spans[:, j * block_hours : j * block_hours + 2 * block_hours] for j in range(blocks)],
        axis=1,
    )
    windows = windows.reshape(groups, group_rows, blocks, 2 * block_hours)
    lag_groups = reach_lag.reshape(groups, group_rows)
    hour_within = jnp.arange(block_hours, dtype=jnp.int32)
    source_within = jnp.arange(2 * block_hours, dtype=jnp.int32)

    def one_group(pieces):
        window_rows, lag_values = pieces
        marks = (
            source_within[None, None, :]
            == hour_within[None, :, None] + block_hours - lag_values[:, None, None]
        ).astype(jnp.float32)
        return jnp.einsum("rjs,rus->rju", window_rows, marks, precision=PRECISE)

    shifted = lax.map(one_group, (windows, lag_groups))
    return shifted.reshape(reach_rows, hour_count)


def per_device(
    rain,
    soil,
    tile_area,
    tile_dest,
    tile_reach,
    reach_basin,
    reach_kind,
    reach_lag,
    irf,
    outlet_level,
    outlet_parent,
):
    owners = lax.axis_size("tile")
    position = lax.axis_index("tile")
    tile_rows, hour_count = rain.shape
    reach_rows = reach_basin.shape[0]
    basin_rows = outlet_level.shape[0]
    kind_count, tap_count = irf.shape
    slot_width = 2 * tile_rows // owners
    rainfall = rain.astype(jnp.float32)
    storage = soil[:, None]
    excess = jnp.maximum(rainfall - 0.2 * storage, 0.0)
    runoff_rows = (tile_area[:, None] * excess * excess / (rainfall + 0.8 * storage)).astype(
        jnp.bfloat16
    )
    target = tile_dest[:, 0]
    slot_rank = slot_ranks(target, target >= 0, owners)
    slot_index = target * slot_width + slot_rank
    placement = slot_index[:, None] == jnp.arange(owners * slot_width, dtype=jnp.int32)[None, :]
    outgoing = lax.dot_general(
        placement.astype(jnp.bfloat16),
        runoff_rows,
        (((0,), (0,)), ((), ())),
        preferred_element_type=jnp.float32,
    ).astype(jnp.bfloat16)
    labels = jnp.sum(jnp.where(placement, tile_reach[:, None] + 1, 0), axis=0) - 1
    arrived, arrived_reach = (
        lax.all_to_all(
            outgoing.reshape(owners, slot_width, hour_count),
            "tile",
            split_axis=0,
            concat_axis=0,
            tiled=True,
        ),
        lax.all_to_all(
            labels.reshape(owners, slot_width), "tile", split_axis=0, concat_axis=0, tiled=True
        ),
    )
    arrived = arrived.reshape(owners * slot_width, hour_count)
    arrived_reach = arrived_reach.reshape(owners * slot_width)
    collect = (jnp.arange(reach_rows, dtype=jnp.int32)[:, None] == arrived_reach[None, :]).astype(
        jnp.bfloat16
    )
    inflow = jnp.dot(collect, arrived, preferred_element_type=jnp.float32)
    lagged = lag_rows(inflow, reach_lag)
    group_index = reach_basin * kind_count + reach_kind
    pool_map = (
        jnp.arange(basin_rows * kind_count, dtype=jnp.int32)[:, None] == group_index[None, :]
    ).astype(jnp.float32)
    pooled = jnp.dot(pool_map, lagged, precision=PRECISE, preferred_element_type=jnp.float32)
    block_hours = 128
    blocks = hour_count // block_hours
    pooled = pooled.reshape(basin_rows, kind_count, blocks, block_hours)
    offset = (
        jnp.arange(block_hours, dtype=jnp.int32)[None, :]
        - jnp.arange(block_hours, dtype=jnp.int32)[:, None]
    )
    tap_index = jnp.arange(tap_count, dtype=jnp.int32)

    def toeplitz(shift_hours):
        tap_marks = (offset[None, :, :] + shift_hours == tap_index[:, None, None]).astype(
            jnp.float32
        )
        return jnp.einsum("ks,sut->kut", irf, tap_marks, precision=PRECISE)

    outflow = jnp.einsum("bkju,kut->bjt", pooled, toeplitz(0), precision=PRECISE)
    earlier = jnp.concatenate([jnp.zeros_like(pooled[:, :, :1]), pooled[:, :, :-1]], axis=2)
    outflow = outflow + jnp.einsum(
        "bkju,kut->bjt", earlier, toeplitz(block_hours), precision=PRECISE
    )
    outflow = outflow.reshape(basin_rows, hour_count)
    own_ids = jnp.arange(basin_rows, dtype=jnp.int32) + position * basin_rows
    for tree_level in range(2):
        chosen = outlet_level == tree_level
        moving = jnp.where(chosen[:, None], delayed(outflow, LINK), 0.0)
        level_count = basin_rows // 2 if tree_level == 0 else basin_rows // 4
        level_rank = jnp.cumsum(chosen.astype(jnp.int32)) - 1
        selector = jnp.logical_and(
            level_rank[None, :] == jnp.arange(level_count, dtype=jnp.int32)[:, None],
            chosen[None, :],
        )
        level_rows = jnp.dot(
            selector.astype(jnp.float32),
            moving,
            precision=PRECISE,
            preferred_element_type=jnp.float32,
        )
        parents = jnp.sum(jnp.where(selector, outlet_parent[None, :], 0), axis=1)
        sink_map = (
            own_ids[:, None] == lax.all_gather(parents, "tile", axis=0, tiled=True)[None, :]
        ).astype(jnp.float32)
        outflow = outflow + jnp.dot(
            sink_map,
            lax.all_gather(level_rows, "tile", axis=0, tiled=True),
            precision=PRECISE,
            preferred_element_type=jnp.float32,
        )
    return jnp.log(1.0 + outflow)


def solution(mesh):
    in_specs = (
        P(("ens", "tile"), None),
        P(("ens", "tile")),
        P(("ens", "tile")),
        P(("ens", "tile"), None),
        P(("ens", "tile")),
        P(("ens", "tile")),
        P(("ens", "tile")),
        P(("ens", "tile")),
        P(),
        P(("ens", "tile")),
        P(("ens", "tile")),
    )
    out_specs = P(("ens", "tile"), None)
    return jax.shard_map(
        per_device, mesh=mesh, in_specs=in_specs, out_specs=out_specs, check_vma=False
    )
```

profile of v0, /device:TPU:0, one launch (start us, length us, event | category | flops | bytes accessed | tf_op | source)
XLA Modules:
  0.0 103.9 jit_solution(4053725663019606936)
XLA Ops:
  0.0 0.7 compare_reduce_fusion
  0.7 0.7 fusion.56
  2.2 0.8 fusion.47
  3.0 0.7 multiply_add_fusion.1
  4.5 0.7 sub.75
  5.2 7.4 %all-to-all-start = ((s32[16,1,32]{2,1,0:T(1,128)}), s32[16,1,32]{2,1,0:T(1,128)S(1)}, u32[]{:S(2)}, u32[]{:S(2)}) async-start(s32[16,1,32]{2,1,0:T(1,128)} %sub.75), calls=%async_computation | async-start | bytes 16384 | tf_op jit(solution)/shard_map/all_to_all | solution.py:98
  12.6 0.7 broadcast_multiply_fusion.1
  14.5 0.8 select_reduce_fusion.1
  15.3 2.1 %convolution_convert_fusion = bf16[512,256]{1,0:T(8,128)(2,1)} fusion(s32[256]{0:T(256)S(1)} %bitcast.117, bf16[256,256]{1,0:T(8,128)(2,1)} %param.13, f32[256]{0:T(256)S(1)} %get-tuple-element.60, f32[256]{0:T(256)S(1)} %get-tuple-element.59, f32[256]{0:T(256)} %param.15), kind=kOutput, calls=%fused_computation.22 | convolution fusion | flops 67895296 | bytes 397312 | tf_op jit(solution)/shard_map/dot_general | solution.py:83
  17.5 1.4 %all-to-all-done = s32[16,1,32]{2,1,0:T(1,128)S(1)} async-done(((s32[16,1,32]{2,1,0:T(1,128)}), s32[16,1,32]{2,1,0:T(1,128)S(1)}, u32[]{:S(2)}, u32[]{:S(2)}) %all-to-all-start) | async-done | bytes 2080 | tf_op jit(solution)/shard_map/all_to_all | solution.py:98
  18.9 4.6 %all-to-all-start.1 = ((bf16[16,32,256]{2,1,0:T(8,128)(2,1)}), bf16[16,32,256]{2,1,0:T(8,128)(2,1)S(1)}, u32[]{:S(2)}, u32[]{:S(2)}) async-start(bf16[16,32,256]{2,1,0:T(8,128)(2,1)} %bitcast.7), calls=%async_computation.1 | async-start | bytes 524288 | tf_op jit(solution)/shard_map/all_to_all | solution.py:91
  26.0 12.4 %all-reduce.6 = (s32[256]{0:T(256)S(1)}, s32[128]{0:T(128)S(1)}) all-reduce(s32[256]{0:T(256)S(1)} %dynamic-update-slice, s32[128]{0:T(128)S(1)} %dynamic-update-slice.1), channel_id=1, replica_groups=mesh['ens'=2,'tile'=16] {'tile'}, use_global_device_ids=true, to_apply=%add.4 | all-reduce | flops 384 | bytes 3072
  38.4 1.1 %fusion.17 = f32[8,128,128,1]{2,0,1,3:T(8,128)S(1)} fusion(s32[128,128]{1,0:T(8,128)S(1)} %iota_subtract_fusion, f32[8,48]{1,0:T(8,128)S(1)} %copy-done), kind=kOutput, calls=%fused_computation.21 | convolution fusion | flops 76283904 | bytes 591360 | tf_op jit(solution)/shard_map/ks,sut->kut/dot_general | solution.py:127
  39.4 1.1 %fusion.16 = f32[8,128,128,1]{2,0,1,3:T(8,128)S(1)} fusion(s32[128,128]{1,0:T(8,128)S(1)} %broadcast_add_fusion, f32[8,48]{1,0:T(8,128)S(1)} %copy-done), kind=kOutput, calls=%fused_computation.20 | convolution fusion | flops 76283904 | bytes 591360 | tf_op jit(solution)/shard_map/ks,sut->kut/dot_general | solution.py:127
  43.1 17.8 %while.11 = (s32[]{:T(128)}, f32[4,64,2,128]{3,2,1,0:T(2,128)S(1)}, f32[4,64,2,256]{3,2,1,0:T(2,128)S(1)}, s32[4,64]{1,0:T(4,128)S(1)}, s32[]{:T(128)}) while((s32[]{:T(128)}, f32[4,64,2,128]{3,2,1,0:T(2,128)S(1)}, f32[4,64,2,256]{3,2,1,0:T(2,128)S(1)}, s32[4,64]{1,0:T(4,128)S(1)}, s32[]{:T(128)}) %tuple.25), condition=%wide.region_5.6_spmd.clone, body=%wide.region_4.5_spmd.clone.sunk | while | flops 52437120 | bytes 265025 | solution.py:49
  43.2 4.4 %fusion.86 = f32[4,64,2,128]{3,2,1,0:T(2,128)S(1)} fusion(f32[4,64,2,128]{3,2,1,0:T(2,128)S(1)} %get-tuple-element.96, s32[]{:T(128)} %get-tuple-element.95, s32[64,128]{1,0:T(8,128)S(1)} %broadcast_subtract_fusion.2, f32[4,64,2,256]{3,2,1,0:T(2,128)S(1)} %get-tuple-element.102), kind=kOutput, calls=%fused_computation.6.clone.1 | convolution fusion | flops 52428800 | bytes 230400 | tf_op jit(solution)/shard_map/while/body/eval_jaxpr/rjs,rus->rju/dot_general | solution.py:47
  47.7 4.4 %fusion.86 = f32[4,64,2,128]{3,2,1,0:T(2,128)S(1)} fusion(f32[4,64,2,128]{3,2,1,0:T(2,128)S(1)} %get-tuple-element.96, s32[]{:T(128)} %get-tuple-element.95, s32[64,128]{1,0:T(8,128)S(1)} %broadcast_subtract_fusion.2, f32[4,64,2,256]{3,2,1,0:T(2,128)S(1)} %get-tuple-element.102), kind=kOutput, calls=%fused_computation.6.clone.1 | convolution fusion | flops 52428800 | bytes 230400 | tf_op jit(solution)/shard_map/while/body/eval_jaxpr/rjs,rus->rju/dot_general | solution.py:47
  52.1 4.4 %fusion.86 = f32[4,64,2,128]{3,2,1,0:T(2,128)S(1)} fusion(f32[4,64,2,128]{3,2,1,0:T(2,128)S(1)} %get-tuple-element.96, s32[]{:T(128)} %get-tuple-element.95, s32[64,128]{1,0:T(8,128)S(1)} %broadcast_subtract_fusion.2, f32[4,64,2,256]{3,2,1,0:T(2,128)S(1)} %get-tuple-element.102), kind=kOutput, calls=%fused_computation.6.clone.1 | convolution fusion | flops 52428800 | bytes 230400 | tf_op jit(solution)/shard_map/while/body/eval_jaxpr/rjs,rus->rju/dot_general | solution.py:47
  56.6 4.4 %fusion.86 = f32[4,64,2,128]{3,2,1,0:T(2,128)S(1)} fusion(f32[4,64,2,128]{3,2,1,0:T(2,128)S(1)} %get-tuple-element.96, s32[]{:T(128)} %get-tuple-element.95, s32[64,128]{1,0:T(8,128)S(1)} %broadcast_subtract_fusion.2, f32[4,64,2,256]{3,2,1,0:T(2,128)S(1)} %get-tuple-element.102), kind=kOutput, calls=%fused_computation.6.clone.1 | convolution fusion | flops 52428800 | bytes 230400 | tf_op jit(solution)/shard_map/while/body/eval_jaxpr/rjs,rus->rju/dot_general | solution.py:47
  62.2 1.8 %convolution_bitcast_fusion = f32[32,2,128]{2,0,1:T(8,128)S(1)} fusion(f32[32,8,2,128]{0,1,3,2:T(8,128)S(1)} %copy.40, f32[8,128,128,1]{2,0,1,3:T(8,128)S(1)} %fusion.17), kind=kOutput, calls=%fused_computation.23 | convolution fusion | flops 100663296 | bytes 819200 | tf_op jit(solution)/shard_map/bkju,kut->bjt/dot_general | solution.py:129
  64.0 1.0 fusion.21
  65.2 18.7 %all_gather.13 = f32[256,256]{1,0:T(8,128)S(1)} all-gather(f32[16,256]{1,0:T(8,128)S(1)} %fusion.41), channel_id=1, replica_groups=mesh['ens'=2,'tile'=16] {'tile'}, dimensions={0}, use_global_device_ids=true | all-gather | bytes 278528 | tf_op jit(solution)/shard_map/all_gather | solution.py:157
  84.4 18.7 %all_gather.15 = f32[128,256]{1,0:T(8,128)S(1)} all-gather(f32[8,256]{1,0:T(8,128)S(1)} %fusion.38), channel_id=1, replica_groups=mesh['ens'=2,'tile'=16] {'tile'}, dimensions={0}, use_global_device_ids=true | all-gather | bytes 139264 | tf_op jit(solution)/shard_map/all_gather | solution.py:157
  103.1 0.8 fusion.19
  (70 shorter events, 8.8 us)
Async XLA Ops:
  0.0 38.4 %copy-start = (f32[8,48]{1,0:T(8,128)S(1)}, f32[8,48]{1,0:T(8,128)}, u32[]{:S(2)}) copy-start(f32[8,48]{1,0:T(8,128)} %param.21) | copy-start | bytes 4612
  0.0 17.4 %copy-start.1 = (s32[32]{0:T(128)S(1)}, s32[32]{0:T(128)}, u32[]{:S(2)}) copy-start(s32[32]{0:T(128)} %param.23) | copy-start | bytes 388
  5.2 13.7 %all-to-all-start = ((s32[16,1,32]{2,1,0:T(1,128)}), s32[16,1,32]{2,1,0:T(1,128)S(1)}, u32[]{:S(2)}, u32[]{:S(2)}) async-start(s32[16,1,32]{2,1,0:T(1,128)} %sub.75), calls=%async_computation | async-start | bytes 16384 | tf_op jit(solution)/shard_map/all_to_all | solution.py:98
  15.3 8.3 %copy-start.2 = (s32[256]{0:T(256)S(1)}, s32[256]{0:T(256)}, u32[]{:S(2)}) copy-start(s32[256]{0:T(256)} %param.20) | copy-start | bytes 3076
  15.3 8.4 %copy-start.5 = (u32[32]{0:T(128)S(1)}, u32[32]{0:T(128)}, u32[]{:S(2)}) copy-start(u32[32]{0:T(128)} %constant.68) | copy-start | bytes 388
  17.4 23.1 %copy-start.3 = (s32[256]{0:T(256)S(1)}, s32[256]{0:T(256)}, u32[]{:S(2)}) copy-start(s32[256]{0:T(256)} %param.19) | copy-start | bytes 3076
  17.4 23.1 %copy-start.4 = (s32[256]{0:T(256)S(1)}, s32[256]{0:T(256)}, u32[]{:S(2)}) copy-start(s32[256]{0:T(256)} %param.18) | copy-start | bytes 3076
  18.9 22.9 %all-to-all-start.1 = ((bf16[16,32,256]{2,1,0:T(8,128)(2,1)}), bf16[16,32,256]{2,1,0:T(8,128)(2,1)S(1)}, u32[]{:S(2)}, u32[]{:S(2)}) async-start(bf16[16,32,256]{2,1,0:T(8,128)(2,1)} %bitcast.7), calls=%async_computation.1 | async-start | bytes 524288 | tf_op jit(solution)/shard_map/all_to_all | solution.py:91
where the time goes:
time: 104 us
  blocking collectives  49.7 us (48%)
  matrix products  26.5 us (25%)
  starting transfers between devices  12 us (12%)
  other arithmetic  8.37 us (8%)
  local copies, waits for them, and re-layouts  4.21 us (4%)
  between operations  1.53 us (1%)
  waiting for transfers between devices  1.41 us (1%)
    all_gather x2, blocking collectives, per_device(): lax.all_gather(level_rows, 'tile', axis=0, tiled=True)  37.4 us
    dot_general x4, matrix products, one_group(): return jnp.einsum('rjs,rus->rju', window_rows, marks, precision=PRECISE)  17.4 us
    unnamed x1, blocking collectives  12.4 us
    all_to_all x1, starting transfers between devices, per_device(): lax.all_to_all(labels.reshape(owners, slot_width), 'tile', split_axis=0,...  7.39 us
    all_to_all x1, starting transfers between devices, per_device(): lax.all_to_all(outgoing.reshape(owners, slot_width, hour_count), 'tile',...  4.62 us
    dot_general x2, matrix products, toeplitz(): return jnp.einsum('ks,sut->kut', irf, tap_marks, precision=PRECISE)  2.12 us
    dot_general x1, matrix products, per_device(): lax.dot_general(placement.astype(jnp.bfloat16), runoff_rows, (((0,), (0,)...  2.09 us
  transfers between devices with their start and end apart: 2, of which 1 were waited for; matrix products, arithmetic and copies ran while one was open for 9% of the time, Pallas kernels for 0%

commit v1 on v0

v1 whole, which is shorter than its diff:
```python
import jax
import jax.numpy as jnp
from jax import lax
from jax.experimental import pallas as pl
from jax.experimental.pallas import tpu as pltpu
from jax.sharding import PartitionSpec as P

LINK = 6
LANES = 128
VMEM_BYTES = 40 * 1024 * 1024

NT = (((1,), (1,)), ((), ()))
NN = (((1,), (0,)), ((), ()))


def iota(shape, axis):
    return lax.broadcasted_iota(jnp.int32, shape, axis)


def split(values):
    high = values.astype(jnp.bfloat16)
    return high, (values - high.astype(jnp.float32)).astype(jnp.bfloat16)


def later(values, hours):
    rows = values.shape[0]
    if hours % 8 == 0:
        padding = jnp.zeros((hours, values.shape[1]), values.dtype)
        return jnp.concatenate([padding, values[: rows - hours]], axis=0)
    return jnp.where(iota(values.shape, 0) < hours, 0.0, pltpu.roll(values, hours, 0))


def prepare_kernel(rain_ref, soil_ref, area_ref, irf_ref, runoff_ref, response_ref):
    hours = rain_ref.shape[1]
    kinds, taps = irf_ref.shape
    rainfall = rain_ref[...].astype(jnp.float32).T
    storage = soil_ref[...]
    excess = jnp.maximum(rainfall - 0.2 * storage, 0.0)
    runoff = area_ref[...] * excess * excess / (rainfall + 0.8 * storage)
    runoff_ref[...] = runoff.astype(jnp.bfloat16).astype(jnp.float32)
    backward = (
        iota((taps, hours), 1) == lax.rem(hours - iota((taps, hours), 0), hours)
    ).astype(jnp.float32)
    reversed_taps = lax.dot_general(
        irf_ref[...], backward, NN, precision=lax.Precision.HIGHEST, preferred_element_type=jnp.float32
    )
    causal = iota((hours, hours), 1) <= iota((hours, hours), 0)
    for kind in range(kinds):
        row = jnp.broadcast_to(reversed_taps[kind : kind + 1], (hours, hours))
        matrix = jnp.where(causal, pltpu.roll(row, 0, 1, stride=1, stride_axis=0), 0.0)
        high, low = split(matrix)
        response_ref[:hours, kind * hours : (kind + 1) * hours] = high
        response_ref[hours:, kind * hours : (kind + 1) * hours] = low


def route_kernel(
    runoff_ref, response_ref, meta_ref, dest_ref, reach_ref, flow_ref, *, kinds, reach_rows, basin_rows
):
    hours, tiles = runoff_ref.shape
    owners = meta_ref.shape[0]
    outlets = owners * basin_rows
    shift = basin_rows.bit_length() - 1
    dest = dest_ref[...]
    reach = reach_ref[...]

    def table(first, count):
        return jnp.concatenate([meta_ref[:, first + j, :] for j in range(count)], axis=1)

    spans = reach_rows // LANES
    basin_table = table(0, spans)
    kind_table = table(spans, spans)
    lag_table = table(2 * spans, spans)
    parent_table = meta_ref[:, 3 * spans, :]
    group_table = basin_table * kinds + kind_table
    reach_table = (
        jnp.concatenate([group_table, lag_table], axis=1).astype(jnp.float32).T.astype(jnp.bfloat16)
    )
    tree_table = jnp.concatenate(
        [lax.shift_right_arithmetic(parent_table, shift) + 1, parent_table & (basin_rows - 1)], axis=1
    )
    tree_table = tree_table.astype(jnp.float32).T.astype(jnp.bfloat16)

    def marks(row, count, offset=0):
        return (iota((count, tiles), 0) + offset == row).astype(jnp.float32).astype(jnp.bfloat16)

    def picked(values, chosen):
        return jnp.sum(jnp.where(chosen, values, 0.0), axis=0, keepdims=True).astype(jnp.int32)

    def lookup(table_rows, mark):
        return lax.dot_general(table_rows, mark, NN, preferred_element_type=jnp.float32)

    owner_marks = marks(dest, owners)
    by_reach = lookup(reach_table, owner_marks)
    at_reach = iota((reach_rows, tiles), 0) == reach
    group = picked(by_reach[:reach_rows], at_reach)
    lag = picked(by_reach[reach_rows:], at_reach)
    basin = group // kinds
    kind = group - basin * kinds

    def parent_of(owner_mark, local):
        by_basin = lookup(tree_table, owner_mark)
        at_basin = iota((basin_rows, tiles), 0) == local
        return (
            picked(by_basin[:basin_rows], at_basin),
            picked(by_basin[LANES : LANES + basin_rows], at_basin),
        )

    parent_owner, parent_local = parent_of(owner_marks, basin)
    second_owner, second_local = parent_of(marks(parent_owner, owners, 1), parent_local)
    targets = [
        dest * basin_rows + basin,
        (parent_owner - 1) * basin_rows + parent_local,
        (second_owner - 1) * basin_rows + second_local,
    ]

    lagged = runoff_ref[...]
    step = 64
    while step:
        lagged = jnp.where((lag & step) != 0, later(lagged, step), lagged)
        step //= 2
    lagged = lagged.astype(jnp.bfloat16)
    by_kind = jnp.concatenate(
        [
            lagged * (kind == k).astype(jnp.float32).astype(jnp.bfloat16)
            for k in range(kinds)
        ],
        axis=0,
    )
    routed = lax.dot_general(response_ref[...], by_kind, NN, preferred_element_type=jnp.float32)
    routed = routed[:hours] + routed[hours:]
    pieces, placements = [], []
    for target in targets:
        pieces.extend(split(routed))
        mark = marks(target, outlets)
        placements.extend([mark, mark])
        routed = later(routed, LINK)
    flow_ref[...] = lax.dot_general(
        jnp.concatenate(placements, axis=1),
        jnp.concatenate(pieces, axis=1),
        NT,
        preferred_element_type=jnp.float32,
    )


def finish_kernel(parts_ref, section_ref):
    section_ref[...] = jnp.log(1.0 + jnp.sum(parts_ref[...], axis=0))


def per_device(
    rain,
    soil,
    tile_area,
    tile_dest,
    tile_reach,
    reach_basin,
    reach_kind,
    reach_lag,
    irf,
    outlet_level,
    outlet_parent,
):
    owners = lax.axis_size("tile")
    tile_rows, hours = rain.shape
    basin_rows = outlet_parent.shape[0]
    kinds = irf.shape[0]
    params = pltpu.CompilerParams(vmem_limit_bytes=VMEM_BYTES)

    meta = jnp.concatenate(
        [
            reach_basin,
            reach_kind,
            reach_lag,
            outlet_parent,
            jnp.zeros((2 * LANES - basin_rows,), jnp.int32),
        ]
    ).reshape(-1, LANES)
    meta = lax.all_to_all(
        jnp.broadcast_to(meta[None], (owners,) + meta.shape), "tile", split_axis=0, concat_axis=0, tiled=True
    )

    runoff, response = pl.pallas_call(
        prepare_kernel,
        out_shape=(
            jax.ShapeDtypeStruct((hours, tile_rows), jnp.float32),
            jax.ShapeDtypeStruct((2 * hours, kinds * hours), jnp.bfloat16),
        ),
        compiler_params=params,
        name="prepare",
    )(rain, soil.reshape(1, -1), tile_area.reshape(1, -1), irf)

    flow = pl.pallas_call(
        lambda *refs: route_kernel(
            *refs, kinds=kinds, reach_rows=reach_basin.shape[0], basin_rows=basin_rows
        ),
        out_shape=jax.ShapeDtypeStruct((owners * basin_rows, hours), jnp.float32),
        compiler_params=params,
        name="route",
    )(runoff, response, meta, tile_dest.reshape(1, -1), tile_reach.reshape(1, -1))

    parts = lax.all_to_all(
        flow.reshape(owners, basin_rows, hours), "tile", split_axis=0, concat_axis=0, tiled=True
    )
    return pl.pallas_call(
        finish_kernel,
        out_shape=jax.ShapeDtypeStruct((basin_rows, hours), jnp.float32),
        compiler_params=params,
        name="finish",
    )(parts)


def solution(mesh):
    rows = P(("ens", "tile"))
    table = P(("ens", "tile"), None)
    in_specs = (table, rows, rows, table, rows, rows, rows, rows, P(), rows, rows)
    return jax.shard_map(
        per_device, mesh=mesh, in_specs=in_specs, out_specs=table, check_vma=False
    )
```

time: 104 us -> 37.7 us (0.36)
  blocking collectives: 49.7 us -> 17.1 us
  matrix products: 26.5 us -> 0 us
  other arithmetic: 8.37 us -> 0 us
  starting transfers between devices: 12 us -> 7.39 us
  Pallas kernels: 0 us -> 3.75 us
  waiting for transfers between devices: 1.41 us -> 3.38 us
  local copies, waits for them, and re-layouts: 4.21 us -> 5.73 us
  between operations: 1.53 us -> 0.04 us
    all_gather x2 -> x0, blocking collectives: 37.4 us -> none  [per_device(): lax.all_gather(level_rows, 'tile', axis=0, tiled=True)]
    dot_general x15 -> x0, matrix products: 26.5 us -> none  [the longest x4 17.4 us: one_group(): return jnp.einsum('rjs,rus->rju', window_rows, marks, precision=PRECISE)]
    all_to_all x0 -> x1, blocking collectives: none -> 17.1 us  [per_device(): lax.all_to_all(flow.reshape(owners, basin_rows, hours), 'tile', split_axi...]
    unnamed x1 -> x0, blocking collectives: 12.4 us -> none
    all_to_all x2 -> x1, starting transfers between devices: 12 us -> 7.39 us  [per_device(): lax.all_to_all(jnp.broadcast_to(meta[None], (owners,) + meta.shape), 'til...]
    pallas_call x0 -> x3, Pallas kernels: none -> 3.75 us  [the longest x1 2.55 us: per_device(): pl.pallas_call(lambda *refs: route_kernel(*refs, kinds=kinds, reach_rows=...]
    unnamed x19 -> x12, local copies, waits for them, and re-layouts: 1.34 us -> 4.3 us
    all_to_all x2 -> x1, waiting for transfers between devices: 1.41 us -> 3.38 us  [per_device(): lax.all_to_all(jnp.broadcast_to(meta[None], (owners,) + meta.shape), 'til...]
  transfers between devices with their start and end apart: 2 -> 1, of which waited for: 1 -> 1; matrix products, arithmetic and copies ran while one was open for 9% -> 0% of each run, Pallas kernels for 0% -> 1%
where the time goes in v1:
time: 37.7 us; the launch traced here: 37.4 us
  blocking collectives  17.1 us (45%)
  starting transfers between devices  7.39 us (20%)
  local copies, waits for them, and re-layouts  5.73 us (15%)
  Pallas kernels  3.75 us (10%)
  waiting for transfers between devices  3.38 us (9%)
    all_to_all x1, blocking collectives, per_device(): lax.all_to_all(flow.reshape(owners, basin_rows, hours), 'tile', split_axi...  17.1 us
    all_to_all x1, starting transfers between devices, per_device(): lax.all_to_all(jnp.broadcast_to(meta[None], (owners,) + meta.shape), 'til...  7.39 us
    unnamed x12, local copies, waits for them, and re-layouts  4.3 us
    all_to_all x1, waiting for transfers between devices, per_device(): lax.all_to_all(jnp.broadcast_to(meta[None], (owners,) + meta.shape), 'til...  3.38 us
    pallas_call x1, Pallas kernels, per_device(): pl.pallas_call(lambda *refs: route_kernel(*refs, kinds=kinds, reach_rows=...  2.55 us
    concatenate x1, local copies, waits for them, and re-layouts, per_device(): jnp.concatenate([reach_basin, reach_kind, reach_lag, outlet_parent, jnp.z...  0.79 us
  transfers between devices with their start and end apart: 1, of which 1 were waited for; matrix products, arithmetic and copies ran while one was open for 0% of the time, Pallas kernels for 1%

profile of v1, /device:TPU:0, one launch (start us, length us, event | category | flops | bytes accessed | tf_op | source)
XLA Modules:
  0.0 37.4 jit_solution(13089530820372329621)
XLA Ops:
  0.0 0.8 %concatenate.3 = s32[1024]{0:T(1024)S(1)} concatenate(s32[256]{0:T(256)} %param.16, s32[256]{0:T(256)} %param.17, s32[256]{0:T(256)} %param.18, s32[32]{0:T(128)} %param.20, s32[224]{0:T(256)S(1)} %broadcast_in_dim.10), dimensions={0} | concatenate | bytes 8192 | tf_op jit(solution)/shard_map/concatenate | solution.py:168
  0.8 0.6 %broadcast_in_dim.12 = s32[16,8,128]{2,1,0:T(8,128)} broadcast(s32[8,128]{1,0:T(8,128)S(1)} %bitcast.11), dimensions={1,2} | broadcast | bytes 69632 | tf_op jit(solution)/shard_map/broadcast_in_dim | solution.py:178
  1.4 7.4 %all-to-all-start = ((s32[16,8,128]{2,1,0:T(8,128)}), s32[16,8,128]{2,1,0:T(8,128)S(1)}, u32[]{:S(2)}, u32[]{:S(2)}) async-start(s32[16,8,128]{2,1,0:T(8,128)} %broadcast_in_dim.12), calls=%async_computation | async-start | bytes 131072 | tf_op jit(solution)/shard_map/all_to_all | solution.py:177
  8.8 0.0 copy-start
  8.8 0.9 %copy-done = bf16[256,256]{1,0:T(8,128)(2,1)S(1)} copy-done((bf16[256,256]{1,0:T(8,128)(2,1)S(1)}, bf16[256,256]{1,0:T(8,128)(2,1)}, u32[]{:S(2)}) %copy-start) | copy-done | bytes 131096
  9.7 0.0 copy-start.1
  9.7 0.7 %copy-done.1 = f32[8,48]{1,0:T(8,128)S(1)} copy-done((f32[8,48]{1,0:T(8,128)S(1)}, f32[8,48]{1,0:T(8,128)}, u32[]{:S(2)}) %copy-start.1) | copy-done | bytes 1560
  10.4 0.0 copy-start.4
  10.4 0.7 %copy-done.4 = f32[256]{0:T(256)S(1)} copy-done((f32[256]{0:T(256)S(1)}, f32[256]{0:T(256)}, u32[]{:S(2)}) %copy-start.4) | copy-done | bytes 1048
  11.1 0.0 copy-start.5
  11.1 0.7 %copy-done.5 = f32[256]{0:T(256)S(1)} copy-done((f32[256]{0:T(256)S(1)}, f32[256]{0:T(256)}, u32[]{:S(2)}) %copy-start.5) | copy-done | bytes 1048
  11.8 0.5 %prepare.1 = (f32[256,256]{1,0:T(8,128)S(1)}, bf16[512,2048]{1,0:T(8,128)(2,1)S(1)}) custom-call(bf16[256,256]{1,0:T(8,128)(2,1)S(1)} %copy-done, f32[1,256]{1,0:T(1,128)S(1)} %bitcast.9, f32[1,256]{1,0:T(1,128)S(1)} %bitcast.10, f32[8,48]{1,0:T(8,128)S(1)} %copy-done.1), custom_call_target="tpu_custom_call" | custom-call | tf_op jit(solution)/shard_map/prepare/pallas_call | solution.py:181
  12.3 3.4 %all-to-all-done.refs_2_ = s32[16,8,128]{2,1,0:T(8,128)S(1)} async-done(((s32[16,8,128]{2,1,0:T(8,128)}), s32[16,8,128]{2,1,0:T(8,128)S(1)}, u32[]{:S(2)}, u32[]{:S(2)}) %all-to-all-start) | async-done | bytes 65568 | tf_op jit(solution)/shard_map/all_to_all | solution.py:177
  15.7 0.0 copy-start.2
  15.7 0.7 %copy-done.2 = s32[256,1]{0,1:T(1,128)S(1)} copy-done((s32[256,1]{0,1:T(1,128)S(1)}, s32[256,1]{0,1:T(1,128)}, u32[]{:S(2)}) %copy-start.2) | copy-done | bytes 1048
  16.4 0.0 copy-start.3
  16.4 0.7 %copy-done.3 = s32[256]{0:T(256)S(1)} copy-done((s32[256]{0:T(256)S(1)}, s32[256]{0:T(256)}, u32[]{:S(2)}) %copy-start.3) | copy-done | bytes 1048
  17.1 2.5 %route.1 = f32[512,256]{1,0:T(8,128)S(1)} custom-call(f32[256,256]{1,0:T(8,128)S(1)} %get-tuple-element.7.refs_0_, bf16[512,2048]{1,0:T(8,128)(2,1)S(1)} %get-tuple-element.8.refs_1_, s32[16,8,128]{2,1,0:T(8,128)S(1)} %all-to-all-done.refs_2_, s32[1,256]{1,0:T(1,128)S(1)} %bitcast.7, s32[1,256]{1,0:T(1,128)S(1)} %bitcast.8), custom_call_target="tpu_custom_call" | custom-call | tf_op jit(solution)/shard_map/route/pallas_call | solution.py:191
  19.6 17.1 %all_to_all.10.parts_ref = f32[16,32,256]{2,1,0:T(8,128)S(1)} all-to-all(f32[16,32,256]{2,1,0:T(8,128)S(1)} %bitcast.6), channel_id=1, replica_groups=mesh['ens'=2,'tile'=16] {'tile'}, dimensions={0} | all-to-all | bytes 1048576 | tf_op jit(solution)/shard_map/all_to_all | solution.py:200
  36.7 0.7 %finish.1 = f32[32,256]{1,0:T(8,128)} custom-call(f32[16,32,256]{2,1,0:T(8,128)S(1)} %all_to_all.10.parts_ref), custom_call_target="tpu_custom_call" | custom-call | tf_op jit(solution)/shard_map/finish/pallas_call | solution.py:203
  (1 shorter events, 0.0 us)
Async XLA Ops:
  1.4 14.3 %all-to-all-start = ((s32[16,8,128]{2,1,0:T(8,128)}), s32[16,8,128]{2,1,0:T(8,128)S(1)}, u32[]{:S(2)}, u32[]{:S(2)}) async-start(s32[16,8,128]{2,1,0:T(8,128)} %broadcast_in_dim.12), calls=%async_computation | async-start | bytes 131072 | tf_op jit(solution)/shard_map/all_to_all | solution.py:177
  8.8 0.9 %copy-start = (bf16[256,256]{1,0:T(8,128)(2,1)S(1)}, bf16[256,256]{1,0:T(8,128)(2,1)}, u32[]{:S(2)}) copy-start(bf16[256,256]{1,0:T(8,128)(2,1)} %rain_ref.1) | copy-start | bytes 393220
  9.7 0.7 %copy-start.1 = (f32[8,48]{1,0:T(8,128)S(1)}, f32[8,48]{1,0:T(8,128)}, u32[]{:S(2)}) copy-start(f32[8,48]{1,0:T(8,128)} %irf_ref.1) | copy-start | bytes 4612
  10.4 0.7 %copy-start.4 = (f32[256]{0:T(256)S(1)}, f32[256]{0:T(256)}, u32[]{:S(2)}) copy-start(f32[256]{0:T(256)} %param.12) | copy-start | bytes 3076
  11.1 0.7 %copy-start.5 = (f32[256]{0:T(256)S(1)}, f32[256]{0:T(256)}, u32[]{:S(2)}) copy-start(f32[256]{0:T(256)} %param.13) | copy-start | bytes 3076
  15.7 0.7 %copy-start.2 = (s32[256,1]{0,1:T(1,128)S(1)}, s32[256,1]{0,1:T(1,128)}, u32[]{:S(2)}) copy-start(s32[256,1]{0,1:T(1,128)} %param.14) | copy-start | bytes 3076
  16.4 0.7 %copy-start.3 = (s32[256]{0:T(256)S(1)}, s32[256]{0:T(256)}, u32[]{:S(2)}) copy-start(s32[256]{0:T(256)} %param.15) | copy-start | bytes 3076

commit v2 on v1

v2 whole, which is shorter than its diff:
```python
import math

import jax
import jax.numpy as jnp
from jax import lax
from jax.experimental import pallas as pl
from jax.experimental.pallas import tpu as pltpu
from jax.sharding import PartitionSpec as P

LINK = 6
LANES = 128
VMEM_BYTES = 40 * 1024 * 1024
CODE_TOP = 32767
CODE_OCTAVES = 44
CODE_LOWEST = -26
CODE_SCALE = 2 * CODE_TOP / (CODE_OCTAVES * math.log(2.0))
CODE_LEAST = 2.0**CODE_LOWEST
CODE_ZERO = -CODE_TOP + 1 - CODE_LOWEST * math.log(2.0) * CODE_SCALE

NT = (((1,), (1,)), ((), ()))
NN = (((1,), (0,)), ((), ()))


def iota(shape, axis):
    return lax.broadcasted_iota(jnp.int32, shape, axis)


def split(values):
    high = values.astype(jnp.bfloat16)
    return high, (values - high.astype(jnp.float32)).astype(jnp.bfloat16)


def later(values, hours):
    rows = values.shape[0]
    if hours % 8 == 0:
        padding = jnp.zeros((hours, values.shape[1]), values.dtype)
        return jnp.concatenate([padding, values[: rows - hours]], axis=0)
    return jnp.where(iota(values.shape, 0) < hours, 0.0, pltpu.roll(values, hours, 0))


def prepare_kernel(
    rain_hbm, soil_hbm, area_hbm, dest_hbm, reach_hbm, irf_hbm,
    runoff_ref, response_ref, dest_ref, reach_ref,
    rain_ref, soil_ref, area_ref, irf_ref, arrived,
):
    copies = [
        pltpu.make_async_copy(source, target, arrived.at[j])
        for j, (source, target) in enumerate(
            [
                (rain_hbm, rain_ref),
                (soil_hbm, soil_ref),
                (area_hbm, area_ref),
                (irf_hbm, irf_ref),
                (dest_hbm, dest_ref),
                (reach_hbm, reach_ref),
            ]
        )
    ]
    for copy in copies:
        copy.start()
    for copy in copies:
        copy.wait()
    hours = rain_ref.shape[1]
    kinds, taps = irf_ref.shape
    rainfall = rain_ref[...].astype(jnp.float32).T
    storage = soil_ref[...]
    excess = jnp.maximum(rainfall - 0.2 * storage, 0.0)
    runoff = area_ref[...] * excess * excess / (rainfall + 0.8 * storage)
    runoff_ref[...] = runoff.astype(jnp.bfloat16).astype(jnp.float32)
    backward = (
        iota((taps, hours), 1) == lax.rem(hours - iota((taps, hours), 0), hours)
    ).astype(jnp.float32)
    reversed_taps = lax.dot_general(
        irf_ref[...], backward, NN, precision=lax.Precision.HIGHEST, preferred_element_type=jnp.float32
    )
    causal = iota((hours, hours), 1) <= iota((hours, hours), 0)
    for kind in range(kinds):
        row = jnp.broadcast_to(reversed_taps[kind : kind + 1], (hours, hours))
        matrix = jnp.where(causal, pltpu.roll(row, 0, 1, stride=1, stride_axis=0), 0.0)
        high, low = split(matrix)
        response_ref[:hours, kind * hours : (kind + 1) * hours] = high
        response_ref[hours:, kind * hours : (kind + 1) * hours] = low


def route_kernel(*refs, kinds, reach_rows, basin_rows):
    *piece_refs, runoff_ref, response_ref, dest_ref, reach_ref, flow_ref = refs
    hours, tiles = runoff_ref.shape
    owners = len(piece_refs)
    outlets = owners * basin_rows
    shift = basin_rows.bit_length() - 1
    me = lax.axis_index("tile")
    dest = dest_ref[...]
    reach = reach_ref[...]

    stack = jnp.concatenate([piece[...] for piece in piece_refs], axis=0)
    spans = reach_rows // LANES
    fields = piece_refs[0].shape[0]
    field = iota(stack.shape, 0) % fields
    stack = jnp.where(field == 3 * spans, lax.shift_right_arithmetic(stack, shift) + 1, stack)
    stack = jnp.where(field == 3 * spans + 1, stack & (basin_rows - 1), stack)
    stack = stack.astype(jnp.float32).T.astype(jnp.bfloat16)

    def marks(row, count):
        return (iota((count, tiles), 0) == row).astype(jnp.float32).astype(jnp.bfloat16)

    def picked(values, chosen):
        return jnp.sum(jnp.where(chosen, values, 0.0), axis=0, keepdims=True).astype(jnp.int32)

    def lookup(owner, first, count):
        place = lax.rem(me - owner + owners, owners) * fields
        place = jnp.where(owner < 0, -fields, place)
        mark = jnp.concatenate([marks(place + first + j, owners * fields) for j in range(count)], axis=1)
        found = lax.dot_general(stack, mark, NN, preferred_element_type=jnp.float32)
        return [found[:, j * tiles : (j + 1) * tiles] for j in range(count)]

    by_reach = lookup(dest, 0, 3 * spans)
    at_reach = [iota((LANES, tiles), 0) + j * LANES == reach for j in range(spans)]
    basin, kind, lag = [
        sum(picked(by_reach[c * spans + j], at_reach[j]) for j in range(spans)) for c in range(3)
    ]

    def parent_of(owner, local):
        by_basin = lookup(owner, 3 * spans, 2)
        at_basin = iota((LANES, tiles), 0) == local
        return picked(by_basin[0], at_basin) - 1, picked(by_basin[1], at_basin)

    parent_owner, parent_local = parent_of(dest, basin)
    second_owner, second_local = parent_of(parent_owner, parent_local)
    targets = [
        dest * basin_rows + basin,
        parent_owner * basin_rows + parent_local,
        second_owner * basin_rows + second_local,
    ]

    lagged = runoff_ref[...]
    step = 64
    while step:
        lagged = jnp.where((lag & step) != 0, later(lagged, step), lagged)
        step //= 2
    lagged = lagged.astype(jnp.bfloat16)
    by_kind = jnp.concatenate(
        [
            lagged * (kind == k).astype(jnp.float32).astype(jnp.bfloat16)
            for k in range(kinds)
        ],
        axis=0,
    )
    routed = lax.dot_general(response_ref[...], by_kind, NN, preferred_element_type=jnp.float32)
    routed = routed[:hours] + routed[hours:]
    pieces, placements = [], []
    for target in targets:
        pieces.extend(split(routed))
        mark = marks(target, outlets)
        placements.extend([mark, mark])
        routed = later(routed, LINK)
    flow = lax.dot_general(
        jnp.concatenate(placements, axis=1),
        jnp.concatenate(pieces, axis=1),
        NT,
        preferred_element_type=jnp.float32,
    )
    level = jnp.log(jnp.maximum(flow, CODE_LEAST)) * CODE_SCALE + CODE_ZERO
    level = jnp.minimum(jnp.round(level), CODE_TOP).astype(jnp.int32)
    flow_ref[...] = jnp.where(flow < CODE_LEAST, -CODE_TOP, level).astype(jnp.int16)


def finish_kernel(parts_ref, section_ref):
    level = parts_ref[...].astype(jnp.int32)
    flow = jnp.exp((level.astype(jnp.float32) - CODE_ZERO) * (1.0 / CODE_SCALE))
    flow = jnp.sum(jnp.where(level == -CODE_TOP, 0.0, flow), axis=0)
    section_ref[...] = jnp.log(1.0 + flow)


def per_device(
    rain,
    soil,
    tile_area,
    tile_dest,
    tile_reach,
    reach_basin,
    reach_kind,
    reach_lag,
    irf,
    outlet_level,
    outlet_parent,
):
    owners = lax.axis_size("tile")
    tile_rows, hours = rain.shape
    basin_rows = outlet_parent.shape[0]
    kinds = irf.shape[0]
    params = pltpu.CompilerParams(vmem_limit_bytes=VMEM_BYTES)

    parent_rows = jnp.pad(outlet_parent, (0, LANES - basin_rows))
    meta = jnp.concatenate([reach_basin, reach_kind, reach_lag, parent_rows, parent_rows])
    meta = meta.reshape(-1, LANES)
    metas = [meta] + [
        lax.ppermute(meta, "tile", [(i, (i + step) % owners) for i in range(owners)])
        for step in range(1, owners)
    ]

    held = pl.BlockSpec(memory_space=pltpu.HBM)
    row = (1, tile_rows)
    runoff, response, dest, reach = pl.pallas_call(
        prepare_kernel,
        out_shape=(
            jax.ShapeDtypeStruct((hours, tile_rows), jnp.float32),
            jax.ShapeDtypeStruct((2 * hours, kinds * hours), jnp.bfloat16),
            jax.ShapeDtypeStruct(row, jnp.int32),
            jax.ShapeDtypeStruct(row, jnp.int32),
        ),
        in_specs=[held] * 6,
        scratch_shapes=[
            pltpu.VMEM(rain.shape, rain.dtype),
            pltpu.VMEM(row, jnp.float32),
            pltpu.VMEM(row, jnp.float32),
            pltpu.VMEM(irf.shape, jnp.float32),
            pltpu.SemaphoreType.DMA((6,)),
        ],
        compiler_params=params,
        name="prepare",
    )(
        rain,
        soil.reshape(row),
        tile_area.reshape(row),
        tile_dest.reshape(row),
        tile_reach.reshape(row),
        irf,
    )

    flow = pl.pallas_call(
        lambda *refs: route_kernel(
            *refs, kinds=kinds, reach_rows=reach_basin.shape[0], basin_rows=basin_rows
        ),
        out_shape=jax.ShapeDtypeStruct((owners * basin_rows, hours), jnp.int16),
        compiler_params=params,
        name="route",
    )(*metas, runoff, response, dest, reach)

    parts = lax.all_to_all(
        flow.reshape(owners, basin_rows, hours), "tile", split_axis=0, concat_axis=0, tiled=True
    )
    return pl.pallas_call(
        finish_kernel,
        out_shape=jax.ShapeDtypeStruct((basin_rows, hours), jnp.float32),
        compiler_params=params,
        name="finish",
    )(parts)


def solution(mesh):
    rows = P(("ens", "tile"))
    table = P(("ens", "tile"), None)
    in_specs = (table, rows, rows, table, rows, rows, rows, rows, P(), rows, rows)
    return jax.shard_map(
        per_device, mesh=mesh, in_specs=in_specs, out_specs=table, check_vma=False
    )
```

time: 37.7 us -> 49.9 us (1.32)
  starting transfers between devices: 7.39 us -> 21.7 us
  waiting for transfers between devices: 3.38 us -> 0.69 us
  local copies, waits for them, and re-layouts: 5.73 us -> 7.68 us
  blocking collectives: 17.1 us -> 15.3 us
    ppermute x0 -> x15, starting transfers between devices: none -> 21.7 us  [per_device(): lax.ppermute(meta, 'tile', [(i, (i + step) % owners) for i in range(owner...]
    all_to_all x1 -> x0, starting transfers between devices: 7.39 us -> none  [per_device(): lax.all_to_all(jnp.broadcast_to(meta[None], (owners,) + meta.shape), 'til...]
    all_to_all x1 -> x0, waiting for transfers between devices: 3.38 us -> none  [per_device(): lax.all_to_all(jnp.broadcast_to(meta[None], (owners,) + meta.shape), 'til...]
    unnamed x12 -> x16, local copies, waits for them, and re-layouts: 4.3 us -> 7.02 us
    all_to_all x1, blocking collectives: 17.1 us -> 15.3 us  [per_device(): lax.all_to_all(flow.reshape(owners, basin_rows, hours), 'tile', split_axi...]
    ppermute x0 -> x15, waiting for transfers between devices: none -> 0.69 us  [per_device(): lax.ppermute(meta, 'tile', [(i, (i + step) % owners) for i in range(owner...]
    broadcast_in_dim x2 -> x0, local copies, waits for them, and re-layouts: 0.64 us -> none  [the longest x1 0.64 us: per_device(): jnp.broadcast_to(meta[None], (owners,) + meta.shape)]
  transfers between devices with their start and end apart: 1 -> 15, of which waited for: 1 -> 1; matrix products, arithmetic and copies ran while one was open for 0% -> 0% of each run, Pallas kernels for 1% -> 2%
where the time goes in v2:
time: 49.9 us; the launch traced here: 49.6 us
  starting transfers between devices  21.7 us (43%)
  blocking collectives  15.3 us (31%)
  local copies, waits for them, and re-layouts  7.68 us (15%)
  Pallas kernels  4.21 us (8%)
  waiting for transfers between devices  0.69 us (1%)
    ppermute x15, starting transfers between devices, per_device(): lax.ppermute(meta, 'tile', [(i, (i + step) % owners) for i in range(owner...  21.7 us
    all_to_all x1, blocking collectives, per_device(): lax.all_to_all(flow.reshape(owners, basin_rows, hours), 'tile', split_axi...  15.3 us
    unnamed x16, local copies, waits for them, and re-layouts  7.02 us
    pallas_call x1, Pallas kernels, per_device(): pl.pallas_call(lambda *refs: route_kernel(*refs, kinds=kinds, reach_rows=...  2.66 us
  transfers between devices with their start and end apart: 15, of which 1 were waited for; matrix products, arithmetic and copies ran while one was open for 0% of the time, Pallas kernels for 2%

profile of v2, /device:TPU:0, one launch (start us, length us, event | category | flops | bytes accessed | tf_op | source)
XLA Modules:
  0.0 49.6 jit_solution(5424575433700787713)
XLA Ops:
  0.0 0.7 %constant_dynamic-update-slice_fusion.4 = s32[1024]{0:T(1024)S(1)} fusion(s32[1024]{0:T(1024)S(1)} %custom-call, s32[256]{0:T(256)} %param.16), kind=kLoop, calls=%fused_computation.4 | loop fusion | bytes 2048
  0.7 0.7 %constant_dynamic-update-slice_fusion.3 = s32[1024]{0:T(1024)S(1)} fusion(s32[1024]{0:T(1024)S(1)} %constant_dynamic-update-slice_fusion.4, s32[256]{0:T(256)} %param.17), kind=kLoop, calls=%fused_computation.3 | loop fusion | bytes 2048
  1.4 0.7 %constant_dynamic-update-slice_fusion.2 = s32[1024]{0:T(1024)S(1)} fusion(s32[1024]{0:T(1024)S(1)} %constant_dynamic-update-slice_fusion.3, s32[256]{0:T(256)} %param.18), kind=kLoop, calls=%fused_computation.2 | loop fusion | bytes 2048
  2.1 0.7 %constant_dynamic-update-slice_fusion.1 = s32[1024]{0:T(1024)S(1)} fusion(s32[1024]{0:T(1024)S(1)} %constant_dynamic-update-slice_fusion.2, s32[32]{0:T(128)} %param.20), kind=kLoop, calls=%fused_computation.1 | loop fusion | bytes 640
  2.7 0.7 %constant_dynamic-update-slice_fusion = s32[1024]{0:T(1024)S(1)} fusion(s32[1024]{0:T(1024)S(1)} %constant_dynamic-update-slice_fusion.1, s32[32]{0:T(128)} %param.20), kind=kLoop, calls=%fused_computation | loop fusion | bytes 640 | tf_op jit(solution)/shard_map/concatenate | solution.py:194
  3.4 5.4 %collective-permute-start.14 = (s32[8,128]{1,0:T(8,128)S(1)}, s32[8,128]{1,0:T(8,128)S(1)}, u32[]{:S(2)}, u32[]{:S(2)}) collective-permute-start(s32[8,128]{1,0:T(8,128)S(1)} %bitcast.7), channel_id=1, source_target_pairs={{0,15},{1,0},{2,1},{3,2},{4,3},{5,4},{6,5},{7,6},{8,7},{9,8},{10,9... | collective-permute-start | bytes 12296 | tf_op jit(solution)/shard_map/ppermute | solution.py:197
  10.2 4.4 %collective-permute-start.9 = (s32[8,128]{1,0:T(8,128)S(1)}, s32[8,128]{1,0:T(8,128)S(1)}, u32[]{:S(2)}, u32[]{:S(2)}) collective-permute-start(s32[8,128]{1,0:T(8,128)S(1)} %bitcast.12), channel_id=1, source_target_pairs={{0,10},{1,11},{2,12},{3,13},{4,14},{5,15},{6,0},{7,1},{8,2},{9,3},... | collective-permute-start | bytes 12296 | tf_op jit(solution)/shard_map/ppermute | solution.py:197
  14.6 1.6 %collective-permute-start.7 = (s32[8,128]{1,0:T(8,128)S(1)}, s32[8,128]{1,0:T(8,128)S(1)}, u32[]{:S(2)}, u32[]{:S(2)}) collective-permute-start(s32[8,128]{1,0:T(8,128)S(1)} %bitcast.14), channel_id=1, source_target_pairs={{0,8},{1,9},{2,10},{3,11},{4,12},{5,13},{6,14},{7,15},{8,0},{9,1},... | collective-permute-start | bytes 12296 | tf_op jit(solution)/shard_map/ppermute | solution.py:197
  16.2 1.1 %collective-permute-start.6 = (s32[8,128]{1,0:T(8,128)S(1)}, s32[8,128]{1,0:T(8,128)S(1)}, u32[]{:S(2)}, u32[]{:S(2)}) collective-permute-start(s32[8,128]{1,0:T(8,128)S(1)} %bitcast.15), channel_id=1, source_target_pairs={{0,7},{1,8},{2,9},{3,10},{4,11},{5,12},{6,13},{7,14},{8,15},{9,0},... | collective-permute-start | bytes 12296 | tf_op jit(solution)/shard_map/ppermute | solution.py:197
  17.3 2.6 %collective-permute-start.5 = (s32[8,128]{1,0:T(8,128)S(1)}, s32[8,128]{1,0:T(8,128)S(1)}, u32[]{:S(2)}, u32[]{:S(2)}) collective-permute-start(s32[8,128]{1,0:T(8,128)S(1)} %bitcast.16), channel_id=1, source_target_pairs={{0,6},{1,7},{2,8},{3,9},{4,10},{5,11},{6,12},{7,13},{8,14},{9,15},... | collective-permute-start | bytes 12296 | tf_op jit(solution)/shard_map/ppermute | solution.py:197
  20.4 2.0 %collective-permute-start.3 = (s32[8,128]{1,0:T(8,128)S(1)}, s32[8,128]{1,0:T(8,128)S(1)}, u32[]{:S(2)}, u32[]{:S(2)}) collective-permute-start(s32[8,128]{1,0:T(8,128)S(1)} %bitcast.18), channel_id=1, source_target_pairs={{0,4},{1,5},{2,6},{3,7},{4,8},{5,9},{6,10},{7,11},{8,12},{9,13},{1... | collective-permute-start | bytes 12296 | tf_op jit(solution)/shard_map/ppermute | solution.py:197
  22.4 2.1 %collective-permute-start.2 = (s32[8,128]{1,0:T(8,128)S(1)}, s32[8,128]{1,0:T(8,128)S(1)}, u32[]{:S(2)}, u32[]{:S(2)}) collective-permute-start(s32[8,128]{1,0:T(8,128)S(1)} %bitcast.19), channel_id=1, source_target_pairs={{0,3},{1,4},{2,5},{3,6},{4,7},{5,8},{6,9},{7,10},{8,11},{9,12},{10... | collective-permute-start | bytes 12296 | tf_op jit(solution)/shard_map/ppermute | solution.py:197
  24.5 0.6 %collective-permute-start.1 = (s32[8,128]{1,0:T(8,128)S(1)}, s32[8,128]{1,0:T(8,128)S(1)}, u32[]{:S(2)}, u32[]{:S(2)}) collective-permute-start(s32[8,128]{1,0:T(8,128)S(1)} %bitcast.20), channel_id=1, source_target_pairs={{0,2},{1,3},{2,4},{3,5},{4,6},{5,7},{6,8},{7,9},{8,10},{9,11},{10,... | collective-permute-start | bytes 12296 | tf_op jit(solution)/shard_map/ppermute | solution.py:197
  25.1 0.9 %copy-done = bf16[256,256]{1,0:T(8,128)(2,1)S(1)} copy-done((bf16[256,256]{1,0:T(8,128)(2,1)S(1)}, bf16[256,256]{1,0:T(8,128)(2,1)}, u32[]{:S(2)}) %copy-start) | copy-done | bytes 131096
  26.0 0.7 %copy-done.1 = f32[8,48]{1,0:T(8,128)S(1)} copy-done((f32[8,48]{1,0:T(8,128)S(1)}, f32[8,48]{1,0:T(8,128)}, u32[]{:S(2)}) %copy-start.1) | copy-done | bytes 1560
  26.7 0.7 %copy-done.2 = f32[256]{0:T(256)S(1)} copy-done((f32[256]{0:T(256)S(1)}, f32[256]{0:T(256)}, u32[]{:S(2)}) %copy-start.2) | copy-done | bytes 1048
  27.4 0.7 %copy-done.3 = f32[256]{0:T(256)S(1)} copy-done((f32[256]{0:T(256)S(1)}, f32[256]{0:T(256)}, u32[]{:S(2)}) %copy-start.3) | copy-done | bytes 1048
  28.0 0.7 %copy-done.4 = s32[256,1]{0,1:T(1,128)S(1)} copy-done((s32[256,1]{0,1:T(1,128)S(1)}, s32[256,1]{0,1:T(1,128)}, u32[]{:S(2)}) %copy-start.4) | copy-done | bytes 1048
  28.7 0.7 %copy-done.5 = s32[256]{0:T(256)S(1)} copy-done((s32[256]{0:T(256)S(1)}, s32[256]{0:T(256)}, u32[]{:S(2)}) %copy-start.5) | copy-done | bytes 1048
  29.4 0.8 %prepare.1 = (f32[256,256]{1,0:T(8,128)S(1)}, bf16[512,2048]{1,0:T(8,128)(2,1)S(1)}, s32[1,256]{1,0:T(1,128)S(1)}, s32[1,256]{1,0:T(1,128)S(1)}) custom-call(bf16[256,256]{1,0:T(8,128)(2,1)S(1)} %copy-done, f32[1,256]{1,0:T(1,128)S(1)} %bitcast.23, f32[1,256]{1,0:T(1,128)S(1)} %bitcast.24, s32[1,256]{1,0:T(1,128)S(1)} %bitcast.25, s32[1,256]{1,0:T(1,128)S(1)} %bitcast.26, ...), custom_call_target="tpu_custom_call" | custom-call | tf_op jit(solution)/shard_map/prepare/pallas_call | solution.py:203
  30.2 0.7 %collective-permute-done.1.refs_2_ = s32[8,128]{1,0:T(8,128)S(1)} collective-permute-done((s32[8,128]{1,0:T(8,128)S(1)}, s32[8,128]{1,0:T(8,128)S(1)}, u32[]{:S(2)}, u32[]{:S(2)}) %collective-permute-start.1) | collective-permute-done | bytes 4128 | tf_op jit(solution)/shard_map/ppermute | solution.py:197
  30.9 2.7 %route.1 = s16[512,256]{1,0:T(8,128)(2,1)S(1)} custom-call(s32[8,128]{1,0:T(8,128)S(1)} %bitcast.22, s32[8,128]{1,0:T(8,128)S(1)} %collective-permute-done.refs_1_, s32[8,128]{1,0:T(8,128)S(1)} %collective-permute-done.1.refs_2_, s32[8,128]{1,0:T(8,128)S(1)} %collective-permute-done.2.refs_3_, s32[8,128]{1,0:T(8,128)S(1)} %collective-permute-done.3.refs_4_, ...), custom_call_target="tpu_custom_call" | custom-call | tf_op jit(solution)/shard_map/route/pallas_call | solution.py:230
  33.5 15.3 %all_to_all.5.parts_ref = s16[16,32,256]{2,1,0:T(8,128)(2,1)S(1)} all-to-all(s16[16,32,256]{2,1,0:T(8,128)(2,1)S(1)} %bitcast.6), channel_id=1, replica_groups=mesh['ens'=2,'tile'=16] {'tile'}, dimensions={0} | all-to-all | bytes 524288 | tf_op jit(solution)/shard_map/all_to_all | solution.py:239
  48.8 0.8 %finish.1 = f32[32,256]{1,0:T(8,128)} custom-call(s16[16,32,256]{2,1,0:T(8,128)(2,1)S(1)} %all_to_all.5.parts_ref), custom_call_target="tpu_custom_call" | custom-call | tf_op jit(solution)/shard_map/finish/pallas_call | solution.py:242
  (28 shorter events, 1.9 us)
Async XLA Ops:
  3.4 6.8 %collective-permute-start.14 = (s32[8,128]{1,0:T(8,128)S(1)}, s32[8,128]{1,0:T(8,128)S(1)}, u32[]{:S(2)}, u32[]{:S(2)}) collective-permute-start(s32[8,128]{1,0:T(8,128)S(1)} %bitcast.7), channel_id=1, source_target_pairs={{0,15},{1,0},{2,1},{3,2},{4,3},{5,4},{6,5},{7,6},{8,7},{9,8},{10,9... | collective-permute-start | bytes 12296 | tf_op jit(solution)/shard_map/ppermute | solution.py:197
  8.8 5.7 %collective-permute-start.13 = (s32[8,128]{1,0:T(8,128)S(1)}, s32[8,128]{1,0:T(8,128)S(1)}, u32[]{:S(2)}, u32[]{:S(2)}) collective-permute-start(s32[8,128]{1,0:T(8,128)S(1)} %bitcast.8), channel_id=1, source_target_pairs={{0,14},{1,15},{2,0},{3,1},{4,2},{5,3},{6,4},{7,5},{8,6},{9,7},{10,... | collective-permute-start | bytes 12296 | tf_op jit(solution)/shard_map/ppermute | solution.py:197
  9.4 5.2 %collective-permute-start.12 = (s32[8,128]{1,0:T(8,128)S(1)}, s32[8,128]{1,0:T(8,128)S(1)}, u32[]{:S(2)}, u32[]{:S(2)}) collective-permute-start(s32[8,128]{1,0:T(8,128)S(1)} %bitcast.9), channel_id=1, source_target_pairs={{0,13},{1,14},{2,15},{3,0},{4,1},{5,2},{6,3},{7,4},{8,5},{9,6},{10... | collective-permute-start | bytes 12296 | tf_op jit(solution)/shard_map/ppermute | solution.py:197
  9.7 6.5 %collective-permute-start.11 = (s32[8,128]{1,0:T(8,128)S(1)}, s32[8,128]{1,0:T(8,128)S(1)}, u32[]{:S(2)}, u32[]{:S(2)}) collective-permute-start(s32[8,128]{1,0:T(8,128)S(1)} %bitcast.10), channel_id=1, source_target_pairs={{0,12},{1,13},{2,14},{3,15},{4,0},{5,1},{6,2},{7,3},{8,4},{9,5},{1... | collective-permute-start | bytes 12296 | tf_op jit(solution)/shard_map/ppermute | solution.py:197
  10.1 7.2 %collective-permute-start.10 = (s32[8,128]{1,0:T(8,128)S(1)}, s32[8,128]{1,0:T(8,128)S(1)}, u32[]{:S(2)}, u32[]{:S(2)}) collective-permute-start(s32[8,128]{1,0:T(8,128)S(1)} %bitcast.11), channel_id=1, source_target_pairs={{0,11},{1,12},{2,13},{3,14},{4,15},{5,0},{6,1},{7,2},{8,3},{9,4},{... | collective-permute-start | bytes 12296 | tf_op jit(solution)/shard_map/ppermute | solution.py:197
  10.2 9.7 %collective-permute-start.9 = (s32[8,128]{1,0:T(8,128)S(1)}, s32[8,128]{1,0:T(8,128)S(1)}, u32[]{:S(2)}, u32[]{:S(2)}) collective-permute-start(s32[8,128]{1,0:T(8,128)S(1)} %bitcast.12), channel_id=1, source_target_pairs={{0,10},{1,11},{2,12},{3,13},{4,14},{5,15},{6,0},{7,1},{8,2},{9,3},... | collective-permute-start | bytes 12296 | tf_op jit(solution)/shard_map/ppermute | solution.py:197
  14.6 5.8 %collective-permute-start.8 = (s32[8,128]{1,0:T(8,128)S(1)}, s32[8,128]{1,0:T(8,128)S(1)}, u32[]{:S(2)}, u32[]{:S(2)}) collective-permute-start(s32[8,128]{1,0:T(8,128)S(1)} %bitcast.13), channel_id=1, source_target_pairs={{0,9},{1,10},{2,11},{3,12},{4,13},{5,14},{6,15},{7,0},{8,1},{9,2},... | collective-permute-start | bytes 12296 | tf_op jit(solution)/shard_map/ppermute | solution.py:197
  14.6 7.8 %collective-permute-start.7 = (s32[8,128]{1,0:T(8,128)S(1)}, s32[8,128]{1,0:T(8,128)S(1)}, u32[]{:S(2)}, u32[]{:S(2)}) collective-permute-start(s32[8,128]{1,0:T(8,128)S(1)} %bitcast.14), channel_id=1, source_target_pairs={{0,8},{1,9},{2,10},{3,11},{4,12},{5,13},{6,14},{7,15},{8,0},{9,1},... | collective-permute-start | bytes 12296 | tf_op jit(solution)/shard_map/ppermute | solution.py:197
  16.2 8.3 %collective-permute-start.6 = (s32[8,128]{1,0:T(8,128)S(1)}, s32[8,128]{1,0:T(8,128)S(1)}, u32[]{:S(2)}, u32[]{:S(2)}) collective-permute-start(s32[8,128]{1,0:T(8,128)S(1)} %bitcast.15), channel_id=1, source_target_pairs={{0,7},{1,8},{2,9},{3,10},{4,11},{5,12},{6,13},{7,14},{8,15},{9,0},... | collective-permute-start | bytes 12296 | tf_op jit(solution)/shard_map/ppermute | solution.py:197
  17.3 7.8 %collective-permute-start.5 = (s32[8,128]{1,0:T(8,128)S(1)}, s32[8,128]{1,0:T(8,128)S(1)}, u32[]{:S(2)}, u32[]{:S(2)}) collective-permute-start(s32[8,128]{1,0:T(8,128)S(1)} %bitcast.16), channel_id=1, source_target_pairs={{0,6},{1,7},{2,8},{3,9},{4,10},{5,11},{6,12},{7,13},{8,14},{9,15},... | collective-permute-start | bytes 12296 | tf_op jit(solution)/shard_map/ppermute | solution.py:197
  19.9 10.3 %collective-permute-start.4 = (s32[8,128]{1,0:T(8,128)S(1)}, s32[8,128]{1,0:T(8,128)S(1)}, u32[]{:S(2)}, u32[]{:S(2)}) collective-permute-start(s32[8,128]{1,0:T(8,128)S(1)} %bitcast.17), channel_id=1, source_target_pairs={{0,5},{1,6},{2,7},{3,8},{4,9},{5,10},{6,11},{7,12},{8,13},{9,14},{... | collective-permute-start | bytes 12296 | tf_op jit(solution)/shard_map/ppermute | solution.py:197
  20.4 9.8 %collective-permute-start.3 = (s32[8,128]{1,0:T(8,128)S(1)}, s32[8,128]{1,0:T(8,128)S(1)}, u32[]{:S(2)}, u32[]{:S(2)}) collective-permute-start(s32[8,128]{1,0:T(8,128)S(1)} %bitcast.18), channel_id=1, source_target_pairs={{0,4},{1,5},{2,6},{3,7},{4,8},{5,9},{6,10},{7,11},{8,12},{9,13},{1... | collective-permute-start | bytes 12296 | tf_op jit(solution)/shard_map/ppermute | solution.py:197
  22.4 7.8 %collective-permute-start.2 = (s32[8,128]{1,0:T(8,128)S(1)}, s32[8,128]{1,0:T(8,128)S(1)}, u32[]{:S(2)}, u32[]{:S(2)}) collective-permute-start(s32[8,128]{1,0:T(8,128)S(1)} %bitcast.19), channel_id=1, source_target_pairs={{0,3},{1,4},{2,5},{3,6},{4,7},{5,8},{6,9},{7,10},{8,11},{9,12},{10... | collective-permute-start | bytes 12296 | tf_op jit(solution)/shard_map/ppermute | solution.py:197
  24.5 6.3 %collective-permute-start.1 = (s32[8,128]{1,0:T(8,128)S(1)}, s32[8,128]{1,0:T(8,128)S(1)}, u32[]{:S(2)}, u32[]{:S(2)}) collective-permute-start(s32[8,128]{1,0:T(8,128)S(1)} %bitcast.20), channel_id=1, source_target_pairs={{0,2},{1,3},{2,4},{3,5},{4,6},{5,7},{6,8},{7,9},{8,10},{9,11},{10,... | collective-permute-start | bytes 12296 | tf_op jit(solution)/shard_map/ppermute | solution.py:197
  25.1 5.8 %collective-permute-start = (s32[8,128]{1,0:T(8,128)S(1)}, s32[8,128]{1,0:T(8,128)S(1)}, u32[]{:S(2)}, u32[]{:S(2)}) collective-permute-start(s32[8,128]{1,0:T(8,128)S(1)} %bitcast.21), channel_id=1, source_target_pairs={{0,1},{1,2},{2,3},{3,4},{4,5},{5,6},{6,7},{7,8},{8,9},{9,10},{10,1... | collective-permute-start | bytes 12296 | tf_op jit(solution)/shard_map/ppermute | solution.py:197
  25.1 0.9 %copy-start = (bf16[256,256]{1,0:T(8,128)(2,1)S(1)}, bf16[256,256]{1,0:T(8,128)(2,1)}, u32[]{:S(2)}) copy-start(bf16[256,256]{1,0:T(8,128)(2,1)} %rain_hbm.1) | copy-start | bytes 393220
  26.0 0.7 %copy-start.1 = (f32[8,48]{1,0:T(8,128)S(1)}, f32[8,48]{1,0:T(8,128)}, u32[]{:S(2)}) copy-start(f32[8,48]{1,0:T(8,128)} %irf_hbm.1) | copy-start | bytes 4612
  26.7 0.7 %copy-start.2 = (f32[256]{0:T(256)S(1)}, f32[256]{0:T(256)}, u32[]{:S(2)}) copy-start(f32[256]{0:T(256)} %param.12) | copy-start | bytes 3076
  27.4 0.7 %copy-start.3 = (f32[256]{0:T(256)S(1)}, f32[256]{0:T(256)}, u32[]{:S(2)}) copy-start(f32[256]{0:T(256)} %param.13) | copy-start | bytes 3076
  28.0 0.7 %copy-start.4 = (s32[256,1]{0,1:T(1,128)S(1)}, s32[256,1]{0,1:T(1,128)}, u32[]{:S(2)}) copy-start(s32[256,1]{0,1:T(1,128)} %param.14) | copy-start | bytes 3076
  28.7 0.7 %copy-start.5 = (s32[256]{0:T(256)S(1)}, s32[256]{0:T(256)}, u32[]{:S(2)}) copy-start(s32[256]{0:T(256)} %param.15) | copy-start | bytes 3076

commit v3 on v2

--- a/solution.py
+++ b/solution.py
@@ -82,22 +82,22 @@
         response_ref[hours:, kind * hours : (kind + 1) * hours] = low
 
 
-def route_kernel(*refs, kinds, reach_rows, basin_rows):
-    *piece_refs, runoff_ref, response_ref, dest_ref, reach_ref, flow_ref = refs
+def route_kernel(
+    meta_ref, runoff_ref, response_ref, dest_ref, reach_ref, flow_ref, *, owners, kinds, reach_rows, basin_rows
+):
     hours, tiles = runoff_ref.shape
-    owners = len(piece_refs)
     outlets = owners * basin_rows
     shift = basin_rows.bit_length() - 1
-    me = lax.axis_index("tile")
     dest = dest_ref[...]
     reach = reach_ref[...]
 
-    stack = jnp.concatenate([piece[...] for piece in piece_refs], axis=0)
+    stack = meta_ref[...]
     spans = reach_rows // LANES
-    fields = piece_refs[0].shape[0]
+    fields = stack.shape[0] // owners
     field = iota(stack.shape, 0) % fields
-    stack = jnp.where(field == 3 * spans, lax.shift_right_arithmetic(stack, shift) + 1, stack)
-    stack = jnp.where(field == 3 * spans + 1, stack & (basin_rows - 1), stack)
+    parents = jnp.where(field == 3 * spans, stack, pltpu.roll(stack, 1, 0))
+    stack = jnp.where(field == 3 * spans, lax.shift_right_arithmetic(parents, shift) + 1, stack)
+    stack = jnp.where(field == 3 * spans + 1, parents & (basin_rows - 1), stack)
     stack = stack.astype(jnp.float32).T.astype(jnp.bfloat16)
 
     def marks(row, count):
@@ -107,8 +107,7 @@
         return jnp.sum(jnp.where(chosen, values, 0.0), axis=0, keepdims=True).astype(jnp.int32)
 
     def lookup(owner, first, count):
-        place = lax.rem(me - owner + owners, owners) * fields
-        place = jnp.where(owner < 0, -fields, place)
+        place = owner * fields
         mark = jnp.concatenate([marks(place + first + j, owners * fields) for j in range(count)], axis=1)
         found = lax.dot_general(stack, mark, NN, preferred_element_type=jnp.float32)
         return [found[:, j * tiles : (j + 1) * tiles] for j in range(count)]
@@ -190,13 +189,28 @@
     kinds = irf.shape[0]
     params = pltpu.CompilerParams(vmem_limit_bytes=VMEM_BYTES)
 
-    parent_rows = jnp.pad(outlet_parent, (0, LANES - basin_rows))
-    meta = jnp.concatenate([reach_basin, reach_kind, reach_lag, parent_rows, parent_rows])
-    meta = meta.reshape(-1, LANES)
-    metas = [meta] + [
-        lax.ppermute(meta, "tile", [(i, (i + step) % owners) for i in range(owners)])
-        for step in range(1, owners)
-    ]
+    meta = jnp.concatenate(
+        [
+            reach_basin,
+            reach_kind,
+            reach_lag,
+            outlet_parent,
+            jnp.zeros((2 * LANES - basin_rows,), jnp.int32),
+        ]
+    ).reshape(-1, LANES)
+    near = 1 << ((owners.bit_length() - 1) // 2)
+    far = owners // near
+    near_groups = [[f * near + j for j in range(near)] for f in range(far)]
+    far_groups = [[f * near + j for f in range(far)] for j in range(near)]
+    for groups in (near_groups, far_groups):
+        meta = lax.all_to_all(
+            jnp.broadcast_to(meta[None], (len(groups[0]),) + meta.shape),
+            "tile",
+            split_axis=0,
+            concat_axis=0,
+            axis_index_groups=groups,
+            tiled=True,
+        ).reshape(-1, LANES)
 
     held = pl.BlockSpec(memory_space=pltpu.HBM)
     row = (1, tile_rows)
@@ -229,12 +243,12 @@
 
     flow = pl.pallas_call(
         lambda *refs: route_kernel(
-            *refs, kinds=kinds, reach_rows=reach_basin.shape[0], basin_rows=basin_rows
+            *refs, owners=owners, kinds=kinds, reach_rows=reach_basin.shape[0], basin_rows=basin_rows
         ),
         out_shape=jax.ShapeDtypeStruct((owners * basin_rows, hours), jnp.int16),
         compiler_params=params,
         name="route",
-    )(*metas, runoff, response, dest, reach)
+    )(meta, runoff, response, dest, reach)
 
     parts = lax.all_to_all(
         flow.reshape(owners, basin_rows, hours), "tile", split_axis=0, concat_axis=0, tiled=True

time: 49.9 us -> 38.2 us (0.77)
  starting transfers between devices: 21.7 us -> 4.87 us
  blocking collectives: 15.3 us -> 22.3 us
  local copies, waits for them, and re-layouts: 7.68 us -> 5.73 us
    ppermute x15 -> x0, starting transfers between devices: 21.7 us -> none  [per_device(): lax.ppermute(meta, 'tile', [(i, (i + step) % owners) for i in range(owner...]
    all_to_all x0 -> x1, blocking collectives: none -> 7.88 us  [per_device(): lax.all_to_all(jnp.broadcast_to(meta[None], (len(groups[0]),) + meta.shap...]
    all_to_all x0 -> x1, starting transfers between devices: none -> 4.87 us  [per_device(): lax.all_to_all(jnp.broadcast_to(meta[None], (len(groups[0]),) + meta.shap...]
    unnamed x16 -> x12, local copies, waits for them, and re-layouts: 7.02 us -> 4.3 us
    all_to_all x1, blocking collectives: 15.3 us -> 14.4 us  [per_device(): lax.all_to_all(flow.reshape(owners, basin_rows, hours), 'tile', split_axi...]
    ppermute x15 -> x0, waiting for transfers between devices: 0.69 us -> none  [per_device(): lax.ppermute(meta, 'tile', [(i, (i + step) % owners) for i in range(owner...]
    all_to_all x0 -> x1, waiting for transfers between devices: none -> 0.67 us  [per_device(): lax.all_to_all(jnp.broadcast_to(meta[None], (len(groups[0]),) + meta.shap...]
    broadcast_in_dim x0 -> x3, local copies, waits for them, and re-layouts: none -> 0.64 us  [the longest x2 0.64 us: per_device(): jnp.broadcast_to(meta[None], (len(groups[0]),) + meta.shape)]
  transfers between devices with their start and end apart: 15 -> 1, of which waited for: 1 -> 1; matrix products, arithmetic and copies ran while one was open for 0% -> 0% of each run, Pallas kernels for 2% -> 2%
where the time goes in v3:
time: 38.2 us; the launch traced here: 37.8 us
  blocking collectives  22.3 us (58%)
  local copies, waits for them, and re-layouts  5.73 us (15%)
  starting transfers between devices  4.87 us (13%)
  Pallas kernels  4.19 us (11%)
  waiting for transfers between devices  0.67 us (2%)
    all_to_all x1, blocking collectives, per_device(): lax.all_to_all(flow.reshape(owners, basin_rows, hours), 'tile', split_axi...  14.4 us
    all_to_all x1, blocking collectives, per_device(): lax.all_to_all(jnp.broadcast_to(meta[None], (len(groups[0]),) + meta.shap...  7.88 us
    all_to_all x1, starting transfers between devices, per_device(): lax.all_to_all(jnp.broadcast_to(meta[None], (len(groups[0]),) + meta.shap...  4.87 us
    unnamed x12, local copies, waits for them, and re-layouts  4.3 us
    pallas_call x1, Pallas kernels, per_device(): pl.pallas_call(lambda *refs: route_kernel(*refs, owners=owners, kinds=kin...  2.64 us
    pallas_call x1, Pallas kernels, per_device(): pl.pallas_call(finish_kernel, out_shape=jax.ShapeDtypeStruct((basin_rows,...  0.79 us
    concatenate x1, local copies, waits for them, and re-layouts, per_device(): jnp.concatenate([reach_basin, reach_kind, reach_lag, outlet_parent, jnp.z...  0.79 us
  transfers between devices with their start and end apart: 1, of which 1 were waited for; matrix products, arithmetic and copies ran while one was open for 0% of the time, Pallas kernels for 2%

profile of v3, /device:TPU:0, one launch (start us, length us, event | category | flops | bytes accessed | tf_op | source)
XLA Modules:
  0.0 37.8 jit_solution(5574011513720804502)
XLA Ops:
  0.0 0.8 %concatenate.3 = s32[1024]{0:T(1024)S(1)} concatenate(s32[256]{0:T(256)} %param.16, s32[256]{0:T(256)} %param.17, s32[256]{0:T(256)} %param.18, s32[32]{0:T(128)} %param.20, s32[224]{0:T(256)S(1)} %broadcast_in_dim.17), dimensions={0} | concatenate | bytes 8192 | tf_op jit(solution)/shard_map/concatenate | solution.py:192
  0.8 7.9 %all_to_all.15 = s32[4,8,128]{2,1,0:T(8,128)S(1)} all-to-all(s32[4,8,128]{2,1,0:T(8,128)S(1)} %broadcast_in_dim.19), channel_id=1, replica_groups={{0,1,2,3},{4,5,6,7},{8,9,10,11},{12,13,14,15},{16,17,18,19},{20,21,22,2..., dimensions={0} | all-to-all | bytes 32768 | tf_op jit(solution)/shard_map/all_to_all | solution.py:206
  8.7 0.6 %broadcast_in_dim.21 = s32[4,32,128]{2,1,0:T(8,128)} broadcast(s32[32,128]{1,0:T(8,128)S(1)} %bitcast.14), dimensions={1,2} | broadcast | bytes 81920 | tf_op jit(solution)/shard_map/broadcast_in_dim | solution.py:207
  9.3 4.9 %all-to-all-start.1 = ((s32[4,32,128]{2,1,0:T(8,128)}), s32[4,32,128]{2,1,0:T(8,128)S(1)}, u32[]{:S(2)}, u32[]{:S(2)}) async-start(s32[4,32,128]{2,1,0:T(8,128)} %broadcast_in_dim.21), calls=%async_computation.1 | async-start | bytes 131072 | tf_op jit(solution)/shard_map/all_to_all | solution.py:206
  14.2 0.0 copy-start
  14.2 0.9 %copy-done = bf16[256,256]{1,0:T(8,128)(2,1)S(1)} copy-done((bf16[256,256]{1,0:T(8,128)(2,1)S(1)}, bf16[256,256]{1,0:T(8,128)(2,1)}, u32[]{:S(2)}) %copy-start) | copy-done | bytes 131096
  15.1 0.0 copy-start.1
  15.1 0.7 %copy-done.1 = f32[8,48]{1,0:T(8,128)S(1)} copy-done((f32[8,48]{1,0:T(8,128)S(1)}, f32[8,48]{1,0:T(8,128)}, u32[]{:S(2)}) %copy-start.1) | copy-done | bytes 1560
  15.8 0.0 copy-start.2
  15.8 0.7 %copy-done.2 = f32[256]{0:T(256)S(1)} copy-done((f32[256]{0:T(256)S(1)}, f32[256]{0:T(256)}, u32[]{:S(2)}) %copy-start.2) | copy-done | bytes 1048
  16.5 0.0 copy-start.3
  16.5 0.7 %copy-done.3 = f32[256]{0:T(256)S(1)} copy-done((f32[256]{0:T(256)S(1)}, f32[256]{0:T(256)}, u32[]{:S(2)}) %copy-start.3) | copy-done | bytes 1048
  17.1 0.0 copy-start.4
  17.1 0.7 %copy-done.4 = s32[256,1]{0,1:T(1,128)S(1)} copy-done((s32[256,1]{0,1:T(1,128)S(1)}, s32[256,1]{0,1:T(1,128)}, u32[]{:S(2)}) %copy-start.4) | copy-done | bytes 1048
  17.8 0.0 copy-start.5
  17.8 0.7 %copy-done.5 = s32[256]{0:T(256)S(1)} copy-done((s32[256]{0:T(256)S(1)}, s32[256]{0:T(256)}, u32[]{:S(2)}) %copy-start.5) | copy-done | bytes 1048
  18.5 0.8 %prepare.1 = (f32[256,256]{1,0:T(8,128)S(1)}, bf16[512,2048]{1,0:T(8,128)(2,1)S(1)}, s32[1,256]{1,0:T(1,128)S(1)}, s32[1,256]{1,0:T(1,128)S(1)}) custom-call(bf16[256,256]{1,0:T(8,128)(2,1)S(1)} %copy-done, f32[1,256]{1,0:T(1,128)S(1)} %bitcast.10, f32[1,256]{1,0:T(1,128)S(1)} %bitcast.11, s32[1,256]{1,0:T(1,128)S(1)} %bitcast.12, s32[1,256]{1,0:T(1,128)S(1)} %bitcast.13, ...), custom_call_target="tpu_custom_call" | custom-call | tf_op jit(solution)/shard_map/prepare/pallas_call | solution.py:217
  19.3 0.7 %all-to-all-done.1 = s32[4,32,128]{2,1,0:T(8,128)S(1)} async-done(((s32[4,32,128]{2,1,0:T(8,128)}), s32[4,32,128]{2,1,0:T(8,128)S(1)}, u32[]{:S(2)}, u32[]{:S(2)}) %all-to-all-start.1) | async-done | bytes 65568 | tf_op jit(solution)/shard_map/all_to_all | solution.py:206
  19.9 2.6 %route.1 = s16[512,256]{1,0:T(8,128)(2,1)S(1)} custom-call(s32[128,128]{1,0:T(8,128)S(1)} %bitcast.9, f32[256,256]{1,0:T(8,128)S(1)} %get-tuple-element.9.refs_1_, bf16[512,2048]{1,0:T(8,128)(2,1)S(1)} %get-tuple-element.10.refs_2_, s32[1,256]{1,0:T(1,128)S(1)} %get-tuple-element.11.refs_3_, s32[1,256]{1,0:T(1,128)S(1)} %get-tuple-element.12.refs_4_), custom_call_target="tpu_custom_call" | custom-call | tf_op jit(solution)/shard_map/route/pallas_call | solution.py:244
  22.6 14.4 %all_to_all.16.parts_ref = s16[16,32,256]{2,1,0:T(8,128)(2,1)S(1)} all-to-all(s16[16,32,256]{2,1,0:T(8,128)(2,1)S(1)} %bitcast.8), channel_id=1, replica_groups=mesh['ens'=2,'tile'=16] {'tile'}, dimensions={0} | all-to-all | bytes 524288 | tf_op jit(solution)/shard_map/all_to_all | solution.py:253
  37.0 0.8 %finish.1 = f32[32,256]{1,0:T(8,128)} custom-call(s16[16,32,256]{2,1,0:T(8,128)(2,1)S(1)} %all_to_all.16.parts_ref), custom_call_target="tpu_custom_call" | custom-call | tf_op jit(solution)/shard_map/finish/pallas_call | solution.py:256
  (2 shorter events, 0.0 us)
Async XLA Ops:
  9.3 10.6 %all-to-all-start.1 = ((s32[4,32,128]{2,1,0:T(8,128)}), s32[4,32,128]{2,1,0:T(8,128)S(1)}, u32[]{:S(2)}, u32[]{:S(2)}) async-start(s32[4,32,128]{2,1,0:T(8,128)} %broadcast_in_dim.21), calls=%async_computation.1 | async-start | bytes 131072 | tf_op jit(solution)/shard_map/all_to_all | solution.py:206
  14.2 0.9 %copy-start = (bf16[256,256]{1,0:T(8,128)(2,1)S(1)}, bf16[256,256]{1,0:T(8,128)(2,1)}, u32[]{:S(2)}) copy-start(bf16[256,256]{1,0:T(8,128)(2,1)} %rain_hbm.1) | copy-start | bytes 393220
  15.1 0.7 %copy-start.1 = (f32[8,48]{1,0:T(8,128)S(1)}, f32[8,48]{1,0:T(8,128)}, u32[]{:S(2)}) copy-start(f32[8,48]{1,0:T(8,128)} %irf_hbm.1) | copy-start | bytes 4612
  15.8 0.7 %copy-start.2 = (f32[256]{0:T(256)S(1)}, f32[256]{0:T(256)}, u32[]{:S(2)}) copy-start(f32[256]{0:T(256)} %param.12) | copy-start | bytes 3076
  16.5 0.7 %copy-start.3 = (f32[256]{0:T(256)S(1)}, f32[256]{0:T(256)}, u32[]{:S(2)}) copy-start(f32[256]{0:T(256)} %param.13) | copy-start | bytes 3076
  17.1 0.7 %copy-start.4 = (s32[256,1]{0,1:T(1,128)S(1)}, s32[256,1]{0,1:T(1,128)}, u32[]{:S(2)}) copy-start(s32[256,1]{0,1:T(1,128)} %param.14) | copy-start | bytes 3076
  17.8 0.7 %copy-start.5 = (s32[256]{0:T(256)S(1)}, s32[256]{0:T(256)}, u32[]{:S(2)}) copy-start(s32[256]{0:T(256)} %param.15) | copy-start | bytes 3076

commit v4 on v3

--- a/solution.py
+++ b/solution.py
@@ -38,34 +38,13 @@
     return jnp.where(iota(values.shape, 0) < hours, 0.0, pltpu.roll(values, hours, 0))
 
 
-def prepare_kernel(
-    rain_hbm, soil_hbm, area_hbm, dest_hbm, reach_hbm, irf_hbm,
-    runoff_ref, response_ref, dest_ref, reach_ref,
-    rain_ref, soil_ref, area_ref, irf_ref, arrived,
-):
-    copies = [
-        pltpu.make_async_copy(source, target, arrived.at[j])
-        for j, (source, target) in enumerate(
-            [
-                (rain_hbm, rain_ref),
-                (soil_hbm, soil_ref),
-                (area_hbm, area_ref),
-                (irf_hbm, irf_ref),
-                (dest_hbm, dest_ref),
-                (reach_hbm, reach_ref),
-            ]
-        )
-    ]
-    for copy in copies:
-        copy.start()
-    for copy in copies:
-        copy.wait()
+def prepare_kernel(rain_ref, tile_ref, irf_ref, runoff_ref, response_ref):
     hours = rain_ref.shape[1]
     kinds, taps = irf_ref.shape
     rainfall = rain_ref[...].astype(jnp.float32).T
-    storage = soil_ref[...]
+    storage = tile_ref[0:1]
     excess = jnp.maximum(rainfall - 0.2 * storage, 0.0)
-    runoff = area_ref[...] * excess * excess / (rainfall + 0.8 * storage)
+    runoff = tile_ref[1:2] * excess * excess / (rainfall + 0.8 * storage)
     runoff_ref[...] = runoff.astype(jnp.bfloat16).astype(jnp.float32)
     backward = (
         iota((taps, hours), 1) == lax.rem(hours - iota((taps, hours), 0), hours)
@@ -83,13 +62,13 @@
 
 
 def route_kernel(
-    meta_ref, runoff_ref, response_ref, dest_ref, reach_ref, flow_ref, *, owners, kinds, reach_rows, basin_rows
+    meta_ref, runoff_ref, response_ref, tile_ref, flow_ref, *, owners, kinds, reach_rows, basin_rows
 ):
     hours, tiles = runoff_ref.shape
     outlets = owners * basin_rows
     shift = basin_rows.bit_length() - 1
-    dest = dest_ref[...]
-    reach = reach_ref[...]
+    dest = tile_ref[0:1]
+    reach = tile_ref[1:2]
 
     stack = meta_ref[...]
     spans = reach_rows // LANES
@@ -198,48 +177,19 @@
             jnp.zeros((2 * LANES - basin_rows,), jnp.int32),
         ]
     ).reshape(-1, LANES)
-    near = 1 << ((owners.bit_length() - 1) // 2)
-    far = owners // near
-    near_groups = [[f * near + j for j in range(near)] for f in range(far)]
-    far_groups = [[f * near + j for f in range(far)] for j in range(near)]
-    for groups in (near_groups, far_groups):
-        meta = lax.all_to_all(
-            jnp.broadcast_to(meta[None], (len(groups[0]),) + meta.shape),
-            "tile",
-            split_axis=0,
-            concat_axis=0,
-            axis_index_groups=groups,
-            tiled=True,
-        ).reshape(-1, LANES)
-
-    held = pl.BlockSpec(memory_space=pltpu.HBM)
-    row = (1, tile_rows)
-    runoff, response, dest, reach = pl.pallas_call(
+    meta = lax.all_to_all(
+        jnp.broadcast_to(meta[None], (owners,) + meta.shape), "tile", split_axis=0, concat_axis=0, tiled=True
+    ).reshape(-1, LANES)
+
+    runoff, response = pl.pallas_call(
         prepare_kernel,
         out_shape=(
             jax.ShapeDtypeStruct((hours, tile_rows), jnp.float32),
             jax.ShapeDtypeStruct((2 * hours, kinds * hours), jnp.bfloat16),
-            jax.ShapeDtypeStruct(row, jnp.int32),
-            jax.ShapeDtypeStruct(row, jnp.int32),
         ),
-        in_specs=[held] * 6,
-        scratch_shapes=[
-            pltpu.VMEM(rain.shape, rain.dtype),
-            pltpu.VMEM(row, jnp.float32),
-            pltpu.VMEM(row, jnp.float32),
-            pltpu.VMEM(irf.shape, jnp.float32),
-            pltpu.SemaphoreType.DMA((6,)),
-        ],
         compiler_params=params,
         name="prepare",
-    )(
-        rain,
-        soil.reshape(row),
-        tile_area.reshape(row),
-        tile_dest.reshape(row),
-        tile_reach.reshape(row),
-        irf,
-    )
+    )(rain, jnp.stack([soil, tile_area]), irf)
 
     flow = pl.pallas_call(
         lambda *refs: route_kernel(
@@ -248,7 +198,7 @@
         out_shape=jax.ShapeDtypeStruct((owners * basin_rows, hours), jnp.int16),
         compiler_params=params,
         name="route",
-    )(meta, runoff, response, dest, reach)
+    )(meta, runoff, response, jnp.stack([tile_dest[:, 0], tile_reach]))
 
     parts = lax.all_to_all(
         flow.reshape(owners, basin_rows, hours), "tile", split_axis=0, concat_axis=0, tiled=True

time: 38.2 us -> 32.1 us (0.84)
  blocking collectives: 22.3 us -> 12.6 us
  local copies, waits for them, and re-layouts: 5.73 us -> 3 us
  waiting for transfers between devices: 0.67 us -> 3.33 us
  starting transfers between devices: 4.87 us -> 7.39 us
  other arithmetic: 0 us -> 1.41 us
    all_to_all x1 -> x0, blocking collectives: 7.88 us -> none  [per_device(): lax.all_to_all(jnp.broadcast_to(meta[None], (len(groups[0]),) + meta.shap...]
    unnamed x12 -> x4, local copies, waits for them, and re-layouts: 4.3 us -> 1.59 us
    all_to_all x1, waiting for transfers between devices: 0.67 us -> 3.33 us  [per_device(): lax.all_to_all(jnp.broadcast_to(meta[None], (owners,) + meta.shape), 'til...]
    all_to_all x1, starting transfers between devices: 4.87 us -> 7.39 us  [per_device(): lax.all_to_all(jnp.broadcast_to(meta[None], (owners,) + meta.shape), 'til...]
    all_to_all x1, blocking collectives: 14.4 us -> 12.6 us  [per_device(): lax.all_to_all(flow.reshape(owners, basin_rows, hours), 'tile', split_axi...]
    another operation x0 -> x2, other arithmetic: none -> 1.41 us  [the longest x1 0.71 us: per_device(): jnp.stack([soil, tile_area])]
  transfers between devices with their start and end apart: 1 -> 1, of which waited for: 1 -> 1; matrix products, arithmetic and copies ran while one was open for 0% -> 4% of each run, Pallas kernels for 2% -> 2%
where the time goes in v4:
time: 32.1 us; the launch traced here: 31.8 us
  blocking collectives  12.6 us (39%)
  starting transfers between devices  7.39 us (23%)
  Pallas kernels  3.98 us (12%)
  waiting for transfers between devices  3.33 us (10%)
  local copies, waits for them, and re-layouts  3 us (9%)
  other arithmetic  1.41 us (4%)
    all_to_all x1, blocking collectives, per_device(): lax.all_to_all(flow.reshape(owners, basin_rows, hours), 'tile', split_axi...  12.6 us
    all_to_all x1, starting transfers between devices, per_device(): lax.all_to_all(jnp.broadcast_to(meta[None], (owners,) + meta.shape), 'til...  7.39 us
    all_to_all x1, waiting for transfers between devices, per_device(): lax.all_to_all(jnp.broadcast_to(meta[None], (owners,) + meta.shape), 'til...  3.33 us
    pallas_call x1, Pallas kernels, per_device(): pl.pallas_call(lambda *refs: route_kernel(*refs, owners=owners, kinds=kin...  2.64 us
    unnamed x4, local copies, waits for them, and re-layouts  1.59 us
    pallas_call x1, Pallas kernels, per_device(): pl.pallas_call(finish_kernel, out_shape=jax.ShapeDtypeStruct((basin_rows,...  0.79 us
    concatenate x1, local copies, waits for them, and re-layouts, per_device(): jnp.concatenate([reach_basin, reach_kind, reach_lag, outlet_parent, jnp.z...  0.79 us
    another operation x1, other arithmetic, per_device(): jnp.stack([soil, tile_area])  0.71 us
  transfers between devices with their start and end apart: 1, of which 1 were waited for; matrix products, arithmetic and copies ran while one was open for 4% of the time, Pallas kernels for 2%

profile of v4, /device:TPU:0, one launch (start us, length us, event | category | flops | bytes accessed | tf_op | source)
XLA Modules:
  0.0 31.8 jit_solution(11484064982464253166)
XLA Ops:
  0.0 0.8 %concatenate.3 = s32[1024]{0:T(1024)S(1)} concatenate(s32[256]{0:T(256)} %param.16, s32[256]{0:T(256)} %param.17, s32[256]{0:T(256)} %param.18, s32[32]{0:T(128)} %param.20, s32[224]{0:T(256)S(1)} %broadcast_in_dim.10), dimensions={0} | concatenate | bytes 8192 | tf_op jit(solution)/shard_map/concatenate | solution.py:171
  0.8 0.6 %broadcast_in_dim.12 = s32[16,8,128]{2,1,0:T(8,128)} broadcast(s32[8,128]{1,0:T(8,128)S(1)} %bitcast.9), dimensions={1,2} | broadcast | bytes 69632 | tf_op jit(solution)/shard_map/broadcast_in_dim | solution.py:181
  1.4 7.4 %all-to-all-start = ((s32[16,8,128]{2,1,0:T(8,128)}), s32[16,8,128]{2,1,0:T(8,128)S(1)}, u32[]{:S(2)}, u32[]{:S(2)}) async-start(s32[16,8,128]{2,1,0:T(8,128)} %broadcast_in_dim.12), calls=%async_computation | async-start | bytes 131072 | tf_op jit(solution)/shard_map/all_to_all | solution.py:180
  8.8 0.7 %pad_maximum_fusion.tile_ref = f32[2,256]{1,0:T(2,128)S(1)} fusion(f32[1,256]{1,0:T(1,128)} %bitcast.10, f32[1,256]{1,0:T(1,128)} %bitcast.11), kind=kLoop, calls=%fused_computation | loop fusion | flops 512 | bytes 4096 | tf_op jit(solution)/shard_map/stack | solution.py:192
  9.5 0.0 copy-start
  9.5 0.9 %copy-done = bf16[256,256]{1,0:T(8,128)(2,1)S(1)} copy-done((bf16[256,256]{1,0:T(8,128)(2,1)S(1)}, bf16[256,256]{1,0:T(8,128)(2,1)}, u32[]{:S(2)}) %copy-start) | copy-done | bytes 131096
  10.4 0.0 copy-start.1
  10.4 0.7 %copy-done.1 = f32[8,48]{1,0:T(8,128)S(1)} copy-done((f32[8,48]{1,0:T(8,128)S(1)}, f32[8,48]{1,0:T(8,128)}, u32[]{:S(2)}) %copy-start.1) | copy-done | bytes 1560
  11.1 0.6 %prepare.1 = (f32[256,256]{1,0:T(8,128)S(1)}, bf16[512,2048]{1,0:T(8,128)(2,1)S(1)}) custom-call(bf16[256,256]{1,0:T(8,128)(2,1)S(1)} %copy-done, f32[2,256]{1,0:T(2,128)S(1)} %pad_maximum_fusion.tile_ref, f32[8,48]{1,0:T(8,128)S(1)} %copy-done.1), custom_call_target="tpu_custom_call" | custom-call | tf_op jit(solution)/shard_map/prepare/pallas_call | solution.py:184
  11.7 0.7 %pad_add_fusion.refs_3_ = s32[2,256]{1,0:T(2,128)S(1)} fusion(s32[1,256]{1,0:T(1,128)} %bitcast.12, s32[1,256]{1,0:T(1,128)} %bitcast.13), kind=kLoop, calls=%fused_computation.1 | loop fusion | flops 512 | bytes 4096 | tf_op jit(solution)/shard_map/stack | solution.py:201
  12.4 3.3 %all-to-all-done = s32[16,8,128]{2,1,0:T(8,128)S(1)} async-done(((s32[16,8,128]{2,1,0:T(8,128)}), s32[16,8,128]{2,1,0:T(8,128)S(1)}, u32[]{:S(2)}, u32[]{:S(2)}) %all-to-all-start) | async-done | bytes 65568 | tf_op jit(solution)/shard_map/all_to_all | solution.py:180
  15.7 2.6 %route.1 = s16[512,256]{1,0:T(8,128)(2,1)S(1)} custom-call(s32[128,128]{1,0:T(8,128)S(1)} %bitcast.8, f32[256,256]{1,0:T(8,128)S(1)} %get-tuple-element.7.refs_1_, bf16[512,2048]{1,0:T(8,128)(2,1)S(1)} %get-tuple-element.8.refs_2_, s32[2,256]{1,0:T(2,128)S(1)} %pad_add_fusion.refs_3_), custom_call_target="tpu_custom_call" | custom-call | tf_op jit(solution)/shard_map/route/pallas_call | solution.py:194
  18.4 12.6 %all_to_all.10.parts_ref = s16[16,32,256]{2,1,0:T(8,128)(2,1)S(1)} all-to-all(s16[16,32,256]{2,1,0:T(8,128)(2,1)S(1)} %bitcast.7), channel_id=1, replica_groups=mesh['ens'=2,'tile'=16] {'tile'}, dimensions={0} | all-to-all | bytes 524288 | tf_op jit(solution)/shard_map/all_to_all | solution.py:203
  31.0 0.8 %finish.1 = f32[32,256]{1,0:T(8,128)} custom-call(s16[16,32,256]{2,1,0:T(8,128)(2,1)S(1)} %all_to_all.10.parts_ref), custom_call_target="tpu_custom_call" | custom-call | tf_op jit(solution)/shard_map/finish/pallas_call | solution.py:206
  (1 shorter events, 0.0 us)
Async XLA Ops:
  1.4 14.3 %all-to-all-start = ((s32[16,8,128]{2,1,0:T(8,128)}), s32[16,8,128]{2,1,0:T(8,128)S(1)}, u32[]{:S(2)}, u32[]{:S(2)}) async-start(s32[16,8,128]{2,1,0:T(8,128)} %broadcast_in_dim.12), calls=%async_computation | async-start | bytes 131072 | tf_op jit(solution)/shard_map/all_to_all | solution.py:180
  9.5 0.9 %copy-start = (bf16[256,256]{1,0:T(8,128)(2,1)S(1)}, bf16[256,256]{1,0:T(8,128)(2,1)}, u32[]{:S(2)}) copy-start(bf16[256,256]{1,0:T(8,128)(2,1)} %rain_ref.1) | copy-start | bytes 393220
  10.4 0.7 %copy-start.1 = (f32[8,48]{1,0:T(8,128)S(1)}, f32[8,48]{1,0:T(8,128)}, u32[]{:S(2)}) copy-start(f32[8,48]{1,0:T(8,128)} %irf_ref.1) | copy-start | bytes 4612

commit v5 on v3

--- a/solution.py
+++ b/solution.py
@@ -38,28 +38,48 @@
     return jnp.where(iota(values.shape, 0) < hours, 0.0, pltpu.roll(values, hours, 0))
 
 
-def prepare_kernel(
-    rain_hbm, soil_hbm, area_hbm, dest_hbm, reach_hbm, irf_hbm,
-    runoff_ref, response_ref, dest_ref, reach_ref,
-    rain_ref, soil_ref, area_ref, irf_ref, arrived,
-):
+def load(sources, targets, arrived):
     copies = [
         pltpu.make_async_copy(source, target, arrived.at[j])
-        for j, (source, target) in enumerate(
-            [
-                (rain_hbm, rain_ref),
-                (soil_hbm, soil_ref),
-                (area_hbm, area_ref),
-                (irf_hbm, irf_ref),
-                (dest_hbm, dest_ref),
-                (reach_hbm, reach_ref),
-            ]
-        )
+        for j, (source, target) in enumerate(zip(sources, targets))
     ]
     for copy in copies:
         copy.start()
     for copy in copies:
         copy.wait()
+
+
+def pack_kernel(basin_hbm, kind_hbm, lag_hbm, parent_hbm, meta_ref, basin_ref, kind_ref, lag_ref, parent_ref, arrived):
+    load(
+        (basin_hbm, kind_hbm, lag_hbm, parent_hbm),
+        (basin_ref, kind_ref, lag_ref, parent_ref),
+        arrived,
+    )
+    owners, fields, _ = meta_ref.shape
+    rows = [
+        values[:, first : first + LANES]
+        for values in (basin_ref[...], kind_ref[...], lag_ref[...])
+        for first in range(0, values.shape[1], LANES)
+    ]
+    parents = parent_ref[...]
+    empty = jnp.zeros((1, LANES - parents.shape[1]), jnp.int32)
+    rows.append(jnp.concatenate([parents, empty], axis=1))
+    rows.extend([jnp.zeros((1, LANES), jnp.int32)] * (fields - len(rows)))
+    block = jnp.concatenate(rows, axis=0)
+    for owner in range(owners):
+        meta_ref[owner] = block
+
+
+def prepare_kernel(
+    rain_hbm, soil_hbm, area_hbm, irf_hbm, dest_hbm, reach_hbm,
+    runoff_ref, response_ref, dest_ref, reach_ref,
+    rain_ref, soil_ref, area_ref, irf_ref, arrived,
+):
+    load(
+        (rain_hbm, soil_hbm, area_hbm, irf_hbm, dest_hbm, reach_hbm),
+        (rain_ref, soil_ref, area_ref, irf_ref, dest_ref, reach_ref),
+        arrived,
+    )
     hours = rain_ref.shape[1]
     kinds, taps = irf_ref.shape
     rainfall = rain_ref[...].astype(jnp.float32).T
@@ -189,31 +209,34 @@
     kinds = irf.shape[0]
     params = pltpu.CompilerParams(vmem_limit_bytes=VMEM_BYTES)
 
-    meta = jnp.concatenate(
-        [
-            reach_basin,
-            reach_kind,
-            reach_lag,
-            outlet_parent,
-            jnp.zeros((2 * LANES - basin_rows,), jnp.int32),
-        ]
-    ).reshape(-1, LANES)
-    near = 1 << ((owners.bit_length() - 1) // 2)
-    far = owners // near
-    near_groups = [[f * near + j for j in range(near)] for f in range(far)]
-    far_groups = [[f * near + j for f in range(far)] for j in range(near)]
-    for groups in (near_groups, far_groups):
-        meta = lax.all_to_all(
-            jnp.broadcast_to(meta[None], (len(groups[0]),) + meta.shape),
-            "tile",
-            split_axis=0,
-            concat_axis=0,
-            axis_index_groups=groups,
-            tiled=True,
-        ).reshape(-1, LANES)
+    row = (1, tile_rows)
+    fields = 8 * pl.cdiv(3 * reach_basin.size // LANES + 2, 8)
+
+    def in_hbm(values, shape):
+        return pltpu.with_memory_space_constraint(values.reshape(shape), pltpu.HBM)
 
     held = pl.BlockSpec(memory_space=pltpu.HBM)
-    row = (1, tile_rows)
+    meta = pl.pallas_call(
+        pack_kernel,
+        out_shape=jax.ShapeDtypeStruct((owners, fields, LANES), jnp.int32),
+        in_specs=[held] * 4,
+        scratch_shapes=[
+            pltpu.VMEM((1, reach_basin.size), jnp.int32),
+            pltpu.VMEM((1, reach_basin.size), jnp.int32),
+            pltpu.VMEM((1, reach_basin.size), jnp.int32),
+            pltpu.VMEM((1, basin_rows), jnp.int32),
+            pltpu.SemaphoreType.DMA((4,)),
+        ],
+        compiler_params=params,
+        name="pack",
+    )(
+        in_hbm(reach_basin, (1, -1)),
+        in_hbm(reach_kind, (1, -1)),
+        in_hbm(reach_lag, (1, -1)),
+        in_hbm(outlet_parent, (1, -1)),
+    )
+    meta = lax.all_to_all(meta, "tile", split_axis=0, concat_axis=0, tiled=True).reshape(-1, LANES)
+
     runoff, response, dest, reach = pl.pallas_call(
         prepare_kernel,
         out_shape=(
@@ -233,12 +256,12 @@
         compiler_params=params,
         name="prepare",
     )(
-        rain,
-        soil.reshape(row),
-        tile_area.reshape(row),
-        tile_dest.reshape(row),
-        tile_reach.reshape(row),
-        irf,
+        in_hbm(rain, rain.shape),
+        in_hbm(soil, row),
+        in_hbm(tile_area, row),
+        in_hbm(irf, irf.shape),
+        in_hbm(tile_dest, row),
+        in_hbm(tile_reach, row),
     )
 
     flow = pl.pallas_call(

time: 38.2 us -> 32 us (0.84)
  blocking collectives: 22.3 us -> 12.6 us
  local copies, waits for them, and re-layouts: 5.73 us -> 0 us
  waiting for transfers between devices: 0.67 us -> 5.36 us
  starting transfers between devices: 4.87 us -> 7.4 us
  Pallas kernels: 4.19 us -> 6.32 us
    all_to_all x1 -> x0, blocking collectives: 7.88 us -> none  [per_device(): lax.all_to_all(jnp.broadcast_to(meta[None], (len(groups[0]),) + meta.shap...]
    all_to_all x1, waiting for transfers between devices: 0.67 us -> 5.36 us  [per_device(): lax.all_to_all(meta, 'tile', split_axis=0, concat_axis=0, tiled=True)]
    unnamed x12 -> x0, local copies, waits for them, and re-layouts: 4.3 us -> none
    all_to_all x1, starting transfers between devices: 4.87 us -> 7.4 us  [per_device(): lax.all_to_all(meta, 'tile', split_axis=0, concat_axis=0, tiled=True)]
    all_to_all x1, blocking collectives: 14.4 us -> 12.6 us  [per_device(): lax.all_to_all(flow.reshape(owners, basin_rows, hours), 'tile', split_axi...]
    pallas_call x0 -> x1, Pallas kernels: none -> 1.37 us  [per_device(): pl.pallas_call(pack_kernel, out_shape=jax.ShapeDtypeStruct((owners, field...]
    concatenate x1 -> x0, local copies, waits for them, and re-layouts: 0.79 us -> none  [per_device(): jnp.concatenate([reach_basin, reach_kind, reach_lag, outlet_parent, jnp.z...]
    pallas_call x1, Pallas kernels: 0.76 us -> 1.53 us  [per_device(): pl.pallas_call(prepare_kernel, out_shape=(jax.ShapeDtypeStruct((hours, ti...]
  transfers between devices with their start and end apart: 1 -> 1, of which waited for: 1 -> 1; matrix products, arithmetic and copies ran while one was open for 0% -> 0% of each run, Pallas kernels for 2% -> 5%
where the time goes in v5:
time: 32 us; the launch traced here: 31.8 us
  blocking collectives  12.6 us (39%)
  starting transfers between devices  7.4 us (23%)
  Pallas kernels  6.32 us (20%)
  waiting for transfers between devices  5.36 us (17%)
    all_to_all x1, blocking collectives, per_device(): lax.all_to_all(flow.reshape(owners, basin_rows, hours), 'tile', split_axi...  12.6 us
    all_to_all x1, starting transfers between devices, per_device(): lax.all_to_all(meta, 'tile', split_axis=0, concat_axis=0, tiled=True)  7.4 us
    all_to_all x1, waiting for transfers between devices, per_device(): lax.all_to_all(meta, 'tile', split_axis=0, concat_axis=0, tiled=True)  5.36 us
    pallas_call x1, Pallas kernels, per_device(): pl.pallas_call(lambda *refs: route_kernel(*refs, owners=owners, kinds=kin...  2.64 us
    pallas_call x1, Pallas kernels, per_device(): pl.pallas_call(prepare_kernel, out_shape=(jax.ShapeDtypeStruct((hours, ti...  1.53 us
    pallas_call x1, Pallas kernels, per_device(): pl.pallas_call(pack_kernel, out_shape=jax.ShapeDtypeStruct((owners, field...  1.37 us
    pallas_call x1, Pallas kernels, per_device(): pl.pallas_call(finish_kernel, out_shape=jax.ShapeDtypeStruct((basin_rows,...  0.79 us
  transfers between devices with their start and end apart: 1, of which 1 were waited for; matrix products, arithmetic and copies ran while one was open for 0% of the time, Pallas kernels for 5%

profile of v5, /device:TPU:0, one launch (start us, length us, event | category | flops | bytes accessed | tf_op | source)
XLA Modules:
  0.0 31.8 jit_solution(8454764551791147024)
XLA Ops:
  0.0 1.4 %pack.1 = s32[16,8,128]{2,1,0:T(8,128)} custom-call(s32[1,256]{1,0:T(1,128)} %bitcast.12, s32[1,256]{1,0:T(1,128)} %bitcast.13, s32[1,256]{1,0:T(1,128)} %bitcast.14, s32[1,32]{1,0:T(1,128)} %bitcast.19), custom_call_target="tpu_custom_call" | custom-call | tf_op jit(solution)/shard_map/pack/pallas_call | solution.py:219
  1.4 7.4 %all-to-all-start = ((s32[16,8,128]{2,1,0:T(8,128)}), s32[16,8,128]{2,1,0:T(8,128)S(1)}, u32[]{:S(2)}, u32[]{:S(2)}) async-start(s32[16,8,128]{2,1,0:T(8,128)} %pack.1), calls=%async_computation | async-start | bytes 131072 | tf_op jit(solution)/shard_map/all_to_all | solution.py:238
  8.8 1.5 %prepare.1 = (f32[256,256]{1,0:T(8,128)S(1)}, bf16[512,2048]{1,0:T(8,128)(2,1)S(1)}, s32[1,256]{1,0:T(1,128)S(1)}, s32[1,256]{1,0:T(1,128)S(1)}) custom-call(bf16[256,256]{1,0:T(8,128)(2,1)} %rain_hbm.1, f32[1,256]{1,0:T(1,128)} %bitcast.15, f32[1,256]{1,0:T(1,128)} %bitcast.16, f32[8,48]{1,0:T(8,128)} %irf_hbm.1, s32[1,256]{1,0:T(1,128)} %bitcast.17, ...), custom_call_target="tpu_custom_call" | custom-call | tf_op jit(solution)/shard_map/prepare/pallas_call | solution.py:240
  10.3 5.4 %all-to-all-done = s32[16,8,128]{2,1,0:T(8,128)S(1)} async-done(((s32[16,8,128]{2,1,0:T(8,128)}), s32[16,8,128]{2,1,0:T(8,128)S(1)}, u32[]{:S(2)}, u32[]{:S(2)}) %all-to-all-start) | async-done | bytes 65568 | tf_op jit(solution)/shard_map/all_to_all | solution.py:238
  15.7 2.6 %route.1 = s16[512,256]{1,0:T(8,128)(2,1)S(1)} custom-call(s32[128,128]{1,0:T(8,128)S(1)} %bitcast.11, f32[256,256]{1,0:T(8,128)S(1)} %get-tuple-element.9.refs_1_, bf16[512,2048]{1,0:T(8,128)(2,1)S(1)} %get-tuple-element.10.refs_2_, s32[1,256]{1,0:T(1,128)S(1)} %get-tuple-element.11.refs_3_, s32[1,256]{1,0:T(1,128)S(1)} %get-tuple-element.12.refs_4_), custom_call_target="tpu_custom_call" | custom-call | tf_op jit(solution)/shard_map/route/pallas_call | solution.py:267
  18.3 12.6 %all_to_all.10.parts_ref = s16[16,32,256]{2,1,0:T(8,128)(2,1)S(1)} all-to-all(s16[16,32,256]{2,1,0:T(8,128)(2,1)S(1)} %bitcast.10), channel_id=1, replica_groups=mesh['ens'=2,'tile'=16] {'tile'}, dimensions={0} | all-to-all | bytes 524288 | tf_op jit(solution)/shard_map/all_to_all | solution.py:276
  31.0 0.8 %finish.1 = f32[32,256]{1,0:T(8,128)} custom-call(s16[16,32,256]{2,1,0:T(8,128)(2,1)S(1)} %all_to_all.10.parts_ref), custom_call_target="tpu_custom_call" | custom-call | tf_op jit(solution)/shard_map/finish/pallas_call | solution.py:279
Async XLA Ops:
  1.4 14.3 %all-to-all-start = ((s32[16,8,128]{2,1,0:T(8,128)}), s32[16,8,128]{2,1,0:T(8,128)S(1)}, u32[]{:S(2)}, u32[]{:S(2)}) async-start(s32[16,8,128]{2,1,0:T(8,128)} %pack.1), calls=%async_computation | async-start | bytes 131072 | tf_op jit(solution)/shard_map/all_to_all | solution.py:238

commit v6 on v4

--- a/solution.py
+++ b/solution.py
@@ -38,13 +38,42 @@
     return jnp.where(iota(values.shape, 0) < hours, 0.0, pltpu.roll(values, hours, 0))
 
 
-def prepare_kernel(rain_ref, tile_ref, irf_ref, runoff_ref, response_ref):
+def load(sources, targets, arrived):
+    copies = [
+        pltpu.make_async_copy(source, target, arrived.at[j])
+        for j, (source, target) in enumerate(zip(sources, targets))
+    ]
+    for copy in copies:
+        copy.start()
+    for copy in copies:
+        copy.wait()
+
+
+def prepare_kernel(*refs):
+    sources, refs = refs[:10], refs[10:]
+    meta_ref, runoff_ref, response_ref, dest_ref, reach_ref, *scratch, arrived = refs
+    basin_ref, kind_ref, lag_ref, parent_ref, rain_ref, soil_ref, area_ref, irf_ref = scratch
+    load(sources, (*scratch, dest_ref, reach_ref), arrived)
+    owners, fields, _ = meta_ref.shape
+    rows = [
+        values[:, first : first + LANES]
+        for values in (basin_ref[...], kind_ref[...], lag_ref[...])
+        for first in range(0, values.shape[1], LANES)
+    ]
+    parents = parent_ref[...]
+    empty = jnp.zeros((1, LANES - parents.shape[1]), jnp.int32)
+    rows.append(jnp.concatenate([parents, empty], axis=1))
+    rows.extend([jnp.zeros((1, LANES), jnp.int32)] * (fields - len(rows)))
+    block = jnp.concatenate(rows, axis=0)
+    for owner in range(owners):
+        meta_ref[owner] = block
+
     hours = rain_ref.shape[1]
     kinds, taps = irf_ref.shape
     rainfall = rain_ref[...].astype(jnp.float32).T
-    storage = tile_ref[0:1]
+    storage = soil_ref[...]
     excess = jnp.maximum(rainfall - 0.2 * storage, 0.0)
-    runoff = tile_ref[1:2] * excess * excess / (rainfall + 0.8 * storage)
+    runoff = area_ref[...] * excess * excess / (rainfall + 0.8 * storage)
     runoff_ref[...] = runoff.astype(jnp.bfloat16).astype(jnp.float32)
     backward = (
         iota((taps, hours), 1) == lax.rem(hours - iota((taps, hours), 0), hours)
@@ -62,13 +91,13 @@
 
 
 def route_kernel(
-    meta_ref, runoff_ref, response_ref, tile_ref, flow_ref, *, owners, kinds, reach_rows, basin_rows
+    meta_ref, runoff_ref, response_ref, dest_ref, reach_ref, flow_ref, *, owners, kinds, reach_rows, basin_rows
 ):
     hours, tiles = runoff_ref.shape
     outlets = owners * basin_rows
     shift = basin_rows.bit_length() - 1
-    dest = tile_ref[0:1]
-    reach = tile_ref[1:2]
+    dest = dest_ref[...]
+    reach = reach_ref[...]
 
     stack = meta_ref[...]
     spans = reach_rows // LANES
@@ -168,28 +197,39 @@
     kinds = irf.shape[0]
     params = pltpu.CompilerParams(vmem_limit_bytes=VMEM_BYTES)
 
-    meta = jnp.concatenate(
-        [
-            reach_basin,
-            reach_kind,
-            reach_lag,
-            outlet_parent,
-            jnp.zeros((2 * LANES - basin_rows,), jnp.int32),
-        ]
-    ).reshape(-1, LANES)
-    meta = lax.all_to_all(
-        jnp.broadcast_to(meta[None], (owners,) + meta.shape), "tile", split_axis=0, concat_axis=0, tiled=True
-    ).reshape(-1, LANES)
-
-    runoff, response = pl.pallas_call(
+    row = (1, tile_rows)
+    fields = 8 * pl.cdiv(3 * reach_basin.size // LANES + 2, 8)
+    arguments = [
+        pltpu.with_memory_space_constraint(values.reshape(shape), pltpu.HBM)
+        for values, shape in (
+            (reach_basin, (1, -1)),
+            (reach_kind, (1, -1)),
+            (reach_lag, (1, -1)),
+            (outlet_parent, (1, -1)),
+            (rain, rain.shape),
+            (soil, row),
+            (tile_area, row),
+            (irf, irf.shape),
+            (tile_dest, row),
+            (tile_reach, row),
+        )
+    ]
+    meta, runoff, response, dest, reach = pl.pallas_call(
         prepare_kernel,
         out_shape=(
+            jax.ShapeDtypeStruct((owners, fields, LANES), jnp.int32),
             jax.ShapeDtypeStruct((hours, tile_rows), jnp.float32),
             jax.ShapeDtypeStruct((2 * hours, kinds * hours), jnp.bfloat16),
+            jax.ShapeDtypeStruct(row, jnp.int32),
+            jax.ShapeDtypeStruct(row, jnp.int32),
         ),
+        in_specs=[pl.BlockSpec(memory_space=pltpu.HBM)] * len(arguments),
+        scratch_shapes=[pltpu.VMEM(values.shape, values.dtype) for values in arguments[:-2]]
+        + [pltpu.SemaphoreType.DMA((len(arguments),))],
         compiler_params=params,
         name="prepare",
-    )(rain, jnp.stack([soil, tile_area]), irf)
+    )(*arguments)
+    meta = lax.all_to_all(meta, "tile", split_axis=0, concat_axis=0, tiled=True).reshape(-1, LANES)
 
     flow = pl.pallas_call(
         lambda *refs: route_kernel(
@@ -198,7 +238,7 @@
         out_shape=jax.ShapeDtypeStruct((owners * basin_rows, hours), jnp.int16),
         compiler_params=params,
         name="route",
-    )(meta, runoff, response, jnp.stack([tile_dest[:, 0], tile_reach]))
+    )(meta, runoff, response, dest, reach)
 
     parts = lax.all_to_all(
         flow.reshape(owners, basin_rows, hours), "tile", split_axis=0, concat_axis=0, tiled=True

time: 32.1 us -> 32 us (level)
  blocking collectives: 12.6 us -> 26.7 us
  starting transfers between devices: 7.39 us -> 0 us
  waiting for transfers between devices: 3.33 us -> 0 us
  local copies, waits for them, and re-layouts: 3 us -> 0 us
  other arithmetic: 1.41 us -> 0 us
  Pallas kernels: 3.98 us -> 5.05 us
    all_to_all x0 -> x1, blocking collectives: none -> 14.1 us  [per_device(): lax.all_to_all(meta, 'tile', split_axis=0, concat_axis=0, tiled=True)]
    all_to_all x1 -> x0, starting transfers between devices: 7.39 us -> none  [per_device(): lax.all_to_all(jnp.broadcast_to(meta[None], (owners,) + meta.shape), 'til...]
    all_to_all x1 -> x0, waiting for transfers between devices: 3.33 us -> none  [per_device(): lax.all_to_all(jnp.broadcast_to(meta[None], (owners,) + meta.shape), 'til...]
    unnamed x4 -> x0, local copies, waits for them, and re-layouts: 1.59 us -> none
    another operation x2 -> x0, other arithmetic: 1.41 us -> none  [the longest x1 0.71 us: per_device(): jnp.stack([soil, tile_area])]
    pallas_call x1, Pallas kernels: 0.55 us -> 1.62 us  [per_device(): pl.pallas_call(prepare_kernel, out_shape=(jax.ShapeDtypeStruct((owners, f...]
    concatenate x1 -> x0, local copies, waits for them, and re-layouts: 0.79 us -> none  [per_device(): jnp.concatenate([reach_basin, reach_kind, reach_lag, outlet_parent, jnp.z...]
    broadcast_in_dim x2 -> x0, local copies, waits for them, and re-layouts: 0.63 us -> none  [the longest x1 0.63 us: per_device(): jnp.broadcast_to(meta[None], (owners,) + meta.shape)]
  transfers between devices with their start and end apart: 1 -> 0, of which waited for: 1 -> 0; matrix products, arithmetic and copies ran while one was open for 4% -> 0% of each run, Pallas kernels for 2% -> 0%
where the time goes in v6:
time: 32 us; the launch traced here: 31.8 us
  blocking collectives  26.7 us (83%)
  Pallas kernels  5.05 us (16%)
    all_to_all x1, blocking collectives, per_device(): lax.all_to_all(meta, 'tile', split_axis=0, concat_axis=0, tiled=True)  14.1 us
    all_to_all x1, blocking collectives, per_device(): lax.all_to_all(flow.reshape(owners, basin_rows, hours), 'tile', split_axi...  12.6 us
    pallas_call x1, Pallas kernels, per_device(): pl.pallas_call(lambda *refs: route_kernel(*refs, owners=owners, kinds=kin...  2.64 us
    pallas_call x1, Pallas kernels, per_device(): pl.pallas_call(prepare_kernel, out_shape=(jax.ShapeDtypeStruct((owners, f...  1.62 us
    pallas_call x1, Pallas kernels, per_device(): pl.pallas_call(finish_kernel, out_shape=jax.ShapeDtypeStruct((basin_rows,...  0.79 us

profile of v6, /device:TPU:0, one launch (start us, length us, event | category | flops | bytes accessed | tf_op | source)
XLA Modules:
  0.0 31.8 jit_solution(3319612617593990127)
XLA Ops:
  0.0 1.6 %prepare.1 = (s32[16,8,128]{2,1,0:T(8,128)S(1)}, f32[256,256]{1,0:T(8,128)S(1)}, bf16[512,2048]{1,0:T(8,128)(2,1)S(1)}, s32[1,256]{1,0:T(1,128)S(1)}, s32[1,256]{1,0:T(1,128)S(1)}) custom-call(s32[1,256]{1,0:T(1,128)} %bitcast.12, s32[1,256]{1,0:T(1,128)} %bitcast.13, s32[1,256]{1,0:T(1,128)} %bitcast.14, s32[1,32]{1,0:T(1,128)} %bitcast.19, ...), custom_call_target="tpu_custom_call" | custom-call | tf_op jit(solution)/shard_map/prepare/pallas_call | solution.py:217
  1.6 14.1 %all_to_all.10 = s32[16,8,128]{2,1,0:T(8,128)S(1)} all-to-all(s32[16,8,128]{2,1,0:T(8,128)S(1)} %get-tuple-element.10), channel_id=1, replica_groups=mesh['ens'=2,'tile'=16] {'tile'}, dimensions={0} | all-to-all | bytes 131072 | tf_op jit(solution)/shard_map/all_to_all | solution.py:232
  15.7 2.6 %route.1 = s16[512,256]{1,0:T(8,128)(2,1)S(1)} custom-call(s32[128,128]{1,0:T(8,128)S(1)} %bitcast.11, f32[256,256]{1,0:T(8,128)S(1)} %get-tuple-element.11.refs_1_, bf16[512,2048]{1,0:T(8,128)(2,1)S(1)} %get-tuple-element.12.refs_2_, s32[1,256]{1,0:T(1,128)S(1)} %get-tuple-element.13.refs_3_, s32[1,256]{1,0:T(1,128)S(1)} %get-tuple-element.14.refs_4_), custom_call_target="tpu_custom_call" | custom-call | tf_op jit(solution)/shard_map/route/pallas_call | solution.py:234
  18.4 12.6 %all_to_all.11.parts_ref = s16[16,32,256]{2,1,0:T(8,128)(2,1)S(1)} all-to-all(s16[16,32,256]{2,1,0:T(8,128)(2,1)S(1)} %bitcast.10), channel_id=1, replica_groups=mesh['ens'=2,'tile'=16] {'tile'}, dimensions={0} | all-to-all | bytes 524288 | tf_op jit(solution)/shard_map/all_to_all | solution.py:243
  31.0 0.8 %finish.1 = f32[32,256]{1,0:T(8,128)} custom-call(s16[16,32,256]{2,1,0:T(8,128)(2,1)S(1)} %all_to_all.11.parts_ref), custom_call_target="tpu_custom_call" | custom-call | tf_op jit(solution)/shard_map/finish/pallas_call | solution.py:246

commit v7 on v6

--- a/solution.py
+++ b/solution.py
@@ -50,24 +50,9 @@
 
 
 def prepare_kernel(*refs):
-    sources, refs = refs[:10], refs[10:]
-    meta_ref, runoff_ref, response_ref, dest_ref, reach_ref, *scratch, arrived = refs
-    basin_ref, kind_ref, lag_ref, parent_ref, rain_ref, soil_ref, area_ref, irf_ref = scratch
+    sources, (runoff_ref, response_ref, dest_ref, reach_ref, *scratch, arrived) = refs[:6], refs[6:]
+    rain_ref, soil_ref, area_ref, irf_ref = scratch
     load(sources, (*scratch, dest_ref, reach_ref), arrived)
-    owners, fields, _ = meta_ref.shape
-    rows = [
-        values[:, first : first + LANES]
-        for values in (basin_ref[...], kind_ref[...], lag_ref[...])
-        for first in range(0, values.shape[1], LANES)
-    ]
-    parents = parent_ref[...]
-    empty = jnp.zeros((1, LANES - parents.shape[1]), jnp.int32)
-    rows.append(jnp.concatenate([parents, empty], axis=1))
-    rows.extend([jnp.zeros((1, LANES), jnp.int32)] * (fields - len(rows)))
-    block = jnp.concatenate(rows, axis=0)
-    for owner in range(owners):
-        meta_ref[owner] = block
-
     hours = rain_ref.shape[1]
     kinds, taps = irf_ref.shape
     rainfall = rain_ref[...].astype(jnp.float32).T
@@ -90,16 +75,16 @@
         response_ref[hours:, kind * hours : (kind + 1) * hours] = low
 
 
-def route_kernel(
-    meta_ref, runoff_ref, response_ref, dest_ref, reach_ref, flow_ref, *, owners, kinds, reach_rows, basin_rows
-):
+def route_kernel(*refs, owners, kinds, reach_rows, basin_rows):
+    *meta_refs, runoff_ref, response_ref, dest_ref, reach_ref, flow_ref = refs
+    me = lax.axis_index("tile")
     hours, tiles = runoff_ref.shape
     outlets = owners * basin_rows
     shift = basin_rows.bit_length() - 1
     dest = dest_ref[...]
     reach = reach_ref[...]
 
-    stack = meta_ref[...]
+    stack = jnp.concatenate([meta_ref[...] for meta_ref in meta_refs], axis=0)
     spans = reach_rows // LANES
     fields = stack.shape[0] // owners
     field = iota(stack.shape, 0) % fields
@@ -115,7 +100,7 @@
         return jnp.sum(jnp.where(chosen, values, 0.0), axis=0, keepdims=True).astype(jnp.int32)
 
     def lookup(owner, first, count):
-        place = owner * fields
+        place = jnp.where(owner < 0, -1, owner ^ me) * fields
         mark = jnp.concatenate([marks(place + first + j, owners * fields) for j in range(count)], axis=1)
         found = lax.dot_general(stack, mark, NN, preferred_element_type=jnp.float32)
         return [found[:, j * tiles : (j + 1) * tiles] for j in range(count)]
@@ -197,15 +182,31 @@
     kinds = irf.shape[0]
     params = pltpu.CompilerParams(vmem_limit_bytes=VMEM_BYTES)
 
+    metas = [
+        jnp.concatenate(
+            [
+                reach_basin,
+                reach_kind,
+                reach_lag,
+                outlet_parent,
+                jnp.zeros((2 * LANES - basin_rows,), jnp.int32),
+            ]
+        ).reshape(-1, LANES)
+    ]
+    held = 1
+    while held < owners:
+        radix = min(4, owners // held)
+        block = jnp.concatenate(metas, axis=0) if len(metas) > 1 else metas[0]
+        metas = [block] + [
+            lax.ppermute(block, "tile", [(i, i ^ (held * step)) for i in range(owners)])
+            for step in range(1, radix)
+        ]
+        held *= radix
+
     row = (1, tile_rows)
-    fields = 8 * pl.cdiv(3 * reach_basin.size // LANES + 2, 8)
     arguments = [
         pltpu.with_memory_space_constraint(values.reshape(shape), pltpu.HBM)
         for values, shape in (
-            (reach_basin, (1, -1)),
-            (reach_kind, (1, -1)),
-            (reach_lag, (1, -1)),
-            (outlet_parent, (1, -1)),
             (rain, rain.shape),
             (soil, row),
             (tile_area, row),
@@ -214,10 +215,9 @@
             (tile_reach, row),
         )
     ]
-    meta, runoff, response, dest, reach = pl.pallas_call(
+    runoff, response, dest, reach = pl.pallas_call(
         prepare_kernel,
         out_shape=(
-            jax.ShapeDtypeStruct((owners, fields, LANES), jnp.int32),
             jax.ShapeDtypeStruct((hours, tile_rows), jnp.float32),
             jax.ShapeDtypeStruct((2 * hours, kinds * hours), jnp.bfloat16),
             jax.ShapeDtypeStruct(row, jnp.int32),
@@ -229,7 +229,6 @@
         compiler_params=params,
         name="prepare",
     )(*arguments)
-    meta = lax.all_to_all(meta, "tile", split_axis=0, concat_axis=0, tiled=True).reshape(-1, LANES)
 
     flow = pl.pallas_call(
         lambda *refs: route_kernel(
@@ -238,7 +237,7 @@
         out_shape=jax.ShapeDtypeStruct((owners * basin_rows, hours), jnp.int16),
         compiler_params=params,
         name="route",
-    )(meta, runoff, response, dest, reach)
+    )(*metas, runoff, response, dest, reach)
 
     parts = lax.all_to_all(
         flow.reshape(owners, basin_rows, hours), "tile", split_axis=0, concat_axis=0, tiled=True

time: 32 us -> 32 us (level)
  blocking collectives: 26.7 us -> 13.3 us
  starting transfers between devices: 0 us -> 7.47 us
  waiting for transfers between devices: 0 us -> 5.25 us
  local copies, waits for them, and re-layouts: 0 us -> 0.79 us
    all_to_all x1 -> x0, blocking collectives: 14.1 us -> none  [per_device(): lax.all_to_all(meta, 'tile', split_axis=0, concat_axis=0, tiled=True)]
    ppermute x0 -> x6, starting transfers between devices: none -> 7.47 us  [per_device(): lax.ppermute(block, 'tile', [(i, i ^ held * step) for i in range(owners)])]
    ppermute x0 -> x6, waiting for transfers between devices: none -> 5.25 us  [per_device(): lax.ppermute(block, 'tile', [(i, i ^ held * step) for i in range(owners)])]
    concatenate x0 -> x1, local copies, waits for them, and re-layouts: none -> 0.79 us  [per_device(): jnp.concatenate([reach_basin, reach_kind, reach_lag, outlet_parent, jnp.z...]
    all_to_all x1, blocking collectives: 12.6 us -> 13.3 us  [per_device(): lax.all_to_all(flow.reshape(owners, basin_rows, hours), 'tile', split_axi...]
  transfers between devices with their start and end apart: 0 -> 6, of which waited for: 0 -> 3; matrix products, arithmetic and copies ran while one was open for 0% -> 0% of each run, Pallas kernels for 0% -> 5%
where the time goes in v7:
time: 32 us; the launch traced here: 31.8 us
  blocking collectives  13.3 us (42%)
  starting transfers between devices  7.47 us (23%)
  waiting for transfers between devices  5.25 us (16%)
  Pallas kernels  4.96 us (16%)
  local copies, waits for them, and re-layouts  0.79 us (2%)
    all_to_all x1, blocking collectives, per_device(): lax.all_to_all(flow.reshape(owners, basin_rows, hours), 'tile', split_axi...  13.3 us
    ppermute x6, starting transfers between devices, per_device(): lax.ppermute(block, 'tile', [(i, i ^ held * step) for i in range(owners)])  7.47 us
    ppermute x6, waiting for transfers between devices, per_device(): lax.ppermute(block, 'tile', [(i, i ^ held * step) for i in range(owners)])  5.25 us
    pallas_call x1, Pallas kernels, per_device(): pl.pallas_call(lambda *refs: route_kernel(*refs, owners=owners, kinds=kin...  2.65 us
    pallas_call x1, Pallas kernels, per_device(): pl.pallas_call(prepare_kernel, out_shape=(jax.ShapeDtypeStruct((hours, ti...  1.52 us
    pallas_call x1, Pallas kernels, per_device(): pl.pallas_call(finish_kernel, out_shape=jax.ShapeDtypeStruct((basin_rows,...  0.79 us
    concatenate x1, local copies, waits for them, and re-layouts, per_device(): jnp.concatenate([reach_basin, reach_kind, reach_lag, outlet_parent, jnp.z...  0.79 us
  transfers between devices with their start and end apart: 6, of which 3 were waited for; matrix products, arithmetic and copies ran while one was open for 0% of the time, Pallas kernels for 5%

profile of v7, /device:TPU:0, one launch (start us, length us, event | category | flops | bytes accessed | tf_op | source)
XLA Modules:
  0.0 31.8 jit_solution(16292308918667089475)
XLA Ops:
  0.0 0.8 %concatenate.6 = s32[1024]{0:T(1024)S(1)} concatenate(s32[256]{0:T(256)} %param.16, s32[256]{0:T(256)} %param.17, s32[256]{0:T(256)} %param.18, s32[32]{0:T(128)} %param.20, s32[224]{0:T(256)S(1)} %broadcast_in_dim.3), dimensions={0} | concatenate | bytes 8192 | tf_op jit(solution)/shard_map/concatenate | solution.py:186
  0.8 2.4 %collective-permute-start.2 = (s32[8,128]{1,0:T(8,128)S(1)}, s32[8,128]{1,0:T(8,128)S(1)}, u32[]{:S(2)}, u32[]{:S(2)}) collective-permute-start(s32[8,128]{1,0:T(8,128)S(1)} %bitcast.7), channel_id=1, source_target_pairs={{0,3},{1,2},{2,1},{3,0},{4,7},{5,6},{6,5},{7,4},{8,11},{9,10},{10,... | collective-permute-start | bytes 12296 | tf_op jit(solution)/shard_map/ppermute | solution.py:201
  3.2 0.6 %collective-permute-start.1 = (s32[8,128]{1,0:T(8,128)S(1)}, s32[8,128]{1,0:T(8,128)S(1)}, u32[]{:S(2)}, u32[]{:S(2)}) collective-permute-start(s32[8,128]{1,0:T(8,128)S(1)} %bitcast.8), channel_id=1, source_target_pairs={{0,2},{1,3},{2,0},{3,1},{4,6},{5,7},{6,4},{7,5},{8,10},{9,11},{10,... | collective-permute-start | bytes 12296 | tf_op jit(solution)/shard_map/ppermute | solution.py:201
  3.8 0.1 collective-permute-start
  3.9 0.6 %collective-permute-done.2 = s32[8,128]{1,0:T(8,128)S(1)} collective-permute-done((s32[8,128]{1,0:T(8,128)S(1)}, s32[8,128]{1,0:T(8,128)S(1)}, u32[]{:S(2)}, u32[]{:S(2)}) %collective-permute-start.2) | collective-permute-done | bytes 4128 | tf_op jit(solution)/shard_map/ppermute | solution.py:201
  4.5 2.3 %collective-permute-done.1 = s32[8,128]{1,0:T(8,128)S(1)} collective-permute-done((s32[8,128]{1,0:T(8,128)S(1)}, s32[8,128]{1,0:T(8,128)S(1)}, u32[]{:S(2)}, u32[]{:S(2)}) %collective-permute-start.1) | collective-permute-done | bytes 4128 | tf_op jit(solution)/shard_map/ppermute | solution.py:201
  6.8 0.0 collective-permute-done
  6.8 3.6 %collective-permute-start.5 = (s32[32,128]{1,0:T(8,128)S(1)}, s32[32,128]{1,0:T(8,128)S(1)}, u32[]{:S(2)}, u32[]{:S(2)}) collective-permute-start(s32[32,128]{1,0:T(8,128)S(1)} %pad_add_fusion.refs_0_), channel_id=1, source_target_pairs={{0,12},{1,13},{2,14},{3,15},{4,8},{5,9},{6,10},{7,11},{8,4},{9,5},... | collective-permute-start | bytes 49160 | tf_op jit(solution)/shard_map/ppermute | solution.py:201
  10.4 0.0 collective-permute-start.4
  10.4 0.8 %collective-permute-start.3 = (s32[32,128]{1,0:T(8,128)S(1)}, s32[32,128]{1,0:T(8,128)S(1)}, u32[]{:S(2)}, u32[]{:S(2)}) collective-permute-start(s32[32,128]{1,0:T(8,128)S(1)} %pad_add_fusion.refs_0_), channel_id=1, source_target_pairs={{0,4},{1,5},{2,6},{3,7},{4,0},{5,1},{6,2},{7,3},{8,12},{9,13},{10,... | collective-permute-start | bytes 49160 | tf_op jit(solution)/shard_map/ppermute | solution.py:201
  11.2 1.5 %prepare.1 = (f32[256,256]{1,0:T(8,128)S(1)}, bf16[512,2048]{1,0:T(8,128)(2,1)S(1)}, s32[1,256]{1,0:T(1,128)S(1)}, s32[1,256]{1,0:T(1,128)S(1)}) custom-call(bf16[256,256]{1,0:T(8,128)(2,1)} %refs_0_.1, f32[1,256]{1,0:T(1,128)} %bitcast.11, f32[1,256]{1,0:T(1,128)} %bitcast.12, f32[8,48]{1,0:T(8,128)} %refs_3_.1, s32[1,256]{1,0:T(1,128)} %bitcast.13, ...), custom_call_target="tpu_custom_call" | custom-call | tf_op jit(solution)/shard_map/prepare/pallas_call | solution.py:218
  12.7 0.0 collective-permute-done.5.refs_3_
  12.7 2.3 %collective-permute-done.4.refs_2_ = s32[32,128]{1,0:T(8,128)S(1)} collective-permute-done((s32[32,128]{1,0:T(8,128)S(1)}, s32[32,128]{1,0:T(8,128)S(1)}, u32[]{:S(2)}, u32[]{:S(2)}) %collective-permute-start.4) | collective-permute-done | bytes 16416 | tf_op jit(solution)/shard_map/ppermute | solution.py:201
  15.1 0.0 collective-permute-done.3.refs_1_
  15.1 2.7 %route.1 = s16[512,256]{1,0:T(8,128)(2,1)S(1)} custom-call(s32[32,128]{1,0:T(8,128)S(1)} %pad_add_fusion.refs_0_, s32[32,128]{1,0:T(8,128)S(1)} %collective-permute-done.3.refs_1_, s32[32,128]{1,0:T(8,128)S(1)} %collective-permute-done.4.refs_2_, s32[32,128]{1,0:T(8,128)S(1)} %collective-permute-done.5.refs_3_, f32[256,256]{1,0:T(8,128)S(1)} %get-tuple-element.9.refs_4_, ...), custom_call_target="tpu_custom_call" | custom-call | tf_op jit(solution)/shard_map/route/pallas_call | solution.py:233
  17.7 13.3 %all_to_all.5.parts_ref = s16[16,32,256]{2,1,0:T(8,128)(2,1)S(1)} all-to-all(s16[16,32,256]{2,1,0:T(8,128)(2,1)S(1)} %bitcast.6), channel_id=1, replica_groups=mesh['ens'=2,'tile'=16] {'tile'}, dimensions={0} | all-to-all | bytes 524288 | tf_op jit(solution)/shard_map/all_to_all | solution.py:242
  31.0 0.8 %finish.1 = f32[32,256]{1,0:T(8,128)} custom-call(s16[16,32,256]{2,1,0:T(8,128)(2,1)S(1)} %all_to_all.5.parts_ref), custom_call_target="tpu_custom_call" | custom-call | tf_op jit(solution)/shard_map/finish/pallas_call | solution.py:245
  (2 shorter events, 0.0 us)
Async XLA Ops:
  0.8 3.7 %collective-permute-start.2 = (s32[8,128]{1,0:T(8,128)S(1)}, s32[8,128]{1,0:T(8,128)S(1)}, u32[]{:S(2)}, u32[]{:S(2)}) collective-permute-start(s32[8,128]{1,0:T(8,128)S(1)} %bitcast.7), channel_id=1, source_target_pairs={{0,3},{1,2},{2,1},{3,0},{4,7},{5,6},{6,5},{7,4},{8,11},{9,10},{10,... | collective-permute-start | bytes 12296 | tf_op jit(solution)/shard_map/ppermute | solution.py:201
  3.2 3.6 %collective-permute-start.1 = (s32[8,128]{1,0:T(8,128)S(1)}, s32[8,128]{1,0:T(8,128)S(1)}, u32[]{:S(2)}, u32[]{:S(2)}) collective-permute-start(s32[8,128]{1,0:T(8,128)S(1)} %bitcast.8), channel_id=1, source_target_pairs={{0,2},{1,3},{2,0},{3,1},{4,6},{5,7},{6,4},{7,5},{8,10},{9,11},{10,... | collective-permute-start | bytes 12296 | tf_op jit(solution)/shard_map/ppermute | solution.py:201
  3.8 3.0 %collective-permute-start = (s32[8,128]{1,0:T(8,128)S(1)}, s32[8,128]{1,0:T(8,128)S(1)}, u32[]{:S(2)}, u32[]{:S(2)}) collective-permute-start(s32[8,128]{1,0:T(8,128)S(1)} %bitcast.9), channel_id=1, source_target_pairs={{0,1},{1,0},{2,3},{3,2},{4,5},{5,4},{6,7},{7,6},{8,9},{9,8},{10,11... | collective-permute-start | bytes 12296 | tf_op jit(solution)/shard_map/ppermute | solution.py:201
  6.8 5.9 %collective-permute-start.5 = (s32[32,128]{1,0:T(8,128)S(1)}, s32[32,128]{1,0:T(8,128)S(1)}, u32[]{:S(2)}, u32[]{:S(2)}) collective-permute-start(s32[32,128]{1,0:T(8,128)S(1)} %pad_add_fusion.refs_0_), channel_id=1, source_target_pairs={{0,12},{1,13},{2,14},{3,15},{4,8},{5,9},{6,10},{7,11},{8,4},{9,5},... | collective-permute-start | bytes 49160 | tf_op jit(solution)/shard_map/ppermute | solution.py:201
  10.4 4.6 %collective-permute-start.4 = (s32[32,128]{1,0:T(8,128)S(1)}, s32[32,128]{1,0:T(8,128)S(1)}, u32[]{:S(2)}, u32[]{:S(2)}) collective-permute-start(s32[32,128]{1,0:T(8,128)S(1)} %pad_add_fusion.refs_0_), channel_id=1, source_target_pairs={{0,8},{1,9},{2,10},{3,11},{4,12},{5,13},{6,14},{7,15},{8,0},{9,1},... | collective-permute-start | bytes 49160 | tf_op jit(solution)/shard_map/ppermute | solution.py:201
  10.4 4.6 %collective-permute-start.3 = (s32[32,128]{1,0:T(8,128)S(1)}, s32[32,128]{1,0:T(8,128)S(1)}, u32[]{:S(2)}, u32[]{:S(2)}) collective-permute-start(s32[32,128]{1,0:T(8,128)S(1)} %pad_add_fusion.refs_0_), channel_id=1, source_target_pairs={{0,4},{1,5},{2,6},{3,7},{4,0},{5,1},{6,2},{7,3},{8,12},{9,13},{10,... | collective-permute-start | bytes 49160 | tf_op jit(solution)/shard_map/ppermute | solution.py:201

commit v8 on v5

--- a/solution.py
+++ b/solution.py
@@ -9,12 +9,14 @@
 
 LINK = 6
 LANES = 128
+CORES = 2
+ID_ROWS = 16
 VMEM_BYTES = 40 * 1024 * 1024
 CODE_TOP = 32767
 CODE_OCTAVES = 44
 CODE_LOWEST = -26
 CODE_SCALE = 2 * CODE_TOP / (CODE_OCTAVES * math.log(2.0))
-CODE_LEAST = 2.0**CODE_LOWEST
+CODE_FLOOR = 2.0 ** (2 * CODE_LOWEST)
 CODE_ZERO = -CODE_TOP + 1 - CODE_LOWEST * math.log(2.0) * CODE_SCALE
 
 NT = (((1,), (1,)), ((), ()))
@@ -72,8 +74,8 @@
 
 def prepare_kernel(
     rain_hbm, soil_hbm, area_hbm, irf_hbm, dest_hbm, reach_hbm,
-    runoff_ref, response_ref, dest_ref, reach_ref,
-    rain_ref, soil_ref, area_ref, irf_ref, arrived,
+    tiles_ref, response_ref,
+    rain_ref, soil_ref, area_ref, irf_ref, dest_ref, reach_ref, arrived,
 ):
     load(
         (rain_hbm, soil_hbm, area_hbm, irf_hbm, dest_hbm, reach_hbm),
@@ -86,7 +88,10 @@
     storage = soil_ref[...]
     excess = jnp.maximum(rainfall - 0.2 * storage, 0.0)
     runoff = area_ref[...] * excess * excess / (rainfall + 0.8 * storage)
-    runoff_ref[...] = runoff.astype(jnp.bfloat16).astype(jnp.float32)
+    tiles_ref[:hours] = runoff.astype(jnp.bfloat16)
+    place = iota((ID_ROWS, rain_ref.shape[0]), 0)
+    ids = jnp.where(place == 0, dest_ref[...], jnp.where(place == 1, reach_ref[...], 0))
+    tiles_ref[hours:] = ids.astype(jnp.float32).astype(jnp.bfloat16)
     backward = (
         iota((taps, hours), 1) == lax.rem(hours - iota((taps, hours), 0), hours)
     ).astype(jnp.float32)
@@ -102,14 +107,24 @@
         response_ref[hours:, kind * hours : (kind + 1) * hours] = low
 
 
-def route_kernel(
-    meta_ref, runoff_ref, response_ref, dest_ref, reach_ref, flow_ref, *, owners, kinds, reach_rows, basin_rows
-):
-    hours, tiles = runoff_ref.shape
-    outlets = owners * basin_rows
+def respond_kernel(own_ref, other_ref, response_ref, responses_ref):
+    kinds, hours, _ = responses_ref.shape
+    runoff = jnp.concatenate([own_ref[:hours], other_ref[:hours]], axis=1)
+    for kind in range(kinds):
+        both = lax.dot_general(
+            response_ref[:, kind * hours : (kind + 1) * hours], runoff, NN, preferred_element_type=jnp.float32
+        )
+        responses_ref[kind] = both[:hours] + both[hours:]
+
+
+def route_kernel(meta_ref, own_ref, other_ref, responses_ref, flow_ref, *, owners, reach_rows, basin_rows):
+    kinds, hours, tiles = responses_ref.shape
+    outlets = flow_ref.shape[0]
+    core = lax.rem(lax.axis_index("tile"), CORES)
     shift = basin_rows.bit_length() - 1
-    dest = dest_ref[...]
-    reach = reach_ref[...]
+    ids = jnp.concatenate([own_ref[hours:], other_ref[hours:]], axis=1).astype(jnp.float32)
+    dest = ids[0:1].astype(jnp.int32)
+    reach = ids[1:2].astype(jnp.int32)
 
     stack = meta_ref[...]
     spans = reach_rows // LANES
@@ -145,27 +160,22 @@
 
     parent_owner, parent_local = parent_of(dest, basin)
     second_owner, second_local = parent_of(parent_owner, parent_local)
+    def row_of(owner, local):
+        return jnp.where((owner & (CORES - 1)) == core, (owner // CORES) * basin_rows + local, -1)
+
     targets = [
-        dest * basin_rows + basin,
-        parent_owner * basin_rows + parent_local,
-        second_owner * basin_rows + second_local,
+        row_of(dest, basin),
+        jnp.where(parent_owner < 0, -1, row_of(parent_owner, parent_local)),
+        jnp.where(second_owner < 0, -1, row_of(second_owner, second_local)),
     ]
 
-    lagged = runoff_ref[...]
+    routed = responses_ref[0]
+    for k in range(1, kinds):
+        routed = jnp.where(kind == k, responses_ref[k], routed)
     step = 64
     while step:
-        lagged = jnp.where((lag & step) != 0, later(lagged, step), lagged)
+        routed = jnp.where((lag & step) != 0, later(routed, step), routed)
         step //= 2
-    lagged = lagged.astype(jnp.bfloat16)
-    by_kind = jnp.concatenate(
-        [
-            lagged * (kind == k).astype(jnp.float32).astype(jnp.bfloat16)
-            for k in range(kinds)
-        ],
-        axis=0,
-    )
-    routed = lax.dot_general(response_ref[...], by_kind, NN, preferred_element_type=jnp.float32)
-    routed = routed[:hours] + routed[hours:]
     pieces, placements = [], []
     for target in targets:
         pieces.extend(split(routed))
@@ -178,9 +188,9 @@
         NT,
         preferred_element_type=jnp.float32,
     )
-    level = jnp.log(jnp.maximum(flow, CODE_LEAST)) * CODE_SCALE + CODE_ZERO
-    level = jnp.minimum(jnp.round(level), CODE_TOP).astype(jnp.int32)
-    flow_ref[...] = jnp.where(flow < CODE_LEAST, -CODE_TOP, level).astype(jnp.int16)
+    level = jnp.log(jnp.maximum(flow, CODE_FLOOR)) * CODE_SCALE + (CODE_ZERO + CODE_TOP + 0.5)
+    level = jnp.clip(level, 0.0, 2.0 * CODE_TOP).astype(jnp.int32) - CODE_TOP
+    flow_ref[...] = level.astype(jnp.int16)
 
 
 def finish_kernel(parts_ref, section_ref):
@@ -237,13 +247,11 @@
     )
     meta = lax.all_to_all(meta, "tile", split_axis=0, concat_axis=0, tiled=True).reshape(-1, LANES)
 
-    runoff, response, dest, reach = pl.pallas_call(
+    tiles, response = pl.pallas_call(
         prepare_kernel,
         out_shape=(
-            jax.ShapeDtypeStruct((hours, tile_rows), jnp.float32),
+            jax.ShapeDtypeStruct((hours + ID_ROWS, tile_rows), jnp.bfloat16),
             jax.ShapeDtypeStruct((2 * hours, kinds * hours), jnp.bfloat16),
-            jax.ShapeDtypeStruct(row, jnp.int32),
-            jax.ShapeDtypeStruct(row, jnp.int32),
         ),
         in_specs=[held] * 6,
         scratch_shapes=[
@@ -251,6 +259,8 @@
             pltpu.VMEM(row, jnp.float32),
             pltpu.VMEM(row, jnp.float32),
             pltpu.VMEM(irf.shape, jnp.float32),
+            pltpu.VMEM(row, jnp.int32),
+            pltpu.VMEM(row, jnp.int32),
             pltpu.SemaphoreType.DMA((6,)),
         ],
         compiler_params=params,
@@ -263,18 +273,31 @@
         in_hbm(tile_dest, row),
         in_hbm(tile_reach, row),
     )
+    others = lax.ppermute(tiles, "tile", [(i, i ^ 1) for i in range(owners)])
+
+    responses = pl.pallas_call(
+        respond_kernel,
+        out_shape=jax.ShapeDtypeStruct((kinds, hours, CORES * tile_rows), jnp.float32),
+        compiler_params=params,
+        name="respond",
+    )(tiles, others, response)
 
     flow = pl.pallas_call(
         lambda *refs: route_kernel(
-            *refs, owners=owners, kinds=kinds, reach_rows=reach_basin.shape[0], basin_rows=basin_rows
+            *refs, owners=owners, reach_rows=reach_basin.shape[0], basin_rows=basin_rows
         ),
-        out_shape=jax.ShapeDtypeStruct((owners * basin_rows, hours), jnp.int16),
+        out_shape=jax.ShapeDtypeStruct((owners // CORES * basin_rows, hours), jnp.int16),
         compiler_params=params,
         name="route",
-    )(meta, runoff, response, dest, reach)
+    )(meta, tiles, others, responses)
 
     parts = lax.all_to_all(
-        flow.reshape(owners, basin_rows, hours), "tile", split_axis=0, concat_axis=0, tiled=True
+        flow.reshape(owners // CORES, basin_rows, hours),
+        "tile",
+        split_axis=0,
+        concat_axis=0,
+        axis_index_groups=[list(range(core, owners, CORES)) for core in range(CORES)],
+        tiled=True,
     )
     return pl.pallas_call(
         finish_kernel,

time: 32 us -> 32.5 us (1.016)
  local copies, waits for them, and re-layouts: 0 us -> 4.11 us
  blocking collectives: 12.6 us -> 9.74 us
  waiting for transfers between devices: 5.36 us -> 3.68 us
  Pallas kernels: 6.32 us -> 7.09 us
    unnamed x0 -> x4, local copies, waits for them, and re-layouts: none -> 4.11 us
    all_to_all x1, blocking collectives: 12.6 us -> 9.74 us  [per_device(): lax.all_to_all(flow.reshape(owners // CORES, basin_rows, hours), 'tile',...]
    all_to_all x1, waiting for transfers between devices: 5.36 us -> 3.67 us  [per_device(): lax.all_to_all(meta, 'tile', split_axis=0, concat_axis=0, tiled=True)]
    pallas_call x2 -> x3, Pallas kernels: 4.17 us -> 5.01 us  [the longest x1 2.22 us: per_device(): pl.pallas_call(lambda *refs: route_kernel(*refs, owners=owners, reach_row...]
    ppermute x0 -> x1, starting transfers between devices: none -> 0.52 us  [per_device(): others = lax.ppermute(tiles, 'tile', [(i, i ^ 1) for i in range(owners)])]
    all_to_all x1, starting transfers between devices: 7.4 us -> 7.06 us  [per_device(): lax.all_to_all(meta, 'tile', split_axis=0, concat_axis=0, tiled=True)]
  transfers between devices with their start and end apart: 1 -> 2, of which waited for: 1 -> 1; matrix products, arithmetic and copies ran while one was open for 0% -> 0% of each run, Pallas kernels for 5% -> 8%
where the time goes in v8:
time: 32.5 us; the launch traced here: 32.3 us
  blocking collectives  9.74 us (30%)
  starting transfers between devices  7.58 us (23%)
  Pallas kernels  7.09 us (22%)
  local copies, waits for them, and re-layouts  4.11 us (13%)
  waiting for transfers between devices  3.68 us (11%)
    all_to_all x1, blocking collectives, per_device(): lax.all_to_all(flow.reshape(owners // CORES, basin_rows, hours), 'tile',...  9.74 us
    all_to_all x1, starting transfers between devices, per_device(): lax.all_to_all(meta, 'tile', split_axis=0, concat_axis=0, tiled=True)  7.06 us
    unnamed x4, local copies, waits for them, and re-layouts  4.11 us
    all_to_all x1, waiting for transfers between devices, per_device(): lax.all_to_all(meta, 'tile', split_axis=0, concat_axis=0, tiled=True)  3.67 us
    pallas_call x1, Pallas kernels, per_device(): pl.pallas_call(lambda *refs: route_kernel(*refs, owners=owners, reach_row...  2.22 us
    pallas_call x1, Pallas kernels, per_device(): pl.pallas_call(prepare_kernel, out_shape=(jax.ShapeDtypeStruct((hours + I...  1.52 us
    pallas_call x1, Pallas kernels, per_device(): pl.pallas_call(pack_kernel, out_shape=jax.ShapeDtypeStruct((owners, field...  1.37 us
    pallas_call x1, Pallas kernels, per_device(): pl.pallas_call(respond_kernel, out_shape=jax.ShapeDtypeStruct((kinds, hou...  1.27 us
  transfers between devices with their start and end apart: 2, of which 1 were waited for; matrix products, arithmetic and copies ran while one was open for 0% of the time, Pallas kernels for 8%

profile of v8, /device:TPU:0, one launch (start us, length us, event | category | flops | bytes accessed | tf_op | source)
XLA Modules:
  0.0 32.3 jit_solution(7698627961268479113)
XLA Ops:
  0.0 1.5 %prepare.1 = (bf16[272,256]{1,0:T(8,128)(2,1)S(1)}, bf16[512,2048]{1,0:T(8,128)(2,1)S(1)}) custom-call(bf16[256,256]{1,0:T(8,128)(2,1)} %rain_hbm.1, f32[1,256]{1,0:T(1,128)} %bitcast.12, f32[1,256]{1,0:T(1,128)} %bitcast.13, f32[8,48]{1,0:T(8,128)} %irf_hbm.1, s32[1,256]{1,0:T(1,128)} %bitcast.14, s32[1,256]{1,0:T(1,128)} %bitcast.15), custom_call_target="tpu_custom_call" | custom-call | tf_op jit(solution)/shard_map/prepare/pallas_call | solution.py:250
  1.5 0.5 %collective-permute-start = (bf16[272,256]{1,0:T(8,128)(2,1)S(1)}, bf16[272,256]{1,0:T(8,128)(2,1)S(1)}, u32[]{:S(2)}, u32[]{:S(2)}) collective-permute-start(bf16[272,256]{1,0:T(8,128)(2,1)S(1)} %get-tuple-element.7.own_ref.refs_1_), channel_id=1, source_target_pairs={{0,1},{1,0},{2,3},{3,2},{4,5},{5,4},{6,7},{7,6},{8,9},{9,8},{10,11... | collective-permute-start | bytes 417800 | tf_op jit(solution)/shard_map/ppermute | solution.py:276
  2.0 1.4 %pack.1 = s32[16,8,128]{2,1,0:T(8,128)} custom-call(s32[1,256]{1,0:T(1,128)} %bitcast.16, s32[1,256]{1,0:T(1,128)} %bitcast.17, s32[1,256]{1,0:T(1,128)} %bitcast.18, s32[1,32]{1,0:T(1,128)} %bitcast.19), custom_call_target="tpu_custom_call" | custom-call | tf_op jit(solution)/shard_map/pack/pallas_call | solution.py:229
  3.4 7.1 %all-to-all-start = ((s32[16,8,128]{2,1,0:T(8,128)}), s32[16,8,128]{2,1,0:T(8,128)S(1)}, u32[]{:S(2)}, u32[]{:S(2)}) async-start(s32[16,8,128]{2,1,0:T(8,128)} %pack.1), calls=%async_computation | async-start | bytes 131072 | tf_op jit(solution)/shard_map/all_to_all | solution.py:248
  10.5 0.0 collective-permute-done.other_ref.refs_2_
  10.5 1.3 %respond.1.refs_3_ = f32[8,256,512]{2,1,0:T(8,128)S(1)} custom-call(bf16[272,256]{1,0:T(8,128)(2,1)S(1)} %get-tuple-element.7.own_ref.refs_1_, bf16[272,256]{1,0:T(8,128)(2,1)S(1)} %collective-permute-done.other_ref.refs_2_, bf16[512,2048]{1,0:T(8,128)(2,1)S(1)} %get-tuple-element.8.response_ref), custom_call_target="tpu_custom_call" | custom-call | tf_op jit(solution)/shard_map/respond/pallas_call | solution.py:278
  11.8 0.0 copy-start
  11.8 1.9 %copy-done = f32[8,256,512]{2,1,0:T(8,128)} copy-done((f32[8,256,512]{2,1,0:T(8,128)}, f32[8,256,512]{2,1,0:T(8,128)S(1)}, u32[]{:S(2)}) %copy-start) | copy-done | bytes 4194328
  13.7 3.7 %all-to-all-done = s32[16,8,128]{2,1,0:T(8,128)S(1)} async-done(((s32[16,8,128]{2,1,0:T(8,128)}), s32[16,8,128]{2,1,0:T(8,128)S(1)}, u32[]{:S(2)}, u32[]{:S(2)}) %all-to-all-start) | async-done | bytes 65568 | tf_op jit(solution)/shard_map/all_to_all | solution.py:248
  17.4 0.0 copy-start.1
  17.4 2.2 %copy-done.1 = f32[8,256,512]{2,1,0:T(8,128)S(1)} copy-done((f32[8,256,512]{2,1,0:T(8,128)S(1)}, f32[8,256,512]{2,1,0:T(8,128)}, u32[]{:S(2)}) %copy-start.1) | copy-done | bytes 4194328
  19.6 2.2 %route.1 = s16[256,256]{1,0:T(8,128)(2,1)S(1)} custom-call(s32[128,128]{1,0:T(8,128)S(1)} %bitcast.11, bf16[272,256]{1,0:T(8,128)(2,1)S(1)} %get-tuple-element.7.own_ref.refs_1_, bf16[272,256]{1,0:T(8,128)(2,1)S(1)} %collective-permute-done.other_ref.refs_2_, f32[8,256,512]{2,1,0:T(8,128)S(1)} %copy-done.1), custom_call_target="tpu_custom_call" | custom-call | tf_op jit(solution)/shard_map/route/pallas_call | solution.py:285
  21.8 9.7 %all_to_all.10.parts_ref = s16[8,32,256]{2,1,0:T(8,128)(2,1)S(1)} all-to-all(s16[8,32,256]{2,1,0:T(8,128)(2,1)S(1)} %bitcast.10), channel_id=1, replica_groups={{0,2,4,6,8,10,12,14},{1,3,5,7,9,11,13,15},{16,18,20,22,24,26,28,30},{17..., dimensions={0} | all-to-all | bytes 262144 | tf_op jit(solution)/shard_map/all_to_all | solution.py:294
  31.5 0.7 %finish.1 = f32[32,256]{1,0:T(8,128)} custom-call(s16[8,32,256]{2,1,0:T(8,128)(2,1)S(1)} %all_to_all.10.parts_ref), custom_call_target="tpu_custom_call" | custom-call | tf_op jit(solution)/shard_map/finish/pallas_call | solution.py:302
Async XLA Ops:
  1.5 9.0 %collective-permute-start = (bf16[272,256]{1,0:T(8,128)(2,1)S(1)}, bf16[272,256]{1,0:T(8,128)(2,1)S(1)}, u32[]{:S(2)}, u32[]{:S(2)}) collective-permute-start(bf16[272,256]{1,0:T(8,128)(2,1)S(1)} %get-tuple-element.7.own_ref.refs_1_), channel_id=1, source_target_pairs={{0,1},{1,0},{2,3},{3,2},{4,5},{5,4},{6,7},{7,6},{8,9},{9,8},{10,11... | collective-permute-start | bytes 417800 | tf_op jit(solution)/shard_map/ppermute | solution.py:276
  3.4 14.0 %all-to-all-start = ((s32[16,8,128]{2,1,0:T(8,128)}), s32[16,8,128]{2,1,0:T(8,128)S(1)}, u32[]{:S(2)}, u32[]{:S(2)}) async-start(s32[16,8,128]{2,1,0:T(8,128)} %pack.1), calls=%async_computation | async-start | bytes 131072 | tf_op jit(solution)/shard_map/all_to_all | solution.py:248
  11.8 1.9 %copy-start = (f32[8,256,512]{2,1,0:T(8,128)}, f32[8,256,512]{2,1,0:T(8,128)S(1)}, u32[]{:S(2)}) copy-start(f32[8,256,512]{2,1,0:T(8,128)S(1)} %respond.1.refs_3_) | copy-start | bytes 12582916
  17.4 2.2 %copy-start.1 = (f32[8,256,512]{2,1,0:T(8,128)S(1)}, f32[8,256,512]{2,1,0:T(8,128)}, u32[]{:S(2)}) copy-start(f32[8,256,512]{2,1,0:T(8,128)} %copy-done) | copy-start | bytes 12582916

commit v9 on v6

--- a/solution.py
+++ b/solution.py
@@ -9,12 +9,14 @@
 
 LINK = 6
 LANES = 128
+CORES = 2
+ID_ROWS = 16
 VMEM_BYTES = 40 * 1024 * 1024
 CODE_TOP = 32767
 CODE_OCTAVES = 44
 CODE_LOWEST = -26
 CODE_SCALE = 2 * CODE_TOP / (CODE_OCTAVES * math.log(2.0))
-CODE_LEAST = 2.0**CODE_LOWEST
+CODE_FLOOR = 2.0 ** (2 * CODE_LOWEST)
 CODE_ZERO = -CODE_TOP + 1 - CODE_LOWEST * math.log(2.0) * CODE_SCALE
 
 NT = (((1,), (1,)), ((), ()))
@@ -49,11 +51,13 @@
         copy.wait()
 
 
-def prepare_kernel(*refs):
+def prepare_kernel(*refs, early):
     sources, refs = refs[:10], refs[10:]
-    meta_ref, runoff_ref, response_ref, dest_ref, reach_ref, *scratch, arrived = refs
-    basin_ref, kind_ref, lag_ref, parent_ref, rain_ref, soil_ref, area_ref, irf_ref = scratch
-    load(sources, (*scratch, dest_ref, reach_ref), arrived)
+    meta_ref, tiles_ref, response_ref, late_response_ref, *scratch, arrived = refs
+    load(sources, scratch, arrived)
+    (
+        basin_ref, kind_ref, lag_ref, parent_ref, rain_ref, soil_ref, area_ref, irf_ref, dest_ref, reach_ref,
+    ) = scratch
     owners, fields, _ = meta_ref.shape
     rows = [
         values[:, first : first + LANES]
@@ -67,14 +71,16 @@
     block = jnp.concatenate(rows, axis=0)
     for owner in range(owners):
         meta_ref[owner] = block
-
     hours = rain_ref.shape[1]
     kinds, taps = irf_ref.shape
     rainfall = rain_ref[...].astype(jnp.float32).T
     storage = soil_ref[...]
     excess = jnp.maximum(rainfall - 0.2 * storage, 0.0)
     runoff = area_ref[...] * excess * excess / (rainfall + 0.8 * storage)
-    runoff_ref[...] = runoff.astype(jnp.bfloat16).astype(jnp.float32)
+    tiles_ref[:hours] = runoff.astype(jnp.bfloat16)
+    place = iota((ID_ROWS, rain_ref.shape[0]), 0)
+    ids = jnp.where(place == 0, dest_ref[...], jnp.where(place == 1, reach_ref[...], 0))
+    tiles_ref[hours:] = ids.astype(jnp.float32).astype(jnp.bfloat16)
     backward = (
         iota((taps, hours), 1) == lax.rem(hours - iota((taps, hours), 0), hours)
     ).astype(jnp.float32)
@@ -86,18 +92,33 @@
         row = jnp.broadcast_to(reversed_taps[kind : kind + 1], (hours, hours))
         matrix = jnp.where(causal, pltpu.roll(row, 0, 1, stride=1, stride_axis=0), 0.0)
         high, low = split(matrix)
-        response_ref[:hours, kind * hours : (kind + 1) * hours] = high
-        response_ref[hours:, kind * hours : (kind + 1) * hours] = low
+        target = response_ref if kind < early else late_response_ref
+        first = hours * (kind if kind < early else kind - early)
+        target[:hours, first : first + hours] = high
+        target[hours:, first : first + hours] = low
+
+
+def respond_kernel(own_ref, other_ref, response_ref, responses_ref):
+    kinds, hours, _ = responses_ref.shape
+    runoff = jnp.concatenate([own_ref[:hours], other_ref[:hours]], axis=1)
+    for kind in range(kinds):
+        both = lax.dot_general(
+            response_ref[:, kind * hours : (kind + 1) * hours], runoff, NN, preferred_element_type=jnp.float32
+        )
+        responses_ref[kind] = both[:hours] + both[hours:]
 
 
 def route_kernel(
-    meta_ref, runoff_ref, response_ref, dest_ref, reach_ref, flow_ref, *, owners, kinds, reach_rows, basin_rows
+    meta_ref, own_ref, other_ref, responses_ref, late_response_ref, flow_ref, *, owners, reach_rows, basin_rows
 ):
-    hours, tiles = runoff_ref.shape
-    outlets = owners * basin_rows
+    early, hours, tiles = responses_ref.shape
+    late = late_response_ref.shape[1] // hours
+    outlets = flow_ref.shape[0]
+    core = lax.rem(lax.axis_index("tile"), CORES)
     shift = basin_rows.bit_length() - 1
-    dest = dest_ref[...]
-    reach = reach_ref[...]
+    ids = jnp.concatenate([own_ref[hours:], other_ref[hours:]], axis=1).astype(jnp.float32)
+    dest = ids[0:1].astype(jnp.int32)
+    reach = ids[1:2].astype(jnp.int32)
 
     stack = meta_ref[...]
     spans = reach_rows // LANES
@@ -133,27 +154,31 @@
 
     parent_owner, parent_local = parent_of(dest, basin)
     second_owner, second_local = parent_of(parent_owner, parent_local)
+    def row_of(owner, local):
+        return jnp.where((owner & (CORES - 1)) == core, (owner // CORES) * basin_rows + local, -1)
+
     targets = [
-        dest * basin_rows + basin,
-        parent_owner * basin_rows + parent_local,
-        second_owner * basin_rows + second_local,
-    ]
-
-    lagged = runoff_ref[...]
+        row_of(dest, basin),
+        jnp.where(parent_owner < 0, -1, row_of(parent_owner, parent_local)),
+        jnp.where(second_owner < 0, -1, row_of(second_owner, second_local)),
+    ]
+
+    runoff = jnp.concatenate([own_ref[:hours], other_ref[:hours]], axis=1)
+    by_kind = jnp.concatenate(
+        [
+            runoff * (kind == early + k).astype(jnp.float32).astype(jnp.bfloat16)
+            for k in range(late)
+        ],
+        axis=0,
+    )
+    both = lax.dot_general(late_response_ref[...], by_kind, NN, preferred_element_type=jnp.float32)
+    routed = both[:hours] + both[hours:]
+    for k in range(early):
+        routed = jnp.where(kind == k, responses_ref[k], routed)
     step = 64
     while step:
-        lagged = jnp.where((lag & step) != 0, later(lagged, step), lagged)
+        routed = jnp.where((lag & step) != 0, later(routed, step), routed)
         step //= 2
-    lagged = lagged.astype(jnp.bfloat16)
-    by_kind = jnp.concatenate(
-        [
-            lagged * (kind == k).astype(jnp.float32).astype(jnp.bfloat16)
-            for k in range(kinds)
-        ],
-        axis=0,
-    )
-    routed = lax.dot_general(response_ref[...], by_kind, NN, preferred_element_type=jnp.float32)
-    routed = routed[:hours] + routed[hours:]
     pieces, placements = [], []
     for target in targets:
         pieces.extend(split(routed))
@@ -166,9 +191,9 @@
         NT,
         preferred_element_type=jnp.float32,
     )
-    level = jnp.log(jnp.maximum(flow, CODE_LEAST)) * CODE_SCALE + CODE_ZERO
-    level = jnp.minimum(jnp.round(level), CODE_TOP).astype(jnp.int32)
-    flow_ref[...] = jnp.where(flow < CODE_LEAST, -CODE_TOP, level).astype(jnp.int16)
+    level = jnp.log(jnp.maximum(flow, CODE_FLOOR)) * CODE_SCALE + (CODE_ZERO + CODE_TOP + 0.5)
+    level = jnp.clip(level, 0.0, 2.0 * CODE_TOP).astype(jnp.int32) - CODE_TOP
+    flow_ref[...] = level.astype(jnp.int16)
 
 
 def finish_kernel(parts_ref, section_ref):
@@ -199,6 +224,7 @@
 
     row = (1, tile_rows)
     fields = 8 * pl.cdiv(3 * reach_basin.size // LANES + 2, 8)
+
     arguments = [
         pltpu.with_memory_space_constraint(values.reshape(shape), pltpu.HBM)
         for values, shape in (
@@ -214,34 +240,47 @@
             (tile_reach, row),
         )
     ]
-    meta, runoff, response, dest, reach = pl.pallas_call(
-        prepare_kernel,
+    early = kinds // 2
+    meta, tiles, response, late_response = pl.pallas_call(
+        lambda *refs: prepare_kernel(*refs, early=early),
         out_shape=(
             jax.ShapeDtypeStruct((owners, fields, LANES), jnp.int32),
-            jax.ShapeDtypeStruct((hours, tile_rows), jnp.float32),
-            jax.ShapeDtypeStruct((2 * hours, kinds * hours), jnp.bfloat16),
-            jax.ShapeDtypeStruct(row, jnp.int32),
-            jax.ShapeDtypeStruct(row, jnp.int32),
+            jax.ShapeDtypeStruct((hours + ID_ROWS, tile_rows), jnp.bfloat16),
+            jax.ShapeDtypeStruct((2 * hours, early * hours), jnp.bfloat16),
+            jax.ShapeDtypeStruct((2 * hours, (kinds - early) * hours), jnp.bfloat16),
         ),
         in_specs=[pl.BlockSpec(memory_space=pltpu.HBM)] * len(arguments),
-        scratch_shapes=[pltpu.VMEM(values.shape, values.dtype) for values in arguments[:-2]]
+        scratch_shapes=[pltpu.VMEM(values.shape, values.dtype) for values in arguments]
         + [pltpu.SemaphoreType.DMA((len(arguments),))],
         compiler_params=params,
         name="prepare",
     )(*arguments)
     meta = lax.all_to_all(meta, "tile", split_axis=0, concat_axis=0, tiled=True).reshape(-1, LANES)
+    others = lax.ppermute(tiles, "tile", [(i, i ^ 1) for i in range(owners)])
+
+    responses = pl.pallas_call(
+        respond_kernel,
+        out_shape=jax.ShapeDtypeStruct((early, hours, CORES * tile_rows), jnp.float32),
+        compiler_params=params,
+        name="respond",
+    )(tiles, others, response)
 
     flow = pl.pallas_call(
         lambda *refs: route_kernel(
-            *refs, owners=owners, kinds=kinds, reach_rows=reach_basin.shape[0], basin_rows=basin_rows
+            *refs, owners=owners, reach_rows=reach_basin.shape[0], basin_rows=basin_rows
         ),
-        out_shape=jax.ShapeDtypeStruct((owners * basin_rows, hours), jnp.int16),
+        out_shape=jax.ShapeDtypeStruct((owners // CORES * basin_rows, hours), jnp.int16),
         compiler_params=params,
         name="route",
-    )(meta, runoff, response, dest, reach)
+    )(meta, tiles, others, responses, late_response)
 
     parts = lax.all_to_all(
-        flow.reshape(owners, basin_rows, hours), "tile", split_axis=0, concat_axis=0, tiled=True
+        flow.reshape(owners // CORES, basin_rows, hours),
+        "tile",
+        split_axis=0,
+        concat_axis=0,
+        axis_index_groups=[list(range(core, owners, CORES)) for core in range(CORES)],
+        tiled=True,
     )
     return pl.pallas_call(
         finish_kernel,

time: 32 us -> 31.4 us (0.981)
  blocking collectives: 26.7 us -> 9.74 us
  starting transfers between devices: 0 us -> 7.5 us
  waiting for transfers between devices: 0 us -> 4.94 us
  local copies, waits for them, and re-layouts: 0 us -> 2.18 us
  Pallas kernels: 5.05 us -> 6.68 us
    all_to_all x2 -> x1, blocking collectives: 26.7 us -> 9.74 us  [per_device(): lax.all_to_all(flow.reshape(owners // CORES, basin_rows, hours), 'tile',...]
    all_to_all x0 -> x1, starting transfers between devices: none -> 7.05 us  [per_device(): lax.all_to_all(meta, 'tile', split_axis=0, concat_axis=0, tiled=True)]
    all_to_all x0 -> x1, waiting for transfers between devices: none -> 4.94 us  [per_device(): lax.all_to_all(meta, 'tile', split_axis=0, concat_axis=0, tiled=True)]
    unnamed x0 -> x4, local copies, waits for them, and re-layouts: none -> 2.18 us
    pallas_call x2 -> x3, Pallas kernels: 4.27 us -> 5.97 us  [the longest x1 3.01 us: per_device(): pl.pallas_call(lambda *refs: route_kernel(*refs, owners=owners, reach_row...]
    ppermute x0 -> x1, starting transfers between devices: none -> 0.45 us  [per_device(): others = lax.ppermute(tiles, 'tile', [(i, i ^ 1) for i in range(owners)])]
  transfers between devices with their start and end apart: 0 -> 2, of which waited for: 0 -> 1; matrix products, arithmetic and copies ran while one was open for 0% -> 0% of each run, Pallas kernels for 0% -> 2%
where the time goes in v9:
time: 31.4 us; the launch traced here: 31.1 us
  blocking collectives  9.74 us (31%)
  starting transfers between devices  7.5 us (24%)
  Pallas kernels  6.68 us (21%)
  waiting for transfers between devices  4.94 us (16%)
  local copies, waits for them, and re-layouts  2.18 us (7%)
    all_to_all x1, blocking collectives, per_device(): lax.all_to_all(flow.reshape(owners // CORES, basin_rows, hours), 'tile',...  9.74 us
    all_to_all x1, starting transfers between devices, per_device(): lax.all_to_all(meta, 'tile', split_axis=0, concat_axis=0, tiled=True)  7.05 us
    all_to_all x1, waiting for transfers between devices, per_device(): lax.all_to_all(meta, 'tile', split_axis=0, concat_axis=0, tiled=True)  4.94 us
    pallas_call x1, Pallas kernels, per_device(): pl.pallas_call(lambda *refs: route_kernel(*refs, owners=owners, reach_row...  3.01 us
    pallas_call x1, Pallas kernels, per_device(): pl.pallas_call(lambda *refs: prepare_kernel(*refs, early=early), out_shap...  2.25 us
    unnamed x4, local copies, waits for them, and re-layouts  2.18 us
    pallas_call x1, Pallas kernels, per_device(): pl.pallas_call(respond_kernel, out_shape=jax.ShapeDtypeStruct((early, hou...  0.72 us
    pallas_call x1, Pallas kernels, per_device(): pl.pallas_call(finish_kernel, out_shape=jax.ShapeDtypeStruct((basin_rows,...  0.71 us
  transfers between devices with their start and end apart: 2, of which 1 were waited for; matrix products, arithmetic and copies ran while one was open for 0% of the time, Pallas kernels for 2%

profile of v9, /device:TPU:0, one launch (start us, length us, event | category | flops | bytes accessed | tf_op | source)
XLA Modules:
  0.0 31.1 jit_solution(7533418951229727047)
XLA Ops:
  0.0 2.2 %prepare.1 = (s32[16,8,128]{2,1,0:T(8,128)}, bf16[272,256]{1,0:T(8,128)(2,1)S(1)}, bf16[512,1024]{1,0:T(8,128)(2,1)S(1)}, bf16[512,1024]{1,0:T(8,128)(2,1)S(1)}) custom-call(s32[1,256]{1,0:T(1,128)} %bitcast.12, s32[1,256]{1,0:T(1,128)} %bitcast.13, s32[1,256]{1,0:T(1,128)} %bitcast.14, s32[1,32]{1,0:T(1,128)} %bitcast.19, bf16[256,256]{1,0:T(8,128)(2,1)} %refs_4_.1, ...), custom_call_target="tpu_custom_call" | custom-call | tf_op jit(solution)/shard_map/prepare/pallas_call | solution.py:244
  2.3 0.0 copy-start
  2.3 1.0 %copy-done = bf16[512,1024]{1,0:T(8,128)(2,1)} copy-done((bf16[512,1024]{1,0:T(8,128)(2,1)}, bf16[512,1024]{1,0:T(8,128)(2,1)S(1)}, u32[]{:S(2)}) %copy-start) | copy-done | bytes 1048600
  3.2 0.5 %collective-permute-start = (bf16[272,256]{1,0:T(8,128)(2,1)S(1)}, bf16[272,256]{1,0:T(8,128)(2,1)S(1)}, u32[]{:S(2)}, u32[]{:S(2)}) collective-permute-start(bf16[272,256]{1,0:T(8,128)(2,1)S(1)} %get-tuple-element.10.own_ref.refs_1_), channel_id=1, source_target_pairs={{0,1},{1,0},{2,3},{3,2},{4,5},{5,4},{6,7},{7,6},{8,9},{9,8},{10,11... | collective-permute-start | bytes 417800 | tf_op jit(solution)/shard_map/ppermute | solution.py:259
  3.7 7.0 %all-to-all-start = ((s32[16,8,128]{2,1,0:T(8,128)}), s32[16,8,128]{2,1,0:T(8,128)S(1)}, u32[]{:S(2)}, u32[]{:S(2)}) async-start(s32[16,8,128]{2,1,0:T(8,128)} %get-tuple-element.9), calls=%async_computation | async-start | bytes 131072 | tf_op jit(solution)/shard_map/all_to_all | solution.py:258
  10.7 0.0 collective-permute-done.other_ref.refs_2_
  10.7 0.0 copy-start.1
  10.8 1.2 %copy-done.1 = bf16[512,1024]{1,0:T(8,128)(2,1)S(1)} copy-done((bf16[512,1024]{1,0:T(8,128)(2,1)S(1)}, bf16[512,1024]{1,0:T(8,128)(2,1)}, u32[]{:S(2)}) %copy-start.1) | copy-done | bytes 1048600
  12.0 0.7 %respond.1.refs_3_ = f32[4,256,512]{2,1,0:T(8,128)S(1)} custom-call(bf16[272,256]{1,0:T(8,128)(2,1)S(1)} %get-tuple-element.10.own_ref.refs_1_, bf16[272,256]{1,0:T(8,128)(2,1)S(1)} %collective-permute-done.other_ref.refs_2_, bf16[512,1024]{1,0:T(8,128)(2,1)S(1)} %copy-done.1), custom_call_target="tpu_custom_call" | custom-call | tf_op jit(solution)/shard_map/respond/pallas_call | solution.py:261
  12.7 4.9 %all-to-all-done = s32[16,8,128]{2,1,0:T(8,128)S(1)} async-done(((s32[16,8,128]{2,1,0:T(8,128)}), s32[16,8,128]{2,1,0:T(8,128)S(1)}, u32[]{:S(2)}, u32[]{:S(2)}) %all-to-all-start) | async-done | bytes 65568 | tf_op jit(solution)/shard_map/all_to_all | solution.py:258
  17.6 3.0 %route.1 = s16[256,256]{1,0:T(8,128)(2,1)S(1)} custom-call(s32[128,128]{1,0:T(8,128)S(1)} %bitcast.11, bf16[272,256]{1,0:T(8,128)(2,1)S(1)} %get-tuple-element.10.own_ref.refs_1_, bf16[272,256]{1,0:T(8,128)(2,1)S(1)} %collective-permute-done.other_ref.refs_2_, f32[4,256,512]{2,1,0:T(8,128)S(1)} %respond.1.refs_3_, ...), custom_call_target="tpu_custom_call" | custom-call | tf_op jit(solution)/shard_map/route/pallas_call | solution.py:268
  20.7 9.7 %all_to_all.10.parts_ref = s16[8,32,256]{2,1,0:T(8,128)(2,1)S(1)} all-to-all(s16[8,32,256]{2,1,0:T(8,128)(2,1)S(1)} %bitcast.10), channel_id=1, replica_groups={{0,2,4,6,8,10,12,14},{1,3,5,7,9,11,13,15},{16,18,20,22,24,26,28,30},{17..., dimensions={0} | all-to-all | bytes 262144 | tf_op jit(solution)/shard_map/all_to_all | solution.py:277
  30.4 0.7 %finish.1 = f32[32,256]{1,0:T(8,128)} custom-call(s16[8,32,256]{2,1,0:T(8,128)(2,1)S(1)} %all_to_all.10.parts_ref), custom_call_target="tpu_custom_call" | custom-call | tf_op jit(solution)/shard_map/finish/pallas_call | solution.py:285
Async XLA Ops:
  2.3 1.0 %copy-start = (bf16[512,1024]{1,0:T(8,128)(2,1)}, bf16[512,1024]{1,0:T(8,128)(2,1)S(1)}, u32[]{:S(2)}) copy-start(bf16[512,1024]{1,0:T(8,128)(2,1)S(1)} %get-tuple-element.11.response_ref) | copy-start | bytes 3145732
  3.2 7.5 %collective-permute-start = (bf16[272,256]{1,0:T(8,128)(2,1)S(1)}, bf16[272,256]{1,0:T(8,128)(2,1)S(1)}, u32[]{:S(2)}, u32[]{:S(2)}) collective-permute-start(bf16[272,256]{1,0:T(8,128)(2,1)S(1)} %get-tuple-element.10.own_ref.refs_1_), channel_id=1, source_target_pairs={{0,1},{1,0},{2,3},{3,2},{4,5},{5,4},{6,7},{7,6},{8,9},{9,8},{10,11... | collective-permute-start | bytes 417800 | tf_op jit(solution)/shard_map/ppermute | solution.py:259
  3.7 14.0 %all-to-all-start = ((s32[16,8,128]{2,1,0:T(8,128)}), s32[16,8,128]{2,1,0:T(8,128)S(1)}, u32[]{:S(2)}, u32[]{:S(2)}) async-start(s32[16,8,128]{2,1,0:T(8,128)} %get-tuple-element.9), calls=%async_computation | async-start | bytes 131072 | tf_op jit(solution)/shard_map/all_to_all | solution.py:258
  10.7 1.2 %copy-start.1 = (bf16[512,1024]{1,0:T(8,128)(2,1)S(1)}, bf16[512,1024]{1,0:T(8,128)(2,1)}, u32[]{:S(2)}) copy-start(bf16[512,1024]{1,0:T(8,128)(2,1)} %copy-done) | copy-start | bytes 3145732

commit v10 on v9

--- a/solution.py
+++ b/solution.py
@@ -19,6 +19,7 @@
 CODE_FLOOR = 2.0 ** (2 * CODE_LOWEST)
 CODE_ZERO = -CODE_TOP + 1 - CODE_LOWEST * math.log(2.0) * CODE_SCALE
 
+SMALL = pl.CostEstimate(flops=1, bytes_accessed=1, transcendentals=0)
 NT = (((1,), (1,)), ((), ()))
 NN = (((1,), (0,)), ((), ()))
 
@@ -51,13 +52,12 @@
         copy.wait()
 
 
-def prepare_kernel(*refs, early):
-    sources, refs = refs[:10], refs[10:]
-    meta_ref, tiles_ref, response_ref, late_response_ref, *scratch, arrived = refs
-    load(sources, scratch, arrived)
-    (
-        basin_ref, kind_ref, lag_ref, parent_ref, rain_ref, soil_ref, area_ref, irf_ref, dest_ref, reach_ref,
-    ) = scratch
+def pack_kernel(basin_hbm, kind_hbm, lag_hbm, parent_hbm, meta_ref, basin_ref, kind_ref, lag_ref, parent_ref, arrived):
+    load(
+        (basin_hbm, kind_hbm, lag_hbm, parent_hbm),
+        (basin_ref, kind_ref, lag_ref, parent_ref),
+        arrived,
+    )
     owners, fields, _ = meta_ref.shape
     rows = [
         values[:, first : first + LANES]
@@ -71,6 +71,13 @@
     block = jnp.concatenate(rows, axis=0)
     for owner in range(owners):
         meta_ref[owner] = block
+
+
+def prepare_kernel(after_hbm, *refs, early):
+    del after_hbm
+    sources, (tiles_ref, response_ref, late_response_ref, *scratch, arrived) = refs[:6], refs[6:]
+    rain_ref, soil_ref, area_ref, irf_ref, dest_ref, reach_ref = scratch
+    load(sources, scratch, arrived)
     hours = rain_ref.shape[1]
     kinds, taps = irf_ref.shape
     rainfall = rain_ref[...].astype(jnp.float32).T
@@ -225,43 +232,56 @@
     row = (1, tile_rows)
     fields = 8 * pl.cdiv(3 * reach_basin.size // LANES + 2, 8)
 
+    held = pl.BlockSpec(memory_space=pltpu.HBM)
+
+    def in_hbm(values, shape):
+        return pltpu.with_memory_space_constraint(values.reshape(shape), pltpu.HBM)
+
+    def loaded(arguments):
+        shapes = [pltpu.VMEM(values.shape, values.dtype) for values in arguments]
+        return shapes + [pltpu.SemaphoreType.DMA((len(arguments),))]
+
+    numbers = [in_hbm(values, (1, -1)) for values in (reach_basin, reach_kind, reach_lag, outlet_parent)]
+    packed = pl.pallas_call(
+        pack_kernel,
+        out_shape=jax.ShapeDtypeStruct((owners, fields, LANES), jnp.int32),
+        in_specs=[held] * len(numbers),
+        scratch_shapes=loaded(numbers),
+        compiler_params=params,
+        cost_estimate=SMALL,
+        name="pack",
+    )(*numbers)
+    meta = lax.all_to_all(packed, "tile", split_axis=0, concat_axis=0, tiled=True).reshape(-1, LANES)
+
     arguments = [
-        pltpu.with_memory_space_constraint(values.reshape(shape), pltpu.HBM)
-        for values, shape in (
-            (reach_basin, (1, -1)),
-            (reach_kind, (1, -1)),
-            (reach_lag, (1, -1)),
-            (outlet_parent, (1, -1)),
-            (rain, rain.shape),
-            (soil, row),
-            (tile_area, row),
-            (irf, irf.shape),
-            (tile_dest, row),
-            (tile_reach, row),
-        )
+        in_hbm(rain, rain.shape),
+        in_hbm(soil, row),
+        in_hbm(tile_area, row),
+        in_hbm(irf, irf.shape),
+        in_hbm(tile_dest, row),
+        in_hbm(tile_reach, row),
     ]
     early = kinds // 2
-    meta, tiles, response, late_response = pl.pallas_call(
+    tiles, response, late_response = pl.pallas_call(
         lambda *refs: prepare_kernel(*refs, early=early),
         out_shape=(
-            jax.ShapeDtypeStruct((owners, fields, LANES), jnp.int32),
             jax.ShapeDtypeStruct((hours + ID_ROWS, tile_rows), jnp.bfloat16),
             jax.ShapeDtypeStruct((2 * hours, early * hours), jnp.bfloat16),
             jax.ShapeDtypeStruct((2 * hours, (kinds - early) * hours), jnp.bfloat16),
         ),
-        in_specs=[pl.BlockSpec(memory_space=pltpu.HBM)] * len(arguments),
-        scratch_shapes=[pltpu.VMEM(values.shape, values.dtype) for values in arguments]
-        + [pltpu.SemaphoreType.DMA((len(arguments),))],
-        compiler_params=params,
+        in_specs=[held] * (len(arguments) + 1),
+        scratch_shapes=loaded(arguments),
+        compiler_params=params,
+        cost_estimate=SMALL,
         name="prepare",
-    )(*arguments)
-    meta = lax.all_to_all(meta, "tile", split_axis=0, concat_axis=0, tiled=True).reshape(-1, LANES)
+    )(in_hbm(packed, packed.shape), *arguments)
     others = lax.ppermute(tiles, "tile", [(i, i ^ 1) for i in range(owners)])
 
     responses = pl.pallas_call(
         respond_kernel,
         out_shape=jax.ShapeDtypeStruct((early, hours, CORES * tile_rows), jnp.float32),
         compiler_params=params,
+        cost_estimate=SMALL,
         name="respond",
     )(tiles, others, response)
 

time: 31.4 us -> 32 us (1.019)
  local copies, waits for them, and re-layouts: 2.18 us -> 2.8 us
    pallas_call x0 -> x1, Pallas kernels: none -> 0.76 us  [per_device(): pl.pallas_call(pack_kernel, out_shape=jax.ShapeDtypeStruct((owners, field...]
    pallas_call x1, Pallas kernels: 2.25 us -> 1.52 us  [per_device(): pl.pallas_call(lambda *refs: prepare_kernel(*refs, early=early), out_shap...]
    unnamed x4 -> x6, local copies, waits for them, and re-layouts: 2.18 us -> 2.8 us
where the time goes in v10:
time: 32 us; the launch traced here: 31.8 us
  blocking collectives  9.74 us (30%)
  starting transfers between devices  7.5 us (23%)
  Pallas kernels  6.71 us (21%)
  waiting for transfers between devices  4.94 us (15%)
  local copies, waits for them, and re-layouts  2.8 us (9%)
    all_to_all x1, blocking collectives, per_device(): lax.all_to_all(flow.reshape(owners // CORES, basin_rows, hours), 'tile',...  9.74 us
    all_to_all x1, starting transfers between devices, per_device(): lax.all_to_all(packed, 'tile', split_axis=0, concat_axis=0, tiled=True)  7.05 us
    all_to_all x1, waiting for transfers between devices, per_device(): lax.all_to_all(packed, 'tile', split_axis=0, concat_axis=0, tiled=True)  4.93 us
    pallas_call x1, Pallas kernels, per_device(): pl.pallas_call(lambda *refs: route_kernel(*refs, owners=owners, reach_row...  3.01 us
    unnamed x6, local copies, waits for them, and re-layouts  2.8 us
    pallas_call x1, Pallas kernels, per_device(): pl.pallas_call(lambda *refs: prepare_kernel(*refs, early=early), out_shap...  1.52 us
    pallas_call x1, Pallas kernels, per_device(): pl.pallas_call(pack_kernel, out_shape=jax.ShapeDtypeStruct((owners, field...  0.76 us
    pallas_call x1, Pallas kernels, per_device(): pl.pallas_call(respond_kernel, out_shape=jax.ShapeDtypeStruct((early, hou...  0.72 us
  transfers between devices with their start and end apart: 2, of which 1 were waited for; matrix products, arithmetic and copies ran while one was open for 0% of the time, Pallas kernels for 2%

profile of v10, /device:TPU:0, one launch (start us, length us, event | category | flops | bytes accessed | tf_op | source)
XLA Modules:
  0.0 31.8 jit_solution(9325622904883311179)
XLA Ops:
  0.0 0.8 %pack.1.refs_0_ = s32[16,8,128]{2,1,0:T(8,128)S(1)} custom-call(s32[1,256]{1,0:T(1,128)} %bitcast.12, s32[1,256]{1,0:T(1,128)} %bitcast.13, s32[1,256]{1,0:T(1,128)} %bitcast.14, s32[1,32]{1,0:T(1,128)} %bitcast.19), custom_call_target="tpu_custom_call" | custom-call | flops 1 | bytes 1 | tf_op jit(solution)/shard_map/pack/pallas_call | solution.py:245
  0.8 0.0 copy-start.2
  0.8 0.6 %copy-done.2 = s32[16,8,128]{2,1,0:T(8,128)} copy-done((s32[16,8,128]{2,1,0:T(8,128)}, s32[16,8,128]{2,1,0:T(8,128)S(1)}, u32[]{:S(2)}) %copy-start.2) | copy-done | bytes 65560
  1.4 1.5 %prepare.1 = (bf16[272,256]{1,0:T(8,128)(2,1)S(1)}, bf16[512,1024]{1,0:T(8,128)(2,1)S(1)}, bf16[512,1024]{1,0:T(8,128)(2,1)S(1)}) custom-call(s32[16,8,128]{2,1,0:T(8,128)} %copy-done.2, bf16[256,256]{1,0:T(8,128)(2,1)} %refs_1_.1, f32[1,256]{1,0:T(1,128)} %bitcast.15, f32[1,256]{1,0:T(1,128)} %bitcast.16, f32[8,48]{1,0:T(8,128)} %refs_4_.1, ...), custom_call_target="tpu_custom_call" | custom-call | flops 1 | bytes 1 | tf_op jit(solution)/shard_map/prepare/pallas_call | solution.py:265
  2.9 0.0 copy-start
  2.9 1.0 %copy-done = bf16[512,1024]{1,0:T(8,128)(2,1)} copy-done((bf16[512,1024]{1,0:T(8,128)(2,1)}, bf16[512,1024]{1,0:T(8,128)(2,1)S(1)}, u32[]{:S(2)}) %copy-start) | copy-done | bytes 1048600
  3.9 0.5 %collective-permute-start = (bf16[272,256]{1,0:T(8,128)(2,1)S(1)}, bf16[272,256]{1,0:T(8,128)(2,1)S(1)}, u32[]{:S(2)}, u32[]{:S(2)}) collective-permute-start(bf16[272,256]{1,0:T(8,128)(2,1)S(1)} %get-tuple-element.8.own_ref.refs_1_), channel_id=1, source_target_pairs={{0,1},{1,0},{2,3},{3,2},{4,5},{5,4},{6,7},{7,6},{8,9},{9,8},{10,11... | collective-permute-start | bytes 417800 | tf_op jit(solution)/shard_map/ppermute | solution.py:278
  4.3 7.0 %all-to-all-start = ((s32[16,8,128]{2,1,0:T(8,128)}), s32[16,8,128]{2,1,0:T(8,128)S(1)}, u32[]{:S(2)}, u32[]{:S(2)}) async-start(s32[16,8,128]{2,1,0:T(8,128)} %copy-done.2), calls=%async_computation | async-start | bytes 131072 | tf_op jit(solution)/shard_map/all_to_all | solution.py:254
  11.4 0.0 collective-permute-done.other_ref.refs_2_
  11.4 0.0 copy-start.1
  11.4 1.2 %copy-done.1 = bf16[512,1024]{1,0:T(8,128)(2,1)S(1)} copy-done((bf16[512,1024]{1,0:T(8,128)(2,1)S(1)}, bf16[512,1024]{1,0:T(8,128)(2,1)}, u32[]{:S(2)}) %copy-start.1) | copy-done | bytes 1048600
  12.6 0.7 %respond.1.refs_3_ = f32[4,256,512]{2,1,0:T(8,128)S(1)} custom-call(bf16[272,256]{1,0:T(8,128)(2,1)S(1)} %get-tuple-element.8.own_ref.refs_1_, bf16[272,256]{1,0:T(8,128)(2,1)S(1)} %collective-permute-done.other_ref.refs_2_, bf16[512,1024]{1,0:T(8,128)(2,1)S(1)} %copy-done.1), custom_call_target="tpu_custom_call" | custom-call | flops 1 | bytes 1 | tf_op jit(solution)/shard_map/respond/pallas_call | solution.py:280
  13.4 4.9 %all-to-all-done = s32[16,8,128]{2,1,0:T(8,128)S(1)} async-done(((s32[16,8,128]{2,1,0:T(8,128)}), s32[16,8,128]{2,1,0:T(8,128)S(1)}, u32[]{:S(2)}, u32[]{:S(2)}) %all-to-all-start) | async-done | bytes 65568 | tf_op jit(solution)/shard_map/all_to_all | solution.py:254
  18.3 3.0 %route.1 = s16[256,256]{1,0:T(8,128)(2,1)S(1)} custom-call(s32[128,128]{1,0:T(8,128)S(1)} %bitcast.11, bf16[272,256]{1,0:T(8,128)(2,1)S(1)} %get-tuple-element.8.own_ref.refs_1_, bf16[272,256]{1,0:T(8,128)(2,1)S(1)} %collective-permute-done.other_ref.refs_2_, f32[4,256,512]{2,1,0:T(8,128)S(1)} %respond.1.refs_3_, bf16[512,1024]{1,0:T(8,128)(2,1)S(1)} %get-tuple-element.10.refs_4_), custom_call_target="tpu_custom_call" | custom-call | tf_op jit(solution)/shard_map/route/pallas_call | solution.py:288
  21.3 9.7 %all_to_all.10.parts_ref = s16[8,32,256]{2,1,0:T(8,128)(2,1)S(1)} all-to-all(s16[8,32,256]{2,1,0:T(8,128)(2,1)S(1)} %bitcast.10), channel_id=1, replica_groups={{0,2,4,6,8,10,12,14},{1,3,5,7,9,11,13,15},{16,18,20,22,24,26,28,30},{17..., dimensions={0} | all-to-all | bytes 262144 | tf_op jit(solution)/shard_map/all_to_all | solution.py:297
  31.0 0.7 %finish.1 = f32[32,256]{1,0:T(8,128)} custom-call(s16[8,32,256]{2,1,0:T(8,128)(2,1)S(1)} %all_to_all.10.parts_ref), custom_call_target="tpu_custom_call" | custom-call | tf_op jit(solution)/shard_map/finish/pallas_call | solution.py:305
Async XLA Ops:
  0.8 0.6 %copy-start.2 = (s32[16,8,128]{2,1,0:T(8,128)}, s32[16,8,128]{2,1,0:T(8,128)S(1)}, u32[]{:S(2)}) copy-start(s32[16,8,128]{2,1,0:T(8,128)S(1)} %pack.1.refs_0_) | copy-start | bytes 196612
  2.9 1.0 %copy-start = (bf16[512,1024]{1,0:T(8,128)(2,1)}, bf16[512,1024]{1,0:T(8,128)(2,1)S(1)}, u32[]{:S(2)}) copy-start(bf16[512,1024]{1,0:T(8,128)(2,1)S(1)} %get-tuple-element.9.response_ref) | copy-start | bytes 3145732
  3.9 7.5 %collective-permute-start = (bf16[272,256]{1,0:T(8,128)(2,1)S(1)}, bf16[272,256]{1,0:T(8,128)(2,1)S(1)}, u32[]{:S(2)}, u32[]{:S(2)}) collective-permute-start(bf16[272,256]{1,0:T(8,128)(2,1)S(1)} %get-tuple-element.8.own_ref.refs_1_), channel_id=1, source_target_pairs={{0,1},{1,0},{2,3},{3,2},{4,5},{5,4},{6,7},{7,6},{8,9},{9,8},{10,11... | collective-permute-start | bytes 417800 | tf_op jit(solution)/shard_map/ppermute | solution.py:278
  4.3 14.0 %all-to-all-start = ((s32[16,8,128]{2,1,0:T(8,128)}), s32[16,8,128]{2,1,0:T(8,128)S(1)}, u32[]{:S(2)}, u32[]{:S(2)}) async-start(s32[16,8,128]{2,1,0:T(8,128)} %copy-done.2), calls=%async_computation | async-start | bytes 131072 | tf_op jit(solution)/shard_map/all_to_all | solution.py:254
  11.4 1.2 %copy-start.1 = (bf16[512,1024]{1,0:T(8,128)(2,1)S(1)}, bf16[512,1024]{1,0:T(8,128)(2,1)}, u32[]{:S(2)}) copy-start(bf16[512,1024]{1,0:T(8,128)(2,1)} %copy-done) | copy-start | bytes 3145732

commit v11 on v10

v11 whole, which is shorter than its diff:
```python
import math

import jax
import jax.numpy as jnp
from jax import lax
from jax.experimental import pallas as pl
from jax.experimental.pallas import tpu as pltpu
from jax.sharding import PartitionSpec as P

LINK = 6
LANES = 128
CORES = 2
FIELDS = 8
VMEM_BYTES = 40 * 1024 * 1024
CODE_TOP = 32767
CODE_OCTAVES = 44
CODE_LOWEST = -26
CODE_SCALE = 2 * CODE_TOP / (CODE_OCTAVES * math.log(2.0))
CODE_FLOOR = 2.0 ** (2 * CODE_LOWEST)
CODE_ZERO = -CODE_TOP + 1 - CODE_LOWEST * math.log(2.0) * CODE_SCALE

SMALL = pl.CostEstimate(flops=1, bytes_accessed=1, transcendentals=0)
NT = (((1,), (1,)), ((), ()))
NN = (((1,), (0,)), ((), ()))


def iota(shape, axis):
    return lax.broadcasted_iota(jnp.int32, shape, axis)


def split(values):
    high = values.astype(jnp.bfloat16)
    return high, (values - high.astype(jnp.float32)).astype(jnp.bfloat16)


def one_hot(row, count):
    return (iota((count, row.shape[1]), 0) == row).astype(jnp.float32).astype(jnp.bfloat16)


def later_rows(values, hours):
    rows = values.shape[0]
    if hours % 8 == 0:
        padding = jnp.zeros((hours, values.shape[1]), values.dtype)
        return jnp.concatenate([padding, values[: rows - hours]], axis=0)
    return jnp.where(iota(values.shape, 0) < hours, 0.0, pltpu.roll(values, hours, 0))


def later_lanes(values, hours):
    return jnp.where(iota(values.shape, 1) < hours, 0.0, pltpu.roll(values, hours, 1))


def load(sources, targets, arrived):
    copies = [
        pltpu.make_async_copy(source, target, arrived.at[j])
        for j, (source, target) in enumerate(zip(sources, targets))
    ]
    for copy in copies:
        copy.start()
    for copy in copies:
        copy.wait()


def lane_rows(values):
    return [values[:, first : first + LANES] for first in range(0, values.shape[1], LANES)]


def pack_kernel(*refs, basin_rows):
    sources, (meta_ref, side_ref, *scratch, arrived) = refs[:8], refs[8:]
    load(sources, scratch, arrived)
    basin, kind, lag, parent, soil, area, dest, reach = [ref[...] for ref in scratch]
    shift = basin_rows.bit_length() - 1
    empty = jnp.zeros((1, LANES - basin_rows), jnp.int32)
    rows = lane_rows(basin) + lane_rows(kind) + lane_rows(lag)
    rows.append(jnp.concatenate([lax.shift_right_arithmetic(parent, shift) + 1, empty], axis=1))
    rows.append(jnp.concatenate([parent & (basin_rows - 1), empty], axis=1))
    block = jnp.concatenate(rows, axis=0).astype(jnp.float32)
    meta_ref[...] = jnp.concatenate([block] * (meta_ref.shape[0] // FIELDS), axis=0).astype(jnp.bfloat16)
    side_ref[...] = jnp.concatenate(
        lane_rows(soil)
        + lane_rows(area)
        + lane_rows(dest.astype(jnp.float32))
        + lane_rows(reach.astype(jnp.float32)),
        axis=0,
    )


def prepare_kernel(
    rain_hbm, irf_hbm, other_rain_ref, side_ref, other_side_ref,
    runoff_ref, ids_ref, responses_ref, late_response_ref,
    rain_ref, irf_ref, arrived,
):
    load((rain_hbm, irf_hbm), (rain_ref, irf_ref), arrived)
    tile_rows, hours = rain_ref.shape
    kinds, taps = irf_ref.shape
    early = responses_ref.shape[0]
    spans = tile_rows // LANES
    sides = (side_ref[...], other_side_ref[...])

    def side_row(item):
        return jnp.concatenate(
            [side[j : j + 1] for side in sides for j in range(item * spans, (item + 1) * spans)], axis=1
        )

    rainfall = jnp.concatenate(
        [rain_ref[...].astype(jnp.float32).T, other_rain_ref[...].astype(jnp.float32).T], axis=1
    )
    storage = side_row(0)
    excess = jnp.maximum(rainfall - 0.2 * storage, 0.0)
    runoff = (side_row(1) * excess * excess / (rainfall + 0.8 * storage)).astype(jnp.bfloat16)
    runoff_ref[...] = runoff
    ids_ref[...] = jnp.concatenate([side_row(2), side_row(3)] * 4, axis=0).astype(jnp.int32)
    backward = (
        iota((taps, hours), 1) == lax.rem(hours - iota((taps, hours), 0), hours)
    ).astype(jnp.float32)
    reversed_taps = lax.dot_general(
        irf_ref[...], backward, NN, precision=lax.Precision.HIGHEST, preferred_element_type=jnp.float32
    )
    causal = iota((hours, hours), 1) <= iota((hours, hours), 0)
    for kind in range(kinds):
        row = jnp.broadcast_to(reversed_taps[kind : kind + 1], (hours, hours))
        matrix = jnp.where(causal, pltpu.roll(row, 0, 1, stride=1, stride_axis=0), 0.0)
        matrix = jnp.concatenate(split(matrix), axis=0)
        if kind < early:
            both = lax.dot_general(matrix, runoff, NN, preferred_element_type=jnp.float32)
            responses_ref[kind] = both[:hours] + both[hours:]
        else:
            late_response_ref[:, (kind - early) * hours : (kind - early + 1) * hours] = matrix


def route_kernel(meta_ref, runoff_ref, ids_ref, responses_ref, late_response_ref, flow_ref, stack_ref, *, basin_rows):
    early, hours, tiles = responses_ref.shape
    late = late_response_ref.shape[1] // hours
    outlets = flow_ref.shape[0]
    owners = meta_ref.shape[0] // FIELDS
    core = lax.rem(lax.axis_index("tile"), CORES)
    dest = ids_ref[0:1]
    reach = ids_ref[1:2]

    stack_ref[...] = meta_ref[...].astype(jnp.float32)

    def table(field):
        return stack_ref[pl.ds(field, owners, stride=FIELDS), :].astype(jnp.bfloat16)

    def picked(values, owner):
        chosen = iota((owners, tiles), 0) == owner
        return jnp.sum(jnp.where(chosen, values, 0.0), axis=0, keepdims=True).astype(jnp.int32)

    spans = (FIELDS - 2) // 3
    reach_table = jnp.concatenate(
        [
            jnp.concatenate([table(item * spans + j) for j in range(spans)], axis=1)
            for item in range(3)
        ],
        axis=0,
    )
    by_reach = lax.dot_general(
        reach_table, one_hot(reach, spans * LANES), NN, preferred_element_type=jnp.float32
    )
    basin, kind, lag = [picked(by_reach[j * owners : (j + 1) * owners], dest) for j in range(3)]
    tree_table = jnp.concatenate([table(3 * spans), table(3 * spans + 1)], axis=0)

    def parent_of(owner, local):
        by_basin = lax.dot_general(
            tree_table, one_hot(local, LANES), NN, preferred_element_type=jnp.float32
        )
        return picked(by_basin[:owners], owner) - 1, picked(by_basin[owners:], owner)

    parent_owner, parent_local = parent_of(dest, basin)
    second_owner, second_local = parent_of(parent_owner, parent_local)

    def row_of(owner, local):
        mine = jnp.logical_and(owner >= 0, (owner & (CORES - 1)) == core)
        return jnp.where(mine, (owner // CORES) * basin_rows + local, -1)

    placements = jnp.concatenate(
        [
            one_hot(row_of(owner, local), outlets)
            for owner, local in (
                (dest, basin),
                (parent_owner, parent_local),
                (second_owner, second_local),
            )
        ],
        axis=0,
    )

    runoff = runoff_ref[...]
    by_kind = jnp.concatenate(
        [
            runoff * (kind == early + k).astype(jnp.float32).astype(jnp.bfloat16)
            for k in range(late)
        ],
        axis=0,
    )
    both = lax.dot_general(late_response_ref[...], by_kind, NN, preferred_element_type=jnp.float32)
    routed = both[:hours] + both[hours:]
    for k in range(early):
        routed = jnp.where(kind == k, responses_ref[k], routed)
    step = 64
    while step:
        routed = jnp.where((lag & step) != 0, later_rows(routed, step), routed)
        step //= 2
    flows = lax.dot_general(
        jnp.concatenate([placements, placements], axis=1),
        jnp.concatenate(split(routed), axis=1),
        NT,
        preferred_element_type=jnp.float32,
    )
    flow = later_lanes(flows[2 * outlets :], LINK)
    flow = later_lanes(flows[outlets : 2 * outlets] + flow, LINK)
    flow = flows[:outlets] + flow
    level = jnp.log(jnp.maximum(flow, CODE_FLOOR)) * CODE_SCALE + (CODE_ZERO + CODE_TOP + 0.5)
    level = jnp.clip(level, 0.0, 2.0 * CODE_TOP).astype(jnp.int32) - CODE_TOP
    flow_ref[...] = level.astype(jnp.int16)


def finish_kernel(parts_ref, section_ref):
    level = parts_ref[...].astype(jnp.int32)
    flow = jnp.exp((level.astype(jnp.float32) - CODE_ZERO) * (1.0 / CODE_SCALE))
    flow = jnp.sum(jnp.where(level == -CODE_TOP, 0.0, flow), axis=0)
    section_ref[...] = jnp.log(1.0 + flow)


def per_device(
    rain,
    soil,
    tile_area,
    tile_dest,
    tile_reach,
    reach_basin,
    reach_kind,
    reach_lag,
    irf,
    outlet_level,
    outlet_parent,
):
    owners = lax.axis_size("tile")
    tile_rows, hours = rain.shape
    basin_rows = outlet_parent.shape[0]
    kinds = irf.shape[0]
    params = pltpu.CompilerParams(vmem_limit_bytes=VMEM_BYTES)
    held = pl.BlockSpec(memory_space=pltpu.HBM)
    whole = pl.BlockSpec(memory_space=pltpu.VMEM)

    def in_hbm(values, shape):
        return pltpu.with_memory_space_constraint(values.reshape(shape), pltpu.HBM)

    def loaded(arguments):
        shapes = [pltpu.VMEM(values.shape, values.dtype) for values in arguments]
        return shapes + [pltpu.SemaphoreType.DMA((len(arguments),))]

    swap = [(i, i ^ 1) for i in range(owners)]
    other_rain = lax.ppermute(rain, "tile", swap)

    numbers = [
        in_hbm(values, (1, -1))
        for values in (
            reach_basin, reach_kind, reach_lag, outlet_parent, soil, tile_area, tile_dest, tile_reach,
        )
    ]
    meta, side = pl.pallas_call(
        lambda *refs: pack_kernel(*refs, basin_rows=basin_rows),
        out_shape=(
            jax.ShapeDtypeStruct((owners * FIELDS, LANES), jnp.bfloat16),
            jax.ShapeDtypeStruct((4 * tile_rows // LANES, LANES), jnp.float32),
        ),
        in_specs=[held] * len(numbers),
        scratch_shapes=loaded(numbers),
        compiler_params=params,
        cost_estimate=SMALL,
        name="pack",
    )(*numbers)
    meta = lax.all_to_all(
        meta.reshape(owners, FIELDS, LANES), "tile", split_axis=0, concat_axis=0, tiled=True
    ).reshape(-1, LANES)
    other_side = lax.ppermute(side, "tile", swap)

    early = kinds // 2
    chip_tiles = CORES * tile_rows
    runoff, ids, responses, late_response = pl.pallas_call(
        prepare_kernel,
        out_shape=(
            jax.ShapeDtypeStruct((hours, chip_tiles), jnp.bfloat16),
            jax.ShapeDtypeStruct((8, chip_tiles), jnp.int32),
            jax.ShapeDtypeStruct((early, hours, chip_tiles), jnp.float32),
            jax.ShapeDtypeStruct((2 * hours, (kinds - early) * hours), jnp.bfloat16),
        ),
        in_specs=[held, held, whole, whole, whole],
        scratch_shapes=loaded((rain, irf)),
        compiler_params=params,
        cost_estimate=SMALL,
        name="prepare",
    )(in_hbm(rain, rain.shape), in_hbm(irf, irf.shape), other_rain, side, other_side)

    flow = pl.pallas_call(
        lambda *refs: route_kernel(*refs, basin_rows=basin_rows),
        out_shape=jax.ShapeDtypeStruct((owners // CORES * basin_rows, hours), jnp.int16),
        scratch_shapes=[pltpu.VMEM(meta.shape, jnp.float32)],
        compiler_params=params,
        name="route",
    )(meta, runoff, ids, responses, late_response)

    parts = lax.all_to_all(
        flow.reshape(owners // CORES, basin_rows, hours),
        "tile",
        split_axis=0,
        concat_axis=0,
        axis_index_groups=[list(range(core, owners, CORES)) for core in range(CORES)],
        tiled=True,
    )
    return pl.pallas_call(
        finish_kernel,
        out_shape=jax.ShapeDtypeStruct((basin_rows, hours), jnp.float32),
        compiler_params=params,
        name="finish",
    )(parts)


def solution(mesh):
    rows = P(("ens", "tile"))
    table = P(("ens", "tile"), None)
    in_specs = (table, rows, rows, table, rows, rows, rows, rows, P(), rows, rows)
    return jax.shard_map(
        per_device, mesh=mesh, in_specs=in_specs, out_specs=table, check_vma=False
    )
```

time: 32 us -> 29.9 us (0.934)
  waiting for transfers between devices: 4.94 us -> 2.66 us
  blocking collectives: 9.74 us -> 11.2 us
  local copies, waits for them, and re-layouts: 2.8 us -> 1.56 us
  Pallas kernels: 6.71 us -> 6.29 us
  starting transfers between devices: 7.5 us -> 7.92 us
    all_to_all x1, waiting for transfers between devices: 4.93 us -> 1.83 us  [per_device(): lax.all_to_all(meta.reshape(owners, FIELDS, LANES), 'tile', split_axis=0,...]
    all_to_all x1, blocking collectives: 9.74 us -> 11.2 us  [per_device(): lax.all_to_all(flow.reshape(owners // CORES, basin_rows, hours), 'tile',...]
    unnamed x6 -> x4, local copies, waits for them, and re-layouts: 2.8 us -> 1.56 us
    ppermute x1 -> x2, waiting for transfers between devices: 0.01 us -> 0.83 us  [the longest x1 0.82 us: per_device(): other_side = lax.ppermute(side, 'tile', swap)]
    pallas_call x4 -> x3, Pallas kernels: 6 us -> 5.58 us  [the longest x1 2.1 us: per_device(): pl.pallas_call(lambda *refs: route_kernel(*refs, basin_rows=basin_rows),...]
    ppermute x1 -> x2, starting transfers between devices: 0.45 us -> 0.86 us  [the longest x1 0.45 us: per_device(): other_rain = lax.ppermute(rain, 'tile', swap)]
  transfers between devices with their start and end apart: 2 -> 3, of which waited for: 1 -> 2; matrix products, arithmetic and copies ran while one was open for 0% -> 0% of each run, Pallas kernels for 2% -> 12%
where the time goes in v11:
time: 29.9 us; the launch traced here: 29.6 us
  blocking collectives  11.2 us (37%)
  starting transfers between devices  7.92 us (26%)
  Pallas kernels  6.29 us (21%)
  waiting for transfers between devices  2.66 us (9%)
  local copies, waits for them, and re-layouts  1.56 us (5%)
    all_to_all x1, blocking collectives, per_device(): lax.all_to_all(flow.reshape(owners // CORES, basin_rows, hours), 'tile',...  11.2 us
    all_to_all x1, starting transfers between devices, per_device(): lax.all_to_all(meta.reshape(owners, FIELDS, LANES), 'tile', split_axis=0,...  7.06 us
    pallas_call x1, Pallas kernels, per_device(): pl.pallas_call(lambda *refs: route_kernel(*refs, basin_rows=basin_rows),...  2.1 us
    pallas_call x1, Pallas kernels, per_device(): pl.pallas_call(prepare_kernel, out_shape=(jax.ShapeDtypeStruct((hours, ch...  2 us
    all_to_all x1, waiting for transfers between devices, per_device(): lax.all_to_all(meta.reshape(owners, FIELDS, LANES), 'tile', split_axis=0,...  1.83 us
    unnamed x4, local copies, waits for them, and re-layouts  1.56 us
    pallas_call x1, Pallas kernels, per_device(): pl.pallas_call(lambda *refs: pack_kernel(*refs, basin_rows=basin_rows), o...  1.48 us
    ppermute x1, waiting for transfers between devices, per_device(): other_side = lax.ppermute(side, 'tile', swap)  0.82 us
  transfers between devices with their start and end apart: 3, of which 2 were waited for; matrix products, arithmetic and copies ran while one was open for 0% of the time, Pallas kernels for 12%

profile of v11, /device:TPU:0, one launch (start us, length us, event | category | flops | bytes accessed | tf_op | source)
XLA Modules:
  0.0 29.6 jit_solution(16321731463651848929)
XLA Ops:
  0.0 0.5 %collective-permute-start = (bf16[256,256]{1,0:T(8,128)(2,1)}, bf16[256,256]{1,0:T(8,128)(2,1)S(1)}, u32[]{:S(2)}, u32[]{:S(2)}) collective-permute-start(bf16[256,256]{1,0:T(8,128)(2,1)} %rain_hbm.1), channel_id=1, source_target_pairs={{0,1},{1,0},{2,3},{3,2},{4,5},{5,4},{6,7},{7,6},{8,9},{9,8},{10,11... | collective-permute-start | bytes 393224 | tf_op jit(solution)/shard_map/ppermute | solution.py:253
  0.5 1.5 %pack.1 = (bf16[128,128]{1,0:T(8,128)(2,1)}, f32[8,128]{1,0:T(8,128)S(1)}) custom-call(s32[1,256]{1,0:T(1,128)} %bitcast.13, s32[1,256]{1,0:T(1,128)} %bitcast.14, s32[1,256]{1,0:T(1,128)} %bitcast.15, s32[1,32]{1,0:T(1,128)} %bitcast.20, f32[1,256]{1,0:T(1,128)} %bitcast.16, f32[1,256]{1,0:T(1,128)} %bitcast.17, s32[1,256]{1,0:T(1,128)} %bitcast.18, ...), custom_call_target="tpu_custom_call" | custom-call | flops 1 | bytes 1 | tf_op jit(solution)/shard_map/pack/pallas_call | solution.py:261
  1.9 7.1 %all-to-all-start = ((bf16[16,8,128]{2,1,0:T(8,128)(2,1)}), bf16[16,8,128]{2,1,0:T(8,128)(2,1)S(1)}, u32[]{:S(2)}, u32[]{:S(2)}) async-start(bf16[16,8,128]{2,1,0:T(8,128)(2,1)} %bitcast.8), calls=%async_computation | async-start | bytes 65536 | tf_op jit(solution)/shard_map/all_to_all | solution.py:273
  9.0 0.4 %collective-permute-start.1 = (f32[8,128]{1,0:T(8,128)S(1)}, f32[8,128]{1,0:T(8,128)S(1)}, u32[]{:S(2)}, u32[]{:S(2)}) collective-permute-start(f32[8,128]{1,0:T(8,128)S(1)} %get-tuple-element.12.side_ref), channel_id=1, source_target_pairs={{0,1},{1,0},{2,3},{3,2},{4,5},{5,4},{6,7},{7,6},{8,9},{9,8},{10,11... | collective-permute-start | bytes 12296 | tf_op jit(solution)/shard_map/ppermute | solution.py:276
  9.4 0.8 %collective-permute-done.1.other_side_ref = f32[8,128]{1,0:T(8,128)S(1)} collective-permute-done((f32[8,128]{1,0:T(8,128)S(1)}, f32[8,128]{1,0:T(8,128)S(1)}, u32[]{:S(2)}, u32[]{:S(2)}) %collective-permute-start.1) | collective-permute-done | bytes 4128 | tf_op jit(solution)/shard_map/ppermute | solution.py:276
  10.2 0.0 collective-permute-done.other_rain_ref
  10.2 0.0 copy-start
  10.3 0.7 %copy-done = bf16[256,256]{1,0:T(8,128)(2,1)} copy-done((bf16[256,256]{1,0:T(8,128)(2,1)}, bf16[256,256]{1,0:T(8,128)(2,1)S(1)}, u32[]{:S(2)}) %copy-start) | copy-done | bytes 131096
  10.9 0.0 copy-start.1
  10.9 0.9 %copy-done.1 = bf16[256,256]{1,0:T(8,128)(2,1)S(1)} copy-done((bf16[256,256]{1,0:T(8,128)(2,1)S(1)}, bf16[256,256]{1,0:T(8,128)(2,1)}, u32[]{:S(2)}) %copy-start.1) | copy-done | bytes 131096
  11.8 2.0 %prepare.1 = (bf16[256,512]{1,0:T(8,128)(2,1)S(1)}, s32[8,512]{1,0:T(8,128)S(1)}, f32[4,256,512]{2,1,0:T(8,128)S(1)}, bf16[512,1024]{1,0:T(8,128)(2,1)S(1)}) custom-call(bf16[256,256]{1,0:T(8,128)(2,1)} %rain_hbm.1, f32[8,48]{1,0:T(8,128)} %irf_hbm.1, bf16[256,256]{1,0:T(8,128)(2,1)S(1)} %copy-done.1, f32[8,128]{1,0:T(8,128)S(1)} %get-tuple-element.12.side_ref, ...), custom_call_target="tpu_custom_call" | custom-call | flops 1 | bytes 1 | tf_op jit(solution)/shard_map/prepare/pallas_call | solution.py:280
  13.8 1.8 %all-to-all-done = bf16[16,8,128]{2,1,0:T(8,128)(2,1)S(1)} async-done(((bf16[16,8,128]{2,1,0:T(8,128)(2,1)}), bf16[16,8,128]{2,1,0:T(8,128)(2,1)S(1)}, u32[]{:S(2)}, u32[]{:S(2)}) %all-to-all-start) | async-done | bytes 32800 | tf_op jit(solution)/shard_map/all_to_all | solution.py:273
  15.6 2.1 %route.1 = s16[256,256]{1,0:T(8,128)(2,1)S(1)} custom-call(bf16[128,128]{1,0:T(8,128)(2,1)S(1)} %bitcast.12, bf16[256,512]{1,0:T(8,128)(2,1)S(1)} %get-tuple-element.13.refs_1_, s32[8,512]{1,0:T(8,128)S(1)} %get-tuple-element.14.refs_2_, f32[4,256,512]{2,1,0:T(8,128)S(1)} %get-tuple-element.15.refs_3_, bf16[512,1024]{1,0:T(8,128)(2,1)S(1)} %get-tuple-element.16.refs_4_), custom_call_target="tpu_custom_call" | custom-call | tf_op jit(solution)/shard_map/route/pallas_call | solution.py:295
  17.8 11.2 %all_to_all.10.parts_ref = s16[8,32,256]{2,1,0:T(8,128)(2,1)S(1)} all-to-all(s16[8,32,256]{2,1,0:T(8,128)(2,1)S(1)} %bitcast.11), channel_id=1, replica_groups={{0,2,4,6,8,10,12,14},{1,3,5,7,9,11,13,15},{16,18,20,22,24,26,28,30},{17..., dimensions={0} | all-to-all | bytes 262144 | tf_op jit(solution)/shard_map/all_to_all | solution.py:303
  28.9 0.7 %finish.1 = f32[32,256]{1,0:T(8,128)} custom-call(s16[8,32,256]{2,1,0:T(8,128)(2,1)S(1)} %all_to_all.10.parts_ref), custom_call_target="tpu_custom_call" | custom-call | tf_op jit(solution)/shard_map/finish/pallas_call | solution.py:311
Async XLA Ops:
  0.0 10.2 %collective-permute-start = (bf16[256,256]{1,0:T(8,128)(2,1)}, bf16[256,256]{1,0:T(8,128)(2,1)S(1)}, u32[]{:S(2)}, u32[]{:S(2)}) collective-permute-start(bf16[256,256]{1,0:T(8,128)(2,1)} %rain_hbm.1), channel_id=1, source_target_pairs={{0,1},{1,0},{2,3},{3,2},{4,5},{5,4},{6,7},{7,6},{8,9},{9,8},{10,11... | collective-permute-start | bytes 393224 | tf_op jit(solution)/shard_map/ppermute | solution.py:253
  1.9 13.7 %all-to-all-start = ((bf16[16,8,128]{2,1,0:T(8,128)(2,1)}), bf16[16,8,128]{2,1,0:T(8,128)(2,1)S(1)}, u32[]{:S(2)}, u32[]{:S(2)}) async-start(bf16[16,8,128]{2,1,0:T(8,128)(2,1)} %bitcast.8), calls=%async_computation | async-start | bytes 65536 | tf_op jit(solution)/shard_map/all_to_all | solution.py:273
  9.0 1.2 %collective-permute-start.1 = (f32[8,128]{1,0:T(8,128)S(1)}, f32[8,128]{1,0:T(8,128)S(1)}, u32[]{:S(2)}, u32[]{:S(2)}) collective-permute-start(f32[8,128]{1,0:T(8,128)S(1)} %get-tuple-element.12.side_ref), channel_id=1, source_target_pairs={{0,1},{1,0},{2,3},{3,2},{4,5},{5,4},{6,7},{7,6},{8,9},{9,8},{10,11... | collective-permute-start | bytes 12296 | tf_op jit(solution)/shard_map/ppermute | solution.py:276
  10.2 0.7 %copy-start = (bf16[256,256]{1,0:T(8,128)(2,1)}, bf16[256,256]{1,0:T(8,128)(2,1)S(1)}, u32[]{:S(2)}) copy-start(bf16[256,256]{1,0:T(8,128)(2,1)S(1)} %collective-permute-done.other_rain_ref) | copy-start | bytes 393220
  10.9 0.9 %copy-start.1 = (bf16[256,256]{1,0:T(8,128)(2,1)S(1)}, bf16[256,256]{1,0:T(8,128)(2,1)}, u32[]{:S(2)}) copy-start(bf16[256,256]{1,0:T(8,128)(2,1)} %copy-done) | copy-start | bytes 393220

commit v12 on v11

--- a/solution.py
+++ b/solution.py
@@ -11,6 +11,7 @@
 LANES = 128
 CORES = 2
 FIELDS = 8
+SIDE_ROWS = 16
 VMEM_BYTES = 40 * 1024 * 1024
 CODE_TOP = 32767
 CODE_OCTAVES = 44
@@ -64,77 +65,77 @@
     return [values[:, first : first + LANES] for first in range(0, values.shape[1], LANES)]
 
 
+def parts_of(values):
+    high = values.astype(jnp.bfloat16).astype(jnp.float32)
+    middle = (values - high).astype(jnp.bfloat16).astype(jnp.float32)
+    return [high, middle, values - high - middle]
+
+
 def pack_kernel(*refs, basin_rows):
-    sources, (meta_ref, side_ref, *scratch, arrived) = refs[:8], refs[8:]
-    load(sources, scratch, arrived)
+    sources, (meta_ref, block_ref, *scratch, arrived) = refs[:9], refs[9:]
+    hours = block_ref.shape[1]
+    tile_rows = block_ref.shape[0] - SIDE_ROWS
+    load(sources, (*scratch, block_ref.at[pl.ds(0, tile_rows)]), arrived)
     basin, kind, lag, parent, soil, area, dest, reach = [ref[...] for ref in scratch]
     shift = basin_rows.bit_length() - 1
     empty = jnp.zeros((1, LANES - basin_rows), jnp.int32)
     rows = lane_rows(basin) + lane_rows(kind) + lane_rows(lag)
     rows.append(jnp.concatenate([lax.shift_right_arithmetic(parent, shift) + 1, empty], axis=1))
     rows.append(jnp.concatenate([parent & (basin_rows - 1), empty], axis=1))
-    block = jnp.concatenate(rows, axis=0).astype(jnp.float32)
-    meta_ref[...] = jnp.concatenate([block] * (meta_ref.shape[0] // FIELDS), axis=0).astype(jnp.bfloat16)
-    side_ref[...] = jnp.concatenate(
-        lane_rows(soil)
-        + lane_rows(area)
-        + lane_rows(dest.astype(jnp.float32))
-        + lane_rows(reach.astype(jnp.float32)),
-        axis=0,
-    )
-
-
-def prepare_kernel(
-    rain_hbm, irf_hbm, other_rain_ref, side_ref, other_side_ref,
-    runoff_ref, ids_ref, responses_ref, late_response_ref,
-    rain_ref, irf_ref, arrived,
-):
-    load((rain_hbm, irf_hbm), (rain_ref, irf_ref), arrived)
-    tile_rows, hours = rain_ref.shape
+    numbers = jnp.concatenate(rows, axis=0).astype(jnp.float32)
+    meta_ref[...] = jnp.concatenate([numbers] * (meta_ref.shape[0] // FIELDS), axis=0).astype(jnp.bfloat16)
+    sides = parts_of(soil) + parts_of(area) + [dest.astype(jnp.float32), reach.astype(jnp.float32)]
+    sides = jnp.concatenate(sides + [jnp.zeros((SIDE_ROWS - len(sides), tile_rows), jnp.float32)], axis=0)
+    block_ref[tile_rows:] = sides.astype(jnp.bfloat16)
+
+
+def response_matrix(reversed_taps):
+    hours = reversed_taps.shape[1]
+    causal = iota((hours, hours), 1) <= iota((hours, hours), 0)
+    row = jnp.broadcast_to(reversed_taps, (hours, hours))
+    matrix = jnp.where(causal, pltpu.roll(row, 0, 1, stride=1, stride_axis=0), 0.0)
+    return jnp.concatenate(split(matrix), axis=0)
+
+
+def prepare_kernel(irf_hbm, own_ref, other_ref, runoff_ref, ids_ref, taps_ref, responses_ref, irf_ref, arrived):
+    copy = pltpu.make_async_copy(irf_hbm, irf_ref, arrived.at[0])
+    copy.start()
+    hours = own_ref.shape[1]
+    tile_rows = own_ref.shape[0] - SIDE_ROWS
     kinds, taps = irf_ref.shape
-    early = responses_ref.shape[0]
-    spans = tile_rows // LANES
-    sides = (side_ref[...], other_side_ref[...])
-
-    def side_row(item):
-        return jnp.concatenate(
-            [side[j : j + 1] for side in sides for j in range(item * spans, (item + 1) * spans)], axis=1
-        )
-
+    sides = jnp.concatenate([own_ref[tile_rows:], other_ref[tile_rows:]], axis=1).astype(jnp.float32)
     rainfall = jnp.concatenate(
-        [rain_ref[...].astype(jnp.float32).T, other_rain_ref[...].astype(jnp.float32).T], axis=1
-    )
-    storage = side_row(0)
+        [ref[:tile_rows].astype(jnp.float32).T for ref in (own_ref, other_ref)], axis=1
+    )
+    storage = sides[0:1] + sides[1:2] + sides[2:3]
+    area = sides[3:4] + sides[4:5] + sides[5:6]
     excess = jnp.maximum(rainfall - 0.2 * storage, 0.0)
-    runoff = (side_row(1) * excess * excess / (rainfall + 0.8 * storage)).astype(jnp.bfloat16)
+    runoff = (area * excess * excess / (rainfall + 0.8 * storage)).astype(jnp.bfloat16)
     runoff_ref[...] = runoff
-    ids_ref[...] = jnp.concatenate([side_row(2), side_row(3)] * 4, axis=0).astype(jnp.int32)
+    ids_ref[...] = sides[:8].astype(jnp.int32)
     backward = (
         iota((taps, hours), 1) == lax.rem(hours - iota((taps, hours), 0), hours)
     ).astype(jnp.float32)
+    copy.wait()
     reversed_taps = lax.dot_general(
         irf_ref[...], backward, NN, precision=lax.Precision.HIGHEST, preferred_element_type=jnp.float32
     )
-    causal = iota((hours, hours), 1) <= iota((hours, hours), 0)
-    for kind in range(kinds):
-        row = jnp.broadcast_to(reversed_taps[kind : kind + 1], (hours, hours))
-        matrix = jnp.where(causal, pltpu.roll(row, 0, 1, stride=1, stride_axis=0), 0.0)
-        matrix = jnp.concatenate(split(matrix), axis=0)
-        if kind < early:
-            both = lax.dot_general(matrix, runoff, NN, preferred_element_type=jnp.float32)
-            responses_ref[kind] = both[:hours] + both[hours:]
-        else:
-            late_response_ref[:, (kind - early) * hours : (kind - early + 1) * hours] = matrix
-
-
-def route_kernel(meta_ref, runoff_ref, ids_ref, responses_ref, late_response_ref, flow_ref, stack_ref, *, basin_rows):
+    taps_ref[...] = reversed_taps
+    for kind in range(responses_ref.shape[0]):
+        both = lax.dot_general(
+            response_matrix(reversed_taps[kind : kind + 1]), runoff, NN, preferred_element_type=jnp.float32
+        )
+        responses_ref[kind] = both[:hours] + both[hours:]
+
+
+def route_kernel(meta_ref, runoff_ref, ids_ref, taps_ref, responses_ref, flow_ref, stack_ref, *, basin_rows):
     early, hours, tiles = responses_ref.shape
-    late = late_response_ref.shape[1] // hours
+    kinds = taps_ref.shape[0]
     outlets = flow_ref.shape[0]
     owners = meta_ref.shape[0] // FIELDS
     core = lax.rem(lax.axis_index("tile"), CORES)
-    dest = ids_ref[0:1]
-    reach = ids_ref[1:2]
+    dest = ids_ref[6:7]
+    reach = ids_ref[7:8]
 
     stack_ref[...] = meta_ref[...].astype(jnp.float32)
 
@@ -187,12 +188,15 @@
     runoff = runoff_ref[...]
     by_kind = jnp.concatenate(
         [
-            runoff * (kind == early + k).astype(jnp.float32).astype(jnp.bfloat16)
-            for k in range(late)
+            runoff * (kind == k).astype(jnp.float32).astype(jnp.bfloat16)
+            for k in range(early, kinds)
         ],
         axis=0,
     )
-    both = lax.dot_general(late_response_ref[...], by_kind, NN, preferred_element_type=jnp.float32)
+    matrices = jnp.concatenate(
+        [response_matrix(taps_ref[k : k + 1]) for k in range(early, kinds)], axis=1
+    )
+    both = lax.dot_general(matrices, by_kind, NN, preferred_element_type=jnp.float32)
     routed = both[:hours] + both[hours:]
     for k in range(early):
         routed = jnp.where(kind == k, responses_ref[k], routed)
@@ -241,16 +245,10 @@
     params = pltpu.CompilerParams(vmem_limit_bytes=VMEM_BYTES)
     held = pl.BlockSpec(memory_space=pltpu.HBM)
     whole = pl.BlockSpec(memory_space=pltpu.VMEM)
+    block = (tile_rows + SIDE_ROWS, hours)
 
     def in_hbm(values, shape):
         return pltpu.with_memory_space_constraint(values.reshape(shape), pltpu.HBM)
-
-    def loaded(arguments):
-        shapes = [pltpu.VMEM(values.shape, values.dtype) for values in arguments]
-        return shapes + [pltpu.SemaphoreType.DMA((len(arguments),))]
-
-    swap = [(i, i ^ 1) for i in range(owners)]
-    other_rain = lax.ppermute(rain, "tile", swap)
 
     numbers = [
         in_hbm(values, (1, -1))
@@ -258,39 +256,40 @@
             reach_basin, reach_kind, reach_lag, outlet_parent, soil, tile_area, tile_dest, tile_reach,
         )
     ]
-    meta, side = pl.pallas_call(
+    meta, own = pl.pallas_call(
         lambda *refs: pack_kernel(*refs, basin_rows=basin_rows),
         out_shape=(
             jax.ShapeDtypeStruct((owners * FIELDS, LANES), jnp.bfloat16),
-            jax.ShapeDtypeStruct((4 * tile_rows // LANES, LANES), jnp.float32),
+            jax.ShapeDtypeStruct(block, jnp.bfloat16),
         ),
-        in_specs=[held] * len(numbers),
-        scratch_shapes=loaded(numbers),
+        in_specs=[held] * (len(numbers) + 1),
+        scratch_shapes=[pltpu.VMEM(values.shape, values.dtype) for values in numbers]
+        + [pltpu.SemaphoreType.DMA((len(numbers) + 1,))],
         compiler_params=params,
         cost_estimate=SMALL,
         name="pack",
-    )(*numbers)
+    )(*numbers, in_hbm(rain, rain.shape))
+    other = lax.ppermute(own, "tile", [(i, i ^ 1) for i in range(owners)])
     meta = lax.all_to_all(
         meta.reshape(owners, FIELDS, LANES), "tile", split_axis=0, concat_axis=0, tiled=True
     ).reshape(-1, LANES)
-    other_side = lax.ppermute(side, "tile", swap)
-
-    early = kinds // 2
+
     chip_tiles = CORES * tile_rows
-    runoff, ids, responses, late_response = pl.pallas_call(
+    early = kinds * 3 // 4
+    runoff, ids, taps, responses = pl.pallas_call(
         prepare_kernel,
         out_shape=(
             jax.ShapeDtypeStruct((hours, chip_tiles), jnp.bfloat16),
             jax.ShapeDtypeStruct((8, chip_tiles), jnp.int32),
+            jax.ShapeDtypeStruct((kinds, hours), jnp.float32),
             jax.ShapeDtypeStruct((early, hours, chip_tiles), jnp.float32),
-            jax.ShapeDtypeStruct((2 * hours, (kinds - early) * hours), jnp.bfloat16),
         ),
-        in_specs=[held, held, whole, whole, whole],
-        scratch_shapes=loaded((rain, irf)),
+        in_specs=[held, whole, whole],
+        scratch_shapes=[pltpu.VMEM(irf.shape, irf.dtype), pltpu.SemaphoreType.DMA((1,))],
         compiler_params=params,
         cost_estimate=SMALL,
         name="prepare",
-    )(in_hbm(rain, rain.shape), in_hbm(irf, irf.shape), other_rain, side, other_side)
+    )(in_hbm(irf, irf.shape), own, other)
 
     flow = pl.pallas_call(
         lambda *refs: route_kernel(*refs, basin_rows=basin_rows),
@@ -298,7 +297,7 @@
         scratch_shapes=[pltpu.VMEM(meta.shape, jnp.float32)],
         compiler_params=params,
         name="route",
-    )(meta, runoff, ids, responses, late_response)
+    )(meta, runoff, ids, taps, responses)
 
     parts = lax.all_to_all(
         flow.reshape(owners // CORES, basin_rows, hours),

time: 29.9 us -> 31 us (1.037)
  local copies, waits for them, and re-layouts: 1.56 us -> 2.86 us
  blocking collectives: 11.2 us -> 10.4 us
  Pallas kernels: 6.29 us -> 7.07 us
    unnamed x4 -> x8, local copies, waits for them, and re-layouts: 1.56 us -> 2.86 us
    ppermute x2 -> x1, waiting for transfers between devices: 0.83 us -> 0.01 us  [per_device(): other = lax.ppermute(own, 'tile', [(i, i ^ 1) for i in range(owners)])]
    all_to_all x1, waiting for transfers between devices: 1.83 us -> 2.59 us  [per_device(): lax.all_to_all(meta.reshape(owners, FIELDS, LANES), 'tile', split_axis=0,...]
    all_to_all x1, blocking collectives: 11.2 us -> 10.4 us  [per_device(): lax.all_to_all(flow.reshape(owners // CORES, basin_rows, hours), 'tile',...]
    pallas_call x1, Pallas kernels: 2.1 us -> 2.7 us  [per_device(): pl.pallas_call(lambda *refs: route_kernel(*refs, basin_rows=basin_rows),...]
    ppermute x2 -> x1, starting transfers between devices: 0.86 us -> 0.52 us  [per_device(): other = lax.ppermute(own, 'tile', [(i, i ^ 1) for i in range(owners)])]
  transfers between devices with their start and end apart: 3 -> 2, of which waited for: 2 -> 1; matrix products, arithmetic and copies ran while one was open for 0% -> 0% of each run, Pallas kernels for 12% -> 6%
where the time goes in v12:
time: 31 us; the launch traced here: 30.6 us
  blocking collectives  10.4 us (34%)
  starting transfers between devices  7.62 us (25%)
  Pallas kernels  7.07 us (23%)
  local copies, waits for them, and re-layouts  2.86 us (9%)
  waiting for transfers between devices  2.59 us (8%)
    all_to_all x1, blocking collectives, per_device(): lax.all_to_all(flow.reshape(owners // CORES, basin_rows, hours), 'tile',...  10.4 us
    all_to_all x1, starting transfers between devices, per_device(): lax.all_to_all(meta.reshape(owners, FIELDS, LANES), 'tile', split_axis=0,...  7.1 us
    unnamed x8, local copies, waits for them, and re-layouts  2.86 us
    pallas_call x1, Pallas kernels, per_device(): pl.pallas_call(lambda *refs: route_kernel(*refs, basin_rows=basin_rows),...  2.7 us
    all_to_all x1, waiting for transfers between devices, per_device(): lax.all_to_all(meta.reshape(owners, FIELDS, LANES), 'tile', split_axis=0,...  2.59 us
    pallas_call x1, Pallas kernels, per_device(): pl.pallas_call(prepare_kernel, out_shape=(jax.ShapeDtypeStruct((hours, ch...  1.92 us
    pallas_call x1, Pallas kernels, per_device(): pl.pallas_call(lambda *refs: pack_kernel(*refs, basin_rows=basin_rows), o...  1.73 us
    pallas_call x1, Pallas kernels, per_device(): pl.pallas_call(finish_kernel, out_shape=jax.ShapeDtypeStruct((basin_rows,...  0.71 us
  transfers between devices with their start and end apart: 2, of which 1 were waited for; matrix products, arithmetic and copies ran while one was open for 0% of the time, Pallas kernels for 6%

profile of v12, /device:TPU:0, one launch (start us, length us, event | category | flops | bytes accessed | tf_op | source)
XLA Modules:
  0.0 30.6 jit_solution(12751467183312384618)
XLA Ops:
  0.0 1.7 %pack.1 = (bf16[128,128]{1,0:T(8,128)(2,1)}, bf16[272,256]{1,0:T(8,128)(2,1)S(1)}) custom-call(s32[1,256]{1,0:T(1,128)} %bitcast.12, s32[1,256]{1,0:T(1,128)} %bitcast.13, s32[1,256]{1,0:T(1,128)} %bitcast.14, s32[1,32]{1,0:T(1,128)} %bitcast.19, f32[1,256]{1,0:T(1,128)} %bitcast.15, f32[1,256]{1,0:T(1,128)} %bitcast.16, s32[1,256]{1,0:T(1,128)} %bitcast.17, ...), custom_call_target="tpu_custom_call" | custom-call | flops 1 | bytes 1 | tf_op jit(solution)/shard_map/pack/pallas_call | solution.py:259
  1.7 0.5 %collective-permute-start = (bf16[272,256]{1,0:T(8,128)(2,1)S(1)}, bf16[272,256]{1,0:T(8,128)(2,1)S(1)}, u32[]{:S(2)}, u32[]{:S(2)}) collective-permute-start(bf16[272,256]{1,0:T(8,128)(2,1)S(1)} %get-tuple-element.12.own_ref), channel_id=1, source_target_pairs={{0,1},{1,0},{2,3},{3,2},{4,5},{5,4},{6,7},{7,6},{8,9},{9,8},{10,11... | collective-permute-start | bytes 417800 | tf_op jit(solution)/shard_map/ppermute | solution.py:272
  2.3 7.1 %all-to-all-start = ((bf16[16,8,128]{2,1,0:T(8,128)(2,1)}), bf16[16,8,128]{2,1,0:T(8,128)(2,1)}, u32[]{:S(2)}, u32[]{:S(2)}) async-start(bf16[16,8,128]{2,1,0:T(8,128)(2,1)} %bitcast.8), calls=%async_computation | async-start | bytes 65536 | tf_op jit(solution)/shard_map/all_to_all | solution.py:273
  9.4 0.0 collective-permute-done.other_ref
  9.4 0.0 copy-start
  9.4 0.6 %copy-done = bf16[272,256]{1,0:T(8,128)(2,1)} copy-done((bf16[272,256]{1,0:T(8,128)(2,1)}, bf16[272,256]{1,0:T(8,128)(2,1)S(1)}, u32[]{:S(2)}) %copy-start) | copy-done | bytes 139288
  10.0 0.0 copy-start.1
  10.0 0.9 %copy-done.1 = bf16[272,256]{1,0:T(8,128)(2,1)S(1)} copy-done((bf16[272,256]{1,0:T(8,128)(2,1)S(1)}, bf16[272,256]{1,0:T(8,128)(2,1)}, u32[]{:S(2)}) %copy-start.1) | copy-done | bytes 139288
  10.9 1.9 %prepare.1 = (bf16[256,512]{1,0:T(8,128)(2,1)S(1)}, s32[8,512]{1,0:T(8,128)S(1)}, f32[8,256]{1,0:T(8,128)S(1)}, f32[6,256,512]{2,1,0:T(8,128)S(1)}) custom-call(f32[8,48]{1,0:T(8,128)} %irf_hbm.1, bf16[272,256]{1,0:T(8,128)(2,1)S(1)} %get-tuple-element.12.own_ref, bf16[272,256]{1,0:T(8,128)(2,1)S(1)} %copy-done.1), custom_call_target="tpu_custom_call" | custom-call | flops 1 | bytes 1 | tf_op jit(solution)/shard_map/prepare/pallas_call | solution.py:279
  12.9 0.0 copy-start.2
  12.9 0.6 %copy-done.2 = s32[8,512]{1,0:T(8,128)} copy-done((s32[8,512]{1,0:T(8,128)}, s32[8,512]{1,0:T(8,128)S(1)}, u32[]{:S(2)}) %copy-start.2) | copy-done | bytes 16408
  13.5 2.6 %all-to-all-done = bf16[16,8,128]{2,1,0:T(8,128)(2,1)} async-done(((bf16[16,8,128]{2,1,0:T(8,128)(2,1)}), bf16[16,8,128]{2,1,0:T(8,128)(2,1)}, u32[]{:S(2)}, u32[]{:S(2)}) %all-to-all-start) | async-done | bytes 32800 | tf_op jit(solution)/shard_map/all_to_all | solution.py:273
  16.1 0.0 copy-start.3
  16.1 0.7 %copy-done.3 = s32[8,512]{1,0:T(8,128)S(1)} copy-done((s32[8,512]{1,0:T(8,128)S(1)}, s32[8,512]{1,0:T(8,128)}, u32[]{:S(2)}) %copy-start.3) | copy-done | bytes 16408
  16.8 2.7 %route.1 = s16[256,256]{1,0:T(8,128)(2,1)S(1)} custom-call(bf16[128,128]{1,0:T(8,128)(2,1)} %bitcast.9.refs_0_, bf16[256,512]{1,0:T(8,128)(2,1)S(1)} %get-tuple-element.13.refs_1_, s32[8,512]{1,0:T(8,128)S(1)} %copy-done.3, f32[8,256]{1,0:T(8,128)S(1)} %get-tuple-element.15.refs_3_, f32[6,256,512]{2,1,0:T(8,128)S(1)} %get-tuple-element.16.refs_4_), custom_call_target="tpu_custom_call" | custom-call | tf_op jit(solution)/shard_map/route/pallas_call | solution.py:294
  19.5 10.4 %all_to_all.10.parts_ref = s16[8,32,256]{2,1,0:T(8,128)(2,1)S(1)} all-to-all(s16[8,32,256]{2,1,0:T(8,128)(2,1)S(1)} %bitcast.11), channel_id=1, replica_groups={{0,2,4,6,8,10,12,14},{1,3,5,7,9,11,13,15},{16,18,20,22,24,26,28,30},{17..., dimensions={0} | all-to-all | bytes 262144 | tf_op jit(solution)/shard_map/all_to_all | solution.py:302
  29.9 0.7 %finish.1 = f32[32,256]{1,0:T(8,128)} custom-call(s16[8,32,256]{2,1,0:T(8,128)(2,1)S(1)} %all_to_all.10.parts_ref), custom_call_target="tpu_custom_call" | custom-call | tf_op jit(solution)/shard_map/finish/pallas_call | solution.py:310
Async XLA Ops:
  1.7 7.6 %collective-permute-start = (bf16[272,256]{1,0:T(8,128)(2,1)S(1)}, bf16[272,256]{1,0:T(8,128)(2,1)S(1)}, u32[]{:S(2)}, u32[]{:S(2)}) collective-permute-start(bf16[272,256]{1,0:T(8,128)(2,1)S(1)} %get-tuple-element.12.own_ref), channel_id=1, source_target_pairs={{0,1},{1,0},{2,3},{3,2},{4,5},{5,4},{6,7},{7,6},{8,9},{9,8},{10,11... | collective-permute-start | bytes 417800 | tf_op jit(solution)/shard_map/ppermute | solution.py:272
  2.3 13.8 %all-to-all-start = ((bf16[16,8,128]{2,1,0:T(8,128)(2,1)}), bf16[16,8,128]{2,1,0:T(8,128)(2,1)}, u32[]{:S(2)}, u32[]{:S(2)}) async-start(bf16[16,8,128]{2,1,0:T(8,128)(2,1)} %bitcast.8), calls=%async_computation | async-start | bytes 65536 | tf_op jit(solution)/shard_map/all_to_all | solution.py:273
  9.4 0.6 %copy-start = (bf16[272,256]{1,0:T(8,128)(2,1)}, bf16[272,256]{1,0:T(8,128)(2,1)S(1)}, u32[]{:S(2)}) copy-start(bf16[272,256]{1,0:T(8,128)(2,1)S(1)} %collective-permute-done.other_ref) | copy-start | bytes 417796
  10.0 0.9 %copy-start.1 = (bf16[272,256]{1,0:T(8,128)(2,1)S(1)}, bf16[272,256]{1,0:T(8,128)(2,1)}, u32[]{:S(2)}) copy-start(bf16[272,256]{1,0:T(8,128)(2,1)} %copy-done) | copy-start | bytes 417796
  12.9 0.6 %copy-start.2 = (s32[8,512]{1,0:T(8,128)}, s32[8,512]{1,0:T(8,128)S(1)}, u32[]{:S(2)}) copy-start(s32[8,512]{1,0:T(8,128)S(1)} %get-tuple-element.14.refs_2_) | copy-start | bytes 49156
  16.1 0.7 %copy-start.3 = (s32[8,512]{1,0:T(8,128)S(1)}, s32[8,512]{1,0:T(8,128)}, u32[]{:S(2)}) copy-start(s32[8,512]{1,0:T(8,128)} %copy-done.2) | copy-start | bytes 49156

commit v13 on v12

--- a/solution.py
+++ b/solution.py
@@ -50,33 +50,29 @@
     return jnp.where(iota(values.shape, 1) < hours, 0.0, pltpu.roll(values, hours, 1))
 
 
-def load(sources, targets, arrived):
+def lane_rows(values):
+    return [values[:, first : first + LANES] for first in range(0, values.shape[1], LANES)]
+
+
+def parts_of(values):
+    high = values.astype(jnp.bfloat16).astype(jnp.float32)
+    middle = (values - high).astype(jnp.bfloat16).astype(jnp.float32)
+    return [high, middle, values - high - middle]
+
+
+def pack_kernel(*refs, basin_rows):
+    sources, (meta_hbm, block_ref, *scratch, meta_ref, arrived) = refs[:9], refs[9:]
+    tile_rows = block_ref.shape[0] - SIDE_ROWS
+    targets = (*scratch, block_ref.at[pl.ds(0, tile_rows)])
     copies = [
         pltpu.make_async_copy(source, target, arrived.at[j])
         for j, (source, target) in enumerate(zip(sources, targets))
     ]
     for copy in copies:
         copy.start()
-    for copy in copies:
+    for copy in copies[:4]:
         copy.wait()
-
-
-def lane_rows(values):
-    return [values[:, first : first + LANES] for first in range(0, values.shape[1], LANES)]
-
-
-def parts_of(values):
-    high = values.astype(jnp.bfloat16).astype(jnp.float32)
-    middle = (values - high).astype(jnp.bfloat16).astype(jnp.float32)
-    return [high, middle, values - high - middle]
-
-
-def pack_kernel(*refs, basin_rows):
-    sources, (meta_ref, block_ref, *scratch, arrived) = refs[:9], refs[9:]
-    hours = block_ref.shape[1]
-    tile_rows = block_ref.shape[0] - SIDE_ROWS
-    load(sources, (*scratch, block_ref.at[pl.ds(0, tile_rows)]), arrived)
-    basin, kind, lag, parent, soil, area, dest, reach = [ref[...] for ref in scratch]
+    basin, kind, lag, parent = [ref[...] for ref in scratch[:4]]
     shift = basin_rows.bit_length() - 1
     empty = jnp.zeros((1, LANES - basin_rows), jnp.int32)
     rows = lane_rows(basin) + lane_rows(kind) + lane_rows(lag)
@@ -84,25 +80,28 @@
     rows.append(jnp.concatenate([parent & (basin_rows - 1), empty], axis=1))
     numbers = jnp.concatenate(rows, axis=0).astype(jnp.float32)
     meta_ref[...] = jnp.concatenate([numbers] * (meta_ref.shape[0] // FIELDS), axis=0).astype(jnp.bfloat16)
+    leaving = pltpu.make_async_copy(meta_ref, meta_hbm, arrived.at[len(copies)])
+    leaving.start()
+    for copy in copies[4:8]:
+        copy.wait()
+    soil, area, dest, reach = [ref[...] for ref in scratch[4:]]
     sides = parts_of(soil) + parts_of(area) + [dest.astype(jnp.float32), reach.astype(jnp.float32)]
     sides = jnp.concatenate(sides + [jnp.zeros((SIDE_ROWS - len(sides), tile_rows), jnp.float32)], axis=0)
     block_ref[tile_rows:] = sides.astype(jnp.bfloat16)
-
-
-def response_matrix(reversed_taps):
-    hours = reversed_taps.shape[1]
-    causal = iota((hours, hours), 1) <= iota((hours, hours), 0)
-    row = jnp.broadcast_to(reversed_taps, (hours, hours))
-    matrix = jnp.where(causal, pltpu.roll(row, 0, 1, stride=1, stride_axis=0), 0.0)
-    return jnp.concatenate(split(matrix), axis=0)
-
-
-def prepare_kernel(irf_hbm, own_ref, other_ref, runoff_ref, ids_ref, taps_ref, responses_ref, irf_ref, arrived):
+    copies[8].wait()
+    leaving.wait()
+
+
+def prepare_kernel(
+    irf_hbm, own_ref, other_ref, runoff_ref, dest_ref, reach_marks_ref, late_ref, responses_ref, irf_ref, arrived
+):
     copy = pltpu.make_async_copy(irf_hbm, irf_ref, arrived.at[0])
     copy.start()
     hours = own_ref.shape[1]
+    half = hours // 2
     tile_rows = own_ref.shape[0] - SIDE_ROWS
     kinds, taps = irf_ref.shape
+    early = responses_ref.shape[0]
     sides = jnp.concatenate([own_ref[tile_rows:], other_ref[tile_rows:]], axis=1).astype(jnp.float32)
     rainfall = jnp.concatenate(
         [ref[:tile_rows].astype(jnp.float32).T for ref in (own_ref, other_ref)], axis=1
@@ -112,7 +111,8 @@
     excess = jnp.maximum(rainfall - 0.2 * storage, 0.0)
     runoff = (area * excess * excess / (rainfall + 0.8 * storage)).astype(jnp.bfloat16)
     runoff_ref[...] = runoff
-    ids_ref[...] = sides[:8].astype(jnp.int32)
+    dest_ref[...] = jnp.broadcast_to(sides[6:7], dest_ref.shape).astype(jnp.int32)
+    reach_marks_ref[...] = one_hot(sides[7:8].astype(jnp.int32), reach_marks_ref.shape[0])
     backward = (
         iota((taps, hours), 1) == lax.rem(hours - iota((taps, hours), 0), hours)
     ).astype(jnp.float32)
@@ -120,22 +120,45 @@
     reversed_taps = lax.dot_general(
         irf_ref[...], backward, NN, precision=lax.Precision.HIGHEST, preferred_element_type=jnp.float32
     )
-    taps_ref[...] = reversed_taps
-    for kind in range(responses_ref.shape[0]):
-        both = lax.dot_general(
-            response_matrix(reversed_taps[kind : kind + 1]), runoff, NN, preferred_element_type=jnp.float32
-        )
-        responses_ref[kind] = both[:hours] + both[hours:]
-
-
-def route_kernel(meta_ref, runoff_ref, ids_ref, taps_ref, responses_ref, flow_ref, stack_ref, *, basin_rows):
+    causal = iota((half, hours), 1) <= iota((half, hours), 0) + half
+    for kind in range(kinds):
+        row = jnp.broadcast_to(reversed_taps[kind : kind + 1], (half, hours))
+        matrix = jnp.where(causal, pltpu.roll(row, half, 1, stride=1, stride_axis=0), 0.0)
+        matrix = jnp.concatenate(split(matrix), axis=0)
+        if kind < early:
+            responses_ref[kind] = respond(matrix, runoff)
+        else:
+            late_ref[:, (kind - early) * hours : (kind - early + 1) * hours] = matrix
+
+
+def respond(matrices, runoffs):
+    hours = matrices.shape[0]
+    half = hours // 2
+    count = matrices.shape[1] // hours
+
+    def halves(values, axis, first):
+        pieces = [
+            lax.slice_in_dim(values, j * hours + first, j * hours + first + half, axis=axis)
+            for j in range(count)
+        ]
+        return jnp.concatenate(pieces, axis=axis)
+
+    earlier = lax.dot_general(
+        halves(matrices, 1, half), halves(runoffs, 0, 0), NN, preferred_element_type=jnp.float32
+    )
+    later = lax.dot_general(matrices, runoffs, NN, preferred_element_type=jnp.float32)
+    return jnp.concatenate([earlier[:half] + earlier[half:], later[:half] + later[half:]], axis=0)
+
+
+def route_kernel(
+    meta_ref, runoff_ref, dest_ref, reach_marks_ref, late_ref, responses_ref, flow_ref, stack_ref, *, basin_rows
+):
     early, hours, tiles = responses_ref.shape
-    kinds = taps_ref.shape[0]
+    late = late_ref.shape[1] // hours
     outlets = flow_ref.shape[0]
     owners = meta_ref.shape[0] // FIELDS
     core = lax.rem(lax.axis_index("tile"), CORES)
-    dest = ids_ref[6:7]
-    reach = ids_ref[7:8]
+    dest = dest_ref[0:1]
 
     stack_ref[...] = meta_ref[...].astype(jnp.float32)
 
@@ -155,7 +178,7 @@
         axis=0,
     )
     by_reach = lax.dot_general(
-        reach_table, one_hot(reach, spans * LANES), NN, preferred_element_type=jnp.float32
+        reach_table, reach_marks_ref[...], NN, preferred_element_type=jnp.float32
     )
     basin, kind, lag = [picked(by_reach[j * owners : (j + 1) * owners], dest) for j in range(3)]
     tree_table = jnp.concatenate([table(3 * spans), table(3 * spans + 1)], axis=0)
@@ -188,16 +211,12 @@
     runoff = runoff_ref[...]
     by_kind = jnp.concatenate(
         [
-            runoff * (kind == k).astype(jnp.float32).astype(jnp.bfloat16)
-            for k in range(early, kinds)
+            runoff * (kind == early + k).astype(jnp.float32).astype(jnp.bfloat16)
+            for k in range(late)
         ],
         axis=0,
     )
-    matrices = jnp.concatenate(
-        [response_matrix(taps_ref[k : k + 1]) for k in range(early, kinds)], axis=1
-    )
-    both = lax.dot_general(matrices, by_kind, NN, preferred_element_type=jnp.float32)
-    routed = both[:hours] + both[hours:]
+    routed = respond(late_ref[...], by_kind)
     for k in range(early):
         routed = jnp.where(kind == k, responses_ref[k], routed)
     step = 64
@@ -263,8 +282,12 @@
             jax.ShapeDtypeStruct(block, jnp.bfloat16),
         ),
         in_specs=[held] * (len(numbers) + 1),
+        out_specs=(held, whole),
         scratch_shapes=[pltpu.VMEM(values.shape, values.dtype) for values in numbers]
-        + [pltpu.SemaphoreType.DMA((len(numbers) + 1,))],
+        + [
+            pltpu.VMEM((owners * FIELDS, LANES), jnp.bfloat16),
+            pltpu.SemaphoreType.DMA((len(numbers) + 2,)),
+        ],
         compiler_params=params,
         cost_estimate=SMALL,
         name="pack",
@@ -275,13 +298,14 @@
     ).reshape(-1, LANES)
 
     chip_tiles = CORES * tile_rows
-    early = kinds * 3 // 4
-    runoff, ids, taps, responses = pl.pallas_call(
+    early = kinds // 2
+    prepared = pl.pallas_call(
         prepare_kernel,
         out_shape=(
             jax.ShapeDtypeStruct((hours, chip_tiles), jnp.bfloat16),
             jax.ShapeDtypeStruct((8, chip_tiles), jnp.int32),
-            jax.ShapeDtypeStruct((kinds, hours), jnp.float32),
+            jax.ShapeDtypeStruct((reach_basin.size, chip_tiles), jnp.bfloat16),
+            jax.ShapeDtypeStruct((hours, (kinds - early) * hours), jnp.bfloat16),
             jax.ShapeDtypeStruct((early, hours, chip_tiles), jnp.float32),
         ),
         in_specs=[held, whole, whole],
@@ -297,7 +321,7 @@
         scratch_shapes=[pltpu.VMEM(meta.shape, jnp.float32)],
         compiler_params=params,
         name="route",
-    )(meta, runoff, ids, taps, responses)
+    )(meta, *prepared)
 
     parts = lax.all_to_all(
         flow.reshape(owners // CORES, basin_rows, hours),

time: 31 us -> 28.3 us (0.913)
  local copies, waits for them, and re-layouts: 2.86 us -> 0 us
  waiting for transfers between devices: 2.59 us -> 4.97 us
  Pallas kernels: 7.07 us -> 5.72 us
  blocking collectives: 10.4 us -> 9.74 us
    unnamed x8 -> x0, local copies, waits for them, and re-layouts: 2.86 us -> none
    all_to_all x1, waiting for transfers between devices: 2.59 us -> 4.96 us  [per_device(): lax.all_to_all(meta.reshape(owners, FIELDS, LANES), 'tile', split_axis=0,...]
    pallas_call x1, Pallas kernels: 2.7 us -> 1.94 us  [per_device(): pl.pallas_call(lambda *refs: route_kernel(*refs, basin_rows=basin_rows),...]
    all_to_all x1, blocking collectives: 10.4 us -> 9.74 us  [per_device(): lax.all_to_all(flow.reshape(owners // CORES, basin_rows, hours), 'tile',...]
    pallas_call x1, Pallas kernels: 1.73 us -> 1.42 us  [per_device(): pl.pallas_call(lambda *refs: pack_kernel(*refs, basin_rows=basin_rows), o...]
where the time goes in v13:
time: 28.3 us; the launch traced here: 28 us
  blocking collectives  9.74 us (34%)
  starting transfers between devices  7.57 us (27%)
  Pallas kernels  5.72 us (20%)
  waiting for transfers between devices  4.97 us (18%)
    all_to_all x1, blocking collectives, per_device(): lax.all_to_all(flow.reshape(owners // CORES, basin_rows, hours), 'tile',...  9.74 us
    all_to_all x1, starting transfers between devices, per_device(): lax.all_to_all(meta.reshape(owners, FIELDS, LANES), 'tile', split_axis=0,...  7.05 us
    all_to_all x1, waiting for transfers between devices, per_device(): lax.all_to_all(meta.reshape(owners, FIELDS, LANES), 'tile', split_axis=0,...  4.96 us
    pallas_call x1, Pallas kernels, per_device(): pl.pallas_call(lambda *refs: route_kernel(*refs, basin_rows=basin_rows),...  1.94 us
    pallas_call x1, Pallas kernels, per_device(): pl.pallas_call(prepare_kernel, out_shape=(jax.ShapeDtypeStruct((hours, ch...  1.65 us
    pallas_call x1, Pallas kernels, per_device(): pl.pallas_call(lambda *refs: pack_kernel(*refs, basin_rows=basin_rows), o...  1.42 us
    pallas_call x1, Pallas kernels, per_device(): pl.pallas_call(finish_kernel, out_shape=jax.ShapeDtypeStruct((basin_rows,...  0.71 us
  transfers between devices with their start and end apart: 2, of which 1 were waited for; matrix products, arithmetic and copies ran while one was open for 0% of the time, Pallas kernels for 6%

profile of v13, /device:TPU:0, one launch (start us, length us, event | category | flops | bytes accessed | tf_op | source)
XLA Modules:
  0.0 28.0 jit_solution(13318794930876824021)
XLA Ops:
  0.0 1.4 %pack.1 = (bf16[128,128]{1,0:T(8,128)(2,1)}, bf16[272,256]{1,0:T(8,128)(2,1)S(1)}) custom-call(s32[1,256]{1,0:T(1,128)} %bitcast.13, s32[1,256]{1,0:T(1,128)} %bitcast.14, s32[1,256]{1,0:T(1,128)} %bitcast.15, s32[1,32]{1,0:T(1,128)} %bitcast.20, f32[1,256]{1,0:T(1,128)} %bitcast.16, f32[1,256]{1,0:T(1,128)} %bitcast.17, s32[1,256]{1,0:T(1,128)} %bitcast.18, ...), custom_call_target="tpu_custom_call" | custom-call | flops 1 | bytes 1 | tf_op jit(solution)/shard_map/pack/pallas_call | solution.py:278
  1.4 0.5 %collective-permute-start = (bf16[272,256]{1,0:T(8,128)(2,1)S(1)}, bf16[272,256]{1,0:T(8,128)(2,1)S(1)}, u32[]{:S(2)}, u32[]{:S(2)}) collective-permute-start(bf16[272,256]{1,0:T(8,128)(2,1)S(1)} %get-tuple-element.13.own_ref), channel_id=1, source_target_pairs={{0,1},{1,0},{2,3},{3,2},{4,5},{5,4},{6,7},{7,6},{8,9},{9,8},{10,11... | collective-permute-start | bytes 417800 | tf_op jit(solution)/shard_map/ppermute | solution.py:295
  1.9 7.0 %all-to-all-start = ((bf16[16,8,128]{2,1,0:T(8,128)(2,1)}), bf16[16,8,128]{2,1,0:T(8,128)(2,1)S(1)}, u32[]{:S(2)}, u32[]{:S(2)}) async-start(bf16[16,8,128]{2,1,0:T(8,128)(2,1)} %bitcast.8), calls=%async_computation | async-start | bytes 65536 | tf_op jit(solution)/shard_map/all_to_all | solution.py:296
  9.0 0.0 collective-permute-done.other_ref
  9.0 1.6 %prepare.1 = (bf16[256,512]{1,0:T(8,128)(2,1)S(1)}, s32[8,512]{1,0:T(8,128)S(1)}, bf16[256,512]{1,0:T(8,128)(2,1)S(1)}, bf16[256,1024]{1,0:T(8,128)(2,1)S(1)}, f32[4,256,512]{2,1,0:T(8,128)S(1)}) custom-call(f32[8,48]{1,0:T(8,128)} %irf_hbm.1, bf16[272,256]{1,0:T(8,128)(2,1)S(1)} %get-tuple-element.13.own_ref, ...), custom_call_target="tpu_custom_call" | custom-call | flops 1 | bytes 1 | tf_op jit(solution)/shard_map/prepare/pallas_call | solution.py:302
  10.7 5.0 %all-to-all-done = bf16[16,8,128]{2,1,0:T(8,128)(2,1)S(1)} async-done(((bf16[16,8,128]{2,1,0:T(8,128)(2,1)}), bf16[16,8,128]{2,1,0:T(8,128)(2,1)S(1)}, u32[]{:S(2)}, u32[]{:S(2)}) %all-to-all-start) | async-done | bytes 32800 | tf_op jit(solution)/shard_map/all_to_all | solution.py:296
  15.6 1.9 %route.1 = s16[256,256]{1,0:T(8,128)(2,1)S(1)} custom-call(bf16[128,128]{1,0:T(8,128)(2,1)S(1)} %bitcast.12, bf16[256,512]{1,0:T(8,128)(2,1)S(1)} %get-tuple-element.14.refs_1_, s32[8,512]{1,0:T(8,128)S(1)} %get-tuple-element.15.refs_2_, bf16[256,512]{1,0:T(8,128)(2,1)S(1)} %get-tuple-element.16.refs_3_, bf16[256,1024]{1,0:T(8,128)(2,1)S(1)} %get-tuple-element.17.refs_4_, ...), custom_call_target="tpu_custom_call" | custom-call | tf_op jit(solution)/shard_map/route/pallas_call | solution.py:318
  17.6 9.7 %all_to_all.10.parts_ref = s16[8,32,256]{2,1,0:T(8,128)(2,1)S(1)} all-to-all(s16[8,32,256]{2,1,0:T(8,128)(2,1)S(1)} %bitcast.11), channel_id=1, replica_groups={{0,2,4,6,8,10,12,14},{1,3,5,7,9,11,13,15},{16,18,20,22,24,26,28,30},{17..., dimensions={0} | all-to-all | bytes 262144 | tf_op jit(solution)/shard_map/all_to_all | solution.py:326
  27.3 0.7 %finish.1 = f32[32,256]{1,0:T(8,128)} custom-call(s16[8,32,256]{2,1,0:T(8,128)(2,1)S(1)} %all_to_all.10.parts_ref), custom_call_target="tpu_custom_call" | custom-call | tf_op jit(solution)/shard_map/finish/pallas_call | solution.py:334
Async XLA Ops:
  1.4 7.6 %collective-permute-start = (bf16[272,256]{1,0:T(8,128)(2,1)S(1)}, bf16[272,256]{1,0:T(8,128)(2,1)S(1)}, u32[]{:S(2)}, u32[]{:S(2)}) collective-permute-start(bf16[272,256]{1,0:T(8,128)(2,1)S(1)} %get-tuple-element.13.own_ref), channel_id=1, source_target_pairs={{0,1},{1,0},{2,3},{3,2},{4,5},{5,4},{6,7},{7,6},{8,9},{9,8},{10,11... | collective-permute-start | bytes 417800 | tf_op jit(solution)/shard_map/ppermute | solution.py:295
  1.9 13.7 %all-to-all-start = ((bf16[16,8,128]{2,1,0:T(8,128)(2,1)}), bf16[16,8,128]{2,1,0:T(8,128)(2,1)S(1)}, u32[]{:S(2)}, u32[]{:S(2)}) async-start(bf16[16,8,128]{2,1,0:T(8,128)(2,1)} %bitcast.8), calls=%async_computation | async-start | bytes 65536 | tf_op jit(solution)/shard_map/all_to_all | solution.py:296

commit v14 on v13

--- a/solution.py
+++ b/solution.py
@@ -43,11 +43,15 @@
     if hours % 8 == 0:
         padding = jnp.zeros((hours, values.shape[1]), values.dtype)
         return jnp.concatenate([padding, values[: rows - hours]], axis=0)
-    return jnp.where(iota(values.shape, 0) < hours, 0.0, pltpu.roll(values, hours, 0))
+    rolled = pltpu.roll(values, hours, 0)
+    first = jnp.where(iota((8, values.shape[1]), 0) < hours, 0.0, rolled[:8])
+    return jnp.concatenate([first, rolled[8:]], axis=0)
 
 
 def later_lanes(values, hours):
-    return jnp.where(iota(values.shape, 1) < hours, 0.0, pltpu.roll(values, hours, 1))
+    rolled = pltpu.roll(values, hours, 1)
+    first = jnp.where(iota((values.shape[0], LANES), 1) < hours, 0.0, rolled[:, :LANES])
+    return jnp.concatenate([first, rolled[:, LANES:]], axis=1)
 
 
 def lane_rows(values):
@@ -61,7 +65,7 @@
 
 
 def pack_kernel(*refs, basin_rows):
-    sources, (meta_hbm, block_ref, *scratch, meta_ref, arrived) = refs[:9], refs[9:]
+    sources, (meta_ref, block_ref, *scratch, arrived) = refs[:9], refs[9:]
     tile_rows = block_ref.shape[0] - SIDE_ROWS
     targets = (*scratch, block_ref.at[pl.ds(0, tile_rows)])
     copies = [
@@ -80,8 +84,6 @@
     rows.append(jnp.concatenate([parent & (basin_rows - 1), empty], axis=1))
     numbers = jnp.concatenate(rows, axis=0).astype(jnp.float32)
     meta_ref[...] = jnp.concatenate([numbers] * (meta_ref.shape[0] // FIELDS), axis=0).astype(jnp.bfloat16)
-    leaving = pltpu.make_async_copy(meta_ref, meta_hbm, arrived.at[len(copies)])
-    leaving.start()
     for copy in copies[4:8]:
         copy.wait()
     soil, area, dest, reach = [ref[...] for ref in scratch[4:]]
@@ -89,7 +91,6 @@
     sides = jnp.concatenate(sides + [jnp.zeros((SIDE_ROWS - len(sides), tile_rows), jnp.float32)], axis=0)
     block_ref[tile_rows:] = sides.astype(jnp.bfloat16)
     copies[8].wait()
-    leaving.wait()
 
 
 def prepare_kernel(
@@ -278,16 +279,13 @@
     meta, own = pl.pallas_call(
         lambda *refs: pack_kernel(*refs, basin_rows=basin_rows),
         out_shape=(
-            jax.ShapeDtypeStruct((owners * FIELDS, LANES), jnp.bfloat16),
+            pltpu.VMEM((owners * FIELDS, LANES), jnp.bfloat16),
             jax.ShapeDtypeStruct(block, jnp.bfloat16),
         ),
         in_specs=[held] * (len(numbers) + 1),
-        out_specs=(held, whole),
+        out_specs=(whole, whole),
         scratch_shapes=[pltpu.VMEM(values.shape, values.dtype) for values in numbers]
-        + [
-            pltpu.VMEM((owners * FIELDS, LANES), jnp.bfloat16),
-            pltpu.SemaphoreType.DMA((len(numbers) + 2,)),
-        ],
+        + [pltpu.SemaphoreType.DMA((len(numbers) + 1,))],
         compiler_params=params,
         cost_estimate=SMALL,
         name="pack",

time: 28.3 us -> 28.6 us (1.011)
    pallas_call x1, Pallas kernels: 1.42 us -> 1.72 us  [per_device(): pl.pallas_call(lambda *refs: pack_kernel(*refs, basin_rows=basin_rows), o...]
where the time goes in v14:
time: 28.6 us; the launch traced here: 28.3 us
  blocking collectives  9.74 us (34%)
  starting transfers between devices  7.57 us (26%)
  Pallas kernels  6 us (21%)
  waiting for transfers between devices  4.98 us (17%)
    all_to_all x1, blocking collectives, per_device(): lax.all_to_all(flow.reshape(owners // CORES, basin_rows, hours), 'tile',...  9.74 us
    all_to_all x1, starting transfers between devices, per_device(): lax.all_to_all(meta.reshape(owners, FIELDS, LANES), 'tile', split_axis=0,...  7.05 us
    all_to_all x1, waiting for transfers between devices, per_device(): lax.all_to_all(meta.reshape(owners, FIELDS, LANES), 'tile', split_axis=0,...  4.98 us
    pallas_call x1, Pallas kernels, per_device(): pl.pallas_call(lambda *refs: route_kernel(*refs, basin_rows=basin_rows),...  1.93 us
    pallas_call x1, Pallas kernels, per_device(): pl.pallas_call(lambda *refs: pack_kernel(*refs, basin_rows=basin_rows), o...  1.72 us
    pallas_call x1, Pallas kernels, per_device(): pl.pallas_call(prepare_kernel, out_shape=(jax.ShapeDtypeStruct((hours, ch...  1.64 us
    pallas_call x1, Pallas kernels, per_device(): pl.pallas_call(finish_kernel, out_shape=jax.ShapeDtypeStruct((basin_rows,...  0.71 us
  transfers between devices with their start and end apart: 2, of which 1 were waited for; matrix products, arithmetic and copies ran while one was open for 0% of the time, Pallas kernels for 6%

profile of v14, /device:TPU:0, one launch (start us, length us, event | category | flops | bytes accessed | tf_op | source)
XLA Modules:
  0.0 28.3 jit_solution(12868250554146712982)
XLA Ops:
  0.0 1.7 %pack.1 = (bf16[128,128]{1,0:T(8,128)(2,1)}, bf16[272,256]{1,0:T(8,128)(2,1)S(1)}) custom-call(s32[1,256]{1,0:T(1,128)} %bitcast.13, s32[1,256]{1,0:T(1,128)} %bitcast.14, s32[1,256]{1,0:T(1,128)} %bitcast.15, s32[1,32]{1,0:T(1,128)} %bitcast.20, f32[1,256]{1,0:T(1,128)} %bitcast.16, f32[1,256]{1,0:T(1,128)} %bitcast.17, s32[1,256]{1,0:T(1,128)} %bitcast.18, ...), custom_call_target="tpu_custom_call" | custom-call | flops 1 | bytes 1 | tf_op jit(solution)/shard_map/pack/pallas_call | solution.py:279
  1.7 0.5 %collective-permute-start = (bf16[272,256]{1,0:T(8,128)(2,1)S(1)}, bf16[272,256]{1,0:T(8,128)(2,1)S(1)}, u32[]{:S(2)}, u32[]{:S(2)}) collective-permute-start(bf16[272,256]{1,0:T(8,128)(2,1)S(1)} %get-tuple-element.13.own_ref), channel_id=1, source_target_pairs={{0,1},{1,0},{2,3},{3,2},{4,5},{5,4},{6,7},{7,6},{8,9},{9,8},{10,11... | collective-permute-start | bytes 417800 | tf_op jit(solution)/shard_map/ppermute | solution.py:293
  2.2 7.0 %all-to-all-start = ((bf16[16,8,128]{2,1,0:T(8,128)(2,1)}), bf16[16,8,128]{2,1,0:T(8,128)(2,1)S(1)}, u32[]{:S(2)}, u32[]{:S(2)}) async-start(bf16[16,8,128]{2,1,0:T(8,128)(2,1)} %bitcast.8), calls=%async_computation | async-start | bytes 65536 | tf_op jit(solution)/shard_map/all_to_all | solution.py:294
  9.3 0.0 collective-permute-done.other_ref
  9.3 1.6 %prepare.1 = (bf16[256,512]{1,0:T(8,128)(2,1)S(1)}, s32[8,512]{1,0:T(8,128)S(1)}, bf16[256,512]{1,0:T(8,128)(2,1)S(1)}, bf16[256,1024]{1,0:T(8,128)(2,1)S(1)}, f32[4,256,512]{2,1,0:T(8,128)S(1)}) custom-call(f32[8,48]{1,0:T(8,128)} %irf_hbm.1, bf16[272,256]{1,0:T(8,128)(2,1)S(1)} %get-tuple-element.13.own_ref, ...), custom_call_target="tpu_custom_call" | custom-call | flops 1 | bytes 1 | tf_op jit(solution)/shard_map/prepare/pallas_call | solution.py:300
  11.0 5.0 %all-to-all-done = bf16[16,8,128]{2,1,0:T(8,128)(2,1)S(1)} async-done(((bf16[16,8,128]{2,1,0:T(8,128)(2,1)}), bf16[16,8,128]{2,1,0:T(8,128)(2,1)S(1)}, u32[]{:S(2)}, u32[]{:S(2)}) %all-to-all-start) | async-done | bytes 32800 | tf_op jit(solution)/shard_map/all_to_all | solution.py:294
  15.9 1.9 %route.1 = s16[256,256]{1,0:T(8,128)(2,1)S(1)} custom-call(bf16[128,128]{1,0:T(8,128)(2,1)S(1)} %bitcast.12, bf16[256,512]{1,0:T(8,128)(2,1)S(1)} %get-tuple-element.14.refs_1_, s32[8,512]{1,0:T(8,128)S(1)} %get-tuple-element.15.refs_2_, bf16[256,512]{1,0:T(8,128)(2,1)S(1)} %get-tuple-element.16.refs_3_, bf16[256,1024]{1,0:T(8,128)(2,1)S(1)} %get-tuple-element.17.refs_4_, ...), custom_call_target="tpu_custom_call" | custom-call | tf_op jit(solution)/shard_map/route/pallas_call | solution.py:316
  17.9 9.7 %all_to_all.10.parts_ref = s16[8,32,256]{2,1,0:T(8,128)(2,1)S(1)} all-to-all(s16[8,32,256]{2,1,0:T(8,128)(2,1)S(1)} %bitcast.11), channel_id=1, replica_groups={{0,2,4,6,8,10,12,14},{1,3,5,7,9,11,13,15},{16,18,20,22,24,26,28,30},{17..., dimensions={0} | all-to-all | bytes 262144 | tf_op jit(solution)/shard_map/all_to_all | solution.py:324
  27.6 0.7 %finish.1 = f32[32,256]{1,0:T(8,128)} custom-call(s16[8,32,256]{2,1,0:T(8,128)(2,1)S(1)} %all_to_all.10.parts_ref), custom_call_target="tpu_custom_call" | custom-call | tf_op jit(solution)/shard_map/finish/pallas_call | solution.py:332
Async XLA Ops:
  1.7 7.6 %collective-permute-start = (bf16[272,256]{1,0:T(8,128)(2,1)S(1)}, bf16[272,256]{1,0:T(8,128)(2,1)S(1)}, u32[]{:S(2)}, u32[]{:S(2)}) collective-permute-start(bf16[272,256]{1,0:T(8,128)(2,1)S(1)} %get-tuple-element.13.own_ref), channel_id=1, source_target_pairs={{0,1},{1,0},{2,3},{3,2},{4,5},{5,4},{6,7},{7,6},{8,9},{9,8},{10,11... | collective-permute-start | bytes 417800 | tf_op jit(solution)/shard_map/ppermute | solution.py:293
  2.2 13.7 %all-to-all-start = ((bf16[16,8,128]{2,1,0:T(8,128)(2,1)}), bf16[16,8,128]{2,1,0:T(8,128)(2,1)S(1)}, u32[]{:S(2)}, u32[]{:S(2)}) async-start(bf16[16,8,128]{2,1,0:T(8,128)(2,1)} %bitcast.8), calls=%async_computation | async-start | bytes 65536 | tf_op jit(solution)/shard_map/all_to_all | solution.py:294

commit v15 on v13

--- a/solution.py
+++ b/solution.py
@@ -13,6 +13,7 @@
 FIELDS = 8
 SIDE_ROWS = 16
 VMEM_BYTES = 40 * 1024 * 1024
+CHUNK = 64
 CODE_TOP = 32767
 CODE_OCTAVES = 44
 CODE_LOWEST = -26
@@ -43,11 +44,15 @@
     if hours % 8 == 0:
         padding = jnp.zeros((hours, values.shape[1]), values.dtype)
         return jnp.concatenate([padding, values[: rows - hours]], axis=0)
-    return jnp.where(iota(values.shape, 0) < hours, 0.0, pltpu.roll(values, hours, 0))
+    rolled = pltpu.roll(values, hours, 0)
+    first = jnp.where(iota((8, values.shape[1]), 0) < hours, 0.0, rolled[:8])
+    return jnp.concatenate([first, rolled[8:]], axis=0)
 
 
 def later_lanes(values, hours):
-    return jnp.where(iota(values.shape, 1) < hours, 0.0, pltpu.roll(values, hours, 1))
+    rolled = pltpu.roll(values, hours, 1)
+    first = jnp.where(iota((values.shape[0], LANES), 1) < hours, 0.0, rolled[:, :LANES])
+    return jnp.concatenate([first, rolled[:, LANES:]], axis=1)
 
 
 def lane_rows(values):
@@ -208,40 +213,56 @@
         axis=0,
     )
 
-    runoff = runoff_ref[...]
-    by_kind = jnp.concatenate(
-        [
-            runoff * (kind == early + k).astype(jnp.float32).astype(jnp.bfloat16)
-            for k in range(late)
-        ],
-        axis=0,
-    )
-    routed = respond(late_ref[...], by_kind)
-    for k in range(early):
-        routed = jnp.where(kind == k, responses_ref[k], routed)
-    step = 64
-    while step:
-        routed = jnp.where((lag & step) != 0, later_rows(routed, step), routed)
-        step //= 2
+    highs, lows = [], []
+    for first in range(0, tiles, 2 * LANES):
+        wide = slice(first, first + 2 * LANES)
+        runoff = runoff_ref[:, wide]
+        by_kind = jnp.concatenate(
+            [
+                runoff * (kind[:, wide] == early + k).astype(jnp.float32).astype(jnp.bfloat16)
+                for k in range(late)
+            ],
+            axis=0,
+        )
+        both = respond(late_ref[...], by_kind)
+        for start in (0, LANES):
+            lanes = slice(first + start, first + start + LANES)
+            routed = both[:, start : start + LANES]
+            for k in range(early):
+                routed = jnp.where(kind[:, lanes] == k, responses_ref[k, :, lanes], routed)
+            step = 64
+            while step:
+                routed = jnp.where((lag[:, lanes] & step) != 0, later_rows(routed, step), routed)
+                step //= 2
+            high, low = split(routed)
+            highs.append(high)
+            lows.append(low)
     flows = lax.dot_general(
         jnp.concatenate([placements, placements], axis=1),
-        jnp.concatenate(split(routed), axis=1),
+        jnp.concatenate(highs + lows, axis=1),
         NT,
         preferred_element_type=jnp.float32,
     )
-    flow = later_lanes(flows[2 * outlets :], LINK)
-    flow = later_lanes(flows[outlets : 2 * outlets] + flow, LINK)
-    flow = flows[:outlets] + flow
-    level = jnp.log(jnp.maximum(flow, CODE_FLOOR)) * CODE_SCALE + (CODE_ZERO + CODE_TOP + 0.5)
-    level = jnp.clip(level, 0.0, 2.0 * CODE_TOP).astype(jnp.int32) - CODE_TOP
-    flow_ref[...] = level.astype(jnp.int16)
+    for first in range(0, outlets, CHUNK):
+        direct, second, third = [
+            flows[j * outlets + first : j * outlets + first + CHUNK] for j in range(3)
+        ]
+        flow = direct + later_lanes(second + later_lanes(third, LINK), LINK)
+        level = jnp.log(jnp.maximum(flow, CODE_FLOOR)) * CODE_SCALE + (CODE_ZERO + CODE_TOP + 0.5)
+        level = jnp.clip(level, 0.0, 2.0 * CODE_TOP).astype(jnp.int32) - CODE_TOP
+        flow_ref[first : first + CHUNK] = level.astype(jnp.int16)
 
 
 def finish_kernel(parts_ref, section_ref):
-    level = parts_ref[...].astype(jnp.int32)
-    flow = jnp.exp((level.astype(jnp.float32) - CODE_ZERO) * (1.0 / CODE_SCALE))
-    flow = jnp.sum(jnp.where(level == -CODE_TOP, 0.0, flow), axis=0)
-    section_ref[...] = jnp.log(1.0 + flow)
+    count, rows, _ = parts_ref.shape
+    for first in range(0, rows, 16):
+        chunk = slice(first, first + 16)
+        total = 0.0
+        for part in range(count):
+            level = parts_ref[part, chunk].astype(jnp.int32).astype(jnp.float32)
+            flow = jnp.exp((level - CODE_ZERO) * (1.0 / CODE_SCALE))
+            total += jnp.where(level == -CODE_TOP, 0.0, flow)
+        section_ref[chunk] = jnp.log(1.0 + total)
 
 
 def per_device(

time: 28.3 us -> 28.6 us (1.011)
  Pallas kernels: 5.72 us -> 6.02 us
    pallas_call x1, Pallas kernels: 1.94 us -> 2.24 us  [per_device(): pl.pallas_call(lambda *refs: route_kernel(*refs, basin_rows=basin_rows),...]
where the time goes in v15:
time: 28.6 us; the launch traced here: 28.3 us
  blocking collectives  9.74 us (34%)
  starting transfers between devices  7.57 us (26%)
  Pallas kernels  6.02 us (21%)
  waiting for transfers between devices  4.97 us (17%)
    all_to_all x1, blocking collectives, per_device(): lax.all_to_all(flow.reshape(owners // CORES, basin_rows, hours), 'tile',...  9.74 us
    all_to_all x1, starting transfers between devices, per_device(): lax.all_to_all(meta.reshape(owners, FIELDS, LANES), 'tile', split_axis=0,...  7.05 us
    all_to_all x1, waiting for transfers between devices, per_device(): lax.all_to_all(meta.reshape(owners, FIELDS, LANES), 'tile', split_axis=0,...  4.96 us
    pallas_call x1, Pallas kernels, per_device(): pl.pallas_call(lambda *refs: route_kernel(*refs, basin_rows=basin_rows),...  2.24 us
    pallas_call x1, Pallas kernels, per_device(): pl.pallas_call(prepare_kernel, out_shape=(jax.ShapeDtypeStruct((hours, ch...  1.65 us
    pallas_call x1, Pallas kernels, per_device(): pl.pallas_call(lambda *refs: pack_kernel(*refs, basin_rows=basin_rows), o...  1.42 us
    pallas_call x1, Pallas kernels, per_device(): pl.pallas_call(finish_kernel, out_shape=jax.ShapeDtypeStruct((basin_rows,...  0.71 us
  transfers between devices with their start and end apart: 2, of which 1 were waited for; matrix products, arithmetic and copies ran while one was open for 0% of the time, Pallas kernels for 6%

profile of v15, /device:TPU:0, one launch (start us, length us, event | category | flops | bytes accessed | tf_op | source)
XLA Modules:
  0.0 28.3 jit_solution(482032621680472726)
XLA Ops:
  0.0 1.4 %pack.1 = (bf16[128,128]{1,0:T(8,128)(2,1)}, bf16[272,256]{1,0:T(8,128)(2,1)S(1)}) custom-call(s32[1,256]{1,0:T(1,128)} %bitcast.13, s32[1,256]{1,0:T(1,128)} %bitcast.14, s32[1,256]{1,0:T(1,128)} %bitcast.15, s32[1,32]{1,0:T(1,128)} %bitcast.20, f32[1,256]{1,0:T(1,128)} %bitcast.16, f32[1,256]{1,0:T(1,128)} %bitcast.17, s32[1,256]{1,0:T(1,128)} %bitcast.18, ...), custom_call_target="tpu_custom_call" | custom-call | flops 1 | bytes 1 | tf_op jit(solution)/shard_map/pack/pallas_call | solution.py:299
  1.4 0.5 %collective-permute-start = (bf16[272,256]{1,0:T(8,128)(2,1)S(1)}, bf16[272,256]{1,0:T(8,128)(2,1)S(1)}, u32[]{:S(2)}, u32[]{:S(2)}) collective-permute-start(bf16[272,256]{1,0:T(8,128)(2,1)S(1)} %get-tuple-element.13.own_ref), channel_id=1, source_target_pairs={{0,1},{1,0},{2,3},{3,2},{4,5},{5,4},{6,7},{7,6},{8,9},{9,8},{10,11... | collective-permute-start | bytes 417800 | tf_op jit(solution)/shard_map/ppermute | solution.py:316
  1.9 7.0 %all-to-all-start = ((bf16[16,8,128]{2,1,0:T(8,128)(2,1)}), bf16[16,8,128]{2,1,0:T(8,128)(2,1)S(1)}, u32[]{:S(2)}, u32[]{:S(2)}) async-start(bf16[16,8,128]{2,1,0:T(8,128)(2,1)} %bitcast.8), calls=%async_computation | async-start | bytes 65536 | tf_op jit(solution)/shard_map/all_to_all | solution.py:317
  9.0 0.0 collective-permute-done.other_ref
  9.0 1.6 %prepare.1 = (bf16[256,512]{1,0:T(8,128)(2,1)S(1)}, s32[8,512]{1,0:T(8,128)S(1)}, bf16[256,512]{1,0:T(8,128)(2,1)S(1)}, bf16[256,1024]{1,0:T(8,128)(2,1)S(1)}, f32[4,256,512]{2,1,0:T(8,128)S(1)}) custom-call(f32[8,48]{1,0:T(8,128)} %irf_hbm.1, bf16[272,256]{1,0:T(8,128)(2,1)S(1)} %get-tuple-element.13.own_ref, ...), custom_call_target="tpu_custom_call" | custom-call | flops 1 | bytes 1 | tf_op jit(solution)/shard_map/prepare/pallas_call | solution.py:323
  10.7 5.0 %all-to-all-done = bf16[16,8,128]{2,1,0:T(8,128)(2,1)S(1)} async-done(((bf16[16,8,128]{2,1,0:T(8,128)(2,1)}), bf16[16,8,128]{2,1,0:T(8,128)(2,1)S(1)}, u32[]{:S(2)}, u32[]{:S(2)}) %all-to-all-start) | async-done | bytes 32800 | tf_op jit(solution)/shard_map/all_to_all | solution.py:317
  15.6 2.2 %route.1 = s16[256,256]{1,0:T(8,128)(2,1)S(1)} custom-call(bf16[128,128]{1,0:T(8,128)(2,1)S(1)} %bitcast.12, bf16[256,512]{1,0:T(8,128)(2,1)S(1)} %get-tuple-element.14.refs_1_, s32[8,512]{1,0:T(8,128)S(1)} %get-tuple-element.15.refs_2_, bf16[256,512]{1,0:T(8,128)(2,1)S(1)} %get-tuple-element.16.refs_3_, bf16[256,1024]{1,0:T(8,128)(2,1)S(1)} %get-tuple-element.17.refs_4_, ...), custom_call_target="tpu_custom_call" | custom-call | tf_op jit(solution)/shard_map/route/pallas_call | solution.py:339
  17.9 9.7 %all_to_all.10.parts_ref = s16[8,32,256]{2,1,0:T(8,128)(2,1)S(1)} all-to-all(s16[8,32,256]{2,1,0:T(8,128)(2,1)S(1)} %bitcast.11), channel_id=1, replica_groups={{0,2,4,6,8,10,12,14},{1,3,5,7,9,11,13,15},{16,18,20,22,24,26,28,30},{17..., dimensions={0} | all-to-all | bytes 262144 | tf_op jit(solution)/shard_map/all_to_all | solution.py:347
  27.6 0.7 %finish.1 = f32[32,256]{1,0:T(8,128)} custom-call(s16[8,32,256]{2,1,0:T(8,128)(2,1)S(1)} %all_to_all.10.parts_ref), custom_call_target="tpu_custom_call" | custom-call | tf_op jit(solution)/shard_map/finish/pallas_call | solution.py:355
Async XLA Ops:
  1.4 7.6 %collective-permute-start = (bf16[272,256]{1,0:T(8,128)(2,1)S(1)}, bf16[272,256]{1,0:T(8,128)(2,1)S(1)}, u32[]{:S(2)}, u32[]{:S(2)}) collective-permute-start(bf16[272,256]{1,0:T(8,128)(2,1)S(1)} %get-tuple-element.13.own_ref), channel_id=1, source_target_pairs={{0,1},{1,0},{2,3},{3,2},{4,5},{5,4},{6,7},{7,6},{8,9},{9,8},{10,11... | collective-permute-start | bytes 417800 | tf_op jit(solution)/shard_map/ppermute | solution.py:316
  1.9 13.7 %all-to-all-start = ((bf16[16,8,128]{2,1,0:T(8,128)(2,1)}), bf16[16,8,128]{2,1,0:T(8,128)(2,1)S(1)}, u32[]{:S(2)}, u32[]{:S(2)}) async-start(bf16[16,8,128]{2,1,0:T(8,128)(2,1)} %bitcast.8), calls=%async_computation | async-start | bytes 65536 | tf_op jit(solution)/shard_map/all_to_all | solution.py:317

commit v16 on v14

--- a/solution.py
+++ b/solution.py
@@ -43,15 +43,11 @@
     if hours % 8 == 0:
         padding = jnp.zeros((hours, values.shape[1]), values.dtype)
         return jnp.concatenate([padding, values[: rows - hours]], axis=0)
-    rolled = pltpu.roll(values, hours, 0)
-    first = jnp.where(iota((8, values.shape[1]), 0) < hours, 0.0, rolled[:8])
-    return jnp.concatenate([first, rolled[8:]], axis=0)
+    return jnp.where(iota(values.shape, 0) < hours, 0.0, pltpu.roll(values, hours, 0))
 
 
 def later_lanes(values, hours):
-    rolled = pltpu.roll(values, hours, 1)
-    first = jnp.where(iota((values.shape[0], LANES), 1) < hours, 0.0, rolled[:, :LANES])
-    return jnp.concatenate([first, rolled[:, LANES:]], axis=1)
+    return jnp.where(iota(values.shape, 1) < hours, 0.0, pltpu.roll(values, hours, 1))
 
 
 def lane_rows(values):
@@ -83,7 +79,9 @@
     rows.append(jnp.concatenate([lax.shift_right_arithmetic(parent, shift) + 1, empty], axis=1))
     rows.append(jnp.concatenate([parent & (basin_rows - 1), empty], axis=1))
     numbers = jnp.concatenate(rows, axis=0).astype(jnp.float32)
-    meta_ref[...] = jnp.concatenate([numbers] * (meta_ref.shape[0] // FIELDS), axis=0).astype(jnp.bfloat16)
+    repeated = jnp.concatenate([numbers] * (meta_ref.shape[0] // FIELDS), axis=0)
+    mine = iota(meta_ref.shape, 0) // FIELDS == lax.axis_index("tile")
+    meta_ref[...] = jnp.where(mine, repeated, 0.0).astype(jnp.bfloat16)
     for copy in copies[4:8]:
         copy.wait()
     soil, area, dest, reach = [ref[...] for ref in scratch[4:]]
@@ -279,11 +277,10 @@
     meta, own = pl.pallas_call(
         lambda *refs: pack_kernel(*refs, basin_rows=basin_rows),
         out_shape=(
-            pltpu.VMEM((owners * FIELDS, LANES), jnp.bfloat16),
+            jax.ShapeDtypeStruct((owners * FIELDS, LANES), jnp.bfloat16),
             jax.ShapeDtypeStruct(block, jnp.bfloat16),
         ),
         in_specs=[held] * (len(numbers) + 1),
-        out_specs=(whole, whole),
         scratch_shapes=[pltpu.VMEM(values.shape, values.dtype) for values in numbers]
         + [pltpu.SemaphoreType.DMA((len(numbers) + 1,))],
         compiler_params=params,
@@ -291,9 +288,7 @@
         name="pack",
     )(*numbers, in_hbm(rain, rain.shape))
     other = lax.ppermute(own, "tile", [(i, i ^ 1) for i in range(owners)])
-    meta = lax.all_to_all(
-        meta.reshape(owners, FIELDS, LANES), "tile", split_axis=0, concat_axis=0, tiled=True
-    ).reshape(-1, LANES)
+    meta = lax.psum(meta, "tile")
 
     chip_tiles = CORES * tile_rows
     early = kinds // 2

time: 28.6 us -> 79.1 us (2.77)
  blocking collectives: 9.74 us -> 72.9 us
  starting transfers between devices: 7.57 us -> 0.52 us
  waiting for transfers between devices: 4.98 us -> 0.01 us
    psum x0 -> x1, blocking collectives: none -> 63.2 us  [per_device(): meta = lax.psum(meta, 'tile')]
    all_to_all x1 -> x0, starting transfers between devices: 7.05 us -> none  [per_device(): lax.all_to_all(meta.reshape(owners, FIELDS, LANES), 'tile', split_axis=0,...]
    all_to_all x1 -> x0, waiting for transfers between devices: 4.98 us -> none  [per_device(): lax.all_to_all(meta.reshape(owners, FIELDS, LANES), 'tile', split_axis=0,...]
  transfers between devices with their start and end apart: 2 -> 1, of which waited for: 1 -> 0; matrix products, arithmetic and copies ran while one was open for 0% -> 0% of each run, Pallas kernels for 6% -> 0%
where the time goes in v16:
time: 79.1 us; the launch traced here: 78.9 us
  blocking collectives  72.9 us (92%)
  Pallas kernels  5.4 us (7%)
    psum x1, blocking collectives, per_device(): meta = lax.psum(meta, 'tile')  63.2 us
    all_to_all x1, blocking collectives, per_device(): lax.all_to_all(flow.reshape(owners // CORES, basin_rows, hours), 'tile',...  9.74 us
    pallas_call x1, Pallas kernels, per_device(): pl.pallas_call(lambda *refs: route_kernel(*refs, basin_rows=basin_rows),...  1.93 us
    pallas_call x1, Pallas kernels, per_device(): pl.pallas_call(prepare_kernel, out_shape=(jax.ShapeDtypeStruct((hours, ch...  1.65 us
  transfers between devices with their start and end apart: 1, of which 0 were waited for; matrix products, arithmetic and copies ran while one was open for 0% of the time, Pallas kernels for 0%

profile of v16, /device:TPU:0, one launch (start us, length us, event | category | flops | bytes accessed | tf_op | source)
XLA Modules:
  0.0 78.9 jit_solution(6046219561807616190)
XLA Ops:
  0.0 1.1 %pack.1 = (bf16[128,128]{1,0:T(8,128)(2,1)S(1)}, bf16[272,256]{1,0:T(8,128)(2,1)S(1)}) custom-call(s32[1,256]{1,0:T(1,128)} %bitcast.10, s32[1,256]{1,0:T(1,128)} %bitcast.11, s32[1,256]{1,0:T(1,128)} %bitcast.12, s32[1,32]{1,0:T(1,128)} %bitcast.17, f32[1,256]{1,0:T(1,128)} %bitcast.13, f32[1,256]{1,0:T(1,128)} %bitcast.14, s32[1,256]{1,0:T(1,128)} %bitcast.15, ...), custom_call_target="tpu_custom_call" | custom-call | flops 1 | bytes 1 | tf_op jit(solution)/shard_map/pack/pallas_call | solution.py:277
  1.1 0.5 collective-permute-start
  1.6 63.2 %psum.7.refs_0_ = bf16[128,128]{1,0:T(8,128)(2,1)S(1)} all-reduce(bf16[128,128]{1,0:T(8,128)(2,1)S(1)} %get-tuple-element.12), channel_id=1, replica_groups=mesh['ens'=2,'tile'=16] {'tile'}, use_global_device_ids=true, to_apply=%region_0.0 | all-reduce | flops 16384 | bytes 65536 | tf_op jit(solution)/shard_map/psum | solution.py:291
  64.8 0.0 collective-permute-done.other_ref
  64.8 1.6 %prepare.1 = (bf16[256,512]{1,0:T(8,128)(2,1)S(1)}, s32[8,512]{1,0:T(8,128)S(1)}, bf16[256,512]{1,0:T(8,128)(2,1)S(1)}, bf16[256,1024]{1,0:T(8,128)(2,1)S(1)}, f32[4,256,512]{2,1,0:T(8,128)S(1)}) custom-call(f32[8,48]{1,0:T(8,128)} %irf_hbm.1, bf16[272,256]{1,0:T(8,128)(2,1)S(1)} %get-tuple-element.13.own_ref, ...), custom_call_target="tpu_custom_call" | custom-call | flops 1 | bytes 1 | tf_op jit(solution)/shard_map/prepare/pallas_call | solution.py:295
  66.5 1.9 %route.1 = s16[256,256]{1,0:T(8,128)(2,1)S(1)} custom-call(bf16[128,128]{1,0:T(8,128)(2,1)S(1)} %psum.7.refs_0_, bf16[256,512]{1,0:T(8,128)(2,1)S(1)} %get-tuple-element.14.refs_1_, s32[8,512]{1,0:T(8,128)S(1)} %get-tuple-element.15.refs_2_, bf16[256,512]{1,0:T(8,128)(2,1)S(1)} %get-tuple-element.16.refs_3_, ...), custom_call_target="tpu_custom_call" | custom-call | tf_op jit(solution)/shard_map/route/pallas_call | solution.py:311
  68.4 9.7 %all_to_all.5.parts_ref = s16[8,32,256]{2,1,0:T(8,128)(2,1)S(1)} all-to-all(s16[8,32,256]{2,1,0:T(8,128)(2,1)S(1)} %bitcast.9), channel_id=1, replica_groups={{0,2,4,6,8,10,12,14},{1,3,5,7,9,11,13,15},{16,18,20,22,24,26,28,30},{17..., dimensions={0} | all-to-all | bytes 262144 | tf_op jit(solution)/shard_map/all_to_all | solution.py:319
  78.2 0.7 finish.1
Async XLA Ops:
  1.1 63.7 %collective-permute-start = (bf16[272,256]{1,0:T(8,128)(2,1)S(1)}, bf16[272,256]{1,0:T(8,128)(2,1)S(1)}, u32[]{:S(2)}, u32[]{:S(2)}) collective-permute-start(bf16[272,256]{1,0:T(8,128)(2,1)S(1)} %get-tuple-element.13.own_ref), channel_id=1, source_target_pairs={{0,1},{1,0},{2,3},{3,2},{4,5},{5,4},{6,7},{7,6},{8,9},{9,8},{10,11... | collective-permute-start | bytes 417800 | tf_op jit(solution)/shard_map/ppermute | solution.py:290

commit v17 on v16

--- a/solution.py
+++ b/solution.py
@@ -79,9 +79,7 @@
     rows.append(jnp.concatenate([lax.shift_right_arithmetic(parent, shift) + 1, empty], axis=1))
     rows.append(jnp.concatenate([parent & (basin_rows - 1), empty], axis=1))
     numbers = jnp.concatenate(rows, axis=0).astype(jnp.float32)
-    repeated = jnp.concatenate([numbers] * (meta_ref.shape[0] // FIELDS), axis=0)
-    mine = iota(meta_ref.shape, 0) // FIELDS == lax.axis_index("tile")
-    meta_ref[...] = jnp.where(mine, repeated, 0.0).astype(jnp.bfloat16)
+    meta_ref[...] = numbers.astype(jnp.bfloat16)
     for copy in copies[4:8]:
         copy.wait()
     soil, area, dest, reach = [ref[...] for ref in scratch[4:]]
@@ -92,7 +90,7 @@
 
 
 def prepare_kernel(
-    irf_hbm, own_ref, other_ref, runoff_ref, dest_ref, reach_marks_ref, late_ref, responses_ref, irf_ref, arrived
+    irf_hbm, own_ref, other_ref, dest_ref, reach_marks_ref, responses_ref, irf_ref, arrived
 ):
     copy = pltpu.make_async_copy(irf_hbm, irf_ref, arrived.at[0])
     copy.start()
@@ -100,7 +98,6 @@
     half = hours // 2
     tile_rows = own_ref.shape[0] - SIDE_ROWS
     kinds, taps = irf_ref.shape
-    early = responses_ref.shape[0]
     sides = jnp.concatenate([own_ref[tile_rows:], other_ref[tile_rows:]], axis=1).astype(jnp.float32)
     rainfall = jnp.concatenate(
         [ref[:tile_rows].astype(jnp.float32).T for ref in (own_ref, other_ref)], axis=1
@@ -109,7 +106,6 @@
     area = sides[3:4] + sides[4:5] + sides[5:6]
     excess = jnp.maximum(rainfall - 0.2 * storage, 0.0)
     runoff = (area * excess * excess / (rainfall + 0.8 * storage)).astype(jnp.bfloat16)
-    runoff_ref[...] = runoff
     dest_ref[...] = jnp.broadcast_to(sides[6:7], dest_ref.shape).astype(jnp.int32)
     reach_marks_ref[...] = one_hot(sides[7:8].astype(jnp.int32), reach_marks_ref.shape[0])
     backward = (
@@ -124,48 +120,35 @@
         row = jnp.broadcast_to(reversed_taps[kind : kind + 1], (half, hours))
         matrix = jnp.where(causal, pltpu.roll(row, half, 1, stride=1, stride_axis=0), 0.0)
         matrix = jnp.concatenate(split(matrix), axis=0)
-        if kind < early:
-            responses_ref[kind] = respond(matrix, runoff)
-        else:
-            late_ref[:, (kind - early) * hours : (kind - early + 1) * hours] = matrix
-
-
-def respond(matrices, runoffs):
-    hours = matrices.shape[0]
-    half = hours // 2
-    count = matrices.shape[1] // hours
-
-    def halves(values, axis, first):
-        pieces = [
-            lax.slice_in_dim(values, j * hours + first, j * hours + first + half, axis=axis)
-            for j in range(count)
-        ]
-        return jnp.concatenate(pieces, axis=axis)
-
-    earlier = lax.dot_general(
-        halves(matrices, 1, half), halves(runoffs, 0, 0), NN, preferred_element_type=jnp.float32
-    )
-    later = lax.dot_general(matrices, runoffs, NN, preferred_element_type=jnp.float32)
+        responses_ref[kind] = respond(matrix, runoff)
+
+
+def respond(matrix, runoff):
+    half = matrix.shape[0] // 2
+    earlier = lax.dot_general(matrix[:, half:], runoff[:half], NN, preferred_element_type=jnp.float32)
+    later = lax.dot_general(matrix, runoff, NN, preferred_element_type=jnp.float32)
     return jnp.concatenate([earlier[:half] + earlier[half:], later[:half] + later[half:]], axis=0)
 
 
-def route_kernel(
-    meta_ref, runoff_ref, dest_ref, reach_marks_ref, late_ref, responses_ref, flow_ref, stack_ref, *, basin_rows
-):
-    early, hours, tiles = responses_ref.shape
-    late = late_ref.shape[1] // hours
+def route_kernel(*refs, basin_rows):
+    *meta_refs, dest_ref, reach_marks_ref, responses_ref, flow_ref, stack_ref = refs
+    kinds, _, tiles = responses_ref.shape
     outlets = flow_ref.shape[0]
-    owners = meta_ref.shape[0] // FIELDS
-    core = lax.rem(lax.axis_index("tile"), CORES)
+    owners = (stack_ref.shape[0] - FIELDS) // FIELDS
+    me = lax.axis_index("tile")
+    core = lax.rem(me, CORES)
     dest = dest_ref[0:1]
 
-    stack_ref[...] = meta_ref[...].astype(jnp.float32)
+    first = 0
+    for meta_ref in meta_refs:
+        stack_ref[first : first + meta_ref.shape[0]] = meta_ref[...].astype(jnp.float32)
+        first += meta_ref.shape[0]
 
     def table(field):
         return stack_ref[pl.ds(field, owners, stride=FIELDS), :].astype(jnp.bfloat16)
 
     def picked(values, owner):
-        chosen = iota((owners, tiles), 0) == owner
+        chosen = iota((owners, tiles), 0) == owners - 1 - (owner ^ me)
         return jnp.sum(jnp.where(chosen, values, 0.0), axis=0, keepdims=True).astype(jnp.int32)
 
     spans = (FIELDS - 2) // 3
@@ -207,16 +190,8 @@
         axis=0,
     )
 
-    runoff = runoff_ref[...]
-    by_kind = jnp.concatenate(
-        [
-            runoff * (kind == early + k).astype(jnp.float32).astype(jnp.bfloat16)
-            for k in range(late)
-        ],
-        axis=0,
-    )
-    routed = respond(late_ref[...], by_kind)
-    for k in range(early):
+    routed = responses_ref[0]
+    for k in range(1, kinds):
         routed = jnp.where(kind == k, responses_ref[k], routed)
     step = 64
     while step:
@@ -277,7 +252,7 @@
     meta, own = pl.pallas_call(
         lambda *refs: pack_kernel(*refs, basin_rows=basin_rows),
         out_shape=(
-            jax.ShapeDtypeStruct((owners * FIELDS, LANES), jnp.bfloat16),
+            jax.ShapeDtypeStruct((FIELDS, LANES), jnp.bfloat16),
             jax.ShapeDtypeStruct(block, jnp.bfloat16),
         ),
         in_specs=[held] * (len(numbers) + 1),
@@ -288,18 +263,25 @@
         name="pack",
     )(*numbers, in_hbm(rain, rain.shape))
     other = lax.ppermute(own, "tile", [(i, i ^ 1) for i in range(owners)])
-    meta = lax.psum(meta, "tile")
+    metas = [meta]
+    held_owners = 1
+    while held_owners < owners:
+        radix = min(4, owners // held_owners)
+        stack = jnp.concatenate(metas, axis=0) if len(metas) > 1 else metas[0]
+        met = {
+            step: lax.ppermute(stack, "tile", [(i, i ^ (held_owners * step)) for i in range(owners)])
+            for step in range(1, radix)
+        }
+        metas = [met[step] for step in range(radix - 1, 0, -1)] + [stack]
+        held_owners *= radix
 
     chip_tiles = CORES * tile_rows
-    early = kinds // 2
     prepared = pl.pallas_call(
         prepare_kernel,
         out_shape=(
-            jax.ShapeDtypeStruct((hours, chip_tiles), jnp.bfloat16),
             jax.ShapeDtypeStruct((8, chip_tiles), jnp.int32),
             jax.ShapeDtypeStruct((reach_basin.size, chip_tiles), jnp.bfloat16),
-            jax.ShapeDtypeStruct((hours, (kinds - early) * hours), jnp.bfloat16),
-            jax.ShapeDtypeStruct((early, hours, chip_tiles), jnp.float32),
+            jax.ShapeDtypeStruct((kinds, hours, chip_tiles), jnp.float32),
         ),
         in_specs=[held, whole, whole],
         scratch_shapes=[pltpu.VMEM(irf.shape, irf.dtype), pltpu.SemaphoreType.DMA((1,))],
@@ -311,10 +293,10 @@
     flow = pl.pallas_call(
         lambda *refs: route_kernel(*refs, basin_rows=basin_rows),
         out_shape=jax.ShapeDtypeStruct((owners // CORES * basin_rows, hours), jnp.int16),
-        scratch_shapes=[pltpu.VMEM(meta.shape, jnp.float32)],
+        scratch_shapes=[pltpu.VMEM(((owners + 1) * FIELDS, LANES), jnp.float32)],
         compiler_params=params,
         name="route",
-    )(meta, *prepared)
+    )(*metas, *prepared)
 
     parts = lax.all_to_all(
         flow.reshape(owners // CORES, basin_rows, hours),

time: 79.1 us -> 29.8 us (0.38)
  blocking collectives: 72.9 us -> 9.74 us
  starting transfers between devices: 0.52 us -> 7.8 us
  waiting for transfers between devices: 0.01 us -> 6.26 us
    psum x1 -> x0, blocking collectives: 63.2 us -> none  [per_device(): meta = lax.psum(meta, 'tile')]
    ppermute x0 -> x6, starting transfers between devices: none -> 7.64 us  [per_device(): lax.ppermute(stack, 'tile', [(i, i ^ held_owners * step) for i in range(o...]
    ppermute x0 -> x6, waiting for transfers between devices: none -> 6.26 us  [per_device(): lax.ppermute(stack, 'tile', [(i, i ^ held_owners * step) for i in range(o...]
  transfers between devices with their start and end apart: 1 -> 7, of which waited for: 0 -> 3; matrix products, arithmetic and copies ran while one was open for 0% -> 0% of each run, Pallas kernels for 0% -> 8%
where the time goes in v17:
time: 29.8 us; the launch traced here: 29.6 us
  blocking collectives  9.74 us (33%)
  starting transfers between devices  7.8 us (26%)
  waiting for transfers between devices  6.26 us (21%)
  Pallas kernels  5.76 us (19%)
    all_to_all x1, blocking collectives, per_device(): lax.all_to_all(flow.reshape(owners // CORES, basin_rows, hours), 'tile',...  9.74 us
    ppermute x6, starting transfers between devices, per_device(): lax.ppermute(stack, 'tile', [(i, i ^ held_owners * step) for i in range(o...  7.64 us
    ppermute x6, waiting for transfers between devices, per_device(): lax.ppermute(stack, 'tile', [(i, i ^ held_owners * step) for i in range(o...  6.26 us
    pallas_call x1, Pallas kernels, per_device(): pl.pallas_call(prepare_kernel, out_shape=(jax.ShapeDtypeStruct((8, chip_t...  2.32 us
    pallas_call x1, Pallas kernels, per_device(): pl.pallas_call(lambda *refs: route_kernel(*refs, basin_rows=basin_rows),...  1.62 us
    pallas_call x1, Pallas kernels, per_device(): pl.pallas_call(lambda *refs: pack_kernel(*refs, basin_rows=basin_rows), o...  1.11 us
    pallas_call x1, Pallas kernels, per_device(): pl.pallas_call(finish_kernel, out_shape=jax.ShapeDtypeStruct((basin_rows,...  0.71 us
  transfers between devices with their start and end apart: 7, of which 3 were waited for; matrix products, arithmetic and copies ran while one was open for 0% of the time, Pallas kernels for 8%

profile of v17, /device:TPU:0, one launch (start us, length us, event | category | flops | bytes accessed | tf_op | source)
XLA Modules:
  0.0 29.6 jit_solution(7840218053549841168)
XLA Ops:
  0.0 1.1 %pack.1 = (bf16[8,128]{1,0:T(8,128)(2,1)S(1)}, bf16[272,256]{1,0:T(8,128)(2,1)S(1)}) custom-call(s32[1,256]{1,0:T(1,128)} %bitcast.10, s32[1,256]{1,0:T(1,128)} %bitcast.11, s32[1,256]{1,0:T(1,128)} %bitcast.12, s32[1,32]{1,0:T(1,128)} %bitcast.17, f32[1,256]{1,0:T(1,128)} %bitcast.13, f32[1,256]{1,0:T(1,128)} %bitcast.14, s32[1,256]{1,0:T(1,128)} %bitcast.15, ...), custom_call_target="tpu_custom_call" | custom-call | flops 1 | bytes 1 | tf_op jit(solution)/shard_map/pack/pallas_call | solution.py:252
  1.1 2.5 %collective-permute-start = (bf16[8,128]{1,0:T(8,128)(2,1)S(1)}, bf16[8,128]{1,0:T(8,128)(2,1)S(1)}, u32[]{:S(2)}, u32[]{:S(2)}) collective-permute-start(bf16[8,128]{1,0:T(8,128)(2,1)S(1)} %get-tuple-element.10), channel_id=1, source_target_pairs={{0,3},{1,2},{2,1},{3,0},{4,7},{5,6},{6,5},{7,4},{8,11},{9,10},{10,... | collective-permute-start | bytes 6152 | tf_op jit(solution)/shard_map/ppermute | solution.py:272
  3.6 0.7 %collective-permute-start.2 = (bf16[8,128]{1,0:T(8,128)(2,1)S(1)}, bf16[8,128]{1,0:T(8,128)(2,1)S(1)}, u32[]{:S(2)}, u32[]{:S(2)}) collective-permute-start(bf16[8,128]{1,0:T(8,128)(2,1)S(1)} %get-tuple-element.10), channel_id=1, source_target_pairs={{0,1},{1,0},{2,3},{3,2},{4,5},{5,4},{6,7},{7,6},{8,9},{9,8},{10,11... | collective-permute-start | bytes 6152 | tf_op jit(solution)/shard_map/ppermute | solution.py:272
  4.3 0.0 collective-permute-start.1
  4.3 0.2 collective-permute-start.6
  4.5 0.4 %collective-permute-done = bf16[8,128]{1,0:T(8,128)(2,1)S(1)} collective-permute-done((bf16[8,128]{1,0:T(8,128)(2,1)S(1)}, bf16[8,128]{1,0:T(8,128)(2,1)S(1)}, u32[]{:S(2)}, u32[]{:S(2)}) %collective-permute-start) | collective-permute-done | bytes 2080 | tf_op jit(solution)/shard_map/ppermute | solution.py:272
  4.9 3.0 %collective-permute-done.1 = bf16[8,128]{1,0:T(8,128)(2,1)S(1)} collective-permute-done((bf16[8,128]{1,0:T(8,128)(2,1)S(1)}, bf16[8,128]{1,0:T(8,128)(2,1)S(1)}, u32[]{:S(2)}, u32[]{:S(2)}) %collective-permute-start.1) | collective-permute-done | bytes 2080 | tf_op jit(solution)/shard_map/ppermute | solution.py:272
  7.9 0.0 collective-permute-done.2
  7.9 1.6 %collective-permute-start.5 = (bf16[32,128]{1,0:T(8,128)(2,1)S(1)}, bf16[32,128]{1,0:T(8,128)(2,1)S(1)}, u32[]{:S(2)}, u32[]{:S(2)}) collective-permute-start(bf16[32,128]{1,0:T(8,128)(2,1)S(1)} %constant_dynamic-update-slice_fusion.refs_3_), channel_id=1, source_target_pairs={{0,4},{1,5},{2,6},{3,7},{4,0},{5,1},{6,2},{7,3},{8,12},{9,13},{10,... | collective-permute-start | bytes 24584 | tf_op jit(solution)/shard_map/ppermute | solution.py:272
  9.5 2.6 %collective-permute-start.4 = (bf16[32,128]{1,0:T(8,128)(2,1)S(1)}, bf16[32,128]{1,0:T(8,128)(2,1)S(1)}, u32[]{:S(2)}, u32[]{:S(2)}) collective-permute-start(bf16[32,128]{1,0:T(8,128)(2,1)S(1)} %constant_dynamic-update-slice_fusion.refs_3_), channel_id=1, source_target_pairs={{0,8},{1,9},{2,10},{3,11},{4,12},{5,13},{6,14},{7,15},{8,0},{9,1},... | collective-permute-start | bytes 24584 | tf_op jit(solution)/shard_map/ppermute | solution.py:272
  12.1 0.2 collective-permute-start.3
  12.3 0.0 collective-permute-done.6.other_ref
  12.3 2.3 %prepare.1 = (s32[8,512]{1,0:T(8,128)S(1)}, bf16[256,512]{1,0:T(8,128)(2,1)S(1)}, f32[8,256,512]{2,1,0:T(8,128)S(1)}) custom-call(f32[8,48]{1,0:T(8,128)} %irf_hbm.1, bf16[272,256]{1,0:T(8,128)(2,1)S(1)} %get-tuple-element.11.own_ref, bf16[272,256]{1,0:T(8,128)(2,1)S(1)} %collective-permute-done.6.other_ref), custom_call_target="tpu_custom_call" | custom-call | flops 1 | bytes 1 | tf_op jit(solution)/shard_map/prepare/pallas_call | solution.py:279
  14.7 0.0 collective-permute-done.5.refs_2_
  14.7 0.0 collective-permute-done.4.refs_1_
  14.7 2.9 %collective-permute-done.3.refs_0_ = bf16[32,128]{1,0:T(8,128)(2,1)S(1)} collective-permute-done((bf16[32,128]{1,0:T(8,128)(2,1)S(1)}, bf16[32,128]{1,0:T(8,128)(2,1)S(1)}, u32[]{:S(2)}, u32[]{:S(2)}) %collective-permute-start.3) | collective-permute-done | bytes 8224 | tf_op jit(solution)/shard_map/ppermute | solution.py:272
  17.6 1.6 %route.1 = s16[256,256]{1,0:T(8,128)(2,1)S(1)} custom-call(bf16[32,128]{1,0:T(8,128)(2,1)S(1)} %collective-permute-done.3.refs_0_, bf16[32,128]{1,0:T(8,128)(2,1)S(1)} %collective-permute-done.4.refs_1_, bf16[32,128]{1,0:T(8,128)(2,1)S(1)} %collective-permute-done.5.refs_2_, bf16[32,128]{1,0:T(8,128)(2,1)S(1)} %constant_dynamic-update-slice_fusion.refs_3_, ...), custom_call_target="tpu_custom_call" | custom-call | tf_op jit(solution)/shard_map/route/pallas_call | solution.py:293
  19.2 9.7 %all_to_all.5.parts_ref = s16[8,32,256]{2,1,0:T(8,128)(2,1)S(1)} all-to-all(s16[8,32,256]{2,1,0:T(8,128)(2,1)S(1)} %bitcast.9), channel_id=1, replica_groups={{0,2,4,6,8,10,12,14},{1,3,5,7,9,11,13,15},{16,18,20,22,24,26,28,30},{17..., dimensions={0} | all-to-all | bytes 262144 | tf_op jit(solution)/shard_map/all_to_all | solution.py:301
  28.9 0.7 %finish.1 = f32[32,256]{1,0:T(8,128)} custom-call(s16[8,32,256]{2,1,0:T(8,128)(2,1)S(1)} %all_to_all.5.parts_ref), custom_call_target="tpu_custom_call" | custom-call | tf_op jit(solution)/shard_map/finish/pallas_call | solution.py:309
  (4 shorter events, 0.0 us)
Async XLA Ops:
  1.1 3.8 %collective-permute-start = (bf16[8,128]{1,0:T(8,128)(2,1)S(1)}, bf16[8,128]{1,0:T(8,128)(2,1)S(1)}, u32[]{:S(2)}, u32[]{:S(2)}) collective-permute-start(bf16[8,128]{1,0:T(8,128)(2,1)S(1)} %get-tuple-element.10), channel_id=1, source_target_pairs={{0,3},{1,2},{2,1},{3,0},{4,7},{5,6},{6,5},{7,4},{8,11},{9,10},{10,... | collective-permute-start | bytes 6152 | tf_op jit(solution)/shard_map/ppermute | solution.py:272
  3.6 4.3 %collective-permute-start.2 = (bf16[8,128]{1,0:T(8,128)(2,1)S(1)}, bf16[8,128]{1,0:T(8,128)(2,1)S(1)}, u32[]{:S(2)}, u32[]{:S(2)}) collective-permute-start(bf16[8,128]{1,0:T(8,128)(2,1)S(1)} %get-tuple-element.10), channel_id=1, source_target_pairs={{0,1},{1,0},{2,3},{3,2},{4,5},{5,4},{6,7},{7,6},{8,9},{9,8},{10,11... | collective-permute-start | bytes 6152 | tf_op jit(solution)/shard_map/ppermute | solution.py:272
  4.3 3.6 %collective-permute-start.1 = (bf16[8,128]{1,0:T(8,128)(2,1)S(1)}, bf16[8,128]{1,0:T(8,128)(2,1)S(1)}, u32[]{:S(2)}, u32[]{:S(2)}) collective-permute-start(bf16[8,128]{1,0:T(8,128)(2,1)S(1)} %get-tuple-element.10), channel_id=1, source_target_pairs={{0,2},{1,3},{2,0},{3,1},{4,6},{5,7},{6,4},{7,5},{8,10},{9,11},{10,... | collective-permute-start | bytes 6152 | tf_op jit(solution)/shard_map/ppermute | solution.py:272
  4.3 8.0 %collective-permute-start.6 = (bf16[272,256]{1,0:T(8,128)(2,1)S(1)}, bf16[272,256]{1,0:T(8,128)(2,1)S(1)}, u32[]{:S(2)}, u32[]{:S(2)}) collective-permute-start(bf16[272,256]{1,0:T(8,128)(2,1)S(1)} %get-tuple-element.11.own_ref), channel_id=1, source_target_pairs={{0,1},{1,0},{2,3},{3,2},{4,5},{5,4},{6,7},{7,6},{8,9},{9,8},{10,11... | collective-permute-start | bytes 417800 | tf_op jit(solution)/shard_map/ppermute | solution.py:265
  7.9 6.8 %collective-permute-start.5 = (bf16[32,128]{1,0:T(8,128)(2,1)S(1)}, bf16[32,128]{1,0:T(8,128)(2,1)S(1)}, u32[]{:S(2)}, u32[]{:S(2)}) collective-permute-start(bf16[32,128]{1,0:T(8,128)(2,1)S(1)} %constant_dynamic-update-slice_fusion.refs_3_), channel_id=1, source_target_pairs={{0,4},{1,5},{2,6},{3,7},{4,0},{5,1},{6,2},{7,3},{8,12},{9,13},{10,... | collective-permute-start | bytes 24584 | tf_op jit(solution)/shard_map/ppermute | solution.py:272
  9.5 5.2 %collective-permute-start.4 = (bf16[32,128]{1,0:T(8,128)(2,1)S(1)}, bf16[32,128]{1,0:T(8,128)(2,1)S(1)}, u32[]{:S(2)}, u32[]{:S(2)}) collective-permute-start(bf16[32,128]{1,0:T(8,128)(2,1)S(1)} %constant_dynamic-update-slice_fusion.refs_3_), channel_id=1, source_target_pairs={{0,8},{1,9},{2,10},{3,11},{4,12},{5,13},{6,14},{7,15},{8,0},{9,1},... | collective-permute-start | bytes 24584 | tf_op jit(solution)/shard_map/ppermute | solution.py:272
  12.1 5.4 %collective-permute-start.3 = (bf16[32,128]{1,0:T(8,128)(2,1)S(1)}, bf16[32,128]{1,0:T(8,128)(2,1)S(1)}, u32[]{:S(2)}, u32[]{:S(2)}) collective-permute-start(bf16[32,128]{1,0:T(8,128)(2,1)S(1)} %constant_dynamic-update-slice_fusion.refs_3_), channel_id=1, source_target_pairs={{0,12},{1,13},{2,14},{3,15},{4,8},{5,9},{6,10},{7,11},{8,4},{9,5},... | collective-permute-start | bytes 24584 | tf_op jit(solution)/shard_map/ppermute | solution.py:272

commit v18 on v13

--- a/solution.py
+++ b/solution.py
@@ -36,6 +36,11 @@
 
 def one_hot(row, count):
     return (iota((count, row.shape[1]), 0) == row).astype(jnp.float32).astype(jnp.bfloat16)
+
+
+def group_of(owner, owners):
+    upper = (owner + owners // 2) // owners
+    return (owner + upper) % CORES
 
 
 def later_rows(values, hours):
@@ -157,10 +162,10 @@
     late = late_ref.shape[1] // hours
     outlets = flow_ref.shape[0]
     owners = meta_ref.shape[0] // FIELDS
-    core = lax.rem(lax.axis_index("tile"), CORES)
+    side = group_of(lax.axis_index("tile"), owners)
     dest = dest_ref[0:1]
 
-    stack_ref[...] = meta_ref[...].astype(jnp.float32)
+    stack_ref[: owners * FIELDS] = meta_ref[...].astype(jnp.float32)
 
     def table(field):
         return stack_ref[pl.ds(field, owners, stride=FIELDS), :].astype(jnp.bfloat16)
@@ -193,7 +198,7 @@
     second_owner, second_local = parent_of(parent_owner, parent_local)
 
     def row_of(owner, local):
-        mine = jnp.logical_and(owner >= 0, (owner & (CORES - 1)) == core)
+        mine = jnp.logical_and(owner >= 0, group_of(owner, owners) == side)
         return jnp.where(mine, (owner // CORES) * basin_rows + local, -1)
 
     placements = jnp.concatenate(
@@ -318,7 +323,7 @@
     flow = pl.pallas_call(
         lambda *refs: route_kernel(*refs, basin_rows=basin_rows),
         out_shape=jax.ShapeDtypeStruct((owners // CORES * basin_rows, hours), jnp.int16),
-        scratch_shapes=[pltpu.VMEM(meta.shape, jnp.float32)],
+        scratch_shapes=[pltpu.VMEM(((owners + 1) * FIELDS, LANES), jnp.float32)],
         compiler_params=params,
         name="route",
     )(meta, *prepared)
@@ -328,7 +333,9 @@
         "tile",
         split_axis=0,
         concat_axis=0,
-        axis_index_groups=[list(range(core, owners, CORES)) for core in range(CORES)],
+        axis_index_groups=[
+            [owner for owner in range(owners) if group_of(owner, owners) == side] for side in range(CORES)
+        ],
         tiled=True,
     )
     return pl.pallas_call(

time: 28.3 us -> 28.6 us (1.011)
    all_to_all x1, blocking collectives: 9.74 us -> 10 us  [per_device(): lax.all_to_all(flow.reshape(owners // CORES, basin_rows, hours), 'tile',...]
where the time goes in v18:
time: 28.6 us; the launch traced here: 28.3 us
  blocking collectives  10 us (35%)
  starting transfers between devices  7.57 us (26%)
  Pallas kernels  5.72 us (20%)
  waiting for transfers between devices  4.97 us (17%)
    all_to_all x1, blocking collectives, per_device(): lax.all_to_all(flow.reshape(owners // CORES, basin_rows, hours), 'tile',...  10 us
    all_to_all x1, starting transfers between devices, per_device(): lax.all_to_all(meta.reshape(owners, FIELDS, LANES), 'tile', split_axis=0,...  7.05 us
    all_to_all x1, waiting for transfers between devices, per_device(): lax.all_to_all(meta.reshape(owners, FIELDS, LANES), 'tile', split_axis=0,...  4.96 us
    pallas_call x1, Pallas kernels, per_device(): pl.pallas_call(lambda *refs: route_kernel(*refs, basin_rows=basin_rows),...  1.94 us
    pallas_call x1, Pallas kernels, per_device(): pl.pallas_call(prepare_kernel, out_shape=(jax.ShapeDtypeStruct((hours, ch...  1.65 us
    pallas_call x1, Pallas kernels, per_device(): pl.pallas_call(lambda *refs: pack_kernel(*refs, basin_rows=basin_rows), o...  1.42 us
    pallas_call x1, Pallas kernels, per_device(): pl.pallas_call(finish_kernel, out_shape=jax.ShapeDtypeStruct((basin_rows,...  0.71 us
  transfers between devices with their start and end apart: 2, of which 1 were waited for; matrix products, arithmetic and copies ran while one was open for 0% of the time, Pallas kernels for 6%

profile of v18, /device:TPU:0, one launch (start us, length us, event | category | flops | bytes accessed | tf_op | source)
XLA Modules:
  0.0 28.3 jit_solution(8801799126123308796)
XLA Ops:
  0.0 1.4 %pack.1 = (bf16[128,128]{1,0:T(8,128)(2,1)}, bf16[272,256]{1,0:T(8,128)(2,1)S(1)}) custom-call(s32[1,256]{1,0:T(1,128)} %bitcast.13, s32[1,256]{1,0:T(1,128)} %bitcast.14, s32[1,256]{1,0:T(1,128)} %bitcast.15, s32[1,32]{1,0:T(1,128)} %bitcast.20, f32[1,256]{1,0:T(1,128)} %bitcast.16, f32[1,256]{1,0:T(1,128)} %bitcast.17, s32[1,256]{1,0:T(1,128)} %bitcast.18, ...), custom_call_target="tpu_custom_call" | custom-call | flops 1 | bytes 1 | tf_op jit(solution)/shard_map/pack/pallas_call | solution.py:283
  1.4 0.5 %collective-permute-start = (bf16[272,256]{1,0:T(8,128)(2,1)S(1)}, bf16[272,256]{1,0:T(8,128)(2,1)S(1)}, u32[]{:S(2)}, u32[]{:S(2)}) collective-permute-start(bf16[272,256]{1,0:T(8,128)(2,1)S(1)} %get-tuple-element.13.own_ref), channel_id=1, source_target_pairs={{0,1},{1,0},{2,3},{3,2},{4,5},{5,4},{6,7},{7,6},{8,9},{9,8},{10,11... | collective-permute-start | bytes 417800 | tf_op jit(solution)/shard_map/ppermute | solution.py:300
  1.9 7.0 %all-to-all-start = ((bf16[16,8,128]{2,1,0:T(8,128)(2,1)}), bf16[16,8,128]{2,1,0:T(8,128)(2,1)S(1)}, u32[]{:S(2)}, u32[]{:S(2)}) async-start(bf16[16,8,128]{2,1,0:T(8,128)(2,1)} %bitcast.8), calls=%async_computation | async-start | bytes 65536 | tf_op jit(solution)/shard_map/all_to_all | solution.py:301
  9.0 0.0 collective-permute-done.other_ref
  9.0 1.6 %prepare.1 = (bf16[256,512]{1,0:T(8,128)(2,1)S(1)}, s32[8,512]{1,0:T(8,128)S(1)}, bf16[256,512]{1,0:T(8,128)(2,1)S(1)}, bf16[256,1024]{1,0:T(8,128)(2,1)S(1)}, f32[4,256,512]{2,1,0:T(8,128)S(1)}) custom-call(f32[8,48]{1,0:T(8,128)} %irf_hbm.1, bf16[272,256]{1,0:T(8,128)(2,1)S(1)} %get-tuple-element.13.own_ref, ...), custom_call_target="tpu_custom_call" | custom-call | flops 1 | bytes 1 | tf_op jit(solution)/shard_map/prepare/pallas_call | solution.py:307
  10.7 5.0 %all-to-all-done = bf16[16,8,128]{2,1,0:T(8,128)(2,1)S(1)} async-done(((bf16[16,8,128]{2,1,0:T(8,128)(2,1)}), bf16[16,8,128]{2,1,0:T(8,128)(2,1)S(1)}, u32[]{:S(2)}, u32[]{:S(2)}) %all-to-all-start) | async-done | bytes 32800 | tf_op jit(solution)/shard_map/all_to_all | solution.py:301
  15.6 1.9 %route.1 = s16[256,256]{1,0:T(8,128)(2,1)S(1)} custom-call(bf16[128,128]{1,0:T(8,128)(2,1)S(1)} %bitcast.12, bf16[256,512]{1,0:T(8,128)(2,1)S(1)} %get-tuple-element.14.refs_1_, s32[8,512]{1,0:T(8,128)S(1)} %get-tuple-element.15.refs_2_, bf16[256,512]{1,0:T(8,128)(2,1)S(1)} %get-tuple-element.16.refs_3_, bf16[256,1024]{1,0:T(8,128)(2,1)S(1)} %get-tuple-element.17.refs_4_, ...), custom_call_target="tpu_custom_call" | custom-call | tf_op jit(solution)/shard_map/route/pallas_call | solution.py:323
  17.6 10.0 %all_to_all.10.parts_ref = s16[8,32,256]{2,1,0:T(8,128)(2,1)S(1)} all-to-all(s16[8,32,256]{2,1,0:T(8,128)(2,1)S(1)} %bitcast.11), channel_id=1, replica_groups={{0,2,4,6,9,11,13,15},{1,3,5,7,8,10,12,14},{16,18,20,22,25,27,29,31},{17..., dimensions={0} | all-to-all | bytes 262144 | tf_op jit(solution)/shard_map/all_to_all | solution.py:331
  27.6 0.7 %finish.1 = f32[32,256]{1,0:T(8,128)} custom-call(s16[8,32,256]{2,1,0:T(8,128)(2,1)S(1)} %all_to_all.10.parts_ref), custom_call_target="tpu_custom_call" | custom-call | tf_op jit(solution)/shard_map/finish/pallas_call | solution.py:341
Async XLA Ops:
  1.4 7.6 %collective-permute-start = (bf16[272,256]{1,0:T(8,128)(2,1)S(1)}, bf16[272,256]{1,0:T(8,128)(2,1)S(1)}, u32[]{:S(2)}, u32[]{:S(2)}) collective-permute-start(bf16[272,256]{1,0:T(8,128)(2,1)S(1)} %get-tuple-element.13.own_ref), channel_id=1, source_target_pairs={{0,1},{1,0},{2,3},{3,2},{4,5},{5,4},{6,7},{7,6},{8,9},{9,8},{10,11... | collective-permute-start | bytes 417800 | tf_op jit(solution)/shard_map/ppermute | solution.py:300
  1.9 13.7 %all-to-all-start = ((bf16[16,8,128]{2,1,0:T(8,128)(2,1)}), bf16[16,8,128]{2,1,0:T(8,128)(2,1)S(1)}, u32[]{:S(2)}, u32[]{:S(2)}) async-start(bf16[16,8,128]{2,1,0:T(8,128)(2,1)} %bitcast.8), calls=%async_computation | async-start | bytes 65536 | tf_op jit(solution)/shard_map/all_to_all | solution.py:301

commit v19 on v13

--- a/solution.py
+++ b/solution.py
@@ -160,7 +160,7 @@
     core = lax.rem(lax.axis_index("tile"), CORES)
     dest = dest_ref[0:1]
 
-    stack_ref[...] = meta_ref[...].astype(jnp.float32)
+    stack_ref[: owners * FIELDS] = meta_ref[...].astype(jnp.float32)
 
     def table(field):
         return stack_ref[pl.ds(field, owners, stride=FIELDS), :].astype(jnp.bfloat16)
@@ -181,11 +181,11 @@
         reach_table, reach_marks_ref[...], NN, preferred_element_type=jnp.float32
     )
     basin, kind, lag = [picked(by_reach[j * owners : (j + 1) * owners], dest) for j in range(3)]
-    tree_table = jnp.concatenate([table(3 * spans), table(3 * spans + 1)], axis=0)
+    tree_table = jnp.concatenate([table(3 * spans), table(3 * spans + 1)], axis=0)[:, :basin_rows]
 
     def parent_of(owner, local):
         by_basin = lax.dot_general(
-            tree_table, one_hot(local, LANES), NN, preferred_element_type=jnp.float32
+            tree_table, one_hot(local, basin_rows), NN, preferred_element_type=jnp.float32
         )
         return picked(by_basin[:owners], owner) - 1, picked(by_basin[owners:], owner)
 
@@ -318,7 +318,7 @@
     flow = pl.pallas_call(
         lambda *refs: route_kernel(*refs, basin_rows=basin_rows),
         out_shape=jax.ShapeDtypeStruct((owners // CORES * basin_rows, hours), jnp.int16),
-        scratch_shapes=[pltpu.VMEM(meta.shape, jnp.float32)],
+        scratch_shapes=[pltpu.VMEM(((owners + 1) * FIELDS, LANES), jnp.float32)],
         compiler_params=params,
         name="route",
     )(meta, *prepared)

time: 28.3 us -> 28.3 us (level)
  no operation moved by 1% of the time
where the time goes in v19:
time: 28.3 us; the launch traced here: 28 us
  blocking collectives  9.74 us (34%)
  starting transfers between devices  7.57 us (27%)
  Pallas kernels  5.69 us (20%)
  waiting for transfers between devices  4.97 us (18%)
    all_to_all x1, blocking collectives, per_device(): lax.all_to_all(flow.reshape(owners // CORES, basin_rows, hours), 'tile',...  9.74 us
    all_to_all x1, starting transfers between devices, per_device(): lax.all_to_all(meta.reshape(owners, FIELDS, LANES), 'tile', split_axis=0,...  7.05 us
    all_to_all x1, waiting for transfers between devices, per_device(): lax.all_to_all(meta.reshape(owners, FIELDS, LANES), 'tile', split_axis=0,...  4.96 us
    pallas_call x1, Pallas kernels, per_device(): pl.pallas_call(lambda *refs: route_kernel(*refs, basin_rows=basin_rows),...  1.91 us
    pallas_call x1, Pallas kernels, per_device(): pl.pallas_call(prepare_kernel, out_shape=(jax.ShapeDtypeStruct((hours, ch...  1.65 us
    pallas_call x1, Pallas kernels, per_device(): pl.pallas_call(lambda *refs: pack_kernel(*refs, basin_rows=basin_rows), o...  1.42 us
    pallas_call x1, Pallas kernels, per_device(): pl.pallas_call(finish_kernel, out_shape=jax.ShapeDtypeStruct((basin_rows,...  0.71 us
  transfers between devices with their start and end apart: 2, of which 1 were waited for; matrix products, arithmetic and copies ran while one was open for 0% of the time, Pallas kernels for 6%

profile of v19, /device:TPU:0, one launch (start us, length us, event | category | flops | bytes accessed | tf_op | source)
XLA Modules:
  0.0 28.0 jit_solution(16391658633620670690)
XLA Ops:
  0.0 1.4 %pack.1 = (bf16[128,128]{1,0:T(8,128)(2,1)}, bf16[272,256]{1,0:T(8,128)(2,1)S(1)}) custom-call(s32[1,256]{1,0:T(1,128)} %bitcast.13, s32[1,256]{1,0:T(1,128)} %bitcast.14, s32[1,256]{1,0:T(1,128)} %bitcast.15, s32[1,32]{1,0:T(1,128)} %bitcast.20, f32[1,256]{1,0:T(1,128)} %bitcast.16, f32[1,256]{1,0:T(1,128)} %bitcast.17, s32[1,256]{1,0:T(1,128)} %bitcast.18, ...), custom_call_target="tpu_custom_call" | custom-call | flops 1 | bytes 1 | tf_op jit(solution)/shard_map/pack/pallas_call | solution.py:278
  1.4 0.5 %collective-permute-start = (bf16[272,256]{1,0:T(8,128)(2,1)S(1)}, bf16[272,256]{1,0:T(8,128)(2,1)S(1)}, u32[]{:S(2)}, u32[]{:S(2)}) collective-permute-start(bf16[272,256]{1,0:T(8,128)(2,1)S(1)} %get-tuple-element.13.own_ref), channel_id=1, source_target_pairs={{0,1},{1,0},{2,3},{3,2},{4,5},{5,4},{6,7},{7,6},{8,9},{9,8},{10,11... | collective-permute-start | bytes 417800 | tf_op jit(solution)/shard_map/ppermute | solution.py:295
  1.9 7.0 %all-to-all-start = ((bf16[16,8,128]{2,1,0:T(8,128)(2,1)}), bf16[16,8,128]{2,1,0:T(8,128)(2,1)S(1)}, u32[]{:S(2)}, u32[]{:S(2)}) async-start(bf16[16,8,128]{2,1,0:T(8,128)(2,1)} %bitcast.8), calls=%async_computation | async-start | bytes 65536 | tf_op jit(solution)/shard_map/all_to_all | solution.py:296
  9.0 0.0 collective-permute-done.other_ref
  9.0 1.6 %prepare.1 = (bf16[256,512]{1,0:T(8,128)(2,1)S(1)}, s32[8,512]{1,0:T(8,128)S(1)}, bf16[256,512]{1,0:T(8,128)(2,1)S(1)}, bf16[256,1024]{1,0:T(8,128)(2,1)S(1)}, f32[4,256,512]{2,1,0:T(8,128)S(1)}) custom-call(f32[8,48]{1,0:T(8,128)} %irf_hbm.1, bf16[272,256]{1,0:T(8,128)(2,1)S(1)} %get-tuple-element.13.own_ref, ...), custom_call_target="tpu_custom_call" | custom-call | flops 1 | bytes 1 | tf_op jit(solution)/shard_map/prepare/pallas_call | solution.py:302
  10.7 5.0 %all-to-all-done = bf16[16,8,128]{2,1,0:T(8,128)(2,1)S(1)} async-done(((bf16[16,8,128]{2,1,0:T(8,128)(2,1)}), bf16[16,8,128]{2,1,0:T(8,128)(2,1)S(1)}, u32[]{:S(2)}, u32[]{:S(2)}) %all-to-all-start) | async-done | bytes 32800 | tf_op jit(solution)/shard_map/all_to_all | solution.py:296
  15.6 1.9 %route.1 = s16[256,256]{1,0:T(8,128)(2,1)S(1)} custom-call(bf16[128,128]{1,0:T(8,128)(2,1)S(1)} %bitcast.12, bf16[256,512]{1,0:T(8,128)(2,1)S(1)} %get-tuple-element.14.refs_1_, s32[8,512]{1,0:T(8,128)S(1)} %get-tuple-element.15.refs_2_, bf16[256,512]{1,0:T(8,128)(2,1)S(1)} %get-tuple-element.16.refs_3_, bf16[256,1024]{1,0:T(8,128)(2,1)S(1)} %get-tuple-element.17.refs_4_, ...), custom_call_target="tpu_custom_call" | custom-call | tf_op jit(solution)/shard_map/route/pallas_call | solution.py:318
  17.6 9.7 %all_to_all.10.parts_ref = s16[8,32,256]{2,1,0:T(8,128)(2,1)S(1)} all-to-all(s16[8,32,256]{2,1,0:T(8,128)(2,1)S(1)} %bitcast.11), channel_id=1, replica_groups={{0,2,4,6,8,10,12,14},{1,3,5,7,9,11,13,15},{16,18,20,22,24,26,28,30},{17..., dimensions={0} | all-to-all | bytes 262144 | tf_op jit(solution)/shard_map/all_to_all | solution.py:326
  27.3 0.7 %finish.1 = f32[32,256]{1,0:T(8,128)} custom-call(s16[8,32,256]{2,1,0:T(8,128)(2,1)S(1)} %all_to_all.10.parts_ref), custom_call_target="tpu_custom_call" | custom-call | tf_op jit(solution)/shard_map/finish/pallas_call | solution.py:334
Async XLA Ops:
  1.4 7.6 %collective-permute-start = (bf16[272,256]{1,0:T(8,128)(2,1)S(1)}, bf16[272,256]{1,0:T(8,128)(2,1)S(1)}, u32[]{:S(2)}, u32[]{:S(2)}) collective-permute-start(bf16[272,256]{1,0:T(8,128)(2,1)S(1)} %get-tuple-element.13.own_ref), channel_id=1, source_target_pairs={{0,1},{1,0},{2,3},{3,2},{4,5},{5,4},{6,7},{7,6},{8,9},{9,8},{10,11... | collective-permute-start | bytes 417800 | tf_op jit(solution)/shard_map/ppermute | solution.py:295
  1.9 13.7 %all-to-all-start = ((bf16[16,8,128]{2,1,0:T(8,128)(2,1)}), bf16[16,8,128]{2,1,0:T(8,128)(2,1)S(1)}, u32[]{:S(2)}, u32[]{:S(2)}) async-start(bf16[16,8,128]{2,1,0:T(8,128)(2,1)} %bitcast.8), calls=%async_computation | async-start | bytes 65536 | tf_op jit(solution)/shard_map/all_to_all | solution.py:296

commit v20 on v19

--- a/solution.py
+++ b/solution.py
@@ -39,11 +39,21 @@
 
 
 def later_rows(values, hours):
-    rows = values.shape[0]
-    if hours % 8 == 0:
-        padding = jnp.zeros((hours, values.shape[1]), values.dtype)
-        return jnp.concatenate([padding, values[: rows - hours]], axis=0)
-    return jnp.where(iota(values.shape, 0) < hours, 0.0, pltpu.roll(values, hours, 0))
+    padding = jnp.zeros((hours, values.shape[1]), values.dtype)
+    return jnp.concatenate([padding, values[: values.shape[0] - hours]], axis=0)
+
+
+def turned(values, hours):
+    place = iota((8, values.shape[1]), 0)
+    source = (place - hours) & 7
+    stays = place >= hours
+    before = jnp.zeros((8, values.shape[1]), values.dtype)
+    rows = []
+    for first in range(0, values.shape[0], 8):
+        now = jnp.take_along_axis(values[first : first + 8], source, axis=0, mode="promise_in_bounds")
+        rows.append(jnp.where(stays, now, before))
+        before = now
+    return jnp.concatenate(rows, axis=0)
 
 
 def later_lanes(values, hours):
@@ -219,10 +229,9 @@
     routed = respond(late_ref[...], by_kind)
     for k in range(early):
         routed = jnp.where(kind == k, responses_ref[k], routed)
-    step = 64
-    while step:
+    for step in (64, 32, 16, 8):
         routed = jnp.where((lag & step) != 0, later_rows(routed, step), routed)
-        step //= 2
+    routed = turned(routed, lag & 7)
     flows = lax.dot_general(
         jnp.concatenate([placements, placements], axis=1),
         jnp.concatenate(split(routed), axis=1),

time: 28.3 us -> 28.2 us (level)
  no operation moved by 1% of the time
where the time goes in v20:
time: 28.2 us; the launch traced here: 27.9 us
  blocking collectives  9.74 us (35%)
  starting transfers between devices  7.57 us (27%)
  Pallas kernels  5.59 us (20%)
  waiting for transfers between devices  4.97 us (18%)
    all_to_all x1, blocking collectives, per_device(): lax.all_to_all(flow.reshape(owners // CORES, basin_rows, hours), 'tile',...  9.74 us
    all_to_all x1, starting transfers between devices, per_device(): lax.all_to_all(meta.reshape(owners, FIELDS, LANES), 'tile', split_axis=0,...  7.05 us
    all_to_all x1, waiting for transfers between devices, per_device(): lax.all_to_all(meta.reshape(owners, FIELDS, LANES), 'tile', split_axis=0,...  4.96 us
    pallas_call x1, Pallas kernels, per_device(): pl.pallas_call(lambda *refs: route_kernel(*refs, basin_rows=basin_rows),...  1.81 us
    pallas_call x1, Pallas kernels, per_device(): pl.pallas_call(prepare_kernel, out_shape=(jax.ShapeDtypeStruct((hours, ch...  1.65 us
    pallas_call x1, Pallas kernels, per_device(): pl.pallas_call(lambda *refs: pack_kernel(*refs, basin_rows=basin_rows), o...  1.42 us
    pallas_call x1, Pallas kernels, per_device(): pl.pallas_call(finish_kernel, out_shape=jax.ShapeDtypeStruct((basin_rows,...  0.71 us
  transfers between devices with their start and end apart: 2, of which 1 were waited for; matrix products, arithmetic and copies ran while one was open for 0% of the time, Pallas kernels for 6%

profile of v20, /device:TPU:0, one launch (start us, length us, event | category | flops | bytes accessed | tf_op | source)
XLA Modules:
  0.0 27.9 jit_solution(5842977234845769071)
XLA Ops:
  0.0 1.4 %pack.1 = (bf16[128,128]{1,0:T(8,128)(2,1)}, bf16[272,256]{1,0:T(8,128)(2,1)S(1)}) custom-call(s32[1,256]{1,0:T(1,128)} %bitcast.13, s32[1,256]{1,0:T(1,128)} %bitcast.14, s32[1,256]{1,0:T(1,128)} %bitcast.15, s32[1,32]{1,0:T(1,128)} %bitcast.20, f32[1,256]{1,0:T(1,128)} %bitcast.16, f32[1,256]{1,0:T(1,128)} %bitcast.17, s32[1,256]{1,0:T(1,128)} %bitcast.18, ...), custom_call_target="tpu_custom_call" | custom-call | flops 1 | bytes 1 | tf_op jit(solution)/shard_map/pack/pallas_call | solution.py:287
  1.4 0.5 %collective-permute-start = (bf16[272,256]{1,0:T(8,128)(2,1)S(1)}, bf16[272,256]{1,0:T(8,128)(2,1)S(1)}, u32[]{:S(2)}, u32[]{:S(2)}) collective-permute-start(bf16[272,256]{1,0:T(8,128)(2,1)S(1)} %get-tuple-element.13.own_ref), channel_id=1, source_target_pairs={{0,1},{1,0},{2,3},{3,2},{4,5},{5,4},{6,7},{7,6},{8,9},{9,8},{10,11... | collective-permute-start | bytes 417800 | tf_op jit(solution)/shard_map/ppermute | solution.py:304
  1.9 7.0 %all-to-all-start = ((bf16[16,8,128]{2,1,0:T(8,128)(2,1)}), bf16[16,8,128]{2,1,0:T(8,128)(2,1)S(1)}, u32[]{:S(2)}, u32[]{:S(2)}) async-start(bf16[16,8,128]{2,1,0:T(8,128)(2,1)} %bitcast.8), calls=%async_computation | async-start | bytes 65536 | tf_op jit(solution)/shard_map/all_to_all | solution.py:305
  9.0 0.0 collective-permute-done.other_ref
  9.0 1.6 %prepare.1 = (bf16[256,512]{1,0:T(8,128)(2,1)S(1)}, s32[8,512]{1,0:T(8,128)S(1)}, bf16[256,512]{1,0:T(8,128)(2,1)S(1)}, bf16[256,1024]{1,0:T(8,128)(2,1)S(1)}, f32[4,256,512]{2,1,0:T(8,128)S(1)}) custom-call(f32[8,48]{1,0:T(8,128)} %irf_hbm.1, bf16[272,256]{1,0:T(8,128)(2,1)S(1)} %get-tuple-element.13.own_ref, ...), custom_call_target="tpu_custom_call" | custom-call | flops 1 | bytes 1 | tf_op jit(solution)/shard_map/prepare/pallas_call | solution.py:311
  10.7 5.0 %all-to-all-done = bf16[16,8,128]{2,1,0:T(8,128)(2,1)S(1)} async-done(((bf16[16,8,128]{2,1,0:T(8,128)(2,1)}), bf16[16,8,128]{2,1,0:T(8,128)(2,1)S(1)}, u32[]{:S(2)}, u32[]{:S(2)}) %all-to-all-start) | async-done | bytes 32800 | tf_op jit(solution)/shard_map/all_to_all | solution.py:305
  15.6 1.8 %route.1 = s16[256,256]{1,0:T(8,128)(2,1)S(1)} custom-call(bf16[128,128]{1,0:T(8,128)(2,1)S(1)} %bitcast.12, bf16[256,512]{1,0:T(8,128)(2,1)S(1)} %get-tuple-element.14.refs_1_, s32[8,512]{1,0:T(8,128)S(1)} %get-tuple-element.15.refs_2_, bf16[256,512]{1,0:T(8,128)(2,1)S(1)} %get-tuple-element.16.refs_3_, bf16[256,1024]{1,0:T(8,128)(2,1)S(1)} %get-tuple-element.17.refs_4_, ...), custom_call_target="tpu_custom_call" | custom-call | tf_op jit(solution)/shard_map/route/pallas_call | solution.py:327
  17.5 9.7 %all_to_all.10.parts_ref = s16[8,32,256]{2,1,0:T(8,128)(2,1)S(1)} all-to-all(s16[8,32,256]{2,1,0:T(8,128)(2,1)S(1)} %bitcast.11), channel_id=1, replica_groups={{0,2,4,6,8,10,12,14},{1,3,5,7,9,11,13,15},{16,18,20,22,24,26,28,30},{17..., dimensions={0} | all-to-all | bytes 262144 | tf_op jit(solution)/shard_map/all_to_all | solution.py:335
  27.2 0.7 %finish.1 = f32[32,256]{1,0:T(8,128)} custom-call(s16[8,32,256]{2,1,0:T(8,128)(2,1)S(1)} %all_to_all.10.parts_ref), custom_call_target="tpu_custom_call" | custom-call | tf_op jit(solution)/shard_map/finish/pallas_call | solution.py:343
Async XLA Ops:
  1.4 7.6 %collective-permute-start = (bf16[272,256]{1,0:T(8,128)(2,1)S(1)}, bf16[272,256]{1,0:T(8,128)(2,1)S(1)}, u32[]{:S(2)}, u32[]{:S(2)}) collective-permute-start(bf16[272,256]{1,0:T(8,128)(2,1)S(1)} %get-tuple-element.13.own_ref), channel_id=1, source_target_pairs={{0,1},{1,0},{2,3},{3,2},{4,5},{5,4},{6,7},{7,6},{8,9},{9,8},{10,11... | collective-permute-start | bytes 417800 | tf_op jit(solution)/shard_map/ppermute | solution.py:304
  1.9 13.7 %all-to-all-start = ((bf16[16,8,128]{2,1,0:T(8,128)(2,1)}), bf16[16,8,128]{2,1,0:T(8,128)(2,1)S(1)}, u32[]{:S(2)}, u32[]{:S(2)}) async-start(bf16[16,8,128]{2,1,0:T(8,128)(2,1)} %bitcast.8), calls=%async_computation | async-start | bytes 65536 | tf_op jit(solution)/shard_map/all_to_all | solution.py:305

commit v21 on v20

--- a/solution.py
+++ b/solution.py
@@ -141,22 +141,10 @@
             late_ref[:, (kind - early) * hours : (kind - early + 1) * hours] = matrix
 
 
-def respond(matrices, runoffs):
-    hours = matrices.shape[0]
-    half = hours // 2
-    count = matrices.shape[1] // hours
-
-    def halves(values, axis, first):
-        pieces = [
-            lax.slice_in_dim(values, j * hours + first, j * hours + first + half, axis=axis)
-            for j in range(count)
-        ]
-        return jnp.concatenate(pieces, axis=axis)
-
-    earlier = lax.dot_general(
-        halves(matrices, 1, half), halves(runoffs, 0, 0), NN, preferred_element_type=jnp.float32
-    )
-    later = lax.dot_general(matrices, runoffs, NN, preferred_element_type=jnp.float32)
+def respond(matrix, runoff):
+    half = matrix.shape[0] // 2
+    earlier = lax.dot_general(matrix[:, half:], runoff[:half], NN, preferred_element_type=jnp.float32)
+    later = lax.dot_general(matrix, runoff, NN, preferred_element_type=jnp.float32)
     return jnp.concatenate([earlier[:half] + earlier[half:], later[:half] + later[half:]], axis=0)
 
 
@@ -164,12 +152,15 @@
     meta_ref, runoff_ref, dest_ref, reach_marks_ref, late_ref, responses_ref, flow_ref, stack_ref, *, basin_rows
 ):
     early, hours, tiles = responses_ref.shape
-    late = late_ref.shape[1] // hours
     outlets = flow_ref.shape[0]
     owners = meta_ref.shape[0] // FIELDS
     core = lax.rem(lax.axis_index("tile"), CORES)
     dest = dest_ref[0:1]
 
+    runoff = runoff_ref[...]
+    late_responses = [
+        respond(late_ref[:, first : first + hours], runoff) for first in range(0, late_ref.shape[1], hours)
+    ]
     stack_ref[: owners * FIELDS] = meta_ref[...].astype(jnp.float32)
 
     def table(field):
@@ -218,17 +209,11 @@
         axis=0,
     )
 
-    runoff = runoff_ref[...]
-    by_kind = jnp.concatenate(
-        [
-            runoff * (kind == early + k).astype(jnp.float32).astype(jnp.bfloat16)
-            for k in range(late)
-        ],
-        axis=0,
-    )
-    routed = respond(late_ref[...], by_kind)
-    for k in range(early):
+    routed = responses_ref[0]
+    for k in range(1, early):
         routed = jnp.where(kind == k, responses_ref[k], routed)
+    for k, response in enumerate(late_responses, early):
+        routed = jnp.where(kind == k, response, routed)
     for step in (64, 32, 16, 8):
         routed = jnp.where((lag & step) != 0, later_rows(routed, step), routed)
     routed = turned(routed, lag & 7)

time: 28.2 us -> 28.6 us (1.014)
  Pallas kernels: 5.59 us -> 5.97 us
    pallas_call x1, Pallas kernels: 1.81 us -> 2.19 us  [per_device(): pl.pallas_call(lambda *refs: route_kernel(*refs, basin_rows=basin_rows),...]
where the time goes in v21:
time: 28.6 us; the launch traced here: 28.3 us
  blocking collectives  9.74 us (34%)
  starting transfers between devices  7.57 us (26%)
  Pallas kernels  5.97 us (21%)
  waiting for transfers between devices  4.97 us (17%)
    all_to_all x1, blocking collectives, per_device(): lax.all_to_all(flow.reshape(owners // CORES, basin_rows, hours), 'tile',...  9.74 us
    all_to_all x1, starting transfers between devices, per_device(): lax.all_to_all(meta.reshape(owners, FIELDS, LANES), 'tile', split_axis=0,...  7.05 us
    all_to_all x1, waiting for transfers between devices, per_device(): lax.all_to_all(meta.reshape(owners, FIELDS, LANES), 'tile', split_axis=0,...  4.96 us
    pallas_call x1, Pallas kernels, per_device(): pl.pallas_call(lambda *refs: route_kernel(*refs, basin_rows=basin_rows),...  2.19 us
    pallas_call x1, Pallas kernels, per_device(): pl.pallas_call(prepare_kernel, out_shape=(jax.ShapeDtypeStruct((hours, ch...  1.65 us
    pallas_call x1, Pallas kernels, per_device(): pl.pallas_call(lambda *refs: pack_kernel(*refs, basin_rows=basin_rows), o...  1.42 us
    pallas_call x1, Pallas kernels, per_device(): pl.pallas_call(finish_kernel, out_shape=jax.ShapeDtypeStruct((basin_rows,...  0.71 us
  transfers between devices with their start and end apart: 2, of which 1 were waited for; matrix products, arithmetic and copies ran while one was open for 0% of the time, Pallas kernels for 6%

profile of v21, /device:TPU:0, one launch (start us, length us, event | category | flops | bytes accessed | tf_op | source)
XLA Modules:
  0.0 28.3 jit_solution(6661249965685798969)
XLA Ops:
  0.0 1.4 %pack.1 = (bf16[128,128]{1,0:T(8,128)(2,1)}, bf16[272,256]{1,0:T(8,128)(2,1)S(1)}) custom-call(s32[1,256]{1,0:T(1,128)} %bitcast.13, s32[1,256]{1,0:T(1,128)} %bitcast.14, s32[1,256]{1,0:T(1,128)} %bitcast.15, s32[1,32]{1,0:T(1,128)} %bitcast.20, f32[1,256]{1,0:T(1,128)} %bitcast.16, f32[1,256]{1,0:T(1,128)} %bitcast.17, s32[1,256]{1,0:T(1,128)} %bitcast.18, ...), custom_call_target="tpu_custom_call" | custom-call | flops 1 | bytes 1 | tf_op jit(solution)/shard_map/pack/pallas_call | solution.py:272
  1.4 0.5 %collective-permute-start = (bf16[272,256]{1,0:T(8,128)(2,1)S(1)}, bf16[272,256]{1,0:T(8,128)(2,1)S(1)}, u32[]{:S(2)}, u32[]{:S(2)}) collective-permute-start(bf16[272,256]{1,0:T(8,128)(2,1)S(1)} %get-tuple-element.13.own_ref), channel_id=1, source_target_pairs={{0,1},{1,0},{2,3},{3,2},{4,5},{5,4},{6,7},{7,6},{8,9},{9,8},{10,11... | collective-permute-start | bytes 417800 | tf_op jit(solution)/shard_map/ppermute | solution.py:289
  1.9 7.0 %all-to-all-start = ((bf16[16,8,128]{2,1,0:T(8,128)(2,1)}), bf16[16,8,128]{2,1,0:T(8,128)(2,1)S(1)}, u32[]{:S(2)}, u32[]{:S(2)}) async-start(bf16[16,8,128]{2,1,0:T(8,128)(2,1)} %bitcast.8), calls=%async_computation | async-start | bytes 65536 | tf_op jit(solution)/shard_map/all_to_all | solution.py:290
  9.0 0.0 collective-permute-done.other_ref
  9.0 1.6 %prepare.1 = (bf16[256,512]{1,0:T(8,128)(2,1)S(1)}, s32[8,512]{1,0:T(8,128)S(1)}, bf16[256,512]{1,0:T(8,128)(2,1)S(1)}, bf16[256,1024]{1,0:T(8,128)(2,1)S(1)}, f32[4,256,512]{2,1,0:T(8,128)S(1)}) custom-call(f32[8,48]{1,0:T(8,128)} %irf_hbm.1, bf16[272,256]{1,0:T(8,128)(2,1)S(1)} %get-tuple-element.13.own_ref, ...), custom_call_target="tpu_custom_call" | custom-call | flops 1 | bytes 1 | tf_op jit(solution)/shard_map/prepare/pallas_call | solution.py:296
  10.7 5.0 %all-to-all-done = bf16[16,8,128]{2,1,0:T(8,128)(2,1)S(1)} async-done(((bf16[16,8,128]{2,1,0:T(8,128)(2,1)}), bf16[16,8,128]{2,1,0:T(8,128)(2,1)S(1)}, u32[]{:S(2)}, u32[]{:S(2)}) %all-to-all-start) | async-done | bytes 32800 | tf_op jit(solution)/shard_map/all_to_all | solution.py:290
  15.6 2.2 %route.1 = s16[256,256]{1,0:T(8,128)(2,1)S(1)} custom-call(bf16[128,128]{1,0:T(8,128)(2,1)S(1)} %bitcast.12, bf16[256,512]{1,0:T(8,128)(2,1)S(1)} %get-tuple-element.14.refs_1_, s32[8,512]{1,0:T(8,128)S(1)} %get-tuple-element.15.refs_2_, bf16[256,512]{1,0:T(8,128)(2,1)S(1)} %get-tuple-element.16.refs_3_, bf16[256,1024]{1,0:T(8,128)(2,1)S(1)} %get-tuple-element.17.refs_4_, ...), custom_call_target="tpu_custom_call" | custom-call | tf_op jit(solution)/shard_map/route/pallas_call | solution.py:312
  17.8 9.7 %all_to_all.10.parts_ref = s16[8,32,256]{2,1,0:T(8,128)(2,1)S(1)} all-to-all(s16[8,32,256]{2,1,0:T(8,128)(2,1)S(1)} %bitcast.11), channel_id=1, replica_groups={{0,2,4,6,8,10,12,14},{1,3,5,7,9,11,13,15},{16,18,20,22,24,26,28,30},{17..., dimensions={0} | all-to-all | bytes 262144 | tf_op jit(solution)/shard_map/all_to_all | solution.py:320
  27.6 0.7 %finish.1 = f32[32,256]{1,0:T(8,128)} custom-call(s16[8,32,256]{2,1,0:T(8,128)(2,1)S(1)} %all_to_all.10.parts_ref), custom_call_target="tpu_custom_call" | custom-call | tf_op jit(solution)/shard_map/finish/pallas_call | solution.py:328
Async XLA Ops:
  1.4 7.6 %collective-permute-start = (bf16[272,256]{1,0:T(8,128)(2,1)S(1)}, bf16[272,256]{1,0:T(8,128)(2,1)S(1)}, u32[]{:S(2)}, u32[]{:S(2)}) collective-permute-start(bf16[272,256]{1,0:T(8,128)(2,1)S(1)} %get-tuple-element.13.own_ref), channel_id=1, source_target_pairs={{0,1},{1,0},{2,3},{3,2},{4,5},{5,4},{6,7},{7,6},{8,9},{9,8},{10,11... | collective-permute-start | bytes 417800 | tf_op jit(solution)/shard_map/ppermute | solution.py:289
  1.9 13.7 %all-to-all-start = ((bf16[16,8,128]{2,1,0:T(8,128)(2,1)}), bf16[16,8,128]{2,1,0:T(8,128)(2,1)S(1)}, u32[]{:S(2)}, u32[]{:S(2)}) async-start(bf16[16,8,128]{2,1,0:T(8,128)(2,1)} %bitcast.8), calls=%async_computation | async-start | bytes 65536 | tf_op jit(solution)/shard_map/all_to_all | solution.py:290

commit v22 on v20

--- a/solution.py
+++ b/solution.py
@@ -227,14 +227,20 @@
         axis=0,
     )
     routed = respond(late_ref[...], by_kind)
-    for k in range(early):
-        routed = jnp.where(kind == k, responses_ref[k], routed)
-    for step in (64, 32, 16, 8):
-        routed = jnp.where((lag & step) != 0, later_rows(routed, step), routed)
-    routed = turned(routed, lag & 7)
+    highs, lows = [], []
+    for first in range(0, tiles, LANES):
+        lanes = slice(first, first + LANES)
+        column = routed[:, lanes]
+        for k in range(early):
+            column = jnp.where(kind[:, lanes] == k, responses_ref[k, :, lanes], column)
+        for step in (64, 32, 16, 8):
+            column = jnp.where((lag[:, lanes] & step) != 0, later_rows(column, step), column)
+        high, low = split(turned(column, lag[:, lanes] & 7))
+        highs.append(high)
+        lows.append(low)
     flows = lax.dot_general(
         jnp.concatenate([placements, placements], axis=1),
-        jnp.concatenate(split(routed), axis=1),
+        jnp.concatenate(highs + lows, axis=1),
         NT,
         preferred_element_type=jnp.float32,
     )

time: 28.2 us -> 28.2 us (level)
  no operation moved by 1% of the time
where the time goes in v22:
time: 28.2 us; the launch traced here: 27.9 us
  blocking collectives  9.74 us (35%)
  starting transfers between devices  7.57 us (27%)
  Pallas kernels  5.59 us (20%)
  waiting for transfers between devices  4.97 us (18%)
    all_to_all x1, blocking collectives, per_device(): lax.all_to_all(flow.reshape(owners // CORES, basin_rows, hours), 'tile',...  9.74 us
    all_to_all x1, starting transfers between devices, per_device(): lax.all_to_all(meta.reshape(owners, FIELDS, LANES), 'tile', split_axis=0,...  7.05 us
    all_to_all x1, waiting for transfers between devices, per_device(): lax.all_to_all(meta.reshape(owners, FIELDS, LANES), 'tile', split_axis=0,...  4.96 us
    pallas_call x1, Pallas kernels, per_device(): pl.pallas_call(lambda *refs: route_kernel(*refs, basin_rows=basin_rows),...  1.81 us
    pallas_call x1, Pallas kernels, per_device(): pl.pallas_call(prepare_kernel, out_shape=(jax.ShapeDtypeStruct((hours, ch...  1.65 us
    pallas_call x1, Pallas kernels, per_device(): pl.pallas_call(lambda *refs: pack_kernel(*refs, basin_rows=basin_rows), o...  1.42 us
    pallas_call x1, Pallas kernels, per_device(): pl.pallas_call(finish_kernel, out_shape=jax.ShapeDtypeStruct((basin_rows,...  0.71 us
  transfers between devices with their start and end apart: 2, of which 1 were waited for; matrix products, arithmetic and copies ran while one was open for 0% of the time, Pallas kernels for 6%

profile of v22, /device:TPU:0, one launch (start us, length us, event | category | flops | bytes accessed | tf_op | source)
XLA Modules:
  0.0 27.9 jit_solution(5842977234845769071)
XLA Ops:
  0.0 1.4 %pack.1 = (bf16[128,128]{1,0:T(8,128)(2,1)}, bf16[272,256]{1,0:T(8,128)(2,1)S(1)}) custom-call(s32[1,256]{1,0:T(1,128)} %bitcast.13, s32[1,256]{1,0:T(1,128)} %bitcast.14, s32[1,256]{1,0:T(1,128)} %bitcast.15, s32[1,32]{1,0:T(1,128)} %bitcast.20, f32[1,256]{1,0:T(1,128)} %bitcast.16, f32[1,256]{1,0:T(1,128)} %bitcast.17, s32[1,256]{1,0:T(1,128)} %bitcast.18, ...), custom_call_target="tpu_custom_call" | custom-call | flops 1 | bytes 1 | tf_op jit(solution)/shard_map/pack/pallas_call | solution.py:293
  1.4 0.5 %collective-permute-start = (bf16[272,256]{1,0:T(8,128)(2,1)S(1)}, bf16[272,256]{1,0:T(8,128)(2,1)S(1)}, u32[]{:S(2)}, u32[]{:S(2)}) collective-permute-start(bf16[272,256]{1,0:T(8,128)(2,1)S(1)} %get-tuple-element.13.own_ref), channel_id=1, source_target_pairs={{0,1},{1,0},{2,3},{3,2},{4,5},{5,4},{6,7},{7,6},{8,9},{9,8},{10,11... | collective-permute-start | bytes 417800 | tf_op jit(solution)/shard_map/ppermute | solution.py:310
  1.9 7.0 %all-to-all-start = ((bf16[16,8,128]{2,1,0:T(8,128)(2,1)}), bf16[16,8,128]{2,1,0:T(8,128)(2,1)S(1)}, u32[]{:S(2)}, u32[]{:S(2)}) async-start(bf16[16,8,128]{2,1,0:T(8,128)(2,1)} %bitcast.8), calls=%async_computation | async-start | bytes 65536 | tf_op jit(solution)/shard_map/all_to_all | solution.py:311
  9.0 0.0 collective-permute-done.other_ref
  9.0 1.6 %prepare.1 = (bf16[256,512]{1,0:T(8,128)(2,1)S(1)}, s32[8,512]{1,0:T(8,128)S(1)}, bf16[256,512]{1,0:T(8,128)(2,1)S(1)}, bf16[256,1024]{1,0:T(8,128)(2,1)S(1)}, f32[4,256,512]{2,1,0:T(8,128)S(1)}) custom-call(f32[8,48]{1,0:T(8,128)} %irf_hbm.1, bf16[272,256]{1,0:T(8,128)(2,1)S(1)} %get-tuple-element.13.own_ref, ...), custom_call_target="tpu_custom_call" | custom-call | flops 1 | bytes 1 | tf_op jit(solution)/shard_map/prepare/pallas_call | solution.py:317
  10.7 5.0 %all-to-all-done = bf16[16,8,128]{2,1,0:T(8,128)(2,1)S(1)} async-done(((bf16[16,8,128]{2,1,0:T(8,128)(2,1)}), bf16[16,8,128]{2,1,0:T(8,128)(2,1)S(1)}, u32[]{:S(2)}, u32[]{:S(2)}) %all-to-all-start) | async-done | bytes 32800 | tf_op jit(solution)/shard_map/all_to_all | solution.py:311
  15.6 1.8 %route.1 = s16[256,256]{1,0:T(8,128)(2,1)S(1)} custom-call(bf16[128,128]{1,0:T(8,128)(2,1)S(1)} %bitcast.12, bf16[256,512]{1,0:T(8,128)(2,1)S(1)} %get-tuple-element.14.refs_1_, s32[8,512]{1,0:T(8,128)S(1)} %get-tuple-element.15.refs_2_, bf16[256,512]{1,0:T(8,128)(2,1)S(1)} %get-tuple-element.16.refs_3_, bf16[256,1024]{1,0:T(8,128)(2,1)S(1)} %get-tuple-element.17.refs_4_, ...), custom_call_target="tpu_custom_call" | custom-call | tf_op jit(solution)/shard_map/route/pallas_call | solution.py:333
  17.5 9.7 %all_to_all.10.parts_ref = s16[8,32,256]{2,1,0:T(8,128)(2,1)S(1)} all-to-all(s16[8,32,256]{2,1,0:T(8,128)(2,1)S(1)} %bitcast.11), channel_id=1, replica_groups={{0,2,4,6,8,10,12,14},{1,3,5,7,9,11,13,15},{16,18,20,22,24,26,28,30},{17..., dimensions={0} | all-to-all | bytes 262144 | tf_op jit(solution)/shard_map/all_to_all | solution.py:341
  27.2 0.7 %finish.1 = f32[32,256]{1,0:T(8,128)} custom-call(s16[8,32,256]{2,1,0:T(8,128)(2,1)S(1)} %all_to_all.10.parts_ref), custom_call_target="tpu_custom_call" | custom-call | tf_op jit(solution)/shard_map/finish/pallas_call | solution.py:349
Async XLA Ops:
  1.4 7.6 %collective-permute-start = (bf16[272,256]{1,0:T(8,128)(2,1)S(1)}, bf16[272,256]{1,0:T(8,128)(2,1)S(1)}, u32[]{:S(2)}, u32[]{:S(2)}) collective-permute-start(bf16[272,256]{1,0:T(8,128)(2,1)S(1)} %get-tuple-element.13.own_ref), channel_id=1, source_target_pairs={{0,1},{1,0},{2,3},{3,2},{4,5},{5,4},{6,7},{7,6},{8,9},{9,8},{10,11... | collective-permute-start | bytes 417800 | tf_op jit(solution)/shard_map/ppermute | solution.py:310
  1.9 13.7 %all-to-all-start = ((bf16[16,8,128]{2,1,0:T(8,128)(2,1)}), bf16[16,8,128]{2,1,0:T(8,128)(2,1)S(1)}, u32[]{:S(2)}, u32[]{:S(2)}) async-start(bf16[16,8,128]{2,1,0:T(8,128)(2,1)} %bitcast.8), calls=%async_computation | async-start | bytes 65536 | tf_op jit(solution)/shard_map/all_to_all | solution.py:311

commit v23 on v20

--- a/solution.py
+++ b/solution.py
@@ -204,7 +204,7 @@
 
     def row_of(owner, local):
         mine = jnp.logical_and(owner >= 0, (owner & (CORES - 1)) == core)
-        return jnp.where(mine, (owner // CORES) * basin_rows + local, -1)
+        return jnp.where(mine, (owners // CORES - 1 - owner // CORES) * basin_rows + local, -1)
 
     placements = jnp.concatenate(
         [
@@ -337,7 +337,7 @@
         "tile",
         split_axis=0,
         concat_axis=0,
-        axis_index_groups=[list(range(core, owners, CORES)) for core in range(CORES)],
+        axis_index_groups=[list(range(core, owners, CORES))[::-1] for core in range(CORES)],
         tiled=True,
     )
     return pl.pallas_call(

time: 28.2 us -> 27.9 us (0.989)
  no operation moved by 1% of the time
where the time goes in v23:
time: 27.9 us; the launch traced here: 27.7 us
  blocking collectives  9.5 us (34%)
  starting transfers between devices  7.57 us (27%)
  Pallas kernels  5.59 us (20%)
  waiting for transfers between devices  4.97 us (18%)
    all_to_all x1, blocking collectives, per_device(): lax.all_to_all(flow.reshape(owners // CORES, basin_rows, hours), 'tile',...  9.5 us
    all_to_all x1, starting transfers between devices, per_device(): lax.all_to_all(meta.reshape(owners, FIELDS, LANES), 'tile', split_axis=0,...  7.05 us
    all_to_all x1, waiting for transfers between devices, per_device(): lax.all_to_all(meta.reshape(owners, FIELDS, LANES), 'tile', split_axis=0,...  4.96 us
    pallas_call x1, Pallas kernels, per_device(): pl.pallas_call(lambda *refs: route_kernel(*refs, basin_rows=basin_rows),...  1.81 us
    pallas_call x1, Pallas kernels, per_device(): pl.pallas_call(prepare_kernel, out_shape=(jax.ShapeDtypeStruct((hours, ch...  1.65 us
    pallas_call x1, Pallas kernels, per_device(): pl.pallas_call(lambda *refs: pack_kernel(*refs, basin_rows=basin_rows), o...  1.42 us
    pallas_call x1, Pallas kernels, per_device(): pl.pallas_call(finish_kernel, out_shape=jax.ShapeDtypeStruct((basin_rows,...  0.71 us
  transfers between devices with their start and end apart: 2, of which 1 were waited for; matrix products, arithmetic and copies ran while one was open for 0% of the time, Pallas kernels for 6%

profile of v23, /device:TPU:0, one launch (start us, length us, event | category | flops | bytes accessed | tf_op | source)
XLA Modules:
  0.0 27.7 jit_solution(12116521241070775681)
XLA Ops:
  0.0 1.4 %pack.1 = (bf16[128,128]{1,0:T(8,128)(2,1)}, bf16[272,256]{1,0:T(8,128)(2,1)S(1)}) custom-call(s32[1,256]{1,0:T(1,128)} %bitcast.13, s32[1,256]{1,0:T(1,128)} %bitcast.14, s32[1,256]{1,0:T(1,128)} %bitcast.15, s32[1,32]{1,0:T(1,128)} %bitcast.20, f32[1,256]{1,0:T(1,128)} %bitcast.16, f32[1,256]{1,0:T(1,128)} %bitcast.17, s32[1,256]{1,0:T(1,128)} %bitcast.18, ...), custom_call_target="tpu_custom_call" | custom-call | flops 1 | bytes 1 | tf_op jit(solution)/shard_map/pack/pallas_call | solution.py:287
  1.4 0.5 %collective-permute-start = (bf16[272,256]{1,0:T(8,128)(2,1)S(1)}, bf16[272,256]{1,0:T(8,128)(2,1)S(1)}, u32[]{:S(2)}, u32[]{:S(2)}) collective-permute-start(bf16[272,256]{1,0:T(8,128)(2,1)S(1)} %get-tuple-element.13.own_ref), channel_id=1, source_target_pairs={{0,1},{1,0},{2,3},{3,2},{4,5},{5,4},{6,7},{7,6},{8,9},{9,8},{10,11... | collective-permute-start | bytes 417800 | tf_op jit(solution)/shard_map/ppermute | solution.py:304
  1.9 7.0 %all-to-all-start = ((bf16[16,8,128]{2,1,0:T(8,128)(2,1)}), bf16[16,8,128]{2,1,0:T(8,128)(2,1)S(1)}, u32[]{:S(2)}, u32[]{:S(2)}) async-start(bf16[16,8,128]{2,1,0:T(8,128)(2,1)} %bitcast.8), calls=%async_computation | async-start | bytes 65536 | tf_op jit(solution)/shard_map/all_to_all | solution.py:305
  9.0 0.0 collective-permute-done.other_ref
  9.0 1.6 %prepare.1 = (bf16[256,512]{1,0:T(8,128)(2,1)S(1)}, s32[8,512]{1,0:T(8,128)S(1)}, bf16[256,512]{1,0:T(8,128)(2,1)S(1)}, bf16[256,1024]{1,0:T(8,128)(2,1)S(1)}, f32[4,256,512]{2,1,0:T(8,128)S(1)}) custom-call(f32[8,48]{1,0:T(8,128)} %irf_hbm.1, bf16[272,256]{1,0:T(8,128)(2,1)S(1)} %get-tuple-element.13.own_ref, ...), custom_call_target="tpu_custom_call" | custom-call | flops 1 | bytes 1 | tf_op jit(solution)/shard_map/prepare/pallas_call | solution.py:311
  10.7 5.0 %all-to-all-done = bf16[16,8,128]{2,1,0:T(8,128)(2,1)S(1)} async-done(((bf16[16,8,128]{2,1,0:T(8,128)(2,1)}), bf16[16,8,128]{2,1,0:T(8,128)(2,1)S(1)}, u32[]{:S(2)}, u32[]{:S(2)}) %all-to-all-start) | async-done | bytes 32800 | tf_op jit(solution)/shard_map/all_to_all | solution.py:305
  15.6 1.8 %route.1 = s16[256,256]{1,0:T(8,128)(2,1)S(1)} custom-call(bf16[128,128]{1,0:T(8,128)(2,1)S(1)} %bitcast.12, bf16[256,512]{1,0:T(8,128)(2,1)S(1)} %get-tuple-element.14.refs_1_, s32[8,512]{1,0:T(8,128)S(1)} %get-tuple-element.15.refs_2_, bf16[256,512]{1,0:T(8,128)(2,1)S(1)} %get-tuple-element.16.refs_3_, bf16[256,1024]{1,0:T(8,128)(2,1)S(1)} %get-tuple-element.17.refs_4_, ...), custom_call_target="tpu_custom_call" | custom-call | tf_op jit(solution)/shard_map/route/pallas_call | solution.py:327
  17.5 9.5 %all_to_all.10.parts_ref = s16[8,32,256]{2,1,0:T(8,128)(2,1)S(1)} all-to-all(s16[8,32,256]{2,1,0:T(8,128)(2,1)S(1)} %bitcast.11), channel_id=1, replica_groups={{14,12,10,8,6,4,2,0},{15,13,11,9,7,5,3,1},{30,28,26,24,22,20,18,16},{31..., dimensions={0} | all-to-all | bytes 262144 | tf_op jit(solution)/shard_map/all_to_all | solution.py:335
  27.0 0.7 %finish.1 = f32[32,256]{1,0:T(8,128)} custom-call(s16[8,32,256]{2,1,0:T(8,128)(2,1)S(1)} %all_to_all.10.parts_ref), custom_call_target="tpu_custom_call" | custom-call | tf_op jit(solution)/shard_map/finish/pallas_call | solution.py:343
Async XLA Ops:
  1.4 7.6 %collective-permute-start = (bf16[272,256]{1,0:T(8,128)(2,1)S(1)}, bf16[272,256]{1,0:T(8,128)(2,1)S(1)}, u32[]{:S(2)}, u32[]{:S(2)}) collective-permute-start(bf16[272,256]{1,0:T(8,128)(2,1)S(1)} %get-tuple-element.13.own_ref), channel_id=1, source_target_pairs={{0,1},{1,0},{2,3},{3,2},{4,5},{5,4},{6,7},{7,6},{8,9},{9,8},{10,11... | collective-permute-start | bytes 417800 | tf_op jit(solution)/shard_map/ppermute | solution.py:304
  1.9 13.7 %all-to-all-start = ((bf16[16,8,128]{2,1,0:T(8,128)(2,1)}), bf16[16,8,128]{2,1,0:T(8,128)(2,1)S(1)}, u32[]{:S(2)}, u32[]{:S(2)}) async-start(bf16[16,8,128]{2,1,0:T(8,128)(2,1)} %bitcast.8), calls=%async_computation | async-start | bytes 65536 | tf_op jit(solution)/shard_map/all_to_all | solution.py:305

commit v24 on v23

--- a/solution.py
+++ b/solution.py
@@ -204,7 +204,9 @@
 
     def row_of(owner, local):
         mine = jnp.logical_and(owner >= 0, (owner & (CORES - 1)) == core)
-        return jnp.where(mine, (owners // CORES - 1 - owner // CORES) * basin_rows + local, -1)
+        place = owner // CORES - 1
+        place = jnp.where(place < 0, place + owners // CORES, place)
+        return jnp.where(mine, place * basin_rows + local, -1)
 
     placements = jnp.concatenate(
         [
@@ -337,7 +339,9 @@
         "tile",
         split_axis=0,
         concat_axis=0,
-        axis_index_groups=[list(range(core, owners, CORES))[::-1] for core in range(CORES)],
+        axis_index_groups=[
+            [*range(CORES + core, owners, CORES), core] for core in range(CORES)
+        ],
         tiled=True,
     )
     return pl.pallas_call(

time: 27.9 us -> 27.4 us (0.982)
  blocking collectives: 9.5 us -> 8.98 us
    all_to_all x1, blocking collectives: 9.5 us -> 8.98 us  [per_device(): lax.all_to_all(flow.reshape(owners // CORES, basin_rows, hours), 'tile',...]
where the time goes in v24:
time: 27.4 us; the launch traced here: 27.2 us
  blocking collectives  8.98 us (33%)
  starting transfers between devices  7.57 us (28%)
  Pallas kernels  5.61 us (20%)
  waiting for transfers between devices  4.97 us (18%)
    all_to_all x1, blocking collectives, per_device(): lax.all_to_all(flow.reshape(owners // CORES, basin_rows, hours), 'tile',...  8.98 us
    all_to_all x1, starting transfers between devices, per_device(): lax.all_to_all(meta.reshape(owners, FIELDS, LANES), 'tile', split_axis=0,...  7.05 us
    all_to_all x1, waiting for transfers between devices, per_device(): lax.all_to_all(meta.reshape(owners, FIELDS, LANES), 'tile', split_axis=0,...  4.96 us
    pallas_call x1, Pallas kernels, per_device(): pl.pallas_call(lambda *refs: route_kernel(*refs, basin_rows=basin_rows),...  1.82 us
    pallas_call x1, Pallas kernels, per_device(): pl.pallas_call(prepare_kernel, out_shape=(jax.ShapeDtypeStruct((hours, ch...  1.65 us
    pallas_call x1, Pallas kernels, per_device(): pl.pallas_call(lambda *refs: pack_kernel(*refs, basin_rows=basin_rows), o...  1.42 us
    pallas_call x1, Pallas kernels, per_device(): pl.pallas_call(finish_kernel, out_shape=jax.ShapeDtypeStruct((basin_rows,...  0.71 us
  transfers between devices with their start and end apart: 2, of which 1 were waited for; matrix products, arithmetic and copies ran while one was open for 0% of the time, Pallas kernels for 6%

profile of v24, /device:TPU:0, one launch (start us, length us, event | category | flops | bytes accessed | tf_op | source)
XLA Modules:
  0.0 27.2 jit_solution(12982003933761400933)
XLA Ops:
  0.0 1.4 %pack.1 = (bf16[128,128]{1,0:T(8,128)(2,1)}, bf16[272,256]{1,0:T(8,128)(2,1)S(1)}) custom-call(s32[1,256]{1,0:T(1,128)} %bitcast.13, s32[1,256]{1,0:T(1,128)} %bitcast.14, s32[1,256]{1,0:T(1,128)} %bitcast.15, s32[1,32]{1,0:T(1,128)} %bitcast.20, f32[1,256]{1,0:T(1,128)} %bitcast.16, f32[1,256]{1,0:T(1,128)} %bitcast.17, s32[1,256]{1,0:T(1,128)} %bitcast.18, ...), custom_call_target="tpu_custom_call" | custom-call | flops 1 | bytes 1 | tf_op jit(solution)/shard_map/pack/pallas_call | solution.py:289
  1.4 0.5 %collective-permute-start = (bf16[272,256]{1,0:T(8,128)(2,1)S(1)}, bf16[272,256]{1,0:T(8,128)(2,1)S(1)}, u32[]{:S(2)}, u32[]{:S(2)}) collective-permute-start(bf16[272,256]{1,0:T(8,128)(2,1)S(1)} %get-tuple-element.13.own_ref), channel_id=1, source_target_pairs={{0,1},{1,0},{2,3},{3,2},{4,5},{5,4},{6,7},{7,6},{8,9},{9,8},{10,11... | collective-permute-start | bytes 417800 | tf_op jit(solution)/shard_map/ppermute | solution.py:306
  1.9 7.0 %all-to-all-start = ((bf16[16,8,128]{2,1,0:T(8,128)(2,1)}), bf16[16,8,128]{2,1,0:T(8,128)(2,1)S(1)}, u32[]{:S(2)}, u32[]{:S(2)}) async-start(bf16[16,8,128]{2,1,0:T(8,128)(2,1)} %bitcast.8), calls=%async_computation | async-start | bytes 65536 | tf_op jit(solution)/shard_map/all_to_all | solution.py:307
  9.0 0.0 collective-permute-done.other_ref
  9.0 1.6 %prepare.1 = (bf16[256,512]{1,0:T(8,128)(2,1)S(1)}, s32[8,512]{1,0:T(8,128)S(1)}, bf16[256,512]{1,0:T(8,128)(2,1)S(1)}, bf16[256,1024]{1,0:T(8,128)(2,1)S(1)}, f32[4,256,512]{2,1,0:T(8,128)S(1)}) custom-call(f32[8,48]{1,0:T(8,128)} %irf_hbm.1, bf16[272,256]{1,0:T(8,128)(2,1)S(1)} %get-tuple-element.13.own_ref, ...), custom_call_target="tpu_custom_call" | custom-call | flops 1 | bytes 1 | tf_op jit(solution)/shard_map/prepare/pallas_call | solution.py:313
  10.7 5.0 %all-to-all-done = bf16[16,8,128]{2,1,0:T(8,128)(2,1)S(1)} async-done(((bf16[16,8,128]{2,1,0:T(8,128)(2,1)}), bf16[16,8,128]{2,1,0:T(8,128)(2,1)S(1)}, u32[]{:S(2)}, u32[]{:S(2)}) %all-to-all-start) | async-done | bytes 32800 | tf_op jit(solution)/shard_map/all_to_all | solution.py:307
  15.6 1.8 %route.1 = s16[256,256]{1,0:T(8,128)(2,1)S(1)} custom-call(bf16[128,128]{1,0:T(8,128)(2,1)S(1)} %bitcast.12, bf16[256,512]{1,0:T(8,128)(2,1)S(1)} %get-tuple-element.14.refs_1_, s32[8,512]{1,0:T(8,128)S(1)} %get-tuple-element.15.refs_2_, bf16[256,512]{1,0:T(8,128)(2,1)S(1)} %get-tuple-element.16.refs_3_, bf16[256,1024]{1,0:T(8,128)(2,1)S(1)} %get-tuple-element.17.refs_4_, ...), custom_call_target="tpu_custom_call" | custom-call | tf_op jit(solution)/shard_map/route/pallas_call | solution.py:329
  17.5 9.0 %all_to_all.10.parts_ref = s16[8,32,256]{2,1,0:T(8,128)(2,1)S(1)} all-to-all(s16[8,32,256]{2,1,0:T(8,128)(2,1)S(1)} %bitcast.11), channel_id=1, replica_groups={{2,4,6,8,10,12,14,0},{3,5,7,9,11,13,15,1},{18,20,22,24,26,28,30,16},{19..., dimensions={0} | all-to-all | bytes 262144 | tf_op jit(solution)/shard_map/all_to_all | solution.py:337
  26.4 0.7 %finish.1 = f32[32,256]{1,0:T(8,128)} custom-call(s16[8,32,256]{2,1,0:T(8,128)(2,1)S(1)} %all_to_all.10.parts_ref), custom_call_target="tpu_custom_call" | custom-call | tf_op jit(solution)/shard_map/finish/pallas_call | solution.py:347
Async XLA Ops:
  1.4 7.6 %collective-permute-start = (bf16[272,256]{1,0:T(8,128)(2,1)S(1)}, bf16[272,256]{1,0:T(8,128)(2,1)S(1)}, u32[]{:S(2)}, u32[]{:S(2)}) collective-permute-start(bf16[272,256]{1,0:T(8,128)(2,1)S(1)} %get-tuple-element.13.own_ref), channel_id=1, source_target_pairs={{0,1},{1,0},{2,3},{3,2},{4,5},{5,4},{6,7},{7,6},{8,9},{9,8},{10,11... | collective-permute-start | bytes 417800 | tf_op jit(solution)/shard_map/ppermute | solution.py:306
  1.9 13.7 %all-to-all-start = ((bf16[16,8,128]{2,1,0:T(8,128)(2,1)}), bf16[16,8,128]{2,1,0:T(8,128)(2,1)S(1)}, u32[]{:S(2)}, u32[]{:S(2)}) async-start(bf16[16,8,128]{2,1,0:T(8,128)(2,1)} %bitcast.8), calls=%async_computation | async-start | bytes 65536 | tf_op jit(solution)/shard_map/all_to_all | solution.py:307

commit v25 on v24

--- a/solution.py
+++ b/solution.py
@@ -176,7 +176,8 @@
         return stack_ref[pl.ds(field, owners, stride=FIELDS), :].astype(jnp.bfloat16)
 
     def picked(values, owner):
-        chosen = iota((owners, tiles), 0) == owner
+        place = jnp.where(owner < 0, owners, jnp.where(owner < CORES, owner + owners, owner) - CORES)
+        chosen = iota((owners, tiles), 0) == place
         return jnp.sum(jnp.where(chosen, values, 0.0), axis=0, keepdims=True).astype(jnp.int32)
 
     spans = (FIELDS - 2) // 3
@@ -305,7 +306,12 @@
     )(*numbers, in_hbm(rain, rain.shape))
     other = lax.ppermute(own, "tile", [(i, i ^ 1) for i in range(owners)])
     meta = lax.all_to_all(
-        meta.reshape(owners, FIELDS, LANES), "tile", split_axis=0, concat_axis=0, tiled=True
+        meta.reshape(owners, FIELDS, LANES),
+        "tile",
+        split_axis=0,
+        concat_axis=0,
+        axis_index_groups=[[*range(CORES, owners), *range(CORES)]],
+        tiled=True,
     ).reshape(-1, LANES)
 
     chip_tiles = CORES * tile_rows

time: 27.4 us -> 27.2 us (level)
  waiting for transfers between devices: 4.97 us -> 3.61 us
  blocking collectives: 8.98 us -> 9.72 us
  starting transfers between devices: 7.57 us -> 8.04 us
    all_to_all x1, waiting for transfers between devices: 4.96 us -> 3.61 us  [per_device(): lax.all_to_all(meta.reshape(owners, FIELDS, LANES), 'tile', split_axis=0,...]
    all_to_all x1, blocking collectives: 8.98 us -> 9.72 us  [per_device(): lax.all_to_all(flow.reshape(owners // CORES, basin_rows, hours), 'tile',...]
    all_to_all x1, starting transfers between devices: 7.05 us -> 7.53 us  [per_device(): lax.all_to_all(meta.reshape(owners, FIELDS, LANES), 'tile', split_axis=0,...]
where the time goes in v25:
time: 27.2 us; the launch traced here: 27 us
  blocking collectives  9.72 us (36%)
  starting transfers between devices  8.04 us (30%)
  Pallas kernels  5.56 us (20%)
  waiting for transfers between devices  3.61 us (13%)
    all_to_all x1, blocking collectives, per_device(): lax.all_to_all(flow.reshape(owners // CORES, basin_rows, hours), 'tile',...  9.72 us
    all_to_all x1, starting transfers between devices, per_device(): lax.all_to_all(meta.reshape(owners, FIELDS, LANES), 'tile', split_axis=0,...  7.53 us
    all_to_all x1, waiting for transfers between devices, per_device(): lax.all_to_all(meta.reshape(owners, FIELDS, LANES), 'tile', split_axis=0,...  3.61 us
    pallas_call x1, Pallas kernels, per_device(): pl.pallas_call(lambda *refs: route_kernel(*refs, basin_rows=basin_rows),...  1.79 us
    pallas_call x1, Pallas kernels, per_device(): pl.pallas_call(prepare_kernel, out_shape=(jax.ShapeDtypeStruct((hours, ch...  1.64 us
    pallas_call x1, Pallas kernels, per_device(): pl.pallas_call(lambda *refs: pack_kernel(*refs, basin_rows=basin_rows), o...  1.42 us
    pallas_call x1, Pallas kernels, per_device(): pl.pallas_call(finish_kernel, out_shape=jax.ShapeDtypeStruct((basin_rows,...  0.71 us
  transfers between devices with their start and end apart: 2, of which 1 were waited for; matrix products, arithmetic and copies ran while one was open for 0% of the time, Pallas kernels for 6%

profile of v25, /device:TPU:0, one launch (start us, length us, event | category | flops | bytes accessed | tf_op | source)
XLA Modules:
  0.0 27.0 jit_solution(16001667623021064587)
XLA Ops:
  0.0 1.4 %pack.1 = (bf16[128,128]{1,0:T(8,128)(2,1)}, bf16[272,256]{1,0:T(8,128)(2,1)S(1)}) custom-call(s32[1,256]{1,0:T(1,128)} %bitcast.13, s32[1,256]{1,0:T(1,128)} %bitcast.14, s32[1,256]{1,0:T(1,128)} %bitcast.15, s32[1,32]{1,0:T(1,128)} %bitcast.20, f32[1,256]{1,0:T(1,128)} %bitcast.16, f32[1,256]{1,0:T(1,128)} %bitcast.17, s32[1,256]{1,0:T(1,128)} %bitcast.18, ...), custom_call_target="tpu_custom_call" | custom-call | flops 1 | bytes 1 | tf_op jit(solution)/shard_map/pack/pallas_call | solution.py:290
  1.4 0.5 %collective-permute-start = (bf16[272,256]{1,0:T(8,128)(2,1)S(1)}, bf16[272,256]{1,0:T(8,128)(2,1)S(1)}, u32[]{:S(2)}, u32[]{:S(2)}) collective-permute-start(bf16[272,256]{1,0:T(8,128)(2,1)S(1)} %get-tuple-element.13.own_ref), channel_id=1, source_target_pairs={{0,1},{1,0},{2,3},{3,2},{4,5},{5,4},{6,7},{7,6},{8,9},{9,8},{10,11... | collective-permute-start | bytes 417800 | tf_op jit(solution)/shard_map/ppermute | solution.py:307
  1.9 7.5 %all-to-all-start = ((bf16[16,8,128]{2,1,0:T(8,128)(2,1)}), bf16[16,8,128]{2,1,0:T(8,128)(2,1)S(1)}, u32[]{:S(2)}, u32[]{:S(2)}) async-start(bf16[16,8,128]{2,1,0:T(8,128)(2,1)} %bitcast.8), calls=%async_computation | async-start | bytes 65536 | tf_op jit(solution)/shard_map/all_to_all | solution.py:308
  9.5 0.0 collective-permute-done.other_ref
  9.5 1.6 %prepare.1 = (bf16[256,512]{1,0:T(8,128)(2,1)S(1)}, s32[8,512]{1,0:T(8,128)S(1)}, bf16[256,512]{1,0:T(8,128)(2,1)S(1)}, bf16[256,1024]{1,0:T(8,128)(2,1)S(1)}, f32[4,256,512]{2,1,0:T(8,128)S(1)}) custom-call(f32[8,48]{1,0:T(8,128)} %irf_hbm.1, bf16[272,256]{1,0:T(8,128)(2,1)S(1)} %get-tuple-element.13.own_ref, ...), custom_call_target="tpu_custom_call" | custom-call | flops 1 | bytes 1 | tf_op jit(solution)/shard_map/prepare/pallas_call | solution.py:319
  11.1 3.6 %all-to-all-done = bf16[16,8,128]{2,1,0:T(8,128)(2,1)S(1)} async-done(((bf16[16,8,128]{2,1,0:T(8,128)(2,1)}), bf16[16,8,128]{2,1,0:T(8,128)(2,1)S(1)}, u32[]{:S(2)}, u32[]{:S(2)}) %all-to-all-start) | async-done | bytes 32800 | tf_op jit(solution)/shard_map/all_to_all | solution.py:308
  14.7 1.8 %route.1 = s16[256,256]{1,0:T(8,128)(2,1)S(1)} custom-call(bf16[128,128]{1,0:T(8,128)(2,1)S(1)} %bitcast.12, bf16[256,512]{1,0:T(8,128)(2,1)S(1)} %get-tuple-element.14.refs_1_, s32[8,512]{1,0:T(8,128)S(1)} %get-tuple-element.15.refs_2_, bf16[256,512]{1,0:T(8,128)(2,1)S(1)} %get-tuple-element.16.refs_3_, bf16[256,1024]{1,0:T(8,128)(2,1)S(1)} %get-tuple-element.17.refs_4_, ...), custom_call_target="tpu_custom_call" | custom-call | tf_op jit(solution)/shard_map/route/pallas_call | solution.py:335
  16.5 9.7 %all_to_all.10.parts_ref = s16[8,32,256]{2,1,0:T(8,128)(2,1)S(1)} all-to-all(s16[8,32,256]{2,1,0:T(8,128)(2,1)S(1)} %bitcast.11), channel_id=1, replica_groups={{2,4,6,8,10,12,14,0},{3,5,7,9,11,13,15,1},{18,20,22,24,26,28,30,16},{19..., dimensions={0} | all-to-all | bytes 262144 | tf_op jit(solution)/shard_map/all_to_all | solution.py:343
  26.3 0.7 %finish.1 = f32[32,256]{1,0:T(8,128)} custom-call(s16[8,32,256]{2,1,0:T(8,128)(2,1)S(1)} %all_to_all.10.parts_ref), custom_call_target="tpu_custom_call" | custom-call | tf_op jit(solution)/shard_map/finish/pallas_call | solution.py:353
Async XLA Ops:
  1.4 8.0 %collective-permute-start = (bf16[272,256]{1,0:T(8,128)(2,1)S(1)}, bf16[272,256]{1,0:T(8,128)(2,1)S(1)}, u32[]{:S(2)}, u32[]{:S(2)}) collective-permute-start(bf16[272,256]{1,0:T(8,128)(2,1)S(1)} %get-tuple-element.13.own_ref), channel_id=1, source_target_pairs={{0,1},{1,0},{2,3},{3,2},{4,5},{5,4},{6,7},{7,6},{8,9},{9,8},{10,11... | collective-permute-start | bytes 417800 | tf_op jit(solution)/shard_map/ppermute | solution.py:307
  1.9 12.8 %all-to-all-start = ((bf16[16,8,128]{2,1,0:T(8,128)(2,1)}), bf16[16,8,128]{2,1,0:T(8,128)(2,1)S(1)}, u32[]{:S(2)}, u32[]{:S(2)}) async-start(bf16[16,8,128]{2,1,0:T(8,128)(2,1)} %bitcast.8), calls=%async_computation | async-start | bytes 65536 | tf_op jit(solution)/shard_map/all_to_all | solution.py:308

commit v26 on v25

--- a/solution.py
+++ b/solution.py
@@ -176,8 +176,7 @@
         return stack_ref[pl.ds(field, owners, stride=FIELDS), :].astype(jnp.bfloat16)
 
     def picked(values, owner):
-        place = jnp.where(owner < 0, owners, jnp.where(owner < CORES, owner + owners, owner) - CORES)
-        chosen = iota((owners, tiles), 0) == place
+        chosen = iota((owners, tiles), 0) == owners - 1 - owner
         return jnp.sum(jnp.where(chosen, values, 0.0), axis=0, keepdims=True).astype(jnp.int32)
 
     spans = (FIELDS - 2) // 3
@@ -310,7 +309,7 @@
         "tile",
         split_axis=0,
         concat_axis=0,
-        axis_index_groups=[[*range(CORES, owners), *range(CORES)]],
+        axis_index_groups=[[*range(owners)][::-1]],
         tiled=True,
     ).reshape(-1, LANES)
 

time: 27.2 us -> 28.1 us (1.033)
  waiting for transfers between devices: 3.61 us -> 0.84 us
  blocking collectives: 9.72 us -> 11.8 us
  starting transfers between devices: 8.04 us -> 9.59 us
    all_to_all x1, waiting for transfers between devices: 3.61 us -> 0.84 us  [per_device(): lax.all_to_all(meta.reshape(owners, FIELDS, LANES), 'tile', split_axis=0,...]
    all_to_all x1, blocking collectives: 9.72 us -> 11.8 us  [per_device(): lax.all_to_all(flow.reshape(owners // CORES, basin_rows, hours), 'tile',...]
    all_to_all x1, starting transfers between devices: 7.53 us -> 9.07 us  [per_device(): lax.all_to_all(meta.reshape(owners, FIELDS, LANES), 'tile', split_axis=0,...]
where the time goes in v26:
time: 28.1 us; the launch traced here: 27.8 us
  blocking collectives  11.8 us (42%)
  starting transfers between devices  9.59 us (34%)
  Pallas kernels  5.59 us (20%)
  waiting for transfers between devices  0.84 us (3%)
    all_to_all x1, blocking collectives, per_device(): lax.all_to_all(flow.reshape(owners // CORES, basin_rows, hours), 'tile',...  11.8 us
    all_to_all x1, starting transfers between devices, per_device(): lax.all_to_all(meta.reshape(owners, FIELDS, LANES), 'tile', split_axis=0,...  9.07 us
    pallas_call x1, Pallas kernels, per_device(): pl.pallas_call(lambda *refs: route_kernel(*refs, basin_rows=basin_rows),...  1.82 us
    pallas_call x1, Pallas kernels, per_device(): pl.pallas_call(prepare_kernel, out_shape=(jax.ShapeDtypeStruct((hours, ch...  1.64 us
    pallas_call x1, Pallas kernels, per_device(): pl.pallas_call(lambda *refs: pack_kernel(*refs, basin_rows=basin_rows), o...  1.42 us
    all_to_all x1, waiting for transfers between devices, per_device(): lax.all_to_all(meta.reshape(owners, FIELDS, LANES), 'tile', split_axis=0,...  0.84 us
    pallas_call x1, Pallas kernels, per_device(): pl.pallas_call(finish_kernel, out_shape=jax.ShapeDtypeStruct((basin_rows,...  0.71 us
  transfers between devices with their start and end apart: 2, of which 1 were waited for; matrix products, arithmetic and copies ran while one was open for 0% of the time, Pallas kernels for 6%

profile of v26, /device:TPU:0, one launch (start us, length us, event | category | flops | bytes accessed | tf_op | source)
XLA Modules:
  0.0 27.8 jit_solution(17087034143665745661)
XLA Ops:
  0.0 1.4 %pack.1 = (bf16[128,128]{1,0:T(8,128)(2,1)}, bf16[272,256]{1,0:T(8,128)(2,1)S(1)}) custom-call(s32[1,256]{1,0:T(1,128)} %bitcast.13, s32[1,256]{1,0:T(1,128)} %bitcast.14, s32[1,256]{1,0:T(1,128)} %bitcast.15, s32[1,32]{1,0:T(1,128)} %bitcast.20, f32[1,256]{1,0:T(1,128)} %bitcast.16, f32[1,256]{1,0:T(1,128)} %bitcast.17, s32[1,256]{1,0:T(1,128)} %bitcast.18, ...), custom_call_target="tpu_custom_call" | custom-call | flops 1 | bytes 1 | tf_op jit(solution)/shard_map/pack/pallas_call | solution.py:289
  1.4 0.5 %collective-permute-start = (bf16[272,256]{1,0:T(8,128)(2,1)S(1)}, bf16[272,256]{1,0:T(8,128)(2,1)S(1)}, u32[]{:S(2)}, u32[]{:S(2)}) collective-permute-start(bf16[272,256]{1,0:T(8,128)(2,1)S(1)} %get-tuple-element.13.own_ref), channel_id=1, source_target_pairs={{0,1},{1,0},{2,3},{3,2},{4,5},{5,4},{6,7},{7,6},{8,9},{9,8},{10,11... | collective-permute-start | bytes 417800 | tf_op jit(solution)/shard_map/ppermute | solution.py:306
  1.9 9.1 %all-to-all-start = ((bf16[16,8,128]{2,1,0:T(8,128)(2,1)}), bf16[16,8,128]{2,1,0:T(8,128)(2,1)S(1)}, u32[]{:S(2)}, u32[]{:S(2)}) async-start(bf16[16,8,128]{2,1,0:T(8,128)(2,1)} %bitcast.8), calls=%async_computation | async-start | bytes 65536 | tf_op jit(solution)/shard_map/all_to_all | solution.py:307
  11.0 0.0 collective-permute-done.other_ref
  11.0 1.6 %prepare.1 = (bf16[256,512]{1,0:T(8,128)(2,1)S(1)}, s32[8,512]{1,0:T(8,128)S(1)}, bf16[256,512]{1,0:T(8,128)(2,1)S(1)}, bf16[256,1024]{1,0:T(8,128)(2,1)S(1)}, f32[4,256,512]{2,1,0:T(8,128)S(1)}) custom-call(f32[8,48]{1,0:T(8,128)} %irf_hbm.1, bf16[272,256]{1,0:T(8,128)(2,1)S(1)} %get-tuple-element.13.own_ref, ...), custom_call_target="tpu_custom_call" | custom-call | flops 1 | bytes 1 | tf_op jit(solution)/shard_map/prepare/pallas_call | solution.py:318
  12.7 0.8 %all-to-all-done = bf16[16,8,128]{2,1,0:T(8,128)(2,1)S(1)} async-done(((bf16[16,8,128]{2,1,0:T(8,128)(2,1)}), bf16[16,8,128]{2,1,0:T(8,128)(2,1)S(1)}, u32[]{:S(2)}, u32[]{:S(2)}) %all-to-all-start) | async-done | bytes 32800 | tf_op jit(solution)/shard_map/all_to_all | solution.py:307
  13.5 1.8 %route.1 = s16[256,256]{1,0:T(8,128)(2,1)S(1)} custom-call(bf16[128,128]{1,0:T(8,128)(2,1)S(1)} %bitcast.12, bf16[256,512]{1,0:T(8,128)(2,1)S(1)} %get-tuple-element.14.refs_1_, s32[8,512]{1,0:T(8,128)S(1)} %get-tuple-element.15.refs_2_, bf16[256,512]{1,0:T(8,128)(2,1)S(1)} %get-tuple-element.16.refs_3_, bf16[256,1024]{1,0:T(8,128)(2,1)S(1)} %get-tuple-element.17.refs_4_, ...), custom_call_target="tpu_custom_call" | custom-call | tf_op jit(solution)/shard_map/route/pallas_call | solution.py:334
  15.3 11.8 %all_to_all.10.parts_ref = s16[8,32,256]{2,1,0:T(8,128)(2,1)S(1)} all-to-all(s16[8,32,256]{2,1,0:T(8,128)(2,1)S(1)} %bitcast.11), channel_id=1, replica_groups={{2,4,6,8,10,12,14,0},{3,5,7,9,11,13,15,1},{18,20,22,24,26,28,30,16},{19..., dimensions={0} | all-to-all | bytes 262144 | tf_op jit(solution)/shard_map/all_to_all | solution.py:342
  27.1 0.7 %finish.1 = f32[32,256]{1,0:T(8,128)} custom-call(s16[8,32,256]{2,1,0:T(8,128)(2,1)S(1)} %all_to_all.10.parts_ref), custom_call_target="tpu_custom_call" | custom-call | tf_op jit(solution)/shard_map/finish/pallas_call | solution.py:352
Async XLA Ops:
  1.4 9.6 %collective-permute-start = (bf16[272,256]{1,0:T(8,128)(2,1)S(1)}, bf16[272,256]{1,0:T(8,128)(2,1)S(1)}, u32[]{:S(2)}, u32[]{:S(2)}) collective-permute-start(bf16[272,256]{1,0:T(8,128)(2,1)S(1)} %get-tuple-element.13.own_ref), channel_id=1, source_target_pairs={{0,1},{1,0},{2,3},{3,2},{4,5},{5,4},{6,7},{7,6},{8,9},{9,8},{10,11... | collective-permute-start | bytes 417800 | tf_op jit(solution)/shard_map/ppermute | solution.py:306
  1.9 11.6 %all-to-all-start = ((bf16[16,8,128]{2,1,0:T(8,128)(2,1)}), bf16[16,8,128]{2,1,0:T(8,128)(2,1)S(1)}, u32[]{:S(2)}, u32[]{:S(2)}) async-start(bf16[16,8,128]{2,1,0:T(8,128)(2,1)} %bitcast.8), calls=%async_computation | async-start | bytes 65536 | tf_op jit(solution)/shard_map/all_to_all | solution.py:307

commit v27 on v25

--- a/solution.py
+++ b/solution.py
@@ -36,6 +36,11 @@
 
 def one_hot(row, count):
     return (iota((count, row.shape[1]), 0) == row).astype(jnp.float32).astype(jnp.bfloat16)
+
+
+def group_of(owner, owners):
+    upper = (owner + owners // 2) // owners
+    return (owner + upper) % CORES
 
 
 def later_rows(values, hours):
@@ -167,7 +172,7 @@
     late = late_ref.shape[1] // hours
     outlets = flow_ref.shape[0]
     owners = meta_ref.shape[0] // FIELDS
-    core = lax.rem(lax.axis_index("tile"), CORES)
+    side = group_of(lax.axis_index("tile"), owners)
     dest = dest_ref[0:1]
 
     stack_ref[: owners * FIELDS] = meta_ref[...].astype(jnp.float32)
@@ -204,7 +209,7 @@
     second_owner, second_local = parent_of(parent_owner, parent_local)
 
     def row_of(owner, local):
-        mine = jnp.logical_and(owner >= 0, (owner & (CORES - 1)) == core)
+        mine = jnp.logical_and(owner >= 0, group_of(owner, owners) == side)
         place = owner // CORES - 1
         place = jnp.where(place < 0, place + owners // CORES, place)
         return jnp.where(mine, place * basin_rows + local, -1)
@@ -346,7 +351,8 @@
         split_axis=0,
         concat_axis=0,
         axis_index_groups=[
-            [*range(CORES + core, owners, CORES), core] for core in range(CORES)
+            [owner for owner in (*range(CORES, owners), *range(CORES)) if group_of(owner, owners) == side]
+            for side in range(CORES)
         ],
         tiled=True,
     )

time: 27.2 us -> 27.1 us (level)
  no operation moved by 1% of the time
where the time goes in v27:
time: 27.1 us; the launch traced here: 26.8 us
  blocking collectives  9.53 us (35%)
  starting transfers between devices  8.04 us (30%)
  Pallas kernels  5.57 us (21%)
  waiting for transfers between devices  3.61 us (13%)
    all_to_all x1, blocking collectives, per_device(): lax.all_to_all(flow.reshape(owners // CORES, basin_rows, hours), 'tile',...  9.53 us
    all_to_all x1, starting transfers between devices, per_device(): lax.all_to_all(meta.reshape(owners, FIELDS, LANES), 'tile', split_axis=0,...  7.53 us
    all_to_all x1, waiting for transfers between devices, per_device(): lax.all_to_all(meta.reshape(owners, FIELDS, LANES), 'tile', split_axis=0,...  3.61 us
    pallas_call x1, Pallas kernels, per_device(): pl.pallas_call(lambda *refs: route_kernel(*refs, basin_rows=basin_rows),...  1.8 us
    pallas_call x1, Pallas kernels, per_device(): pl.pallas_call(prepare_kernel, out_shape=(jax.ShapeDtypeStruct((hours, ch...  1.64 us
    pallas_call x1, Pallas kernels, per_device(): pl.pallas_call(lambda *refs: pack_kernel(*refs, basin_rows=basin_rows), o...  1.42 us
    pallas_call x1, Pallas kernels, per_device(): pl.pallas_call(finish_kernel, out_shape=jax.ShapeDtypeStruct((basin_rows,...  0.71 us
  transfers between devices with their start and end apart: 2, of which 1 were waited for; matrix products, arithmetic and copies ran while one was open for 0% of the time, Pallas kernels for 6%

profile of v27, /device:TPU:0, one launch (start us, length us, event | category | flops | bytes accessed | tf_op | source)
XLA Modules:
  0.0 26.8 jit_solution(3813812597348124706)
XLA Ops:
  0.0 1.4 %pack.1 = (bf16[128,128]{1,0:T(8,128)(2,1)}, bf16[272,256]{1,0:T(8,128)(2,1)S(1)}) custom-call(s32[1,256]{1,0:T(1,128)} %bitcast.13, s32[1,256]{1,0:T(1,128)} %bitcast.14, s32[1,256]{1,0:T(1,128)} %bitcast.15, s32[1,32]{1,0:T(1,128)} %bitcast.20, f32[1,256]{1,0:T(1,128)} %bitcast.16, f32[1,256]{1,0:T(1,128)} %bitcast.17, s32[1,256]{1,0:T(1,128)} %bitcast.18, ...), custom_call_target="tpu_custom_call" | custom-call | flops 1 | bytes 1 | tf_op jit(solution)/shard_map/pack/pallas_call | solution.py:295
  1.4 0.5 %collective-permute-start = (bf16[272,256]{1,0:T(8,128)(2,1)S(1)}, bf16[272,256]{1,0:T(8,128)(2,1)S(1)}, u32[]{:S(2)}, u32[]{:S(2)}) collective-permute-start(bf16[272,256]{1,0:T(8,128)(2,1)S(1)} %get-tuple-element.13.own_ref), channel_id=1, source_target_pairs={{0,1},{1,0},{2,3},{3,2},{4,5},{5,4},{6,7},{7,6},{8,9},{9,8},{10,11... | collective-permute-start | bytes 417800 | tf_op jit(solution)/shard_map/ppermute | solution.py:312
  1.9 7.5 %all-to-all-start = ((bf16[16,8,128]{2,1,0:T(8,128)(2,1)}), bf16[16,8,128]{2,1,0:T(8,128)(2,1)S(1)}, u32[]{:S(2)}, u32[]{:S(2)}) async-start(bf16[16,8,128]{2,1,0:T(8,128)(2,1)} %bitcast.8), calls=%async_computation | async-start | bytes 65536 | tf_op jit(solution)/shard_map/all_to_all | solution.py:313
  9.5 0.0 collective-permute-done.other_ref
  9.5 1.6 %prepare.1 = (bf16[256,512]{1,0:T(8,128)(2,1)S(1)}, s32[8,512]{1,0:T(8,128)S(1)}, bf16[256,512]{1,0:T(8,128)(2,1)S(1)}, bf16[256,1024]{1,0:T(8,128)(2,1)S(1)}, f32[4,256,512]{2,1,0:T(8,128)S(1)}) custom-call(f32[8,48]{1,0:T(8,128)} %irf_hbm.1, bf16[272,256]{1,0:T(8,128)(2,1)S(1)} %get-tuple-element.13.own_ref, ...), custom_call_target="tpu_custom_call" | custom-call | flops 1 | bytes 1 | tf_op jit(solution)/shard_map/prepare/pallas_call | solution.py:324
  11.1 3.6 %all-to-all-done = bf16[16,8,128]{2,1,0:T(8,128)(2,1)S(1)} async-done(((bf16[16,8,128]{2,1,0:T(8,128)(2,1)}), bf16[16,8,128]{2,1,0:T(8,128)(2,1)S(1)}, u32[]{:S(2)}, u32[]{:S(2)}) %all-to-all-start) | async-done | bytes 32800 | tf_op jit(solution)/shard_map/all_to_all | solution.py:313
  14.7 1.8 %route.1 = s16[256,256]{1,0:T(8,128)(2,1)S(1)} custom-call(bf16[128,128]{1,0:T(8,128)(2,1)S(1)} %bitcast.12, bf16[256,512]{1,0:T(8,128)(2,1)S(1)} %get-tuple-element.14.refs_1_, s32[8,512]{1,0:T(8,128)S(1)} %get-tuple-element.15.refs_2_, bf16[256,512]{1,0:T(8,128)(2,1)S(1)} %get-tuple-element.16.refs_3_, bf16[256,1024]{1,0:T(8,128)(2,1)S(1)} %get-tuple-element.17.refs_4_, ...), custom_call_target="tpu_custom_call" | custom-call | tf_op jit(solution)/shard_map/route/pallas_call | solution.py:340
  16.5 9.5 %all_to_all.10.parts_ref = s16[8,32,256]{2,1,0:T(8,128)(2,1)S(1)} all-to-all(s16[8,32,256]{2,1,0:T(8,128)(2,1)S(1)} %bitcast.11), channel_id=1, replica_groups={{2,4,6,9,11,13,15,0},{3,5,7,8,10,12,14,1},{18,20,22,25,27,29,31,16},{19..., dimensions={0} | all-to-all | bytes 262144 | tf_op jit(solution)/shard_map/all_to_all | solution.py:348
  26.1 0.7 %finish.1 = f32[32,256]{1,0:T(8,128)} custom-call(s16[8,32,256]{2,1,0:T(8,128)(2,1)S(1)} %all_to_all.10.parts_ref), custom_call_target="tpu_custom_call" | custom-call | tf_op jit(solution)/shard_map/finish/pallas_call | solution.py:359
Async XLA Ops:
  1.4 8.0 %collective-permute-start = (bf16[272,256]{1,0:T(8,128)(2,1)S(1)}, bf16[272,256]{1,0:T(8,128)(2,1)S(1)}, u32[]{:S(2)}, u32[]{:S(2)}) collective-permute-start(bf16[272,256]{1,0:T(8,128)(2,1)S(1)} %get-tuple-element.13.own_ref), channel_id=1, source_target_pairs={{0,1},{1,0},{2,3},{3,2},{4,5},{5,4},{6,7},{7,6},{8,9},{9,8},{10,11... | collective-permute-start | bytes 417800 | tf_op jit(solution)/shard_map/ppermute | solution.py:312
  1.9 12.8 %all-to-all-start = ((bf16[16,8,128]{2,1,0:T(8,128)(2,1)}), bf16[16,8,128]{2,1,0:T(8,128)(2,1)S(1)}, u32[]{:S(2)}, u32[]{:S(2)}) async-start(bf16[16,8,128]{2,1,0:T(8,128)(2,1)} %bitcast.8), calls=%async_computation | async-start | bytes 65536 | tf_op jit(solution)/shard_map/all_to_all | solution.py:313

commit v28 on v25

--- a/solution.py
+++ b/solution.py
@@ -78,8 +78,8 @@
         pltpu.make_async_copy(source, target, arrived.at[j])
         for j, (source, target) in enumerate(zip(sources, targets))
     ]
-    for copy in copies:
-        copy.start()
+    for j, copy in enumerate(copies):
+        copy.start(priority=1 if j < 4 else 0)
     for copy in copies[:4]:
         copy.wait()
     basin, kind, lag, parent = [ref[...] for ref in scratch[:4]]
@@ -91,7 +91,7 @@
     numbers = jnp.concatenate(rows, axis=0).astype(jnp.float32)
     meta_ref[...] = jnp.concatenate([numbers] * (meta_ref.shape[0] // FIELDS), axis=0).astype(jnp.bfloat16)
     leaving = pltpu.make_async_copy(meta_ref, meta_hbm, arrived.at[len(copies)])
-    leaving.start()
+    leaving.start(priority=1)
     for copy in copies[4:8]:
         copy.wait()
     soil, area, dest, reach = [ref[...] for ref in scratch[4:]]
@@ -249,11 +249,18 @@
     flow_ref[...] = level.astype(jnp.int16)
 
 
-def finish_kernel(parts_ref, section_ref):
-    level = parts_ref[...].astype(jnp.int32)
-    flow = jnp.exp((level.astype(jnp.float32) - CODE_ZERO) * (1.0 / CODE_SCALE))
-    flow = jnp.sum(jnp.where(level == -CODE_TOP, 0.0, flow), axis=0)
-    section_ref[...] = jnp.log(1.0 + flow)
+def finish_kernel(parts_ref, section_hbm, section_ref, left):
+    copies = []
+    for j, first in enumerate(range(0, section_ref.shape[0], 16)):
+        rows = pl.ds(first, 16)
+        level = parts_ref[:, first : first + 16].astype(jnp.int32)
+        flow = jnp.exp((level.astype(jnp.float32) - CODE_ZERO) * (1.0 / CODE_SCALE))
+        flow = jnp.sum(jnp.where(level == -CODE_TOP, 0.0, flow), axis=0)
+        section_ref[first : first + 16] = jnp.log(1.0 + flow)
+        copies.append(pltpu.make_async_copy(section_ref.at[rows], section_hbm.at[rows], left.at[j]))
+        copies[-1].start()
+    for copy in copies:
+        copy.wait()
 
 
 def per_device(
@@ -353,6 +360,11 @@
     return pl.pallas_call(
         finish_kernel,
         out_shape=jax.ShapeDtypeStruct((basin_rows, hours), jnp.float32),
+        out_specs=held,
+        scratch_shapes=[
+            pltpu.VMEM((basin_rows, hours), jnp.float32),
+            pltpu.SemaphoreType.DMA((basin_rows // 16,)),
+        ],
         compiler_params=params,
         name="finish",
     )(parts)

time: 27.2 us -> 27.2 us (level)
  no operation moved by 1% of the time
where the time goes in v28:
time: 27.2 us; the launch traced here: 27 us
  blocking collectives  9.72 us (36%)
  starting transfers between devices  8.04 us (30%)
  Pallas kernels  5.57 us (20%)
  waiting for transfers between devices  3.61 us (13%)
    all_to_all x1, blocking collectives, per_device(): lax.all_to_all(flow.reshape(owners // CORES, basin_rows, hours), 'tile',...  9.72 us
    all_to_all x1, starting transfers between devices, per_device(): lax.all_to_all(meta.reshape(owners, FIELDS, LANES), 'tile', split_axis=0,...  7.53 us
    all_to_all x1, waiting for transfers between devices, per_device(): lax.all_to_all(meta.reshape(owners, FIELDS, LANES), 'tile', split_axis=0,...  3.61 us
    pallas_call x1, Pallas kernels, per_device(): pl.pallas_call(lambda *refs: route_kernel(*refs, basin_rows=basin_rows),...  1.79 us
    pallas_call x1, Pallas kernels, per_device(): pl.pallas_call(prepare_kernel, out_shape=(jax.ShapeDtypeStruct((hours, ch...  1.64 us
    pallas_call x1, Pallas kernels, per_device(): pl.pallas_call(lambda *refs: pack_kernel(*refs, basin_rows=basin_rows), o...  1.42 us
    pallas_call x1, Pallas kernels, per_device(): pl.pallas_call(finish_kernel, out_shape=jax.ShapeDtypeStruct((basin_rows,...  0.72 us
  transfers between devices with their start and end apart: 2, of which 1 were waited for; matrix products, arithmetic and copies ran while one was open for 0% of the time, Pallas kernels for 6%

profile of v28, /device:TPU:0, one launch (start us, length us, event | category | flops | bytes accessed | tf_op | source)
XLA Modules:
  0.0 27.0 jit_solution(9323123163777733159)
XLA Ops:
  0.0 1.4 %pack.1 = (bf16[128,128]{1,0:T(8,128)(2,1)}, bf16[272,256]{1,0:T(8,128)(2,1)S(1)}) custom-call(s32[1,256]{1,0:T(1,128)} %bitcast.13, s32[1,256]{1,0:T(1,128)} %bitcast.14, s32[1,256]{1,0:T(1,128)} %bitcast.15, s32[1,32]{1,0:T(1,128)} %bitcast.20, f32[1,256]{1,0:T(1,128)} %bitcast.16, f32[1,256]{1,0:T(1,128)} %bitcast.17, s32[1,256]{1,0:T(1,128)} %bitcast.18, ...), custom_call_target="tpu_custom_call" | custom-call | flops 1 | bytes 1 | tf_op jit(solution)/shard_map/pack/pallas_call | solution.py:297
  1.4 0.5 %collective-permute-start = (bf16[272,256]{1,0:T(8,128)(2,1)S(1)}, bf16[272,256]{1,0:T(8,128)(2,1)S(1)}, u32[]{:S(2)}, u32[]{:S(2)}) collective-permute-start(bf16[272,256]{1,0:T(8,128)(2,1)S(1)} %get-tuple-element.13.own_ref), channel_id=1, source_target_pairs={{0,1},{1,0},{2,3},{3,2},{4,5},{5,4},{6,7},{7,6},{8,9},{9,8},{10,11... | collective-permute-start | bytes 417800 | tf_op jit(solution)/shard_map/ppermute | solution.py:314
  1.9 7.5 %all-to-all-start = ((bf16[16,8,128]{2,1,0:T(8,128)(2,1)}), bf16[16,8,128]{2,1,0:T(8,128)(2,1)S(1)}, u32[]{:S(2)}, u32[]{:S(2)}) async-start(bf16[16,8,128]{2,1,0:T(8,128)(2,1)} %bitcast.8), calls=%async_computation | async-start | bytes 65536 | tf_op jit(solution)/shard_map/all_to_all | solution.py:315
  9.5 0.0 collective-permute-done.other_ref
  9.5 1.6 %prepare.1 = (bf16[256,512]{1,0:T(8,128)(2,1)S(1)}, s32[8,512]{1,0:T(8,128)S(1)}, bf16[256,512]{1,0:T(8,128)(2,1)S(1)}, bf16[256,1024]{1,0:T(8,128)(2,1)S(1)}, f32[4,256,512]{2,1,0:T(8,128)S(1)}) custom-call(f32[8,48]{1,0:T(8,128)} %irf_hbm.1, bf16[272,256]{1,0:T(8,128)(2,1)S(1)} %get-tuple-element.13.own_ref, ...), custom_call_target="tpu_custom_call" | custom-call | flops 1 | bytes 1 | tf_op jit(solution)/shard_map/prepare/pallas_call | solution.py:326
  11.1 3.6 %all-to-all-done = bf16[16,8,128]{2,1,0:T(8,128)(2,1)S(1)} async-done(((bf16[16,8,128]{2,1,0:T(8,128)(2,1)}), bf16[16,8,128]{2,1,0:T(8,128)(2,1)S(1)}, u32[]{:S(2)}, u32[]{:S(2)}) %all-to-all-start) | async-done | bytes 32800 | tf_op jit(solution)/shard_map/all_to_all | solution.py:315
  14.7 1.8 %route.1 = s16[256,256]{1,0:T(8,128)(2,1)S(1)} custom-call(bf16[128,128]{1,0:T(8,128)(2,1)S(1)} %bitcast.12, bf16[256,512]{1,0:T(8,128)(2,1)S(1)} %get-tuple-element.14.refs_1_, s32[8,512]{1,0:T(8,128)S(1)} %get-tuple-element.15.refs_2_, bf16[256,512]{1,0:T(8,128)(2,1)S(1)} %get-tuple-element.16.refs_3_, bf16[256,1024]{1,0:T(8,128)(2,1)S(1)} %get-tuple-element.17.refs_4_, ...), custom_call_target="tpu_custom_call" | custom-call | tf_op jit(solution)/shard_map/route/pallas_call | solution.py:342
  16.5 9.7 %all_to_all.10.parts_ref = s16[8,32,256]{2,1,0:T(8,128)(2,1)S(1)} all-to-all(s16[8,32,256]{2,1,0:T(8,128)(2,1)S(1)} %bitcast.11), channel_id=1, replica_groups={{2,4,6,8,10,12,14,0},{3,5,7,9,11,13,15,1},{18,20,22,24,26,28,30,16},{19..., dimensions={0} | all-to-all | bytes 262144 | tf_op jit(solution)/shard_map/all_to_all | solution.py:350
  26.3 0.7 %finish.1 = f32[32,256]{1,0:T(8,128)} custom-call(s16[8,32,256]{2,1,0:T(8,128)(2,1)S(1)} %all_to_all.10.parts_ref), custom_call_target="tpu_custom_call" | custom-call | tf_op jit(solution)/shard_map/finish/pallas_call | solution.py:360
Async XLA Ops:
  1.4 8.0 %collective-permute-start = (bf16[272,256]{1,0:T(8,128)(2,1)S(1)}, bf16[272,256]{1,0:T(8,128)(2,1)S(1)}, u32[]{:S(2)}, u32[]{:S(2)}) collective-permute-start(bf16[272,256]{1,0:T(8,128)(2,1)S(1)} %get-tuple-element.13.own_ref), channel_id=1, source_target_pairs={{0,1},{1,0},{2,3},{3,2},{4,5},{5,4},{6,7},{7,6},{8,9},{9,8},{10,11... | collective-permute-start | bytes 417800 | tf_op jit(solution)/shard_map/ppermute | solution.py:314
  1.9 12.8 %all-to-all-start = ((bf16[16,8,128]{2,1,0:T(8,128)(2,1)}), bf16[16,8,128]{2,1,0:T(8,128)(2,1)S(1)}, u32[]{:S(2)}, u32[]{:S(2)}) async-start(bf16[16,8,128]{2,1,0:T(8,128)(2,1)} %bitcast.8), calls=%async_computation | async-start | bytes 65536 | tf_op jit(solution)/shard_map/all_to_all | solution.py:315

commit v29 on v25

--- a/solution.py
+++ b/solution.py
@@ -249,11 +249,10 @@
     flow_ref[...] = level.astype(jnp.int16)
 
 
-def finish_kernel(parts_ref, section_ref):
-    level = parts_ref[...].astype(jnp.int32)
-    flow = jnp.exp((level.astype(jnp.float32) - CODE_ZERO) * (1.0 / CODE_SCALE))
-    flow = jnp.sum(jnp.where(level == -CODE_TOP, 0.0, flow), axis=0)
-    section_ref[...] = jnp.log(1.0 + flow)
+def finish(parts):
+    level = parts.astype(jnp.float32)
+    flow = jnp.exp((level - CODE_ZERO) * (1.0 / CODE_SCALE))
+    return jnp.log(1.0 + jnp.sum(jnp.where(level == -CODE_TOP, 0.0, flow), axis=0))
 
 
 def per_device(
@@ -350,12 +349,7 @@
         ],
         tiled=True,
     )
-    return pl.pallas_call(
-        finish_kernel,
-        out_shape=jax.ShapeDtypeStruct((basin_rows, hours), jnp.float32),
-        compiler_params=params,
-        name="finish",
-    )(parts)
+    return finish(parts)
 
 
 def solution(mesh):

time: 27.2 us -> 27.3 us (level)
  other arithmetic: 0 us -> 0.73 us
  Pallas kernels: 5.56 us -> 4.85 us
    pallas_call x1 -> x0, Pallas kernels: 0.71 us -> none  [per_device(): pl.pallas_call(finish_kernel, out_shape=jax.ShapeDtypeStruct((basin_rows,...]
    log x0 -> x1, other arithmetic: none -> 0.63 us  [finish(): jnp.log(1.0 + jnp.sum(jnp.where(level == -CODE_TOP, 0.0, flow), axis=0))]
where the time goes in v29:
time: 27.3 us; the launch traced here: 27 us
  blocking collectives  9.72 us (36%)
  starting transfers between devices  8.04 us (29%)
  Pallas kernels  4.85 us (18%)
  waiting for transfers between devices  3.61 us (13%)
  other arithmetic  0.73 us (3%)
    all_to_all x1, blocking collectives, per_device(): lax.all_to_all(flow.reshape(owners // CORES, basin_rows, hours), 'tile',...  9.72 us
    all_to_all x1, starting transfers between devices, per_device(): lax.all_to_all(meta.reshape(owners, FIELDS, LANES), 'tile', split_axis=0,...  7.53 us
    all_to_all x1, waiting for transfers between devices, per_device(): lax.all_to_all(meta.reshape(owners, FIELDS, LANES), 'tile', split_axis=0,...  3.61 us
    pallas_call x1, Pallas kernels, per_device(): pl.pallas_call(lambda *refs: route_kernel(*refs, basin_rows=basin_rows),...  1.79 us
    pallas_call x1, Pallas kernels, per_device(): pl.pallas_call(prepare_kernel, out_shape=(jax.ShapeDtypeStruct((hours, ch...  1.64 us
    pallas_call x1, Pallas kernels, per_device(): pl.pallas_call(lambda *refs: pack_kernel(*refs, basin_rows=basin_rows), o...  1.42 us
    log x1, other arithmetic, finish(): jnp.log(1.0 + jnp.sum(jnp.where(level == -CODE_TOP, 0.0, flow), axis=0))  0.63 us
  transfers between devices with their start and end apart: 2, of which 1 were waited for; matrix products, arithmetic and copies ran while one was open for 0% of the time, Pallas kernels for 6%

profile of v29, /device:TPU:0, one launch (start us, length us, event | category | flops | bytes accessed | tf_op | source)
XLA Modules:
  0.0 27.0 jit_solution(8973129996406166824)
XLA Ops:
  0.0 1.4 %pack.1 = (bf16[128,128]{1,0:T(8,128)(2,1)}, bf16[272,256]{1,0:T(8,128)(2,1)S(1)}) custom-call(s32[1,256]{1,0:T(1,128)} %bitcast.13, s32[1,256]{1,0:T(1,128)} %bitcast.14, s32[1,256]{1,0:T(1,128)} %bitcast.15, s32[1,32]{1,0:T(1,128)} %bitcast.20, f32[1,256]{1,0:T(1,128)} %bitcast.16, f32[1,256]{1,0:T(1,128)} %bitcast.17, s32[1,256]{1,0:T(1,128)} %bitcast.18, ...), custom_call_target="tpu_custom_call" | custom-call | flops 1 | bytes 1 | tf_op jit(solution)/shard_map/pack/pallas_call | solution.py:289
  1.4 0.5 %collective-permute-start = (bf16[272,256]{1,0:T(8,128)(2,1)S(1)}, bf16[272,256]{1,0:T(8,128)(2,1)S(1)}, u32[]{:S(2)}, u32[]{:S(2)}) collective-permute-start(bf16[272,256]{1,0:T(8,128)(2,1)S(1)} %get-tuple-element.13.own_ref), channel_id=1, source_target_pairs={{0,1},{1,0},{2,3},{3,2},{4,5},{5,4},{6,7},{7,6},{8,9},{9,8},{10,11... | collective-permute-start | bytes 417800 | tf_op jit(solution)/shard_map/ppermute | solution.py:306
  1.9 7.5 %all-to-all-start = ((bf16[16,8,128]{2,1,0:T(8,128)(2,1)}), bf16[16,8,128]{2,1,0:T(8,128)(2,1)S(1)}, u32[]{:S(2)}, u32[]{:S(2)}) async-start(bf16[16,8,128]{2,1,0:T(8,128)(2,1)} %bitcast.8), calls=%async_computation | async-start | bytes 65536 | tf_op jit(solution)/shard_map/all_to_all | solution.py:307
  9.5 0.0 collective-permute-done.other_ref
  9.5 1.6 %prepare.1 = (bf16[256,512]{1,0:T(8,128)(2,1)S(1)}, s32[8,512]{1,0:T(8,128)S(1)}, bf16[256,512]{1,0:T(8,128)(2,1)S(1)}, bf16[256,1024]{1,0:T(8,128)(2,1)S(1)}, f32[4,256,512]{2,1,0:T(8,128)S(1)}) custom-call(f32[8,48]{1,0:T(8,128)} %irf_hbm.1, bf16[272,256]{1,0:T(8,128)(2,1)S(1)} %get-tuple-element.13.own_ref, ...), custom_call_target="tpu_custom_call" | custom-call | flops 1 | bytes 1 | tf_op jit(solution)/shard_map/prepare/pallas_call | solution.py:318
  11.1 3.6 %all-to-all-done = bf16[16,8,128]{2,1,0:T(8,128)(2,1)S(1)} async-done(((bf16[16,8,128]{2,1,0:T(8,128)(2,1)}), bf16[16,8,128]{2,1,0:T(8,128)(2,1)S(1)}, u32[]{:S(2)}, u32[]{:S(2)}) %all-to-all-start) | async-done | bytes 32800 | tf_op jit(solution)/shard_map/all_to_all | solution.py:307
  14.7 1.8 %route.1 = s16[256,256]{1,0:T(8,128)(2,1)S(1)} custom-call(bf16[128,128]{1,0:T(8,128)(2,1)S(1)} %bitcast.12, bf16[256,512]{1,0:T(8,128)(2,1)S(1)} %get-tuple-element.14.refs_1_, s32[8,512]{1,0:T(8,128)S(1)} %get-tuple-element.15.refs_2_, bf16[256,512]{1,0:T(8,128)(2,1)S(1)} %get-tuple-element.16.refs_3_, bf16[256,1024]{1,0:T(8,128)(2,1)S(1)} %get-tuple-element.17.refs_4_, ...), custom_call_target="tpu_custom_call" | custom-call | tf_op jit(solution)/shard_map/route/pallas_call | solution.py:334
  16.5 9.7 %all_to_all.10 = s16[8,32,256]{2,1,0:T(8,128)(2,1)S(1)} all-to-all(s16[8,32,256]{2,1,0:T(8,128)(2,1)S(1)} %bitcast.11), channel_id=1, replica_groups={{2,4,6,8,10,12,14,0},{3,5,7,9,11,13,15,1},{18,20,22,24,26,28,30,16},{19..., dimensions={0} | all-to-all | bytes 262144 | tf_op jit(solution)/shard_map/all_to_all | solution.py:342
  26.3 0.1 fusion.3
  26.4 0.6 %add_log_fusion = f32[32,256]{1,0:T(8,128)} fusion(f32[32,256]{1,0:T(8,128)S(1)} %fusion.3), kind=kLoop, calls=%fused_computation.6 | loop fusion | flops 8192 | bytes 65536 | tf_op jit(solution)/shard_map/log | solution.py:255
Async XLA Ops:
  1.4 8.0 %collective-permute-start = (bf16[272,256]{1,0:T(8,128)(2,1)S(1)}, bf16[272,256]{1,0:T(8,128)(2,1)S(1)}, u32[]{:S(2)}, u32[]{:S(2)}) collective-permute-start(bf16[272,256]{1,0:T(8,128)(2,1)S(1)} %get-tuple-element.13.own_ref), channel_id=1, source_target_pairs={{0,1},{1,0},{2,3},{3,2},{4,5},{5,4},{6,7},{7,6},{8,9},{9,8},{10,11... | collective-permute-start | bytes 417800 | tf_op jit(solution)/shard_map/ppermute | solution.py:306
  1.9 12.8 %all-to-all-start = ((bf16[16,8,128]{2,1,0:T(8,128)(2,1)}), bf16[16,8,128]{2,1,0:T(8,128)(2,1)S(1)}, u32[]{:S(2)}, u32[]{:S(2)}) async-start(bf16[16,8,128]{2,1,0:T(8,128)(2,1)} %bitcast.8), calls=%async_computation | async-start | bytes 65536 | tf_op jit(solution)/shard_map/all_to_all | solution.py:307

commit v30 on v26

--- a/solution.py
+++ b/solution.py
@@ -36,6 +36,20 @@
 
 def one_hot(row, count):
     return (iota((count, row.shape[1]), 0) == row).astype(jnp.float32).astype(jnp.bfloat16)
+
+
+def moves(owners):
+    quarter = owners // 4
+    return ((2 * quarter, quarter - CORES), (3 * quarter, -quarter - CORES))
+
+
+def place_of(owner, owners):
+    if owner < CORES:
+        return owner + owners - CORES
+    place = owner - CORES
+    for start, moved in moves(owners):
+        place = owner + moved if owner >= start else place
+    return place
 
 
 def later_rows(values, hours):
@@ -176,7 +190,11 @@
         return stack_ref[pl.ds(field, owners, stride=FIELDS), :].astype(jnp.bfloat16)
 
     def picked(values, owner):
-        chosen = iota((owners, tiles), 0) == owners - 1 - owner
+        place = owner - CORES
+        for start, moved in moves(owners):
+            place = jnp.where(owner >= start, owner + moved, place)
+        place = jnp.where(owner < CORES, owner + owners - CORES, place)
+        chosen = iota((owners, tiles), 0) == jnp.where(owner < 0, owners, place)
         return jnp.sum(jnp.where(chosen, values, 0.0), axis=0, keepdims=True).astype(jnp.int32)
 
     spans = (FIELDS - 2) // 3
@@ -309,7 +327,7 @@
         "tile",
         split_axis=0,
         concat_axis=0,
-        axis_index_groups=[[*range(owners)][::-1]],
+        axis_index_groups=[sorted(range(owners), key=lambda owner: place_of(owner, owners))],
         tiled=True,
     ).reshape(-1, LANES)
 

time: 28.1 us -> 27.3 us (0.972)
  waiting for transfers between devices: 0.84 us -> 3.41 us
  blocking collectives: 11.8 us -> 9.95 us
  starting transfers between devices: 9.59 us -> 8.04 us
    all_to_all x1, waiting for transfers between devices: 0.84 us -> 3.41 us  [per_device(): lax.all_to_all(meta.reshape(owners, FIELDS, LANES), 'tile', split_axis=0,...]
    all_to_all x1, blocking collectives: 11.8 us -> 9.95 us  [per_device(): lax.all_to_all(flow.reshape(owners // CORES, basin_rows, hours), 'tile',...]
    all_to_all x1, starting transfers between devices: 9.07 us -> 7.53 us  [per_device(): lax.all_to_all(meta.reshape(owners, FIELDS, LANES), 'tile', split_axis=0,...]
where the time goes in v30:
time: 27.3 us; the launch traced here: 27 us
  blocking collectives  9.95 us (36%)
  starting transfers between devices  8.04 us (29%)
  Pallas kernels  5.57 us (20%)
  waiting for transfers between devices  3.41 us (12%)
    all_to_all x1, blocking collectives, per_device(): lax.all_to_all(flow.reshape(owners // CORES, basin_rows, hours), 'tile',...  9.95 us
    all_to_all x1, starting transfers between devices, per_device(): lax.all_to_all(meta.reshape(owners, FIELDS, LANES), 'tile', split_axis=0,...  7.53 us
    all_to_all x1, waiting for transfers between devices, per_device(): lax.all_to_all(meta.reshape(owners, FIELDS, LANES), 'tile', split_axis=0,...  3.41 us
    pallas_call x1, Pallas kernels, per_device(): pl.pallas_call(lambda *refs: route_kernel(*refs, basin_rows=basin_rows),...  1.8 us
    pallas_call x1, Pallas kernels, per_device(): pl.pallas_call(prepare_kernel, out_shape=(jax.ShapeDtypeStruct((hours, ch...  1.64 us
    pallas_call x1, Pallas kernels, per_device(): pl.pallas_call(lambda *refs: pack_kernel(*refs, basin_rows=basin_rows), o...  1.42 us
    pallas_call x1, Pallas kernels, per_device(): pl.pallas_call(finish_kernel, out_shape=jax.ShapeDtypeStruct((basin_rows,...  0.71 us
  transfers between devices with their start and end apart: 2, of which 1 were waited for; matrix products, arithmetic and copies ran while one was open for 0% of the time, Pallas kernels for 6%

profile of v30, /device:TPU:0, one launch (start us, length us, event | category | flops | bytes accessed | tf_op | source)
XLA Modules:
  0.0 27.0 jit_solution(15677116678517078264)
XLA Ops:
  0.0 1.4 %pack.1 = (bf16[128,128]{1,0:T(8,128)(2,1)}, bf16[272,256]{1,0:T(8,128)(2,1)S(1)}) custom-call(s32[1,256]{1,0:T(1,128)} %bitcast.13, s32[1,256]{1,0:T(1,128)} %bitcast.14, s32[1,256]{1,0:T(1,128)} %bitcast.15, s32[1,32]{1,0:T(1,128)} %bitcast.20, f32[1,256]{1,0:T(1,128)} %bitcast.16, f32[1,256]{1,0:T(1,128)} %bitcast.17, s32[1,256]{1,0:T(1,128)} %bitcast.18, ...), custom_call_target="tpu_custom_call" | custom-call | flops 1 | bytes 1 | tf_op jit(solution)/shard_map/pack/pallas_call | solution.py:307
  1.4 0.5 %collective-permute-start = (bf16[272,256]{1,0:T(8,128)(2,1)S(1)}, bf16[272,256]{1,0:T(8,128)(2,1)S(1)}, u32[]{:S(2)}, u32[]{:S(2)}) collective-permute-start(bf16[272,256]{1,0:T(8,128)(2,1)S(1)} %get-tuple-element.13.own_ref), channel_id=1, source_target_pairs={{0,1},{1,0},{2,3},{3,2},{4,5},{5,4},{6,7},{7,6},{8,9},{9,8},{10,11... | collective-permute-start | bytes 417800 | tf_op jit(solution)/shard_map/ppermute | solution.py:324
  1.9 7.5 %all-to-all-start = ((bf16[16,8,128]{2,1,0:T(8,128)(2,1)}), bf16[16,8,128]{2,1,0:T(8,128)(2,1)S(1)}, u32[]{:S(2)}, u32[]{:S(2)}) async-start(bf16[16,8,128]{2,1,0:T(8,128)(2,1)} %bitcast.8), calls=%async_computation | async-start | bytes 65536 | tf_op jit(solution)/shard_map/all_to_all | solution.py:325
  9.5 0.0 collective-permute-done.other_ref
  9.5 1.6 %prepare.1 = (bf16[256,512]{1,0:T(8,128)(2,1)S(1)}, s32[8,512]{1,0:T(8,128)S(1)}, bf16[256,512]{1,0:T(8,128)(2,1)S(1)}, bf16[256,1024]{1,0:T(8,128)(2,1)S(1)}, f32[4,256,512]{2,1,0:T(8,128)S(1)}) custom-call(f32[8,48]{1,0:T(8,128)} %irf_hbm.1, bf16[272,256]{1,0:T(8,128)(2,1)S(1)} %get-tuple-element.13.own_ref, ...), custom_call_target="tpu_custom_call" | custom-call | flops 1 | bytes 1 | tf_op jit(solution)/shard_map/prepare/pallas_call | solution.py:336
  11.1 3.4 %all-to-all-done = bf16[16,8,128]{2,1,0:T(8,128)(2,1)S(1)} async-done(((bf16[16,8,128]{2,1,0:T(8,128)(2,1)}), bf16[16,8,128]{2,1,0:T(8,128)(2,1)S(1)}, u32[]{:S(2)}, u32[]{:S(2)}) %all-to-all-start) | async-done | bytes 32800 | tf_op jit(solution)/shard_map/all_to_all | solution.py:325
  14.5 1.8 %route.1 = s16[256,256]{1,0:T(8,128)(2,1)S(1)} custom-call(bf16[128,128]{1,0:T(8,128)(2,1)S(1)} %bitcast.12, bf16[256,512]{1,0:T(8,128)(2,1)S(1)} %get-tuple-element.14.refs_1_, s32[8,512]{1,0:T(8,128)S(1)} %get-tuple-element.15.refs_2_, bf16[256,512]{1,0:T(8,128)(2,1)S(1)} %get-tuple-element.16.refs_3_, bf16[256,1024]{1,0:T(8,128)(2,1)S(1)} %get-tuple-element.17.refs_4_, ...), custom_call_target="tpu_custom_call" | custom-call | tf_op jit(solution)/shard_map/route/pallas_call | solution.py:352
  16.3 10.0 %all_to_all.10.parts_ref = s16[8,32,256]{2,1,0:T(8,128)(2,1)S(1)} all-to-all(s16[8,32,256]{2,1,0:T(8,128)(2,1)S(1)} %bitcast.11), channel_id=1, replica_groups={{2,4,6,8,10,12,14,0},{3,5,7,9,11,13,15,1},{18,20,22,24,26,28,30,16},{19..., dimensions={0} | all-to-all | bytes 262144 | tf_op jit(solution)/shard_map/all_to_all | solution.py:360
  26.3 0.7 %finish.1 = f32[32,256]{1,0:T(8,128)} custom-call(s16[8,32,256]{2,1,0:T(8,128)(2,1)S(1)} %all_to_all.10.parts_ref), custom_call_target="tpu_custom_call" | custom-call | tf_op jit(solution)/shard_map/finish/pallas_call | solution.py:370
Async XLA Ops:
  1.4 8.0 %collective-permute-start = (bf16[272,256]{1,0:T(8,128)(2,1)S(1)}, bf16[272,256]{1,0:T(8,128)(2,1)S(1)}, u32[]{:S(2)}, u32[]{:S(2)}) collective-permute-start(bf16[272,256]{1,0:T(8,128)(2,1)S(1)} %get-tuple-element.13.own_ref), channel_id=1, source_target_pairs={{0,1},{1,0},{2,3},{3,2},{4,5},{5,4},{6,7},{7,6},{8,9},{9,8},{10,11... | collective-permute-start | bytes 417800 | tf_op jit(solution)/shard_map/ppermute | solution.py:324
  1.9 12.6 %all-to-all-start = ((bf16[16,8,128]{2,1,0:T(8,128)(2,1)}), bf16[16,8,128]{2,1,0:T(8,128)(2,1)S(1)}, u32[]{:S(2)}, u32[]{:S(2)}) async-start(bf16[16,8,128]{2,1,0:T(8,128)(2,1)} %bitcast.8), calls=%async_computation | async-start | bytes 65536 | tf_op jit(solution)/shard_map/all_to_all | solution.py:325

commit v31 on v25

--- a/solution.py
+++ b/solution.py
@@ -176,7 +176,9 @@
         return stack_ref[pl.ds(field, owners, stride=FIELDS), :].astype(jnp.bfloat16)
 
     def picked(values, owner):
-        place = jnp.where(owner < 0, owners, jnp.where(owner < CORES, owner + owners, owner) - CORES)
+        place = jnp.where(owner < 2 * CORES, owner + owners - 3 * CORES, owner - 2 * CORES)
+        place = jnp.where(owner < CORES, owner + owners - CORES, place)
+        place = jnp.where(owner < 0, owners, place)
         chosen = iota((owners, tiles), 0) == place
         return jnp.sum(jnp.where(chosen, values, 0.0), axis=0, keepdims=True).astype(jnp.int32)
 
@@ -310,7 +312,9 @@
         "tile",
         split_axis=0,
         concat_axis=0,
-        axis_index_groups=[[*range(CORES, owners), *range(CORES)]],
+        axis_index_groups=[
+            [*range(2 * CORES, owners), *range(CORES, 2 * CORES), *range(CORES)]
+        ],
         tiled=True,
     ).reshape(-1, LANES)
 

time: 27.2 us -> 27.5 us (1.011)
  blocking collectives: 9.72 us -> 10.2 us
    all_to_all x1, blocking collectives: 9.72 us -> 10.2 us  [per_device(): lax.all_to_all(flow.reshape(owners // CORES, basin_rows, hours), 'tile',...]
where the time goes in v31:
time: 27.5 us; the launch traced here: 27.2 us
  blocking collectives  10.2 us (37%)
  starting transfers between devices  8.04 us (29%)
  Pallas kernels  5.57 us (20%)
  waiting for transfers between devices  3.37 us (12%)
    all_to_all x1, blocking collectives, per_device(): lax.all_to_all(flow.reshape(owners // CORES, basin_rows, hours), 'tile',...  10.2 us
    all_to_all x1, starting transfers between devices, per_device(): lax.all_to_all(meta.reshape(owners, FIELDS, LANES), 'tile', split_axis=0,...  7.53 us
    all_to_all x1, waiting for transfers between devices, per_device(): lax.all_to_all(meta.reshape(owners, FIELDS, LANES), 'tile', split_axis=0,...  3.37 us
    pallas_call x1, Pallas kernels, per_device(): pl.pallas_call(lambda *refs: route_kernel(*refs, basin_rows=basin_rows),...  1.8 us
    pallas_call x1, Pallas kernels, per_device(): pl.pallas_call(prepare_kernel, out_shape=(jax.ShapeDtypeStruct((hours, ch...  1.64 us
    pallas_call x1, Pallas kernels, per_device(): pl.pallas_call(lambda *refs: pack_kernel(*refs, basin_rows=basin_rows), o...  1.42 us
    pallas_call x1, Pallas kernels, per_device(): pl.pallas_call(finish_kernel, out_shape=jax.ShapeDtypeStruct((basin_rows,...  0.71 us
  transfers between devices with their start and end apart: 2, of which 1 were waited for; matrix products, arithmetic and copies ran while one was open for 0% of the time, Pallas kernels for 6%

profile of v31, /device:TPU:0, one launch (start us, length us, event | category | flops | bytes accessed | tf_op | source)
XLA Modules:
  0.0 27.2 jit_solution(12980738671362295551)
XLA Ops:
  0.0 1.4 %pack.1 = (bf16[128,128]{1,0:T(8,128)(2,1)}, bf16[272,256]{1,0:T(8,128)(2,1)S(1)}) custom-call(s32[1,256]{1,0:T(1,128)} %bitcast.13, s32[1,256]{1,0:T(1,128)} %bitcast.14, s32[1,256]{1,0:T(1,128)} %bitcast.15, s32[1,32]{1,0:T(1,128)} %bitcast.20, f32[1,256]{1,0:T(1,128)} %bitcast.16, f32[1,256]{1,0:T(1,128)} %bitcast.17, s32[1,256]{1,0:T(1,128)} %bitcast.18, ...), custom_call_target="tpu_custom_call" | custom-call | flops 1 | bytes 1 | tf_op jit(solution)/shard_map/pack/pallas_call | solution.py:292
  1.4 0.5 %collective-permute-start = (bf16[272,256]{1,0:T(8,128)(2,1)S(1)}, bf16[272,256]{1,0:T(8,128)(2,1)S(1)}, u32[]{:S(2)}, u32[]{:S(2)}) collective-permute-start(bf16[272,256]{1,0:T(8,128)(2,1)S(1)} %get-tuple-element.13.own_ref), channel_id=1, source_target_pairs={{0,1},{1,0},{2,3},{3,2},{4,5},{5,4},{6,7},{7,6},{8,9},{9,8},{10,11... | collective-permute-start | bytes 417800 | tf_op jit(solution)/shard_map/ppermute | solution.py:309
  1.9 7.5 %all-to-all-start = ((bf16[16,8,128]{2,1,0:T(8,128)(2,1)}), bf16[16,8,128]{2,1,0:T(8,128)(2,1)S(1)}, u32[]{:S(2)}, u32[]{:S(2)}) async-start(bf16[16,8,128]{2,1,0:T(8,128)(2,1)} %bitcast.8), calls=%async_computation | async-start | bytes 65536 | tf_op jit(solution)/shard_map/all_to_all | solution.py:310
  9.5 0.0 collective-permute-done.other_ref
  9.5 1.6 %prepare.1 = (bf16[256,512]{1,0:T(8,128)(2,1)S(1)}, s32[8,512]{1,0:T(8,128)S(1)}, bf16[256,512]{1,0:T(8,128)(2,1)S(1)}, bf16[256,1024]{1,0:T(8,128)(2,1)S(1)}, f32[4,256,512]{2,1,0:T(8,128)S(1)}) custom-call(f32[8,48]{1,0:T(8,128)} %irf_hbm.1, bf16[272,256]{1,0:T(8,128)(2,1)S(1)} %get-tuple-element.13.own_ref, ...), custom_call_target="tpu_custom_call" | custom-call | flops 1 | bytes 1 | tf_op jit(solution)/shard_map/prepare/pallas_call | solution.py:323
  11.1 3.4 %all-to-all-done = bf16[16,8,128]{2,1,0:T(8,128)(2,1)S(1)} async-done(((bf16[16,8,128]{2,1,0:T(8,128)(2,1)}), bf16[16,8,128]{2,1,0:T(8,128)(2,1)S(1)}, u32[]{:S(2)}, u32[]{:S(2)}) %all-to-all-start) | async-done | bytes 32800 | tf_op jit(solution)/shard_map/all_to_all | solution.py:310
  14.5 1.8 %route.1 = s16[256,256]{1,0:T(8,128)(2,1)S(1)} custom-call(bf16[128,128]{1,0:T(8,128)(2,1)S(1)} %bitcast.12, bf16[256,512]{1,0:T(8,128)(2,1)S(1)} %get-tuple-element.14.refs_1_, s32[8,512]{1,0:T(8,128)S(1)} %get-tuple-element.15.refs_2_, bf16[256,512]{1,0:T(8,128)(2,1)S(1)} %get-tuple-element.16.refs_3_, bf16[256,1024]{1,0:T(8,128)(2,1)S(1)} %get-tuple-element.17.refs_4_, ...), custom_call_target="tpu_custom_call" | custom-call | tf_op jit(solution)/shard_map/route/pallas_call | solution.py:339
  16.3 10.2 %all_to_all.10.parts_ref = s16[8,32,256]{2,1,0:T(8,128)(2,1)S(1)} all-to-all(s16[8,32,256]{2,1,0:T(8,128)(2,1)S(1)} %bitcast.11), channel_id=1, replica_groups={{2,4,6,8,10,12,14,0},{3,5,7,9,11,13,15,1},{18,20,22,24,26,28,30,16},{19..., dimensions={0} | all-to-all | bytes 262144 | tf_op jit(solution)/shard_map/all_to_all | solution.py:347
  26.5 0.7 %finish.1 = f32[32,256]{1,0:T(8,128)} custom-call(s16[8,32,256]{2,1,0:T(8,128)(2,1)S(1)} %all_to_all.10.parts_ref), custom_call_target="tpu_custom_call" | custom-call | tf_op jit(solution)/shard_map/finish/pallas_call | solution.py:357
Async XLA Ops:
  1.4 8.0 %collective-permute-start = (bf16[272,256]{1,0:T(8,128)(2,1)S(1)}, bf16[272,256]{1,0:T(8,128)(2,1)S(1)}, u32[]{:S(2)}, u32[]{:S(2)}) collective-permute-start(bf16[272,256]{1,0:T(8,128)(2,1)S(1)} %get-tuple-element.13.own_ref), channel_id=1, source_target_pairs={{0,1},{1,0},{2,3},{3,2},{4,5},{5,4},{6,7},{7,6},{8,9},{9,8},{10,11... | collective-permute-start | bytes 417800 | tf_op jit(solution)/shard_map/ppermute | solution.py:309
  1.9 12.5 %all-to-all-start = ((bf16[16,8,128]{2,1,0:T(8,128)(2,1)}), bf16[16,8,128]{2,1,0:T(8,128)(2,1)S(1)}, u32[]{:S(2)}, u32[]{:S(2)}) async-start(bf16[16,8,128]{2,1,0:T(8,128)(2,1)} %bitcast.8), calls=%async_computation | async-start | bytes 65536 | tf_op jit(solution)/shard_map/all_to_all | solution.py:310
